TPU v7x, 128 devices: a whole 4x4x4 slice. The times are simulated.
128 devices in a mesh: doc: 8 (over x, core), ctx: 16 (over y, z).
Axes of the slice: x: 4, y: 4, z: 4, core: 2. Of those that a mesh axis runs over, the one named last changes fastest.
Arguments:
- queries: bfloat16 [8, 2048, 4096], P('doc', 'ctx'), may hold values from -8 to 8
- image_kv: bfloat16 [32, 256, 1024], P('doc', 'ctx'), may hold values from -4 to 4
- d_out: bfloat16 [8, 2048, 4096], P('doc', 'ctx'), may hold values from -24 to 24
- attn_gate: float32 [1], replicated, may hold values from 0.4 to 2
- image_slots: int32 [32], replicated, may hold values from 0 to 31, as said below
- spans: int32 [8, 2048, 2], P('doc', 'ctx'), may hold values from 0 to 4, as said below
Outputs:
- d_queries: bfloat16 [8, 2048, 4096], P('doc', 'ctx')
- d_image_kv: float32 [32, 256, 1024], P('doc', 'ctx')
Inputs may be any that keep to these rules, and one draw needn't show every extreme that they name: `image_slots`: A permutation of the 32 slots; slots s with s // 4 = g form owner group g. No owner group holds two images of one document. spans[d, t, 0] < spans[d, t, 1]; both never decrease along a document's text; the first token sees image 0 and the last token's second entry is 4.
All inputs are finite; a program needn't handle non-finite values.
Results may differ from a plain program's by a relative error of at most 0.022.
Values may be sent and summed in bfloat16 or wider, within the bound.
No kernel may reach another device: no remote copies, remote signals or barrier semaphores. Data moves between devices by JAX's collectives and lax.ppermute only.
A program may use at most 128 MiB of HBM per device.

v0:
```python
import jax
import jax.numpy as jnp
from jax import lax
from jax.sharding import PartitionSpec as P

KEY_VALUE_HEADS = 4
HEAD_WIDTH = 128
HEAD_GROUP_SIZE = 8
KEY_COLUMNS = 512


negative_bound = -1e30


def split_heads(weight_matrix, token_rows):
    return (
        weight_matrix.reshape(token_rows, KEY_VALUE_HEADS, HEAD_GROUP_SIZE, HEAD_WIDTH)
        .transpose(1, 0, 2, 3)
        .reshape(KEY_VALUE_HEADS, token_rows * HEAD_GROUP_SIZE, HEAD_WIDTH)
    )


def merge_heads(weight_matrix, token_rows):
    return (
        weight_matrix.reshape(KEY_VALUE_HEADS, token_rows, HEAD_GROUP_SIZE, HEAD_WIDTH)
        .transpose(1, 0, 2, 3)
        .reshape(token_rows, KEY_VALUE_HEADS * HEAD_GROUP_SIZE * HEAD_WIDTH)
    )


def shards(queries, image_kv, d_out, attn_gate, image_slots, spans):
    document_slices = image_kv.shape[0]
    doc_count = lax.axis_size("doc")
    group_me = lax.axis_index("doc")
    doc_slots = lax.dynamic_slice_in_dim(image_slots, group_me * document_slices, document_slices)
    every_slot = lax.all_gather(image_kv, "doc", axis=0, tiled=True)
    local_rows = jnp.take(every_slot, doc_slots, axis=0)
    key_value_rows = lax.all_gather(local_rows, "ctx", axis=1, tiled=True)
    token_rows = queries.shape[1]
    key_row_block = key_value_rows.shape[1]
    score_scale = HEAD_WIDTH ** (-0.5)
    gate_factor = jnp.tanh(attn_gate[0])
    d_attn = (gate_factor * d_out[0].astype(jnp.float32)).astype(jnp.bfloat16)
    q_heads = split_heads(queries[0], token_rows)
    d_heads = split_heads(d_attn, token_rows)
    span_low = spans[0, :, 0]
    span_high = spans[0, :, 1]
    every_key = key_value_rows[:, :, :KEY_COLUMNS].reshape(
        document_slices, key_row_block, KEY_VALUE_HEADS, HEAD_WIDTH
    )
    every_value = key_value_rows[:, :, KEY_COLUMNS:].reshape(
        document_slices, key_row_block, KEY_VALUE_HEADS, HEAD_WIDTH
    )
    visible_mask = []
    anyone = []
    for slot_pos in range(document_slices):
        seen_mask = (span_low <= slot_pos) & (slot_pos < span_high)
        visible_mask.append(jnp.repeat(seen_mask, HEAD_GROUP_SIZE))
        anyone.append(jnp.any(seen_mask))

    def scores_of(slot_pos):
        return (
            jnp.einsum(
                "hqd,khd->hqk", q_heads, every_key[slot_pos], preferred_element_type=jnp.float32
            )
            * score_scale
        )

    row_maximum = jnp.full(
        (KEY_VALUE_HEADS, token_rows * HEAD_GROUP_SIZE), negative_bound, jnp.float32
    )
    row_total_sum = jnp.zeros((KEY_VALUE_HEADS, token_rows * HEAD_GROUP_SIZE), jnp.float32)
    for slot_pos in range(document_slices):

        def stats_step(slot_pos=slot_pos, row_maximum=row_maximum, row_total_sum=row_total_sum):
            mask_now = visible_mask[slot_pos][None, :, None]
            scores = jnp.where(mask_now, scores_of(slot_pos), negative_bound)
            new_max = jnp.maximum(row_maximum, jnp.max(scores, axis=2))
            terms = jnp.where(mask_now, jnp.exp(scores - new_max[:, :, None]), 0.0)
            return (
                new_max,
                row_total_sum * jnp.exp(row_maximum - new_max) + jnp.sum(terms, axis=2),
            )

        row_maximum, row_total_sum = stats_step()

    def probs_of(slot_pos):
        mask_now = visible_mask[slot_pos][None, :, None]
        return (
            jnp.where(mask_now, jnp.exp(scores_of(slot_pos) - row_maximum[:, :, None]), 0.0)
            / row_total_sum[:, :, None]
        )

    attention_output = jnp.zeros(
        (KEY_VALUE_HEADS, token_rows * HEAD_GROUP_SIZE, HEAD_WIDTH), jnp.float32
    )
    for slot_pos in range(document_slices):

        def out_step(slot_pos=slot_pos, attention_output=attention_output):
            probs_low = probs_of(slot_pos).astype(jnp.bfloat16)
            return attention_output + jnp.einsum(
                "hqk,khd->hqd", probs_low, every_value[slot_pos], preferred_element_type=jnp.float32
            )

        attention_output = out_step()
    delta = jnp.sum(d_heads.astype(jnp.float32) * attention_output, axis=2)
    query_gradient = jnp.zeros(
        (KEY_VALUE_HEADS, token_rows * HEAD_GROUP_SIZE, HEAD_WIDTH), jnp.float32
    )
    partials = []
    for slot_pos in range(document_slices):

        def grad_step(slot_pos=slot_pos, query_gradient=query_gradient):
            probs = probs_of(slot_pos)
            d_probs = jnp.einsum(
                "hqd,khd->hqk", d_heads, every_value[slot_pos], preferred_element_type=jnp.float32
            )
            d_scores = (probs * (d_probs - delta[:, :, None])).astype(jnp.bfloat16)
            probs_low = probs.astype(jnp.bfloat16)
            new_query = query_gradient + jnp.einsum(
                "hqk,khd->hqd", d_scores, every_key[slot_pos], preferred_element_type=jnp.float32
            )
            d_keys = (
                jnp.einsum("hqk,hqd->khd", d_scores, q_heads, preferred_element_type=jnp.float32)
                * score_scale
            )
            d_values = jnp.einsum(
                "hqk,hqd->khd", probs_low, d_heads, preferred_element_type=jnp.float32
            )
            joined = jnp.concatenate(
                [
                    d_keys.reshape(key_row_block, KEY_COLUMNS),
                    d_values.reshape(key_row_block, KEY_COLUMNS),
                ],
                axis=1,
            )
            return (new_query, joined)

        query_gradient, block_grad = grad_step()
        partials.append(block_grad)
    d_queries = merge_heads(query_gradient * score_scale, token_rows).astype(jnp.bfloat16)[None]
    reduced = lax.psum_scatter(
        jnp.stack(partials).astype(jnp.bfloat16), "ctx", scatter_dimension=1, tiled=True
    ).astype(jnp.float32)
    table = (
        jnp.zeros((doc_count * document_slices,) + reduced.shape[1:], jnp.float32)
        .at[doc_slots]
        .set(reduced)
    )
    d_image_kv = lax.psum_scatter(
        table.astype(jnp.bfloat16), "doc", scatter_dimension=0, tiled=True
    ).astype(jnp.float32)
    return (d_queries, d_image_kv)


def solution(mesh):
    return jax.shard_map(
        shards,
        mesh=mesh,
        in_specs=(
            P("doc", "ctx", None),
            P("doc", "ctx", None),
            P("doc", "ctx", None),
            P(),
            P(),
            P("doc", "ctx", None),
        ),
        out_specs=(P("doc", "ctx", None), P("doc", "ctx", None)),
        check_vma=False,
    )
```

profile of v0, /device:TPU:1, one launch (start us, length us, event | category | flops | bytes accessed | tf_op | source)
XLA Modules:
  0.0 280.1 jit_solution(2854739930816849866)
XLA Ops:
  8.7 28.0 %all-gather.3.cloned.1.call-done = bf16[32,16,1024]{2,1,0:T(8,128)(2,1)} async-done(((bf16[4,16,1024]{2,1,0:T(8,128)(2,1)}), bf16[32,16,1024]{2,1,0:T(8,128)(2,1)}) %all-gather.3.cloned.1.call-update) | async-done | bytes 1048592 | tf_op jit(solution)/shard_map/all_gather | solution.py:36
  36.7 1.8 gather_fusion
  46.1 37.1 %all-gather.5.cloned.1.call-done = bf16[4,256,1024]{2,1,0:T(8,128)(2,1)} async-done(((bf16[4,16,1024]{2,1,0:T(8,128)(2,1)}), bf16[4,256,1024]{2,1,0:T(8,128)(2,1)}) %all-gather.5.cloned.1.call-update) | async-done | bytes 2097168 | tf_op jit(solution)/shard_map/all_gather | solution.py:38
  83.2 2.6 fusion.47
  90.8 2.0 fusion.12
  92.9 2.2 fusion.6
  95.1 2.0 convolution_convert_fusion.3
  97.1 2.0 convolution_convert_fusion.2
  99.2 4.8 %fusion.22 = f32[4,1024,128]{1,2,0:T(8,128)} fusion(bf16[256,4,128]{0,2,1:T(8,128)(2,1)S(1)} %bitcast.212, f32[4,256,1024]{2,1,0:T(8,128)} %copy-done.6, f32[4,1024]{1,0:T(4,128)S(1)} %multiply_add_fusion, f32[4,1024]{1,0:T(4,128)S(1)} %get-tuple-element.2, pred[1024]{0:T(1024)(128)(4,1)S(1)} %broadcast_in_dim.166), kind=kOutput, calls=%fused_computation.56 | convolution fusion | flops 273678336 | bytes 6587392 | tf_op jit(solution)/shard_map/hqk,khd->hqd/dot_general | solution.py:101
  104.1 4.8 %fusion.21 = f32[4,1024,128]{1,2,0:T(8,128)} fusion(bf16[256,4,128]{0,2,1:T(8,128)(2,1)S(1)} %bitcast.216, f32[4,256,1024]{2,1,0:T(8,128)} %copy-done.4, f32[4,1024]{1,0:T(4,128)S(1)} %multiply_add_fusion, f32[4,1024]{1,0:T(4,128)S(1)} %get-tuple-element.2, pred[1024]{0:T(1024)(128)(4,1)S(1)} %broadcast_in_dim.158), kind=kOutput, calls=%fused_computation.55 | convolution fusion | flops 273678336 | bytes 6587392 | tf_op jit(solution)/shard_map/hqk,khd->hqd/dot_general | solution.py:101
  109.1 4.7 %fusion.23 = f32[4,1024,128]{1,2,0:T(8,128)} fusion(bf16[256,4,128]{0,2,1:T(8,128)(2,1)S(1)} %bitcast.214, f32[4,256,1024]{2,1,0:T(8,128)} %copy-done.2, f32[4,1024]{1,0:T(4,128)S(1)} %multiply_add_fusion, f32[4,1024]{1,0:T(4,128)S(1)} %get-tuple-element.2, pred[1024]{0:T(1024)(128)(4,1)S(1)} %broadcast_in_dim.169), kind=kOutput, calls=%fused_computation.57 | convolution fusion | flops 273678336 | bytes 6587392 | tf_op jit(solution)/shard_map/hqk,khd->hqd/dot_general | solution.py:101
  114.0 5.9 %multiply_reduce_fusion = f32[4,1024]{1,0:T(4,128)S(1)} fusion(f32[4,1024,128]{1,2,0:T(8,128)} %fusion.23, f32[4,1024,128]{1,2,0:T(8,128)} %fusion.21, f32[4,1024,128]{1,2,0:T(8,128)} %fusion.22, bf16[4,1024,128]{1,2,0:T(8,128)(2,1)} %copy.180, bf16[256,4,128]{0,2,1:T(8,128)(2,1)S(1)} %bitcast.208, f32[4,256,1024]{2,1,0:T(8,128)} %copy-done, ...), kind=kOutput, calls=%fused_computation.40 | convolution fusion | flops 276819968 | bytes 11846656 | tf_op jit(solution)/shard_map/hqk,khd->hqd/dot_general | solution.py:101
  119.9 2.8 fusion.3
  122.7 2.7 fusion.2
  125.4 1.9 convolution_convert_fusion.1
  127.4 3.0 %fusion.1 = bf16[4,1024,256]{1,2,0:T(8,128)(2,1)} fusion(bf16[256,4,128]{0,2,1:T(8,128)(2,1)S(1)} %bitcast.215, f32[4,1024]{1,0:T(4,128)S(1)} %multiply_reduce_fusion, bf16[4,128,8,128]{3,2,1,0:T(8,128)(2,1)S(1)} %copy.177, f32[4,1024]{1,0:T(4,128)S(1)} %multiply_add_fusion, f32[4,1024]{1,0:T(4,128)S(1)} %get-tuple-element.2, ...), kind=kOutput, calls=%fused_computation.7 | convolution fusion | flops 275775488 | bytes 7652352 | tf_op jit(solution)/shard_map/hqd,khd->hqk/dot_general | solution.py:115
  130.3 1.9 convolution_convert_fusion
  132.3 2.6 fusion
  134.9 2.0 copy.209
  136.9 3.1 %fusion.17 = bf16[4,256,128]{1,2,0:T(8,128)(2,1)} fusion(bf16[4,1024,256]{1,2,0:T(8,128)(2,1)} %fusion.3, bf16[4,128,8,128]{3,2,1,0:T(8,128)(2,1)S(1)} %copy.168), kind=kOutput, calls=%fused_computation.47 | convolution fusion | flops 268697600 | bytes 3407872 | tf_op jit(solution)/shard_map/hqk,hqd->khd/dot_general | solution.py:124
  140.0 1.8 copy.208
  141.8 1.8 copy.215
  143.6 3.1 %fusion.18 = bf16[4,256,128]{1,2,0:T(8,128)(2,1)} fusion(bf16[4,1024,256]{1,2,0:T(8,128)(2,1)} %fusion.2, bf16[4,128,8,128]{3,2,1,0:T(8,128)(2,1)S(1)} %copy.168), kind=kOutput, calls=%fused_computation.48 | convolution fusion | flops 268697600 | bytes 3407872 | tf_op jit(solution)/shard_map/hqk,hqd->khd/dot_general | solution.py:124
  146.7 1.8 copy.214
  148.5 1.8 copy.221
  150.4 3.1 %fusion.19 = bf16[4,256,128]{1,2,0:T(8,128)(2,1)} fusion(bf16[4,1024,256]{1,2,0:T(8,128)(2,1)} %fusion.1, bf16[4,128,8,128]{3,2,1,0:T(8,128)(2,1)S(1)} %copy.168), kind=kOutput, calls=%fused_computation.49 | convolution fusion | flops 268697600 | bytes 3407872 | tf_op jit(solution)/shard_map/hqk,hqd->khd/dot_general | solution.py:124
  153.5 1.8 copy.220
  155.3 1.8 copy.227
  165.7 73.3 %reduce-scatter.3.cloned.1.call-done = bf16[4,16,1024]{2,1,0:T(8,128)(2,1)} async-done(((bf16[4,256,1024]{2,1,0:T(8,128)(2,1)}), bf16[4,16,1024]{2,1,0:T(8,128)(2,1)}) %reduce-scatter.3.cloned.1.call-update) | async-done | bytes 131088 | tf_op jit(solution)/shard_map/reduce_scatter | solution.py:142
  242.0 2.7 fusion.49
  249.1 22.9 %reduce-scatter.5.cloned.1.call-done = bf16[4,16,1024]{2,1,0:T(8,128)(2,1)} async-done(((bf16[32,16,1024]{2,1,0:T(8,128)(2,1)}), bf16[4,16,1024]{2,1,0:T(8,128)(2,1)}) %reduce-scatter.5.cloned.1.call-update) | async-done | bytes 131088 | tf_op jit(solution)/shard_map/reduce_scatter | solution.py:150
  272.0 1.6 convert_element_type.90
  (112 shorter events, 29.7 us)
Async XLA Ops:
  7.2 34.5 %copy-start.27 = (s32[1,128,2]{1,2,0:T(2,128)S(1)}, s32[1,128,2]{1,2,0:T(2,128)}, u32[]{:S(2)}) copy-start(s32[1,128,2]{1,2,0:T(2,128)} %param.11) | copy-start | bytes 3076
  7.2 35.3 %copy-start.22 = (bf16[1,128,4096]{2,1,0:T(8,128)(2,1)S(1)}, bf16[1,128,4096]{2,1,0:T(8,128)(2,1)}, u32[]{:S(2)}) copy-start(bf16[1,128,4096]{2,1,0:T(8,128)(2,1)} %param.8) | copy-start | bytes 3145732
  7.2 29.5 %all-gather.3.cloned.1.call-start = ((), (), s32[]{:S(2)}) async-start(), calls=%async_computation.2 | async-start | bytes 1179648 | tf_op jit(solution)/shard_map/all_gather | solution.py:36
  7.9 75.3 %all-gather.5.cloned.1.call-start = ((), (), s32[]{:S(2)}) async-start(), calls=%async_computation.3 | async-start | bytes 2228224 | tf_op jit(solution)/shard_map/all_gather | solution.py:38
  39.3 199.7 %reduce-scatter.3.cloned.1.call-start = ((), (), s32[]{:S(2)}) async-start(), calls=%async_computation.4 | async-start | bytes 2228224 | tf_op jit(solution)/shard_map/reduce_scatter | solution.py:142
  44.8 85.5 %copy-start.12 = (bf16[4,128,8,128]{3,2,1,0:T(8,128)(2,1)}, bf16[4,128,8,128]{3,2,1,0:T(8,128)(2,1)S(1)}, u32[]{:S(2)}) copy-start(bf16[4,128,8,128]{3,2,1,0:T(8,128)(2,1)S(1)} %copy.177) | copy-start | bytes 3145732
  85.9 3.2 %copy-start.13 = (bf16[1,256,512]{1,2,0:T(8,128)(2,1)}, bf16[1,256,512]{1,2,0:T(8,128)(2,1)S(1)}, u32[]{:S(2)}) copy-start(bf16[1,256,512]{1,2,0:T(8,128)(2,1)S(1)} %copy.166) | copy-start | bytes 786436
  86.2 2.9 %copy-start.15 = (bf16[1,256,512]{1,2,0:T(8,128)(2,1)}, bf16[1,256,512]{1,2,0:T(8,128)(2,1)S(1)}, u32[]{:S(2)}) copy-start(bf16[1,256,512]{1,2,0:T(8,128)(2,1)S(1)} %copy.172) | copy-start | bytes 786436
  87.4 2.6 copy-start.17
  88.2 6.9 %copy-start.4 = (f32[4,256,1024]{2,1,0:T(8,128)}, f32[4,256,1024]{2,1,0:T(8,128)S(1)}, u32[]{:S(2)}) copy-start(f32[4,256,1024]{2,1,0:T(8,128)S(1)} %get-tuple-element.27) | copy-start | bytes 12582916
  89.1 3.8 %copy-start = (f32[4,256,1024]{2,1,0:T(8,128)}, f32[4,256,1024]{2,1,0:T(8,128)S(1)}, u32[]{:S(2)}) copy-start(f32[4,256,1024]{2,1,0:T(8,128)S(1)} %get-tuple-element.21) | copy-start | bytes 12582916
  90.0 2.9 %copy-start.2 = (f32[4,256,1024]{2,1,0:T(8,128)}, f32[4,256,1024]{2,1,0:T(8,128)S(1)}, u32[]{:S(2)}) copy-start(f32[4,256,1024]{2,1,0:T(8,128)S(1)} %get-tuple-element.23) | copy-start | bytes 12582916
  90.8 6.3 %copy-start.6 = (f32[4,256,1024]{2,1,0:T(8,128)}, f32[4,256,1024]{2,1,0:T(8,128)S(1)}, u32[]{:S(2)}) copy-start(f32[4,256,1024]{2,1,0:T(8,128)S(1)} %get-tuple-element.25) | copy-start | bytes 12582916
  97.1 2.0 copy-start.21
  99.2 4.8 %copy-start.20 = (bf16[1,256,512]{2,1,0:T(8,128)(2,1)S(1)}, bf16[1,256,512]{2,1,0:T(8,128)(2,1)}, u32[]{:S(2)}) copy-start(bf16[1,256,512]{2,1,0:T(8,128)(2,1)} %get-tuple-element.10) | copy-start | bytes 786436
  104.1 4.8 %copy-start.25 = (bf16[1,256,512]{1,2,0:T(8,128)(2,1)}, bf16[1,256,512]{1,2,0:T(8,128)(2,1)S(1)}, u32[]{:S(2)}) copy-start(bf16[1,256,512]{1,2,0:T(8,128)(2,1)S(1)} %copy.178) | copy-start | bytes 786436
  104.1 4.8 %copy-start.19 = (bf16[1,256,512]{2,1,0:T(8,128)(2,1)S(1)}, bf16[1,256,512]{2,1,0:T(8,128)(2,1)}, u32[]{:S(2)}) copy-start(bf16[1,256,512]{2,1,0:T(8,128)(2,1)} %get-tuple-element.9) | copy-start | bytes 786436
  114.0 5.9 %copy-start.23 = (bf16[1,256,512]{1,2,0:T(8,128)(2,1)}, bf16[1,256,512]{1,2,0:T(8,128)(2,1)S(1)}, u32[]{:S(2)}) copy-start(bf16[1,256,512]{1,2,0:T(8,128)(2,1)S(1)} %copy.186) | copy-start | bytes 786436
  114.0 5.9 %copy-start.5 = (f32[4,256,1024]{2,1,0:T(8,128)S(1)}, f32[4,256,1024]{2,1,0:T(8,128)}, u32[]{:S(2)}) copy-start(f32[4,256,1024]{2,1,0:T(8,128)} %copy-done.4) | copy-start | bytes 12582916
  114.0 5.9 %copy-start.26 = (bf16[1,256,512]{1,2,0:T(8,128)(2,1)S(1)}, bf16[1,256,512]{1,2,0:T(8,128)(2,1)}, u32[]{:S(2)}) copy-start(bf16[1,256,512]{1,2,0:T(8,128)(2,1)} %copy-done.25) | copy-start | bytes 786436
  119.9 2.8 copy-start.7
  122.7 2.7 copy-start.3
  127.4 3.0 %copy-start.1 = (f32[4,256,1024]{2,1,0:T(8,128)S(1)}, f32[4,256,1024]{2,1,0:T(8,128)}, u32[]{:S(2)}) copy-start(f32[4,256,1024]{2,1,0:T(8,128)} %copy-done) | copy-start | bytes 12582916
  130.3 1.9 copy-start.24
  134.9 22.2 %copy-start.8 = (bf16[4,1024,256]{1,2,0:T(8,128)(2,1)}, bf16[4,1024,256]{1,2,0:T(8,128)(2,1)S(1)}, u32[]{:S(2)}) copy-start(bf16[4,1024,256]{1,2,0:T(8,128)(2,1)S(1)} %fusion) | copy-start | bytes 6291460
  165.6 76.4 %copy-start.18 = (bf16[1,256,512]{1,2,0:T(8,128)(2,1)S(1)}, bf16[1,256,512]{1,2,0:T(8,128)(2,1)}, u32[]{:S(2)}) copy-start(bf16[1,256,512]{1,2,0:T(8,128)(2,1)} %copy-done.17) | copy-start | bytes 786436
  165.6 106.4 %reduce-scatter.5.cloned.1.call-start = ((), (), s32[]{:S(2)}) async-start(), calls=%async_computation.5 | async-start | bytes 1179648 | tf_op jit(solution)/shard_map/reduce_scatter | solution.py:150
  240.8 3.9 %copy-start.14 = (bf16[1,256,512]{1,2,0:T(8,128)(2,1)S(1)}, bf16[1,256,512]{1,2,0:T(8,128)(2,1)}, u32[]{:S(2)}) copy-start(bf16[1,256,512]{1,2,0:T(8,128)(2,1)} %copy-done.13) | copy-start | bytes 786436
  241.9 2.7 copy-start.10
  242.0 3.6 %copy-start.11 = (bf16[4,1024,256]{1,2,0:T(8,128)(2,1)S(1)}, bf16[4,1024,256]{1,2,0:T(8,128)(2,1)}, u32[]{:S(2)}) copy-start(bf16[4,1024,256]{1,2,0:T(8,128)(2,1)} %fusion.1) | copy-start | bytes 6291460
  242.0 3.6 %copy-start.16 = (bf16[1,256,512]{1,2,0:T(8,128)(2,1)S(1)}, bf16[1,256,512]{1,2,0:T(8,128)(2,1)}, u32[]{:S(2)}) copy-start(bf16[1,256,512]{1,2,0:T(8,128)(2,1)} %copy-done.15) | copy-start | bytes 786436
  244.7 1.9 copy-start.9
Sparse Core Ops, SparseCore 0:
  9.7 26.9 all-gather.2
  39.5 43.6 all-gather.4
  165.7 73.1 reduce-scatter.2
  242.1 29.8 reduce-scatter.4
where the time goes:
time: 283 us; the launch traced here: 280 us
  waiting for transfers between devices  162 us (57%)
  matrix products  58.8 us (21%)
  local copies, waits for them, and re-layouts  28.6 us (10%)
  other arithmetic  15.5 us (5%)
  between operations  15.1 us (5%)
    reduce_scatter x1, waiting for transfers between devices, shards(): lax.psum_scatter(jnp.stack(partials).astype(jnp.bfloat16), 'ctx', scatter...  73.3 us
    all_gather x1, waiting for transfers between devices, shards(): key_value_rows = lax.all_gather(local_rows, 'ctx', axis=1, tiled=True)  37.1 us
    all_gather x1, waiting for transfers between devices, shards(): every_slot = lax.all_gather(image_kv, 'doc', axis=0, tiled=True)  28 us
    reduce_scatter x1, waiting for transfers between devices, shards(): lax.psum_scatter(table.astype(jnp.bfloat16), 'doc', scatter_dimension=0,...  22.9 us
    dot_general x4, matrix products, out_step(): jnp.einsum('hqk,khd->hqd', probs_low, every_value[slot_pos], preferred_el...  20.2 us
    dot_general x4, matrix products, grad_step(): jnp.einsum('hqd,khd->hqk', d_heads, every_value[slot_pos], preferred_elem...  11.1 us
    dot_general x4, matrix products, grad_step(): jnp.einsum('hqk,hqd->khd', d_scores, q_heads, preferred_element_type=jnp....  10.9 us
    dot_general x4, matrix products, grad_step(): jnp.einsum('hqk,hqd->khd', probs_low, d_heads, preferred_element_type=jnp...  7.8 us
  transfers between devices with their start and end apart: 4, of which 4 were waited for; matrix products, arithmetic and copies ran while one was open for 5% of the time, Pallas kernels for 0%

commit v1 on v0

v1 whole, which is shorter than its diff:
```python
import functools

import jax
import jax.numpy as jnp
from jax import lax
from jax.experimental import pallas as pl
from jax.experimental.pallas import tpu as pltpu
from jax.sharding import PartitionSpec as P

KV_HEADS = 4
WIDTH = 128
GROUP = 8
KEY_COLUMNS = 512
IMAGES = 4
LOW = -1e30
SCALE = WIDTH ** (-0.5)
LOG2E = 1.4426950408889634
VMEM_LIMIT = 48 * 1024 * 1024

SMEM = pltpu.MemorySpace.SMEM
VMEM = pltpu.MemorySpace.VMEM


def pack_kernel(docs, me, slots, kv, out):
    for d in range(docs):
        local = 0
        for j in range(IMAGES):
            s = slots[d * IMAGES + j]
            local += jnp.where(s // IMAGES == me[0], s % IMAGES, 0)
        out[d] = kv[local]


def pick_kernel(me, slots, got, out):
    for j in range(IMAGES):
        out[j] = got[slots[me[0] * IMAGES + j] // IMAGES]


def grad_kernel(steps, gate, spans, q, d_out, keys, values, dq, dkv, acc, keys_t):
    step = pl.program_id(1)
    rows = 2 * WIDTH

    @pl.when(step == 0)
    def _():
        keys_t[...] = keys[...].T

    def rows_of(ref):
        return jnp.concatenate([ref[:, :WIDTH], ref[:, WIDTH:]], axis=0)

    q_rows = rows_of(q)
    factor = jnp.tanh(gate[...])
    d_rows = (rows_of(d_out).astype(jnp.float32) * factor).astype(jnp.bfloat16)
    nt = (((1,), (1,)), ((), ()))
    scores = lax.dot_general(keys[...], q_rows, nt, preferred_element_type=jnp.float32)
    d_probs = lax.dot_general(values[...], d_rows, nt, preferred_element_type=jnp.float32)
    low = jnp.concatenate([spans[0:1, :], spans[0:1, :]], axis=1)
    high = jnp.concatenate([spans[1:2, :], spans[1:2, :]], axis=1)
    scores = scores.reshape(-1, IMAGES, 16, rows)
    d_probs = d_probs.reshape(-1, IMAGES, 16, rows)
    seen = [(low <= j) & (j < high) for j in range(IMAGES)]
    row_max = None
    for j in range(IMAGES):
        top = jnp.max(jnp.max(scores[:, j], axis=0), axis=0, keepdims=True)
        top = jnp.where(seen[j], top, LOW)
        row_max = top if row_max is None else jnp.maximum(row_max, top)
    row_max = row_max * (SCALE * LOG2E)
    terms = []
    total = 0.0
    dots = 0.0
    for j in range(IMAGES):
        term = jnp.exp2(scores[:, j] * (SCALE * LOG2E) - jnp.where(seen[j], row_max, -LOW))
        total += jnp.sum(jnp.sum(term, axis=0), axis=0, keepdims=True)
        dots += jnp.sum(jnp.sum(term * d_probs[:, j], axis=0), axis=0, keepdims=True)
        terms.append(term)
    inverse = 1.0 / total
    delta = dots * inverse
    low_probs = []
    d_scores = []
    for j in range(IMAGES):
        probs = terms[j] * inverse
        low_probs.append(probs.astype(jnp.bfloat16)[:, None])
        d_scores.append((probs * (d_probs[:, j] - delta)).astype(jnp.bfloat16)[:, None])
    low_probs = jnp.concatenate(low_probs, axis=1).reshape(-1, rows)
    d_scores = jnp.concatenate(d_scores, axis=1).reshape(-1, rows)
    d_keys = jnp.dot(d_scores, q_rows, preferred_element_type=jnp.float32)
    d_values = jnp.dot(low_probs, d_rows, preferred_element_type=jnp.float32)
    dq_t = jnp.dot(keys_t[...], d_scores, preferred_element_type=jnp.float32) * SCALE
    dq_rows = dq_t.T.astype(jnp.bfloat16)
    dq[:, :WIDTH] = dq_rows[:WIDTH]
    dq[:, WIDTH:] = dq_rows[WIDTH:]

    @pl.when(step == 0)
    def _():
        acc[:, :WIDTH] = d_keys
        acc[:, WIDTH:] = d_values

    @pl.when(step > 0)
    def _():
        acc[:, :WIDTH] += d_keys
        acc[:, WIDTH:] += d_values

    @pl.when(step == steps - 1)
    def _():
        dkv[:, :WIDTH] = (acc[:, :WIDTH] * SCALE).astype(jnp.bfloat16)
        dkv[:, WIDTH:] = acc[:, WIDTH:].astype(jnp.bfloat16)


def gradients(gate, spans, q, d_out, kv):
    tokens = q.shape[0]
    key_rows = kv.shape[0]
    steps = GROUP // 2
    block = lambda c, i: (0, c * steps + i)
    return pl.pallas_call(
        functools.partial(grad_kernel, steps),
        grid=(KV_HEADS, steps),
        in_specs=[
            pl.BlockSpec((1, 1), lambda c, i: (0, 0)),
            pl.BlockSpec((2, tokens), lambda c, i: (0, 0)),
            pl.BlockSpec((tokens, 2 * WIDTH), block),
            pl.BlockSpec((tokens, 2 * WIDTH), block),
            pl.BlockSpec((key_rows, WIDTH), lambda c, i: (0, c)),
            pl.BlockSpec((key_rows, WIDTH), lambda c, i: (0, KV_HEADS + c)),
        ],
        out_specs=[
            pl.BlockSpec((tokens, 2 * WIDTH), block),
            pl.BlockSpec((key_rows, 2 * WIDTH), lambda c, i: (0, c)),
        ],
        out_shape=[
            jax.ShapeDtypeStruct(q.shape, jnp.bfloat16),
            jax.ShapeDtypeStruct((key_rows, 2 * KEY_COLUMNS), jnp.bfloat16),
        ],
        scratch_shapes=[
            pltpu.VMEM((key_rows, 2 * WIDTH), jnp.float32),
            pltpu.VMEM((WIDTH, key_rows), jnp.bfloat16),
        ],
        compiler_params=pltpu.CompilerParams(vmem_limit_bytes=VMEM_LIMIT),
        name="gradients",
    )(gate, spans, q, d_out, kv, kv)


def sum_kernel(me, slots, got, out):
    out[...] = jnp.zeros_like(out)
    for j in range(IMAGES):
        total = got[0, j].astype(jnp.float32)
        for part in range(1, got.shape[0]):
            total += got[part, j].astype(jnp.float32)
        out[slots[me[0] * IMAGES + j] // IMAGES] = total.astype(jnp.bfloat16)


def place_kernel(docs, me, slots, got, out):
    for s in range(IMAGES):
        doc = 0
        for d in range(docs):
            for j in range(IMAGES):
                doc += jnp.where(slots[d * IMAGES + j] == me[0] * IMAGES + s, d, 0)
        rows = got[doc].astype(jnp.float32)
        for c in range(KV_HEADS):
            at = 2 * c * WIDTH
            out[s, :, c * WIDTH : (c + 1) * WIDTH] = rows[:, at : at + WIDTH]
            out[s, :, KEY_COLUMNS + c * WIDTH : KEY_COLUMNS + (c + 1) * WIDTH] = rows[
                :, at + WIDTH : at + 2 * WIDTH
            ]


def small(kernel, out_shape, name):
    return pl.pallas_call(
        kernel,
        in_specs=[
            pl.BlockSpec(memory_space=SMEM),
            pl.BlockSpec(memory_space=SMEM),
            pl.BlockSpec(memory_space=VMEM),
        ],
        out_specs=pl.BlockSpec(memory_space=VMEM),
        out_shape=out_shape,
        compiler_params=pltpu.CompilerParams(vmem_limit_bytes=VMEM_LIMIT),
        name=name,
    )


def shards(queries, image_kv, d_out, attn_gate, image_slots, spans):
    docs = lax.axis_size("doc")
    texts = lax.axis_size("ctx")
    me = lax.axis_index("doc").astype(jnp.int32)[None]
    images, rows, columns = image_kv.shape
    block = jax.ShapeDtypeStruct((docs, rows, columns), jnp.bfloat16)
    send = small(functools.partial(pack_kernel, docs), block, "pack")(me, image_slots, image_kv)
    got = lax.all_to_all(send, "doc", 0, 0)
    local = small(pick_kernel, jax.ShapeDtypeStruct(image_kv.shape, jnp.bfloat16), "pick")(
        me, image_slots, got
    )
    kv = lax.all_to_all(jnp.broadcast_to(local[None], (texts,) + local.shape), "ctx", 0, 0)
    d_queries, d_kv = gradients(
        attn_gate.reshape(1, 1),
        spans[0].T,
        queries[0],
        d_out[0],
        kv.reshape(texts * images * rows, columns),
    )
    parts = lax.all_to_all(d_kv.reshape(texts, images, rows, columns), "ctx", 0, 0)
    send = small(sum_kernel, block, "sum")(me, image_slots, parts)
    got = lax.all_to_all(send, "doc", 0, 0)
    d_image_kv = small(
        functools.partial(place_kernel, docs),
        jax.ShapeDtypeStruct(image_kv.shape, jnp.float32),
        "place",
    )(me, image_slots, got)
    return d_queries[None], d_image_kv


def solution(mesh):
    return jax.shard_map(
        shards,
        mesh=mesh,
        in_specs=(
            P("doc", "ctx", None),
            P("doc", "ctx", None),
            P("doc", "ctx", None),
            P(),
            P(),
            P("doc", "ctx", None),
        ),
        out_specs=(P("doc", "ctx", None), P("doc", "ctx", None)),
        check_vma=False,
    )
```

time: 283 us -> 125 us (0.44)
  waiting for transfers between devices: 162 us -> 25.1 us
  matrix products: 58.8 us -> 0 us
  blocking collectives: 0 us -> 56 us
  Pallas kernels: 0 us -> 31.3 us
  local copies, waits for them, and re-layouts: 28.6 us -> 3.13 us
  other arithmetic: 15.5 us -> 0 us
  between operations: 15.1 us -> 1.33 us
  starting transfers between devices: 0.16 us -> 7.95 us
    reduce_scatter x2 -> x0, waiting for transfers between devices: 96.2 us -> none  [the longest x1 73.3 us: shards(): lax.psum_scatter(jnp.stack(partials).astype(jnp.bfloat16), 'ctx', scatter...]
    all_gather x2 -> x0, waiting for transfers between devices: 65.1 us -> none  [the longest x1 37.1 us: shards(): key_value_rows = lax.all_gather(local_rows, 'ctx', axis=1, tiled=True)]
    dot_general x24 -> x0, matrix products: 58.8 us -> none  [the longest x4 20.2 us: out_step(): jnp.einsum('hqk,khd->hqd', probs_low, every_value[slot_pos], preferred_el...]
    all_to_all x0 -> x3, blocking collectives: none -> 56 us  [the longest x1 30.2 us: shards(): lax.all_to_all(d_kv.reshape(texts, images, rows, columns), 'ctx', 0, 0)]
    pallas_call x0 -> x5, Pallas kernels: none -> 31.3 us  [the longest x1 27.8 us: gradients(): pl.pallas_call(functools.partial(grad_kernel, steps), grid=(KV_HEADS, ste...]
    all_to_all x0 -> x1, waiting for transfers between devices: none -> 25.1 us  [shards(): lax.all_to_all(jnp.broadcast_to(local[None], (texts,) + local.shape), 'ct...]
    reshape x9 -> x0, local copies, waits for them, and re-layouts: 15.2 us -> none  [the longest x4 7.38 us: grad_step(): d_values.reshape(key_row_block, KEY_COLUMNS)]
    all_to_all x0 -> x1, starting transfers between devices: none -> 7.95 us  [shards(): lax.all_to_all(jnp.broadcast_to(local[None], (texts,) + local.shape), 'ct...]
  transfers between devices with their start and end apart: 4 -> 1, of which waited for: 4 -> 1; matrix products, arithmetic and copies ran while one was open for 5% -> 0% of each run, Pallas kernels for 0% -> 0%
where the time goes in v1:
time: 125 us
  blocking collectives  56 us (45%)
  Pallas kernels  31.3 us (25%)
  waiting for transfers between devices  25.1 us (20%)
  starting transfers between devices  7.95 us (6%)
  local copies, waits for them, and re-layouts  3.13 us (3%)
  between operations  1.33 us (1%)
    all_to_all x1, blocking collectives, shards(): lax.all_to_all(d_kv.reshape(texts, images, rows, columns), 'ctx', 0, 0)  30.2 us
    pallas_call x1, Pallas kernels, gradients(): pl.pallas_call(functools.partial(grad_kernel, steps), grid=(KV_HEADS, ste...  27.8 us
    all_to_all x2, blocking collectives, shards(): got = lax.all_to_all(send, 'doc', 0, 0)  25.8 us
    all_to_all x1, waiting for transfers between devices, shards(): lax.all_to_all(jnp.broadcast_to(local[None], (texts,) + local.shape), 'ct...  25.1 us
    all_to_all x1, starting transfers between devices, shards(): lax.all_to_all(jnp.broadcast_to(local[None], (texts,) + local.shape), 'ct...  7.95 us
  transfers between devices with their start and end apart: 1, of which 1 were waited for; matrix products, arithmetic and copies ran while one was open for 0% of the time, Pallas kernels for 0%

profile of v1, /device:TPU:1, one launch (start us, length us, event | category | flops | bytes accessed | tf_op | source)
XLA Modules:
  0.0 124.9 jit_solution(15195820175162651962)
XLA Ops:
  0.6 0.0 copy-start.2
  0.6 0.9 copy-done.2
  1.5 0.0 copy-start.3
  1.5 0.7 copy-done.3
  2.2 0.7 pack.1
  2.9 12.1 %all_to_all.20.got = bf16[8,16,1024]{2,1,0:T(8,128)(2,1)S(1)} all-to-all(bf16[8,16,1024]{2,1,0:T(8,128)(2,1)S(1)} %pack.1), channel_id=1, replica_groups=mesh['doc'=8,'ctx'=16] {'doc'}, dimensions={0} | all-to-all | bytes 524288 | tf_op jit(solution)/shard_map/all_to_all | solution.py:186
  15.0 0.6 pick.1
  15.6 1.6 %broadcast_in_dim.13 = bf16[16,4,16,1024]{3,2,1,0:T(8,128)(2,1)} broadcast(bf16[4,16,1024]{2,1,0:T(8,128)(2,1)S(1)} %pick.1), dimensions={1,2,3} | broadcast | bytes 2228224 | tf_op jit(solution)/shard_map/broadcast_in_dim | solution.py:190
  17.2 0.0 copy-start
  17.2 0.0 copy-start.1
  17.2 0.0 copy-start.5
  17.2 8.0 %all-to-all-start.1 = ((bf16[16,4,16,1024]{3,2,1,0:T(8,128)(2,1)}), bf16[16,4,16,1024]{3,2,1,0:T(8,128)(2,1)}, u32[]{:S(2)}, u32[]{:S(2)}) async-start(bf16[16,4,16,1024]{3,2,1,0:T(8,128)(2,1)} %broadcast_in_dim.13), calls=%async_computation.1 | async-start | bytes 4194304 | tf_op jit(solution)/shard_map/all_to_all | solution.py:190
  25.8 25.1 %all-to-all-done.1 = bf16[16,4,16,1024]{3,2,1,0:T(8,128)(2,1)} async-done(((bf16[16,4,16,1024]{3,2,1,0:T(8,128)(2,1)}), bf16[16,4,16,1024]{3,2,1,0:T(8,128)(2,1)}, u32[]{:S(2)}, u32[]{:S(2)}) %all-to-all-start.1) | async-done | bytes 2097184 | tf_op jit(solution)/shard_map/all_to_all | solution.py:190
  51.0 0.0 copy-done
  51.0 0.0 copy-done.1
  51.0 0.0 copy-done.5
  51.0 27.8 %gradients.1 = (bf16[128,4096]{1,0:T(8,128)(2,1)}, bf16[1024,1024]{1,0:T(8,128)(2,1)S(1)}) custom-call(f32[1,1]{1,0:T(1,128)} %bitcast.10.gate, s32[2,128]{1,0:T(2,128)S(1)} %bitcast.14, bf16[128,4096]{1,0:T(8,128)(2,1)S(1)} %bitcast.12, bf16[128,4096]{1,0:T(8,128)(2,1)S(1)} %bitcast.13, bf16[1024,1024]{1,0:T(8,128)(2,1)} %bitcast.6.keys.values, ...), custom_call_target="tpu_custom_call" | custom-call | tf_op jit(solution)/shard_map/gradients/pallas_call | solution.py:112
  78.7 0.0 copy-start.4
  78.7 30.2 %all_to_all.21.got = bf16[16,4,16,1024]{3,2,1,0:T(8,128)(2,1)S(1)} all-to-all(bf16[16,4,16,1024]{3,2,1,0:T(8,128)(2,1)S(1)} %bitcast.11), channel_id=1, replica_groups=mesh['doc'=8,'ctx'=16] {'ctx'}, dimensions={0} | all-to-all | bytes 4194304 | tf_op jit(solution)/shard_map/all_to_all | solution.py:198
  108.9 0.0 copy-done.4
  108.9 0.8 sum.1
  109.7 13.7 %all_to_all.22.got = bf16[8,16,1024]{2,1,0:T(8,128)(2,1)S(1)} all-to-all(bf16[8,16,1024]{2,1,0:T(8,128)(2,1)S(1)} %sum.1), channel_id=1, replica_groups=mesh['doc'=8,'ctx'=16] {'doc'}, dimensions={0} | all-to-all | bytes 524288 | tf_op jit(solution)/shard_map/all_to_all | solution.py:200
  123.5 1.4 %place.1 = f32[4,16,1024]{2,1,0:T(8,128)} custom-call(s32[1]{0:T(128)} %bitcast.5.me, s32[32]{0:T(128)S(1)} %copy-done.4, bf16[8,16,1024]{2,1,0:T(8,128)(2,1)S(1)} %all_to_all.22.got), custom_call_target="tpu_custom_call" | custom-call | tf_op jit(solution)/shard_map/place/pallas_call | solution.py:201
Async XLA Ops:
  0.6 0.9 copy-start.2
  1.5 0.7 copy-start.3
  17.2 33.8 %copy-start = (bf16[1,128,4096]{2,1,0:T(8,128)(2,1)S(1)}, bf16[1,128,4096]{2,1,0:T(8,128)(2,1)}, u32[]{:S(2)}) copy-start(bf16[1,128,4096]{2,1,0:T(8,128)(2,1)} %param.6) | copy-start | bytes 3145732
  17.2 33.8 %copy-start.1 = (bf16[1,128,4096]{2,1,0:T(8,128)(2,1)S(1)}, bf16[1,128,4096]{2,1,0:T(8,128)(2,1)}, u32[]{:S(2)}) copy-start(bf16[1,128,4096]{2,1,0:T(8,128)(2,1)} %param.8) | copy-start | bytes 3145732
  17.2 33.8 %copy-start.5 = (s32[1,128,2]{1,2,0:T(2,128)S(1)}, s32[1,128,2]{1,2,0:T(2,128)}, u32[]{:S(2)}) copy-start(s32[1,128,2]{1,2,0:T(2,128)} %param.11) | copy-start | bytes 3076
  17.2 33.8 %all-to-all-start.1 = ((bf16[16,4,16,1024]{3,2,1,0:T(8,128)(2,1)}), bf16[16,4,16,1024]{3,2,1,0:T(8,128)(2,1)}, u32[]{:S(2)}, u32[]{:S(2)}) async-start(bf16[16,4,16,1024]{3,2,1,0:T(8,128)(2,1)} %broadcast_in_dim.13), calls=%async_computation.1 | async-start | bytes 4194304 | tf_op jit(solution)/shard_map/all_to_all | solution.py:190
  78.7 30.2 %copy-start.4 = (s32[32]{0:T(128)S(1)}, s32[32]{0:T(128)}, u32[]{:S(2)}) copy-start(s32[32]{0:T(128)} %slots.7) | copy-start | bytes 388

commit v2 on v1

v2 whole, which is shorter than its diff:
```python
import functools

import jax
import jax.numpy as jnp
from jax import lax
from jax.experimental import pallas as pl
from jax.experimental.pallas import tpu as pltpu
from jax.sharding import PartitionSpec as P

KV_HEADS = 4
WIDTH = 128
GROUP = 8
KEY_COLUMNS = 512
IMAGES = 4
LOW = -1e30
SCALE = WIDTH ** (-0.5)
LOG2E = 1.4426950408889634
LINE = 4
BLOCK_HEADS = 2
PAD = 16
VMEM_LIMIT = 48 * 1024 * 1024

SMEM = pltpu.MemorySpace.SMEM
VMEM = pltpu.MemorySpace.VMEM


def pack_kernel(docs, me, slots, kv, out):
    for d in range(docs):
        local = 0
        for j in range(IMAGES):
            s = slots[d * IMAGES + j]
            local += jnp.where(s // IMAGES == me[0], s % IMAGES, 0)
        out[d] = kv[local]


def pick_kernel(me, slots, got, out):
    for j in range(IMAGES):
        rows = got[slots[me[0] * IMAGES + j] // IMAGES]
        heads = [
            jnp.concatenate(
                [
                    rows[:, c * WIDTH : (c + 1) * WIDTH],
                    rows[:, KEY_COLUMNS + c * WIDTH : KEY_COLUMNS + (c + 1) * WIDTH],
                ],
                axis=1,
            )
            for c in range(KV_HEADS)
        ]
        along_z = me[0] % 2 == 0
        for y in range(LINE):
            for z in range(LINE):
                out[y * LINE + z, j] = jnp.where(along_z, heads[z], heads[y])


def payload_kernel(q, d_out, spans, out):
    tokens = q.shape[0]
    for c in range(KV_HEADS):
        columns = slice(c * GROUP * WIDTH, (c + 1) * GROUP * WIDTH)
        out[c, :tokens] = q[:, columns]
        out[c, tokens : 2 * tokens] = d_out[:, columns]
        out[c, 2 * tokens :] = jnp.zeros_like(out[c, 2 * tokens :])
        out[c, 2 * tokens : 2 * tokens + 2, :tokens] = spans[...].astype(jnp.bfloat16)


def softmax_gradients(scores, d_probs, seen):
    keys, rows = scores.shape
    scores = scores.reshape(-1, IMAGES, 16, rows)
    d_probs = d_probs.reshape(-1, IMAGES, 16, rows)
    row_max = None
    for j in range(IMAGES):
        top = jnp.max(jnp.max(scores[:, j], axis=0), axis=0, keepdims=True)
        top = jnp.where(seen[j], top, LOW)
        row_max = top if row_max is None else jnp.maximum(row_max, top)
    row_max = row_max * (SCALE * LOG2E)
    terms = []
    total = 0.0
    dots = 0.0
    for j in range(IMAGES):
        term = jnp.exp2(scores[:, j] * (SCALE * LOG2E) - jnp.where(seen[j], row_max, -LOW))
        total += jnp.sum(jnp.sum(term, axis=0), axis=0, keepdims=True)
        dots += jnp.sum(jnp.sum(term * d_probs[:, j], axis=0), axis=0, keepdims=True)
        terms.append(term)
    inverse = 1.0 / total
    delta = dots * inverse
    low_probs = []
    d_scores = []
    for j in range(IMAGES):
        probs = terms[j] * inverse
        low_probs.append(probs.astype(jnp.bfloat16)[:, None])
        d_scores.append((probs * (d_probs[:, j] - delta)).astype(jnp.bfloat16)[:, None])
    low_probs = jnp.concatenate(low_probs, axis=1).reshape(keys, rows)
    d_scores = jnp.concatenate(d_scores, axis=1).reshape(keys, rows)
    return low_probs, d_scores


def grad_kernel(gate, kv, piece, dq, dkv, keys_t, probs, d_scores, q_rows, d_rows, acc):
    step = pl.program_id(0)
    tokens = dq.shape[1]
    block = BLOCK_HEADS * tokens

    @pl.when(step == 0)
    def _():
        keys_t[...] = kv[:, :WIDTH].T
        acc[...] = jnp.zeros_like(acc)

    factor = jnp.tanh(gate[...])
    for h in range(GROUP):
        rows, columns = slice(h * tokens, (h + 1) * tokens), slice(h * WIDTH, (h + 1) * WIDTH)
        q_rows[rows] = piece[0, :tokens, columns]
        wide = piece[0, tokens : 2 * tokens, columns].astype(jnp.float32)
        d_rows[rows] = (wide * factor).astype(jnp.bfloat16)
    low = piece[0, 2 * tokens : 2 * tokens + 1, :tokens].astype(jnp.float32)
    high = piece[0, 2 * tokens + 1 : 2 * tokens + 2, :tokens].astype(jnp.float32)
    low = jnp.concatenate([low] * BLOCK_HEADS, axis=1)
    high = jnp.concatenate([high] * BLOCK_HEADS, axis=1)
    seen = [(low <= j) & (j < high) for j in range(IMAGES)]
    transposed = (((1,), (1,)), ((), ()))
    for at in range(0, GROUP * tokens, block):
        rows = slice(at, at + block)
        scores = lax.dot_general(
            kv[:, :WIDTH], q_rows[rows], transposed, preferred_element_type=jnp.float32
        )
        d_probs = lax.dot_general(
            kv[:, WIDTH:], d_rows[rows], transposed, preferred_element_type=jnp.float32
        )
        probs[:, rows], d_scores[:, rows] = softmax_gradients(scores, d_probs, seen)
    acc[:, :WIDTH] += jnp.dot(d_scores[...], q_rows[...], preferred_element_type=jnp.float32)
    acc[:, WIDTH:] += jnp.dot(probs[...], d_rows[...], preferred_element_type=jnp.float32)
    dq_t = jnp.dot(keys_t[...], d_scores[...], preferred_element_type=jnp.float32) * SCALE
    dq_rows = dq_t.T.astype(jnp.bfloat16)
    for h in range(GROUP):
        dq[0, :, h * WIDTH : (h + 1) * WIDTH] = dq_rows[h * tokens : (h + 1) * tokens]

    @pl.when(step == LINE - 1)
    def _():
        dkv[:, :WIDTH] = (acc[:, :WIDTH] * SCALE).astype(jnp.bfloat16)
        dkv[:, WIDTH:] = acc[:, WIDTH:].astype(jnp.bfloat16)


def gradients(gate, kv, pieces):
    key_rows = kv.shape[0]
    tokens = (pieces.shape[1] - PAD) // 2
    width = pieces.shape[2]
    rows = GROUP * tokens
    return pl.pallas_call(
        grad_kernel,
        grid=(LINE,),
        in_specs=[
            pl.BlockSpec((1, 1), lambda i: (0, 0)),
            pl.BlockSpec(kv.shape, lambda i: (0, 0)),
            pl.BlockSpec((1,) + pieces.shape[1:], lambda i: (i, 0, 0)),
        ],
        out_specs=[
            pl.BlockSpec((1, tokens, width), lambda i: (i, 0, 0)),
            pl.BlockSpec(kv.shape, lambda i: (0, 0)),
        ],
        out_shape=[
            jax.ShapeDtypeStruct((LINE, tokens, width), jnp.bfloat16),
            jax.ShapeDtypeStruct(kv.shape, jnp.bfloat16),
        ],
        scratch_shapes=[
            pltpu.VMEM((WIDTH, key_rows), jnp.bfloat16),
            pltpu.VMEM((key_rows, rows), jnp.bfloat16),
            pltpu.VMEM((key_rows, rows), jnp.bfloat16),
            pltpu.VMEM((rows, WIDTH), jnp.bfloat16),
            pltpu.VMEM((rows, WIDTH), jnp.bfloat16),
            pltpu.VMEM(kv.shape, jnp.float32),
        ],
        compiler_params=pltpu.CompilerParams(vmem_limit_bytes=VMEM_LIMIT),
        cost_estimate=pl.CostEstimate(
            flops=10 * LINE * rows * key_rows * WIDTH,
            bytes_accessed=4 * 1024 * 1024,
            transcendentals=LINE * rows * key_rows,
        ),
        name="gradients",
    )(gate, kv, pieces)


def sum_kernel(me, slots, got, out):
    out[...] = jnp.zeros_like(out)
    along_z = me[0] % 2 == 0
    for j in range(IMAGES):
        owner = slots[me[0] * IMAGES + j] // IMAGES
        for c in range(KV_HEADS):
            total = 0.0
            for line in range(LINE):
                at = jnp.where(along_z, line * LINE + c, c * LINE + line)
                total += got[at, j].astype(jnp.float32)
            out[owner, :, c * WIDTH : (c + 1) * WIDTH] = total[:, :WIDTH].astype(jnp.bfloat16)
            out[owner, :, KEY_COLUMNS + c * WIDTH : KEY_COLUMNS + (c + 1) * WIDTH] = total[
                :, WIDTH:
            ].astype(jnp.bfloat16)


def place_kernel(docs, me, slots, got, out):
    for s in range(IMAGES):
        doc = 0
        for d in range(docs):
            for j in range(IMAGES):
                doc += jnp.where(slots[d * IMAGES + j] == me[0] * IMAGES + s, d, 0)
        out[s] = got[doc].astype(jnp.float32)


def small(kernel, out_shape, name):
    return pl.pallas_call(
        kernel,
        in_specs=[
            pl.BlockSpec(memory_space=SMEM),
            pl.BlockSpec(memory_space=SMEM),
            pl.BlockSpec(memory_space=VMEM),
        ],
        out_specs=pl.BlockSpec(memory_space=VMEM),
        out_shape=out_shape,
        compiler_params=pltpu.CompilerParams(vmem_limit_bytes=VMEM_LIMIT),
        name=name,
    )


def line_groups(docs):
    groups = []
    for d in range(docs):
        for a in range(LINE):
            if d % 2 == 0:
                groups.append([d * LINE * LINE + a * LINE + b for b in range(LINE)])
            else:
                groups.append([d * LINE * LINE + b * LINE + a for b in range(LINE)])
    return groups


def shards(queries, image_kv, d_out, attn_gate, image_slots, spans):
    docs = lax.axis_size("doc")
    texts = lax.axis_size("ctx")
    me = lax.axis_index("doc").astype(jnp.int32)[None]
    images, rows, columns = image_kv.shape
    tokens, width = queries.shape[1] , queries.shape[2] // KV_HEADS
    groups = line_groups(docs)
    both = ("doc", "ctx")
    payload = pl.pallas_call(
        payload_kernel,
        out_shape=jax.ShapeDtypeStruct((LINE, 2 * tokens + PAD, width), jnp.bfloat16),
        compiler_params=pltpu.CompilerParams(vmem_limit_bytes=VMEM_LIMIT),
        name="payload",
    )(queries[0], d_out[0], spans[0].T)
    pieces = lax.all_to_all(payload, both, 0, 0, axis_index_groups=groups)
    block = jax.ShapeDtypeStruct((docs, rows, columns), jnp.bfloat16)
    send = small(functools.partial(pack_kernel, docs), block, "pack")(me, image_slots, image_kv)
    got = lax.all_to_all(send, "doc", 0, 0)
    one_head = jax.ShapeDtypeStruct((texts, images, rows, 2 * WIDTH), jnp.bfloat16)
    send = small(pick_kernel, one_head, "pick")(me, image_slots, got)
    kv = lax.all_to_all(send, "ctx", 0, 0).reshape(texts * images * rows, 2 * WIDTH)
    dq, dkv = gradients(attn_gate.reshape(1, 1), kv, pieces)
    parts = lax.all_to_all(dkv.reshape(texts, images, rows, 2 * WIDTH), "ctx", 0, 0)
    back = lax.all_to_all(dq, both, 0, 0, axis_index_groups=groups)
    d_queries = back.transpose(1, 0, 2).reshape(1, tokens, LINE * width)
    send = small(sum_kernel, block, "sum")(me, image_slots, parts)
    got = lax.all_to_all(send, "doc", 0, 0)
    d_image_kv = small(
        functools.partial(place_kernel, docs),
        jax.ShapeDtypeStruct(image_kv.shape, jnp.float32),
        "place",
    )(me, image_slots, got)
    return d_queries, d_image_kv


def solution(mesh):
    return jax.shard_map(
        shards,
        mesh=mesh,
        in_specs=(
            P("doc", "ctx", None),
            P("doc", "ctx", None),
            P("doc", "ctx", None),
            P(),
            P(),
            P("doc", "ctx", None),
        ),
        out_specs=(P("doc", "ctx", None), P("doc", "ctx", None)),
        check_vma=False,
    )
```

time: 125 us -> 115 us (0.920); the launches traced: 125 us -> 114 us
  blocking collectives: 56 us -> 38.3 us
  Pallas kernels: 31.3 us -> 23.6 us
  starting transfers between devices: 7.95 us -> 14.9 us
  waiting for transfers between devices: 25.1 us -> 31.7 us
    all_to_all x1, blocking collectives: 30.2 us -> 12.4 us  [shards(): lax.all_to_all(dkv.reshape(texts, images, rows, 2 * WIDTH), 'ctx', 0, 0)]
    pallas_call x2 -> x3, Pallas kernels: 28.3 us -> 20.8 us  [the longest x1 17.9 us: gradients(): pl.pallas_call(grad_kernel, grid=(LINE,), in_specs=[pl.BlockSpec((1, 1),...]
    all_to_all x1 -> x3, starting transfers between devices: 7.95 us -> 14.9 us  [the longest x1 7.77 us: shards(): lax.all_to_all(send, 'ctx', 0, 0).reshape(texts * images * rows, 2 * WIDTH)]
    all_to_all x1 -> x3, waiting for transfers between devices: 25.1 us -> 31.7 us  [the longest x1 15.7 us: shards(): pieces = lax.all_to_all(payload, both, 0, 0, axis_index_groups=groups)]
    broadcast_in_dim x1 -> x0, local copies, waits for them, and re-layouts: 1.57 us -> none  [shards(): jnp.broadcast_to(local[None], (texts,) + local.shape)]
    unnamed x12 -> x13, local copies, waits for them, and re-layouts: 1.57 us -> 3.03 us
  transfers between devices with their start and end apart: 1 -> 3, of which waited for: 1 -> 3; matrix products, arithmetic and copies ran while one was open for 0% -> 0% of each run, Pallas kernels for 0% -> 3%
where the time goes in v2:
time: 115 us; the launch traced here: 114 us
  blocking collectives  38.3 us (33%)
  waiting for transfers between devices  31.7 us (28%)
  Pallas kernels  23.6 us (21%)
  starting transfers between devices  14.9 us (13%)
  local copies, waits for them, and re-layouts  3.68 us (3%)
  between operations  1.38 us (1%)
    all_to_all x2, blocking collectives, shards(): got = lax.all_to_all(send, 'doc', 0, 0)  25.9 us
    pallas_call x1, Pallas kernels, gradients(): pl.pallas_call(grad_kernel, grid=(LINE,), in_specs=[pl.BlockSpec((1, 1),...  17.9 us
    all_to_all x1, waiting for transfers between devices, shards(): pieces = lax.all_to_all(payload, both, 0, 0, axis_index_groups=groups)  15.7 us
    all_to_all x1, blocking collectives, shards(): lax.all_to_all(dkv.reshape(texts, images, rows, 2 * WIDTH), 'ctx', 0, 0)  12.4 us
    all_to_all x1, waiting for transfers between devices, shards(): back = lax.all_to_all(dq, both, 0, 0, axis_index_groups=groups)  8.6 us
    all_to_all x1, starting transfers between devices, shards(): lax.all_to_all(send, 'ctx', 0, 0).reshape(texts * images * rows, 2 * WIDTH)  7.77 us
    all_to_all x1, waiting for transfers between devices, shards(): lax.all_to_all(send, 'ctx', 0, 0).reshape(texts * images * rows, 2 * WIDTH)  7.45 us
    all_to_all x1, starting transfers between devices, shards(): pieces = lax.all_to_all(payload, both, 0, 0, axis_index_groups=groups)  3.62 us
  transfers between devices with their start and end apart: 3, of which 3 were waited for; matrix products, arithmetic and copies ran while one was open for 0% of the time, Pallas kernels for 3%

profile of v2, /device:TPU:1, one launch (start us, length us, event | category | flops | bytes accessed | tf_op | source)
XLA Modules:
  0.0 113.5 jit_solution(7084773747513499342)
XLA Ops:
  0.6 0.0 copy-start
  0.6 0.0 copy-start.1
  0.7 0.0 copy-start.2
  0.7 1.0 copy-done.2
  1.7 0.0 copy-start.3
  1.7 0.7 copy-done.3
  2.4 0.0 copy-start.5
  2.4 0.7 pack.1
  3.1 12.1 %all_to_all.30.got = bf16[8,16,1024]{2,1,0:T(8,128)(2,1)S(1)} all-to-all(bf16[8,16,1024]{2,1,0:T(8,128)(2,1)S(1)} %pack.1), channel_id=1, replica_groups=mesh['doc'=8,'ctx'=16] {'doc'}, dimensions={0} | all-to-all | bytes 524288 | tf_op jit(solution)/shard_map/all_to_all | solution.py:247
  15.2 1.4 %pick.1 = bf16[16,4,16,256]{3,2,1,0:T(8,128)(2,1)} custom-call(s32[1]{0:T(128)} %bitcast.1.me, s32[32]{0:T(128)S(1)} %copy-done.3, bf16[8,16,1024]{2,1,0:T(8,128)(2,1)S(1)} %all_to_all.30.got), custom_call_target="tpu_custom_call" | custom-call | tf_op jit(solution)/shard_map/pick/pallas_call | solution.py:249
  16.6 7.8 %all-to-all-start.1 = ((bf16[16,4,16,256]{3,2,1,0:T(8,128)(2,1)}), bf16[16,4,16,256]{3,2,1,0:T(8,128)(2,1)S(1)}, u32[]{:S(2)}, u32[]{:S(2)}) async-start(bf16[16,4,16,256]{3,2,1,0:T(8,128)(2,1)} %pick.1), calls=%async_computation.1 | async-start | bytes 1048576 | tf_op jit(solution)/shard_map/all_to_all | solution.py:250
  24.4 0.0 copy-done
  24.4 0.0 copy-done.1
  24.4 0.0 copy-done.5
  24.4 1.5 %payload.1 = bf16[4,272,1024]{2,1,0:T(8,128)(2,1)} custom-call(bf16[128,4096]{1,0:T(8,128)(2,1)S(1)} %bitcast.12, bf16[128,4096]{1,0:T(8,128)(2,1)S(1)} %bitcast.13, s32[2,128]{1,0:T(2,128)S(1)} %bitcast.16), custom_call_target="tpu_custom_call" | custom-call | tf_op jit(solution)/shard_map/payload/pallas_call | solution.py:238
  25.9 7.4 %all-to-all-done.1 = bf16[16,4,16,256]{3,2,1,0:T(8,128)(2,1)S(1)} async-done(((bf16[16,4,16,256]{3,2,1,0:T(8,128)(2,1)}), bf16[16,4,16,256]{3,2,1,0:T(8,128)(2,1)S(1)}, u32[]{:S(2)}, u32[]{:S(2)}) %all-to-all-start.1) | async-done | bytes 524320 | tf_op jit(solution)/shard_map/all_to_all | solution.py:250
  33.4 3.6 %all-to-all-start.2 = ((bf16[4,272,1024]{2,1,0:T(8,128)(2,1)}), bf16[4,272,1024]{2,1,0:T(8,128)(2,1)S(1)}, u32[]{:S(2)}, u32[]{:S(2)}) async-start(bf16[4,272,1024]{2,1,0:T(8,128)(2,1)} %payload.1), calls=%async_computation.2 | async-start | bytes 4456448 | tf_op jit(solution)/shard_map/all_to_all | solution.py:244
  37.7 15.7 %all-to-all-done.2.piece = bf16[4,272,1024]{2,1,0:T(8,128)(2,1)S(1)} async-done(((bf16[4,272,1024]{2,1,0:T(8,128)(2,1)}), bf16[4,272,1024]{2,1,0:T(8,128)(2,1)S(1)}, u32[]{:S(2)}, u32[]{:S(2)}) %all-to-all-start.2) | async-done | bytes 2228256 | tf_op jit(solution)/shard_map/all_to_all | solution.py:244
  53.3 0.0 copy-start.4
  53.3 17.9 %gradients.1 = (bf16[4,128,1024]{2,1,0:T(8,128)(2,1)}, bf16[1024,256]{1,0:T(8,128)(2,1)S(1)}) custom-call(f32[1,1]{1,0:T(1,128)} %bitcast.11.gate, bf16[1024,256]{1,0:T(8,128)(2,1)S(1)} %bitcast.14, bf16[4,272,1024]{2,1,0:T(8,128)(2,1)S(1)} %all-to-all-done.2.piece), custom_call_target="tpu_custom_call" | custom-call | flops 5368709120 | bytes 4194304 | tf_op jit(solution)/shard_map/gradients/pallas_call | solution.py:145
  71.2 12.4 %all_to_all.31.got = bf16[16,4,16,256]{3,2,1,0:T(8,128)(2,1)S(1)} all-to-all(bf16[16,4,16,256]{3,2,1,0:T(8,128)(2,1)S(1)} %bitcast.15), channel_id=1, replica_groups=mesh['doc'=8,'ctx'=16] {'ctx'}, dimensions={0} | all-to-all | bytes 1048576 | tf_op jit(solution)/shard_map/all_to_all | solution.py:252
  83.6 0.0 copy-done.4
  83.6 0.6 sum.1
  84.2 13.8 %all_to_all.32.got = bf16[8,16,1024]{2,1,0:T(8,128)(2,1)S(1)} all-to-all(bf16[8,16,1024]{2,1,0:T(8,128)(2,1)S(1)} %sum.1), channel_id=1, replica_groups=mesh['doc'=8,'ctx'=16] {'doc'}, dimensions={0} | all-to-all | bytes 524288 | tf_op jit(solution)/shard_map/all_to_all | solution.py:256
  98.0 3.5 %all-to-all-start.3 = ((bf16[4,128,1024]{2,1,0:T(8,128)(2,1)}), bf16[4,128,1024]{2,1,0:T(8,128)(2,1)S(1)}, u32[]{:S(2)}, u32[]{:S(2)}) async-start(bf16[4,128,1024]{2,1,0:T(8,128)(2,1)} %get-tuple-element.4), calls=%async_computation.3 | async-start | bytes 2097152 | tf_op jit(solution)/shard_map/all_to_all | solution.py:253
  101.5 1.4 %place.1 = f32[4,16,1024]{2,1,0:T(8,128)} custom-call(s32[1]{0:T(128)} %bitcast.1.me, s32[32]{0:T(128)S(1)} %copy-done.4, bf16[8,16,1024]{2,1,0:T(8,128)(2,1)S(1)} %all_to_all.32.got), custom_call_target="tpu_custom_call" | custom-call | tf_op jit(solution)/shard_map/place/pallas_call | solution.py:257
  102.9 8.6 %all-to-all-done.3 = bf16[4,128,1024]{2,1,0:T(8,128)(2,1)S(1)} async-done(((bf16[4,128,1024]{2,1,0:T(8,128)(2,1)}), bf16[4,128,1024]{2,1,0:T(8,128)(2,1)S(1)}, u32[]{:S(2)}, u32[]{:S(2)}) %all-to-all-start.3) | async-done | bytes 1048608 | tf_op jit(solution)/shard_map/all_to_all | solution.py:253
  111.6 0.7 copy.8
  112.2 1.3 %copy.9 = bf16[1,128,4096]{2,1,0:T(8,128)(2,1)} copy(bf16[1,128,4096]{1,2,0:T(8,128)(2,1)S(1)} %bitcast.18) | data formatting | bytes 2097152
Async XLA Ops:
  0.6 23.8 %copy-start = (bf16[1,128,4096]{2,1,0:T(8,128)(2,1)S(1)}, bf16[1,128,4096]{2,1,0:T(8,128)(2,1)}, u32[]{:S(2)}) copy-start(bf16[1,128,4096]{2,1,0:T(8,128)(2,1)} %param.6) | copy-start | bytes 3145732
  0.6 23.8 %copy-start.1 = (bf16[1,128,4096]{2,1,0:T(8,128)(2,1)S(1)}, bf16[1,128,4096]{2,1,0:T(8,128)(2,1)}, u32[]{:S(2)}) copy-start(bf16[1,128,4096]{2,1,0:T(8,128)(2,1)} %param.8) | copy-start | bytes 3145732
  0.7 1.1 copy-start.2
  1.7 0.7 copy-start.3
  2.4 22.0 %copy-start.5 = (s32[1,128,2]{1,2,0:T(2,128)S(1)}, s32[1,128,2]{1,2,0:T(2,128)}, u32[]{:S(2)}) copy-start(s32[1,128,2]{1,2,0:T(2,128)} %param.11) | copy-start | bytes 3076
  16.6 16.8 %all-to-all-start.1 = ((bf16[16,4,16,256]{3,2,1,0:T(8,128)(2,1)}), bf16[16,4,16,256]{3,2,1,0:T(8,128)(2,1)S(1)}, u32[]{:S(2)}, u32[]{:S(2)}) async-start(bf16[16,4,16,256]{3,2,1,0:T(8,128)(2,1)} %pick.1), calls=%async_computation.1 | async-start | bytes 1048576 | tf_op jit(solution)/shard_map/all_to_all | solution.py:250
  33.4 19.9 %all-to-all-start.2 = ((bf16[4,272,1024]{2,1,0:T(8,128)(2,1)}), bf16[4,272,1024]{2,1,0:T(8,128)(2,1)S(1)}, u32[]{:S(2)}, u32[]{:S(2)}) async-start(bf16[4,272,1024]{2,1,0:T(8,128)(2,1)} %payload.1), calls=%async_computation.2 | async-start | bytes 4456448 | tf_op jit(solution)/shard_map/all_to_all | solution.py:244
  53.3 30.2 %copy-start.4 = (s32[32]{0:T(128)S(1)}, s32[32]{0:T(128)}, u32[]{:S(2)}) copy-start(s32[32]{0:T(128)} %slots.7) | copy-start | bytes 388
  98.0 13.5 %all-to-all-start.3 = ((bf16[4,128,1024]{2,1,0:T(8,128)(2,1)}), bf16[4,128,1024]{2,1,0:T(8,128)(2,1)S(1)}, u32[]{:S(2)}, u32[]{:S(2)}) async-start(bf16[4,128,1024]{2,1,0:T(8,128)(2,1)} %get-tuple-element.4), calls=%async_computation.3 | async-start | bytes 2097152 | tf_op jit(solution)/shard_map/all_to_all | solution.py:253

commit v3 on v2

--- a/solution.py
+++ b/solution.py
@@ -52,14 +52,23 @@
                 out[y * LINE + z, j] = jnp.where(along_z, heads[z], heads[y])
 
 
-def payload_kernel(q, d_out, spans, out):
+def payload_kernel(me, q, d_out, spans, *outs):
     tokens = q.shape[0]
-    for c in range(KV_HEADS):
-        columns = slice(c * GROUP * WIDTH, (c + 1) * GROUP * WIDTH)
-        out[c, :tokens] = q[:, columns]
-        out[c, tokens : 2 * tokens] = d_out[:, columns]
-        out[c, 2 * tokens :] = jnp.zeros_like(out[c, 2 * tokens :])
-        out[c, 2 * tokens : 2 * tokens + 2, :tokens] = spans[...].astype(jnp.bfloat16)
+    width = q.shape[1] // KV_HEADS
+    for k, out in enumerate(outs):
+        columns = pl.ds(pl.multiple_of(lax.rem(me[1] + k, LINE) * width, WIDTH), width)
+        out[:tokens] = q[:, columns]
+        out[tokens : 2 * tokens] = d_out[:, columns]
+        out[2 * tokens :] = jnp.zeros_like(out[2 * tokens :])
+        out[2 * tokens : 2 * tokens + 2, :tokens] = spans[...].astype(jnp.bfloat16)
+
+
+def merge_kernel(me, *refs):
+    *parts, out = refs
+    width = out.shape[1] // KV_HEADS
+    for k, part in enumerate(parts):
+        columns = pl.ds(pl.multiple_of(lax.rem(me[1] + k, LINE) * width, WIDTH), width)
+        out[:, columns] = part[...]
 
 
 def softmax_gradients(scores, d_probs, seen):
@@ -93,9 +102,11 @@
     return low_probs, d_scores
 
 
-def grad_kernel(gate, kv, piece, dq, dkv, keys_t, probs, d_scores, q_rows, d_rows, acc):
+def grad_kernel(gate, kv, *refs):
+    pieces, dqs, dkv = refs[:LINE], refs[LINE : 2 * LINE], refs[2 * LINE]
+    keys_t, probs, d_scores, q_rows, d_rows, spans, acc = refs[2 * LINE + 1 :]
     step = pl.program_id(0)
-    tokens = dq.shape[1]
+    tokens = dqs[0].shape[0]
     block = BLOCK_HEADS * tokens
 
     @pl.when(step == 0)
@@ -103,16 +114,20 @@
         keys_t[...] = kv[:, :WIDTH].T
         acc[...] = jnp.zeros_like(acc)
 
-    factor = jnp.tanh(gate[...])
-    for h in range(GROUP):
-        rows, columns = slice(h * tokens, (h + 1) * tokens), slice(h * WIDTH, (h + 1) * WIDTH)
-        q_rows[rows] = piece[0, :tokens, columns]
-        wide = piece[0, tokens : 2 * tokens, columns].astype(jnp.float32)
-        d_rows[rows] = (wide * factor).astype(jnp.bfloat16)
-    low = piece[0, 2 * tokens : 2 * tokens + 1, :tokens].astype(jnp.float32)
-    high = piece[0, 2 * tokens + 1 : 2 * tokens + 2, :tokens].astype(jnp.float32)
-    low = jnp.concatenate([low] * BLOCK_HEADS, axis=1)
-    high = jnp.concatenate([high] * BLOCK_HEADS, axis=1)
+    for k, piece in enumerate(pieces):
+
+        @pl.when(step == k)
+        def _(piece=piece):
+            factor = jnp.tanh(gate[...])
+            for h in range(GROUP):
+                rows, columns = slice(h * tokens, (h + 1) * tokens), slice(h * WIDTH, (h + 1) * WIDTH)
+                q_rows[rows] = piece[:tokens, columns]
+                wide = piece[tokens : 2 * tokens, columns].astype(jnp.float32)
+                d_rows[rows] = (wide * factor).astype(jnp.bfloat16)
+            spans[...] = piece[2 * tokens :, :tokens].astype(jnp.float32)
+
+    low = jnp.concatenate([spans[0:1]] * BLOCK_HEADS, axis=1)
+    high = jnp.concatenate([spans[1:2]] * BLOCK_HEADS, axis=1)
     seen = [(low <= j) & (j < high) for j in range(IMAGES)]
     transposed = (((1,), (1,)), ((), ()))
     for at in range(0, GROUP * tokens, block):
@@ -128,8 +143,12 @@
     acc[:, WIDTH:] += jnp.dot(probs[...], d_rows[...], preferred_element_type=jnp.float32)
     dq_t = jnp.dot(keys_t[...], d_scores[...], preferred_element_type=jnp.float32) * SCALE
     dq_rows = dq_t.T.astype(jnp.bfloat16)
-    for h in range(GROUP):
-        dq[0, :, h * WIDTH : (h + 1) * WIDTH] = dq_rows[h * tokens : (h + 1) * tokens]
+    for k, dq in enumerate(dqs):
+
+        @pl.when(step == k)
+        def _(dq=dq):
+            for h in range(GROUP):
+                dq[:, h * WIDTH : (h + 1) * WIDTH] = dq_rows[h * tokens : (h + 1) * tokens]
 
     @pl.when(step == LINE - 1)
     def _():
@@ -139,31 +158,24 @@
 
 def gradients(gate, kv, pieces):
     key_rows = kv.shape[0]
-    tokens = (pieces.shape[1] - PAD) // 2
-    width = pieces.shape[2]
+    tokens = (pieces[0].shape[0] - PAD) // 2
+    width = pieces[0].shape[1]
     rows = GROUP * tokens
+    whole = lambda shape: pl.BlockSpec(shape, lambda i: (0, 0))
     return pl.pallas_call(
         grad_kernel,
         grid=(LINE,),
-        in_specs=[
-            pl.BlockSpec((1, 1), lambda i: (0, 0)),
-            pl.BlockSpec(kv.shape, lambda i: (0, 0)),
-            pl.BlockSpec((1,) + pieces.shape[1:], lambda i: (i, 0, 0)),
-        ],
-        out_specs=[
-            pl.BlockSpec((1, tokens, width), lambda i: (i, 0, 0)),
-            pl.BlockSpec(kv.shape, lambda i: (0, 0)),
-        ],
-        out_shape=[
-            jax.ShapeDtypeStruct((LINE, tokens, width), jnp.bfloat16),
-            jax.ShapeDtypeStruct(kv.shape, jnp.bfloat16),
-        ],
+        in_specs=[whole((1, 1)), whole(kv.shape)] + [whole(p.shape) for p in pieces],
+        out_specs=[whole((tokens, width))] * LINE + [whole(kv.shape)],
+        out_shape=[jax.ShapeDtypeStruct((tokens, width), jnp.bfloat16)] * LINE
+        + [jax.ShapeDtypeStruct(kv.shape, jnp.bfloat16)],
         scratch_shapes=[
             pltpu.VMEM((WIDTH, key_rows), jnp.bfloat16),
             pltpu.VMEM((key_rows, rows), jnp.bfloat16),
             pltpu.VMEM((key_rows, rows), jnp.bfloat16),
             pltpu.VMEM((rows, WIDTH), jnp.bfloat16),
             pltpu.VMEM((rows, WIDTH), jnp.bfloat16),
+            pltpu.VMEM((PAD, tokens), jnp.float32),
             pltpu.VMEM(kv.shape, jnp.float32),
         ],
         compiler_params=pltpu.CompilerParams(vmem_limit_bytes=VMEM_LIMIT),
@@ -173,7 +185,7 @@
             transcendentals=LINE * rows * key_rows,
         ),
         name="gradients",
-    )(gate, kv, pieces)
+    )(gate, kv, *pieces)
 
 
 def sum_kernel(me, slots, got, out):
@@ -216,42 +228,45 @@
     )
 
 
-def line_groups(docs):
-    groups = []
+def shift(docs, k):
+    pairs = []
     for d in range(docs):
         for a in range(LINE):
-            if d % 2 == 0:
-                groups.append([d * LINE * LINE + a * LINE + b for b in range(LINE)])
-            else:
-                groups.append([d * LINE * LINE + b * LINE + a for b in range(LINE)])
-    return groups
+            for b in range(LINE):
+                to = (b + k) % LINE
+                ends = (a * LINE + b, a * LINE + to) if d % 2 == 0 else (b * LINE + a, to * LINE + a)
+                pairs.append((d * LINE * LINE + ends[0], d * LINE * LINE + ends[1]))
+    return pairs
 
 
 def shards(queries, image_kv, d_out, attn_gate, image_slots, spans):
     docs = lax.axis_size("doc")
     texts = lax.axis_size("ctx")
-    me = lax.axis_index("doc").astype(jnp.int32)[None]
+    doc = lax.axis_index("doc").astype(jnp.int32)
+    text = lax.axis_index("ctx").astype(jnp.int32)
+    me = jnp.stack([doc, jnp.where(doc % 2 == 0, text % LINE, text // LINE)])
     images, rows, columns = image_kv.shape
-    tokens, width = queries.shape[1] , queries.shape[2] // KV_HEADS
-    groups = line_groups(docs)
+    tokens, width = queries.shape[1], queries.shape[2] // KV_HEADS
     both = ("doc", "ctx")
-    payload = pl.pallas_call(
+    params = pltpu.CompilerParams(vmem_limit_bytes=VMEM_LIMIT)
+    pieces = pl.pallas_call(
         payload_kernel,
-        out_shape=jax.ShapeDtypeStruct((LINE, 2 * tokens + PAD, width), jnp.bfloat16),
-        compiler_params=pltpu.CompilerParams(vmem_limit_bytes=VMEM_LIMIT),
+        in_specs=[pl.BlockSpec(memory_space=SMEM)] + [pl.BlockSpec(memory_space=VMEM)] * 3,
+        out_specs=[pl.BlockSpec(memory_space=VMEM)] * LINE,
+        out_shape=[jax.ShapeDtypeStruct((2 * tokens + PAD, width), jnp.bfloat16)] * LINE,
+        compiler_params=params,
         name="payload",
-    )(queries[0], d_out[0], spans[0].T)
-    pieces = lax.all_to_all(payload, both, 0, 0, axis_index_groups=groups)
+    )(me, queries[0], d_out[0], spans[0].T)
+    pieces = [pieces[0]] + [lax.ppermute(pieces[k], both, shift(docs, k)) for k in range(1, LINE)]
     block = jax.ShapeDtypeStruct((docs, rows, columns), jnp.bfloat16)
     send = small(functools.partial(pack_kernel, docs), block, "pack")(me, image_slots, image_kv)
     got = lax.all_to_all(send, "doc", 0, 0)
     one_head = jax.ShapeDtypeStruct((texts, images, rows, 2 * WIDTH), jnp.bfloat16)
     send = small(pick_kernel, one_head, "pick")(me, image_slots, got)
     kv = lax.all_to_all(send, "ctx", 0, 0).reshape(texts * images * rows, 2 * WIDTH)
-    dq, dkv = gradients(attn_gate.reshape(1, 1), kv, pieces)
+    *dqs, dkv = gradients(attn_gate.reshape(1, 1), kv, pieces)
+    dqs = [dqs[0]] + [lax.ppermute(dqs[k], both, shift(docs, -k)) for k in range(1, LINE)]
     parts = lax.all_to_all(dkv.reshape(texts, images, rows, 2 * WIDTH), "ctx", 0, 0)
-    back = lax.all_to_all(dq, both, 0, 0, axis_index_groups=groups)
-    d_queries = back.transpose(1, 0, 2).reshape(1, tokens, LINE * width)
     send = small(sum_kernel, block, "sum")(me, image_slots, parts)
     got = lax.all_to_all(send, "doc", 0, 0)
     d_image_kv = small(
@@ -259,7 +274,15 @@
         jax.ShapeDtypeStruct(image_kv.shape, jnp.float32),
         "place",
     )(me, image_slots, got)
-    return d_queries, d_image_kv
+    d_queries = pl.pallas_call(
+        merge_kernel,
+        in_specs=[pl.BlockSpec(memory_space=SMEM)] + [pl.BlockSpec(memory_space=VMEM)] * LINE,
+        out_specs=pl.BlockSpec(memory_space=VMEM),
+        out_shape=jax.ShapeDtypeStruct(queries.shape[1:], jnp.bfloat16),
+        compiler_params=params,
+        name="merge",
+    )(me, *dqs)
+    return d_queries[None], d_image_kv
 
 
 def solution(mesh):

time: 115 us -> 96.7 us (0.84)
  blocking collectives: 38.3 us -> 0 us
  starting transfers between devices: 14.9 us -> 34.4 us
  waiting for transfers between devices: 31.7 us -> 25.6 us
  Pallas kernels: 23.6 us -> 28.6 us
  local copies, waits for them, and re-layouts: 3.68 us -> 6.02 us
    all_to_all x3 -> x0, blocking collectives: 38.3 us -> none  [the longest x2 25.9 us: shards(): got = lax.all_to_all(send, 'doc', 0, 0)]
    all_to_all x2 -> x3, starting transfers between devices: 7.14 us -> 20.3 us  [the longest x2 15.7 us: shards(): got = lax.all_to_all(send, 'doc', 0, 0)]
    all_to_all x2 -> x3, waiting for transfers between devices: 24.3 us -> 11.7 us  [the longest x1 6.79 us: shards(): lax.all_to_all(dkv.reshape(texts, images, rows, 2 * WIDTH), 'ctx', 0, 0)]
    ppermute x0 -> x6, starting transfers between devices: none -> 8.78 us  [the longest x3 4.99 us: shards(): lax.ppermute(pieces[k], both, shift(docs, k))]
    ppermute x0 -> x6, waiting for transfers between devices: none -> 6.59 us  [the longest x3 6.58 us: shards(): lax.ppermute(pieces[k], both, shift(docs, k))]
    pallas_call x2 -> x3, Pallas kernels: 19.4 us -> 23 us  [the longest x1 19.5 us: gradients(): pl.pallas_call(grad_kernel, grid=(LINE,), in_specs=[whole((1, 1)), whole(...]
    unnamed x13 -> x18, local copies, waits for them, and re-layouts: 3.03 us -> 6.02 us
    all_to_all x1, starting transfers between devices: 7.77 us -> 5.25 us  [shards(): lax.all_to_all(send, 'ctx', 0, 0).reshape(texts * images * rows, 2 * WIDTH)]
  transfers between devices with their start and end apart: 3 -> 10, of which waited for: 3 -> 5; matrix products, arithmetic and copies ran while one was open for 0% -> 0% of each run, Pallas kernels for 3% -> 6%
where the time goes in v3:
time: 96.7 us; the launch traced here: 96 us
  starting transfers between devices  34.4 us (36%)
  Pallas kernels  28.6 us (30%)
  waiting for transfers between devices  25.6 us (26%)
  local copies, waits for them, and re-layouts  6.02 us (6%)
  between operations  1.38 us (1%)
    pallas_call x1, Pallas kernels, gradients(): pl.pallas_call(grad_kernel, grid=(LINE,), in_specs=[whole((1, 1)), whole(...  19.5 us
    all_to_all x2, starting transfers between devices, shards(): got = lax.all_to_all(send, 'doc', 0, 0)  15.7 us
    all_to_all x1, waiting for transfers between devices, shards(): lax.all_to_all(send, 'ctx', 0, 0).reshape(texts * images * rows, 2 * WIDTH)  7.32 us
    all_to_all x1, waiting for transfers between devices, shards(): lax.all_to_all(dkv.reshape(texts, images, rows, 2 * WIDTH), 'ctx', 0, 0)  6.79 us
    ppermute x3, waiting for transfers between devices, shards(): lax.ppermute(pieces[k], both, shift(docs, k))  6.58 us
    unnamed x18, local copies, waits for them, and re-layouts  6.02 us
    all_to_all x1, starting transfers between devices, shards(): lax.all_to_all(send, 'ctx', 0, 0).reshape(texts * images * rows, 2 * WIDTH)  5.25 us
    ppermute x3, starting transfers between devices, shards(): lax.ppermute(pieces[k], both, shift(docs, k))  4.99 us
  transfers between devices with their start and end apart: 10, of which 5 were waited for; matrix products, arithmetic and copies ran while one was open for 0% of the time, Pallas kernels for 6%

profile of v3, /device:TPU:1, one launch (start us, length us, event | category | flops | bytes accessed | tf_op | source)
XLA Modules:
  0.0 96.0 jit_solution(3159103445723831561)
XLA Ops:
  0.7 0.1 pad_add_fusion.me
  0.7 0.6 copy-done.3
  1.3 0.9 copy-done.2
  2.2 1.4 %pack.1 = bf16[8,16,1024]{2,1,0:T(8,128)(2,1)} custom-call(s32[2]{0:T(128)S(1)} %pad_add_fusion.me, s32[32]{0:T(128)S(1)} %copy-done.3, bf16[4,16,1024]{2,1,0:T(8,128)(2,1)S(1)} %copy-done.2), custom_call_target="tpu_custom_call" | custom-call | tf_op jit(solution)/shard_map/pack/pallas_call | solution.py:262
  3.7 5.8 %all-to-all-start = ((bf16[8,16,1024]{2,1,0:T(8,128)(2,1)}), bf16[8,16,1024]{2,1,0:T(8,128)(2,1)S(1)}, u32[]{:S(2)}, u32[]{:S(2)}) async-start(bf16[8,16,1024]{2,1,0:T(8,128)(2,1)} %pack.1), calls=%async_computation | async-start | bytes 524288 | tf_op jit(solution)/shard_map/all_to_all | solution.py:263
  9.5 0.7 copy-done.4
  10.2 1.2 %copy-done = bf16[1,128,4096]{2,1,0:T(8,128)(2,1)S(1)} copy-done((bf16[1,128,4096]{2,1,0:T(8,128)(2,1)S(1)}, bf16[1,128,4096]{2,1,0:T(8,128)(2,1)}, u32[]{:S(2)}) %copy-start) | copy-done | bytes 1048600
  11.4 1.2 %copy-done.1 = bf16[1,128,4096]{2,1,0:T(8,128)(2,1)S(1)} copy-done((bf16[1,128,4096]{2,1,0:T(8,128)(2,1)S(1)}, bf16[1,128,4096]{2,1,0:T(8,128)(2,1)}, u32[]{:S(2)}) %copy-start.1) | copy-done | bytes 1048600
  12.6 1.9 %payload.1 = (bf16[272,1024]{1,0:T(8,128)(2,1)S(1)}, bf16[272,1024]{1,0:T(8,128)(2,1)}, bf16[272,1024]{1,0:T(8,128)(2,1)}, bf16[272,1024]{1,0:T(8,128)(2,1)}) custom-call(s32[2]{0:T(128)S(1)} %pad_add_fusion.me, bf16[128,4096]{1,0:T(8,128)(2,1)S(1)} %bitcast.12, bf16[128,4096]{1,0:T(8,128)(2,1)S(1)} %bitcast.13, s32[2,128]{1,0:T(2,128)S(1)} %bitcast.15), custom_call_target="tpu_custom_call" | custom-call | tf_op jit(solution)/shard_map/payload/pallas_call | solution.py:252
  14.5 1.3 %collective-permute-start = (bf16[272,1024]{1,0:T(8,128)(2,1)}, bf16[272,1024]{1,0:T(8,128)(2,1)S(1)}, u32[]{:S(2)}, u32[]{:S(2)}) collective-permute-start(bf16[272,1024]{1,0:T(8,128)(2,1)} %get-tuple-element.12), channel_id=1, source_target_pairs={{0,1},{1,2},{2,3},{3,0},{4,5},{5,6},{6,7},{7,4},{8,9},{9,10},{10,1... | collective-permute-start | bytes 1671176 | tf_op jit(solution)/shard_map/ppermute | solution.py:260
  15.7 2.6 %collective-permute-start.1 = (bf16[272,1024]{1,0:T(8,128)(2,1)}, bf16[272,1024]{1,0:T(8,128)(2,1)S(1)}, u32[]{:S(2)}, u32[]{:S(2)}) collective-permute-start(bf16[272,1024]{1,0:T(8,128)(2,1)} %get-tuple-element.13), channel_id=1, source_target_pairs={{0,2},{1,3},{2,0},{3,1},{4,6},{5,7},{6,4},{7,5},{8,10},{9,11},{10,... | collective-permute-start | bytes 1671176 | tf_op jit(solution)/shard_map/ppermute | solution.py:260
  18.4 1.1 %collective-permute-start.2 = (bf16[272,1024]{1,0:T(8,128)(2,1)}, bf16[272,1024]{1,0:T(8,128)(2,1)S(1)}, u32[]{:S(2)}, u32[]{:S(2)}) collective-permute-start(bf16[272,1024]{1,0:T(8,128)(2,1)} %get-tuple-element.14), channel_id=1, source_target_pairs={{0,3},{1,0},{2,1},{3,2},{4,7},{5,4},{6,5},{7,6},{8,11},{9,8},{10,9... | collective-permute-start | bytes 1671176 | tf_op jit(solution)/shard_map/ppermute | solution.py:260
  19.4 1.4 %pick.1 = bf16[16,4,16,256]{3,2,1,0:T(8,128)(2,1)} custom-call(s32[2]{0:T(128)S(1)} %pad_add_fusion.me, s32[32]{0:T(128)S(1)} %copy-done.3, bf16[8,16,1024]{2,1,0:T(8,128)(2,1)S(1)} %all-to-all-done.got), custom_call_target="tpu_custom_call" | custom-call | tf_op jit(solution)/shard_map/pick/pallas_call | solution.py:265
  20.8 5.3 %all-to-all-start.1 = ((bf16[16,4,16,256]{3,2,1,0:T(8,128)(2,1)}), bf16[16,4,16,256]{3,2,1,0:T(8,128)(2,1)S(1)}, u32[]{:S(2)}, u32[]{:S(2)}) async-start(bf16[16,4,16,256]{3,2,1,0:T(8,128)(2,1)} %pick.1), calls=%async_computation.1 | async-start | bytes 1048576 | tf_op jit(solution)/shard_map/all_to_all | solution.py:266
  26.7 0.0 collective-permute-done.refs_1_
  26.7 5.0 %collective-permute-done.1.refs_2_ = bf16[272,1024]{1,0:T(8,128)(2,1)S(1)} collective-permute-done((bf16[272,1024]{1,0:T(8,128)(2,1)}, bf16[272,1024]{1,0:T(8,128)(2,1)S(1)}, u32[]{:S(2)}, u32[]{:S(2)}) %collective-permute-start.1) | collective-permute-done | bytes 557088 | tf_op jit(solution)/shard_map/ppermute | solution.py:260
  31.8 1.6 %collective-permute-done.2.refs_3_ = bf16[272,1024]{1,0:T(8,128)(2,1)S(1)} collective-permute-done((bf16[272,1024]{1,0:T(8,128)(2,1)}, bf16[272,1024]{1,0:T(8,128)(2,1)S(1)}, u32[]{:S(2)}, u32[]{:S(2)}) %collective-permute-start.2) | collective-permute-done | bytes 557088 | tf_op jit(solution)/shard_map/ppermute | solution.py:260
  33.3 7.3 %all-to-all-done.1 = bf16[16,4,16,256]{3,2,1,0:T(8,128)(2,1)S(1)} async-done(((bf16[16,4,16,256]{3,2,1,0:T(8,128)(2,1)}), bf16[16,4,16,256]{3,2,1,0:T(8,128)(2,1)S(1)}, u32[]{:S(2)}, u32[]{:S(2)}) %all-to-all-start.1) | async-done | bytes 524320 | tf_op jit(solution)/shard_map/all_to_all | solution.py:266
  40.6 19.5 %gradients.1 = (bf16[128,1024]{1,0:T(8,128)(2,1)S(1)}, bf16[128,1024]{1,0:T(8,128)(2,1)S(1)}, bf16[128,1024]{1,0:T(8,128)(2,1)S(1)}, bf16[128,1024]{1,0:T(8,128)(2,1)S(1)}, bf16[1024,256]{1,0:T(8,128)(2,1)}) custom-call(f32[1,1]{1,0:T(1,128)} %bitcast.11.gate, bf16[1024,256]{1,0:T(8,128)(2,1)S(1)} %bitcast.14, ...), custom_call_target="tpu_custom_call" | custom-call | flops 5368709120 | bytes 4194304 | tf_op jit(solution)/shard_map/gradients/pallas_call | solution.py:165
  60.2 0.7 copy-done.5
  60.9 0.7 copy-done.7
  61.6 4.6 %all-to-all-start.2 = ((bf16[16,4,16,256]{3,2,1,0:T(8,128)(2,1)}), bf16[16,4,16,256]{3,2,1,0:T(8,128)(2,1)S(1)}, u32[]{:S(2)}, u32[]{:S(2)}) async-start(bf16[16,4,16,256]{3,2,1,0:T(8,128)(2,1)} %bitcast.9), calls=%async_computation.2 | async-start | bytes 1048576 | tf_op jit(solution)/shard_map/all_to_all | solution.py:269
  66.3 2.6 %collective-permute-start.3 = (bf16[128,1024]{1,0:T(8,128)(2,1)S(1)}, bf16[128,1024]{1,0:T(8,128)(2,1)S(1)}, u32[]{:S(2)}, u32[]{:S(2)}) collective-permute-start(bf16[128,1024]{1,0:T(8,128)(2,1)S(1)} %copy-done.8), channel_id=1, source_target_pairs={{0,3},{1,0},{2,1},{3,2},{4,7},{5,4},{6,5},{7,6},{8,11},{9,8},{10,9... | collective-permute-start | bytes 786440 | tf_op jit(solution)/shard_map/ppermute | solution.py:268
  68.9 0.6 collective-permute-start.4
  69.5 0.6 collective-permute-start.5
  70.1 6.8 %all-to-all-done.2.got = bf16[16,4,16,256]{3,2,1,0:T(8,128)(2,1)S(1)} async-done(((bf16[16,4,16,256]{3,2,1,0:T(8,128)(2,1)}), bf16[16,4,16,256]{3,2,1,0:T(8,128)(2,1)S(1)}, u32[]{:S(2)}, u32[]{:S(2)}) %all-to-all-start.2) | async-done | bytes 524320 | tf_op jit(solution)/shard_map/all_to_all | solution.py:269
  76.8 1.3 %sum.1 = bf16[8,16,1024]{2,1,0:T(8,128)(2,1)} custom-call(s32[2]{0:T(128)S(1)} %pad_add_fusion.me, s32[32]{0:T(128)S(1)} %copy-done.3, bf16[16,4,16,256]{3,2,1,0:T(8,128)(2,1)S(1)} %all-to-all-done.2.got), custom_call_target="tpu_custom_call" | custom-call | tf_op jit(solution)/shard_map/sum/pallas_call | solution.py:270
  78.2 9.9 %all-to-all-start.3 = ((bf16[8,16,1024]{2,1,0:T(8,128)(2,1)}), bf16[8,16,1024]{2,1,0:T(8,128)(2,1)S(1)}, u32[]{:S(2)}, u32[]{:S(2)}) async-start(bf16[8,16,1024]{2,1,0:T(8,128)(2,1)} %sum.1), calls=%async_computation.3 | async-start | bytes 524288 | tf_op jit(solution)/shard_map/all_to_all | solution.py:271
  88.1 0.0 collective-permute-done.3.refs_1_
  88.1 1.6 %merge.1 = bf16[128,4096]{1,0:T(8,128)(2,1)} custom-call(s32[2]{0:T(128)S(1)} %pad_add_fusion.me, bf16[128,1024]{1,0:T(8,128)(2,1)S(1)} %get-tuple-element.15.refs_0_, bf16[128,1024]{1,0:T(8,128)(2,1)S(1)} %collective-permute-done.3.refs_1_, bf16[128,1024]{1,0:T(8,128)(2,1)S(1)} %collective-permute-done.4.refs_2_, ...), custom_call_target="tpu_custom_call" | custom-call | tf_op jit(solution)/shard_map/merge/pallas_call | solution.py:277
  89.7 4.9 %all-to-all-done.3.got = bf16[8,16,1024]{2,1,0:T(8,128)(2,1)S(1)} async-done(((bf16[8,16,1024]{2,1,0:T(8,128)(2,1)}), bf16[8,16,1024]{2,1,0:T(8,128)(2,1)S(1)}, u32[]{:S(2)}, u32[]{:S(2)}) %all-to-all-start.3) | async-done | bytes 262176 | tf_op jit(solution)/shard_map/all_to_all | solution.py:271
  94.6 1.4 %place.1 = f32[4,16,1024]{2,1,0:T(8,128)} custom-call(s32[2]{0:T(128)S(1)} %pad_add_fusion.me, s32[32]{0:T(128)S(1)} %copy-done.3, bf16[8,16,1024]{2,1,0:T(8,128)(2,1)S(1)} %all-to-all-done.3.got), custom_call_target="tpu_custom_call" | custom-call | tf_op jit(solution)/shard_map/place/pallas_call | solution.py:272
  (14 shorter events, 0.0 us)
Async XLA Ops:
  0.7 0.7 copy-start.3
  1.3 0.9 copy-start.2
  3.7 15.8 %all-to-all-start = ((bf16[8,16,1024]{2,1,0:T(8,128)(2,1)}), bf16[8,16,1024]{2,1,0:T(8,128)(2,1)S(1)}, u32[]{:S(2)}, u32[]{:S(2)}) async-start(bf16[8,16,1024]{2,1,0:T(8,128)(2,1)} %pack.1), calls=%async_computation | async-start | bytes 524288 | tf_op jit(solution)/shard_map/all_to_all | solution.py:263
  9.5 0.7 copy-start.4
  10.1 1.2 %copy-start = (bf16[1,128,4096]{2,1,0:T(8,128)(2,1)S(1)}, bf16[1,128,4096]{2,1,0:T(8,128)(2,1)}, u32[]{:S(2)}) copy-start(bf16[1,128,4096]{2,1,0:T(8,128)(2,1)} %param.6) | copy-start | bytes 3145732
  11.4 1.2 %copy-start.1 = (bf16[1,128,4096]{2,1,0:T(8,128)(2,1)S(1)}, bf16[1,128,4096]{2,1,0:T(8,128)(2,1)}, u32[]{:S(2)}) copy-start(bf16[1,128,4096]{2,1,0:T(8,128)(2,1)} %param.8) | copy-start | bytes 3145732
  14.5 12.3 %collective-permute-start = (bf16[272,1024]{1,0:T(8,128)(2,1)}, bf16[272,1024]{1,0:T(8,128)(2,1)S(1)}, u32[]{:S(2)}, u32[]{:S(2)}) collective-permute-start(bf16[272,1024]{1,0:T(8,128)(2,1)} %get-tuple-element.12), channel_id=1, source_target_pairs={{0,1},{1,2},{2,3},{3,0},{4,5},{5,6},{6,7},{7,4},{8,9},{9,10},{10,1... | collective-permute-start | bytes 1671176 | tf_op jit(solution)/shard_map/ppermute | solution.py:260
  15.7 16.0 %collective-permute-start.1 = (bf16[272,1024]{1,0:T(8,128)(2,1)}, bf16[272,1024]{1,0:T(8,128)(2,1)S(1)}, u32[]{:S(2)}, u32[]{:S(2)}) collective-permute-start(bf16[272,1024]{1,0:T(8,128)(2,1)} %get-tuple-element.13), channel_id=1, source_target_pairs={{0,2},{1,3},{2,0},{3,1},{4,6},{5,7},{6,4},{7,5},{8,10},{9,11},{10,... | collective-permute-start | bytes 1671176 | tf_op jit(solution)/shard_map/ppermute | solution.py:260
  18.4 15.0 %collective-permute-start.2 = (bf16[272,1024]{1,0:T(8,128)(2,1)}, bf16[272,1024]{1,0:T(8,128)(2,1)S(1)}, u32[]{:S(2)}, u32[]{:S(2)}) collective-permute-start(bf16[272,1024]{1,0:T(8,128)(2,1)} %get-tuple-element.14), channel_id=1, source_target_pairs={{0,3},{1,0},{2,1},{3,2},{4,7},{5,4},{6,5},{7,6},{8,11},{9,8},{10,9... | collective-permute-start | bytes 1671176 | tf_op jit(solution)/shard_map/ppermute | solution.py:260
  20.8 19.8 %all-to-all-start.1 = ((bf16[16,4,16,256]{3,2,1,0:T(8,128)(2,1)}), bf16[16,4,16,256]{3,2,1,0:T(8,128)(2,1)S(1)}, u32[]{:S(2)}, u32[]{:S(2)}) async-start(bf16[16,4,16,256]{3,2,1,0:T(8,128)(2,1)} %pick.1), calls=%async_computation.1 | async-start | bytes 1048576 | tf_op jit(solution)/shard_map/all_to_all | solution.py:266
  60.2 0.7 copy-start.5
  60.9 0.7 copy-start.7
  61.6 4.6 %copy-start.8 = (bf16[128,1024]{1,0:T(8,128)(2,1)S(1)}, bf16[128,1024]{1,0:T(8,128)(2,1)}, u32[]{:S(2)}) copy-start(bf16[128,1024]{1,0:T(8,128)(2,1)} %copy-done.7) | copy-start | bytes 786436
  61.6 7.3 %copy-start.6 = (bf16[128,1024]{1,0:T(8,128)(2,1)S(1)}, bf16[128,1024]{1,0:T(8,128)(2,1)}, u32[]{:S(2)}) copy-start(bf16[128,1024]{1,0:T(8,128)(2,1)} %copy-done.5) | copy-start | bytes 786436
  61.6 15.2 %all-to-all-start.2 = ((bf16[16,4,16,256]{3,2,1,0:T(8,128)(2,1)}), bf16[16,4,16,256]{3,2,1,0:T(8,128)(2,1)S(1)}, u32[]{:S(2)}, u32[]{:S(2)}) async-start(bf16[16,4,16,256]{3,2,1,0:T(8,128)(2,1)} %bitcast.9), calls=%async_computation.2 | async-start | bytes 1048576 | tf_op jit(solution)/shard_map/all_to_all | solution.py:269
  66.3 21.8 %collective-permute-start.3 = (bf16[128,1024]{1,0:T(8,128)(2,1)S(1)}, bf16[128,1024]{1,0:T(8,128)(2,1)S(1)}, u32[]{:S(2)}, u32[]{:S(2)}) collective-permute-start(bf16[128,1024]{1,0:T(8,128)(2,1)S(1)} %copy-done.8), channel_id=1, source_target_pairs={{0,3},{1,0},{2,1},{3,2},{4,7},{5,4},{6,5},{7,6},{8,11},{9,8},{10,9... | collective-permute-start | bytes 786440 | tf_op jit(solution)/shard_map/ppermute | solution.py:268
  68.9 19.2 %collective-permute-start.4 = (bf16[128,1024]{1,0:T(8,128)(2,1)S(1)}, bf16[128,1024]{1,0:T(8,128)(2,1)S(1)}, u32[]{:S(2)}, u32[]{:S(2)}) collective-permute-start(bf16[128,1024]{1,0:T(8,128)(2,1)S(1)} %copy-done.6), channel_id=1, source_target_pairs={{0,2},{1,3},{2,0},{3,1},{4,6},{5,7},{6,4},{7,5},{8,10},{9,11},{10,... | collective-permute-start | bytes 786440 | tf_op jit(solution)/shard_map/ppermute | solution.py:268
  69.5 18.6 %collective-permute-start.5 = (bf16[128,1024]{1,0:T(8,128)(2,1)S(1)}, bf16[128,1024]{1,0:T(8,128)(2,1)S(1)}, u32[]{:S(2)}, u32[]{:S(2)}) collective-permute-start(bf16[128,1024]{1,0:T(8,128)(2,1)S(1)} %get-tuple-element.18), channel_id=1, source_target_pairs={{0,1},{1,2},{2,3},{3,0},{4,5},{5,6},{6,7},{7,4},{8,9},{9,10},{10,1... | collective-permute-start | bytes 786440 | tf_op jit(solution)/shard_map/ppermute | solution.py:268
  78.2 16.4 %all-to-all-start.3 = ((bf16[8,16,1024]{2,1,0:T(8,128)(2,1)}), bf16[8,16,1024]{2,1,0:T(8,128)(2,1)S(1)}, u32[]{:S(2)}, u32[]{:S(2)}) async-start(bf16[8,16,1024]{2,1,0:T(8,128)(2,1)} %sum.1), calls=%async_computation.3 | async-start | bytes 524288 | tf_op jit(solution)/shard_map/all_to_all | solution.py:271

commit v4 on v3

--- a/solution.py
+++ b/solution.py
@@ -24,51 +24,76 @@
 VMEM = pltpu.MemorySpace.VMEM
 
 
-def pack_kernel(docs, me, slots, kv, out):
+def pack_kernel(docs, me, slots_any, kv, out, slots, sems):
+    fetch = pltpu.make_async_copy(slots_any, slots, sems.at[docs])
+    fetch.start()
+    fetch.wait()
+    copies = []
     for d in range(docs):
         local = 0
         for j in range(IMAGES):
             s = slots[d * IMAGES + j]
             local += jnp.where(s // IMAGES == me[0], s % IMAGES, 0)
-        out[d] = kv[local]
-
-
-def pick_kernel(me, slots, got, out):
-    for j in range(IMAGES):
-        rows = got[slots[me[0] * IMAGES + j] // IMAGES]
-        heads = [
-            jnp.concatenate(
-                [
-                    rows[:, c * WIDTH : (c + 1) * WIDTH],
-                    rows[:, KEY_COLUMNS + c * WIDTH : KEY_COLUMNS + (c + 1) * WIDTH],
-                ],
-                axis=1,
-            )
-            for c in range(KV_HEADS)
-        ]
-        along_z = me[0] % 2 == 0
-        for y in range(LINE):
-            for z in range(LINE):
-                out[y * LINE + z, j] = jnp.where(along_z, heads[z], heads[y])
-
-
-def payload_kernel(me, q, d_out, spans, *outs):
+        copies.append(pltpu.make_async_copy(kv.at[local], out.at[d], sems.at[d]))
+        copies[-1].start()
+    for copy in copies:
+        copy.wait()
+
+
+def pick_kernel(me, slots, got, out, heads, sems):
+    for j in range(IMAGES):
+        owner = slots[me[0] * IMAGES + j] // IMAGES
+        for c in range(KV_HEADS):
+            columns = slice(c * WIDTH, (c + 1) * WIDTH)
+            heads[c, j, :, :WIDTH] = got[owner, :, columns]
+            columns = slice(KEY_COLUMNS + c * WIDTH, KEY_COLUMNS + (c + 1) * WIDTH)
+            heads[c, j, :, WIDTH:] = got[owner, :, columns]
+    along_z = me[0] % 2 == 0
+    copies = []
+    for y in range(LINE):
+        for z in range(LINE):
+            head = jnp.where(along_z, z, y)
+            at = y * LINE + z
+            copies.append(pltpu.make_async_copy(heads.at[head], out.at[at], sems.at[at]))
+            copies[-1].start()
+    for copy in copies:
+        copy.wait()
+
+
+def payload_kernel(me, q, d_out, spans, *refs):
+    outs, wide, sems = refs[:LINE], refs[LINE], refs[LINE + 1]
     tokens = q.shape[0]
     width = q.shape[1] // KV_HEADS
-    for k, out in enumerate(outs):
+    copies = []
+    for k in [1, 2, 3, 0]:
         columns = pl.ds(pl.multiple_of(lax.rem(me[1] + k, LINE) * width, WIDTH), width)
-        out[:tokens] = q[:, columns]
-        out[tokens : 2 * tokens] = d_out[:, columns]
-        out[2 * tokens :] = jnp.zeros_like(out[2 * tokens :])
-        out[2 * tokens : 2 * tokens + 2, :tokens] = spans[...].astype(jnp.bfloat16)
+        copies += [
+            pltpu.make_async_copy(q.at[:, columns], outs[k].at[:tokens], sems.at[3 * k]),
+            pltpu.make_async_copy(
+                d_out.at[:, columns], outs[k].at[tokens : 2 * tokens], sems.at[3 * k + 1]
+            ),
+        ]
+    for copy in copies:
+        copy.start()
+    wide[...] = jnp.zeros_like(wide)
+    wide[:2, :tokens] = spans[...].astype(jnp.bfloat16)
+    for k in range(LINE):
+        copies.append(pltpu.make_async_copy(wide, outs[k].at[2 * tokens :], sems.at[3 * k + 2]))
+        copies[-1].start()
+    for copy in copies:
+        copy.wait()
 
 
 def merge_kernel(me, *refs):
-    *parts, out = refs
+    parts, out, sems = refs[:LINE], refs[LINE], refs[LINE + 1]
     width = out.shape[1] // KV_HEADS
+    copies = []
     for k, part in enumerate(parts):
         columns = pl.ds(pl.multiple_of(lax.rem(me[1] + k, LINE) * width, WIDTH), width)
-        out[:, columns] = part[...]
+        copies.append(pltpu.make_async_copy(part, out.at[:, columns], sems.at[k]))
+        copies[-1].start()
+    for copy in copies:
+        copy.wait()
 
 
 def softmax_gradients(scores, d_probs, seen):
@@ -248,21 +273,44 @@
     images, rows, columns = image_kv.shape
     tokens, width = queries.shape[1], queries.shape[2] // KV_HEADS
     both = ("doc", "ctx")
-    params = pltpu.CompilerParams(vmem_limit_bytes=VMEM_LIMIT)
+    anywhere = pl.BlockSpec(memory_space=pl.ANY)
+    in_smem = pl.BlockSpec(memory_space=SMEM)
+    block = jax.ShapeDtypeStruct((docs, rows, columns), jnp.bfloat16)
+    send = pl.pallas_call(
+        functools.partial(pack_kernel, docs),
+        in_specs=[in_smem, anywhere, anywhere],
+        out_specs=anywhere,
+        out_shape=block,
+        scratch_shapes=[
+            pltpu.SMEM(image_slots.shape, jnp.int32),
+            pltpu.SemaphoreType.DMA((docs + 1,)),
+        ],
+        name="pack",
+    )(me, image_slots, image_kv)
+    got = lax.all_to_all(send, "doc", 0, 0)
     pieces = pl.pallas_call(
         payload_kernel,
-        in_specs=[pl.BlockSpec(memory_space=SMEM)] + [pl.BlockSpec(memory_space=VMEM)] * 3,
-        out_specs=[pl.BlockSpec(memory_space=VMEM)] * LINE,
+        in_specs=[in_smem, anywhere, anywhere, pl.BlockSpec(memory_space=VMEM)],
+        out_specs=[anywhere] * LINE,
         out_shape=[jax.ShapeDtypeStruct((2 * tokens + PAD, width), jnp.bfloat16)] * LINE,
-        compiler_params=params,
+        scratch_shapes=[
+            pltpu.VMEM((PAD, width), jnp.bfloat16),
+            pltpu.SemaphoreType.DMA((3 * LINE,)),
+        ],
         name="payload",
     )(me, queries[0], d_out[0], spans[0].T)
     pieces = [pieces[0]] + [lax.ppermute(pieces[k], both, shift(docs, k)) for k in range(1, LINE)]
-    block = jax.ShapeDtypeStruct((docs, rows, columns), jnp.bfloat16)
-    send = small(functools.partial(pack_kernel, docs), block, "pack")(me, image_slots, image_kv)
-    got = lax.all_to_all(send, "doc", 0, 0)
-    one_head = jax.ShapeDtypeStruct((texts, images, rows, 2 * WIDTH), jnp.bfloat16)
-    send = small(pick_kernel, one_head, "pick")(me, image_slots, got)
+    send = pl.pallas_call(
+        pick_kernel,
+        in_specs=[in_smem, in_smem, pl.BlockSpec(memory_space=VMEM)],
+        out_specs=anywhere,
+        out_shape=jax.ShapeDtypeStruct((texts, images, rows, 2 * WIDTH), jnp.bfloat16),
+        scratch_shapes=[
+            pltpu.VMEM((KV_HEADS, images, rows, 2 * WIDTH), jnp.bfloat16),
+            pltpu.SemaphoreType.DMA((texts,)),
+        ],
+        name="pick",
+    )(me, image_slots, got)
     kv = lax.all_to_all(send, "ctx", 0, 0).reshape(texts * images * rows, 2 * WIDTH)
     *dqs, dkv = gradients(attn_gate.reshape(1, 1), kv, pieces)
     dqs = [dqs[0]] + [lax.ppermute(dqs[k], both, shift(docs, -k)) for k in range(1, LINE)]
@@ -276,10 +324,10 @@
     )(me, image_slots, got)
     d_queries = pl.pallas_call(
         merge_kernel,
-        in_specs=[pl.BlockSpec(memory_space=SMEM)] + [pl.BlockSpec(memory_space=VMEM)] * LINE,
-        out_specs=pl.BlockSpec(memory_space=VMEM),
+        in_specs=[in_smem] + [anywhere] * LINE,
+        out_specs=anywhere,
         out_shape=jax.ShapeDtypeStruct(queries.shape[1:], jnp.bfloat16),
-        compiler_params=params,
+        scratch_shapes=[pltpu.SemaphoreType.DMA((LINE,))],
         name="merge",
     )(me, *dqs)
     return d_queries[None], d_image_kv

time: 96.7 us -> 193 us (2.00)
  Pallas kernels: 28.6 us -> 134 us
  waiting for transfers between devices: 25.6 us -> 18.9 us
  local copies, waits for them, and re-layouts: 6.02 us -> 2.27 us
    pallas_call x4, Pallas kernels: 6.28 us -> 112 us  [the longest x1 65.4 us: shards(): pl.pallas_call(payload_kernel, in_specs=[in_smem, anywhere, anywhere, pl....]
    all_to_all x2, waiting for transfers between devices: 4.9 us -> 0.01 us  [shards(): got = lax.all_to_all(send, 'doc', 0, 0)]
    unnamed x18, local copies, waits for them, and re-layouts: 6.02 us -> 2.27 us
    ppermute x3, waiting for transfers between devices: 6.58 us -> 3.59 us  [shards(): lax.ppermute(pieces[k], both, shift(docs, k))]
  transfers between devices with their start and end apart: 10 -> 10, of which waited for: 5 -> 3; matrix products, arithmetic and copies ran while one was open for 0% -> 0% of each run, Pallas kernels for 6% -> 53%
where the time goes in v4:
time: 193 us; the launch traced here: 192 us
  Pallas kernels  134 us (69%)
  starting transfers between devices  34.8 us (18%)
  waiting for transfers between devices  18.9 us (10%)
  local copies, waits for them, and re-layouts  2.27 us (1%)
    pallas_call x1, Pallas kernels, shards(): pl.pallas_call(payload_kernel, in_specs=[in_smem, anywhere, anywhere, pl....  65.4 us
    pallas_call x1, Pallas kernels, shards(): pl.pallas_call(merge_kernel, in_specs=[in_smem] + [anywhere] * LINE, out_...  33.7 us
    pallas_call x1, Pallas kernels, gradients(): pl.pallas_call(grad_kernel, grid=(LINE,), in_specs=[whole((1, 1)), whole(...  19.5 us
    all_to_all x2, starting transfers between devices, shards(): got = lax.all_to_all(send, 'doc', 0, 0)  15.5 us
    pallas_call x1, Pallas kernels, shards(): pl.pallas_call(functools.partial(pack_kernel, docs), in_specs=[in_smem, a...  10.5 us
    all_to_all x1, waiting for transfers between devices, shards(): lax.all_to_all(send, 'ctx', 0, 0).reshape(texts * images * rows, 2 * WIDTH)  8.27 us
    all_to_all x1, waiting for transfers between devices, shards(): lax.all_to_all(dkv.reshape(texts, images, rows, 2 * WIDTH), 'ctx', 0, 0)  7.06 us
    all_to_all x1, starting transfers between devices, shards(): lax.all_to_all(send, 'ctx', 0, 0).reshape(texts * images * rows, 2 * WIDTH)  5.39 us
  transfers between devices with their start and end apart: 10, of which 3 were waited for; matrix products, arithmetic and copies ran while one was open for 0% of the time, Pallas kernels for 53%

profile of v4, /device:TPU:1, one launch (start us, length us, event | category | flops | bytes accessed | tf_op | source)
XLA Modules:
  0.0 192.0 jit_solution(16619278033981869154)
XLA Ops:
  0.7 0.7 pad_add_fusion.me
  1.3 10.5 %pack.1 = bf16[8,16,1024]{2,1,0:T(8,128)(2,1)} custom-call(s32[2]{0:T(128)} %pad_add_fusion.me, s32[32]{0:T(128)} %slots.5, bf16[4,16,1024]{2,1,0:T(8,128)(2,1)} %kv.1), custom_call_target="tpu_custom_call" | custom-call | tf_op jit(solution)/shard_map/pack/pallas_call | solution.py:279
  11.8 5.8 %all-to-all-start = ((bf16[8,16,1024]{2,1,0:T(8,128)(2,1)}), bf16[8,16,1024]{2,1,0:T(8,128)(2,1)S(1)}, u32[]{:S(2)}, u32[]{:S(2)}) async-start(bf16[8,16,1024]{2,1,0:T(8,128)(2,1)} %pack.1), calls=%async_computation | async-start | bytes 524288 | tf_op jit(solution)/shard_map/all_to_all | solution.py:290
  17.6 65.4 %payload.1 = (bf16[272,1024]{1,0:T(8,128)(2,1)}, bf16[272,1024]{1,0:T(8,128)(2,1)}, bf16[272,1024]{1,0:T(8,128)(2,1)}, bf16[272,1024]{1,0:T(8,128)(2,1)}) custom-call(s32[2]{0:T(128)} %pad_add_fusion.me, bf16[128,4096]{1,0:T(8,128)(2,1)} %bitcast.14, bf16[128,4096]{1,0:T(8,128)(2,1)} %bitcast.15, s32[2,128]{1,0:T(2,128)} %bitcast.16), custom_call_target="tpu_custom_call" | custom-call | tf_op jit(solution)/shard_map/payload/pallas_call | solution.py:291
  83.1 1.4 collective-permute-start
  84.4 2.6 %collective-permute-start.1 = (bf16[272,1024]{1,0:T(8,128)(2,1)}, bf16[272,1024]{1,0:T(8,128)(2,1)S(1)}, u32[]{:S(2)}, u32[]{:S(2)}) collective-permute-start(bf16[272,1024]{1,0:T(8,128)(2,1)} %get-tuple-element.13), channel_id=1, source_target_pairs={{0,2},{1,3},{2,0},{3,1},{4,6},{5,7},{6,4},{7,5},{8,10},{9,11},{10,... | collective-permute-start | bytes 1671176 | tf_op jit(solution)/shard_map/ppermute | solution.py:302
  87.0 1.1 collective-permute-start.2
  88.1 0.0 all-to-all-done.got
  88.1 0.7 copy-done.5
  88.8 1.9 %pick.1 = bf16[16,4,16,256]{3,2,1,0:T(8,128)(2,1)} custom-call(s32[2]{0:T(128)} %pad_add_fusion.me, s32[32]{0:T(128)} %slots.5, bf16[8,16,1024]{2,1,0:T(8,128)(2,1)} %copy-done.5), custom_call_target="tpu_custom_call" | custom-call | tf_op jit(solution)/shard_map/pick/pallas_call | solution.py:303
  90.8 0.0 copy-start.4
  90.8 5.4 %all-to-all-start.1 = ((bf16[16,4,16,256]{3,2,1,0:T(8,128)(2,1)}), bf16[16,4,16,256]{3,2,1,0:T(8,128)(2,1)S(1)}, u32[]{:S(2)}, u32[]{:S(2)}) async-start(bf16[16,4,16,256]{3,2,1,0:T(8,128)(2,1)} %pick.1), calls=%async_computation.1 | async-start | bytes 1048576 | tf_op jit(solution)/shard_map/all_to_all | solution.py:314
  96.8 0.0 collective-permute-done.refs_1_
  96.8 3.6 %collective-permute-done.1.refs_2_ = bf16[272,1024]{1,0:T(8,128)(2,1)S(1)} collective-permute-done((bf16[272,1024]{1,0:T(8,128)(2,1)}, bf16[272,1024]{1,0:T(8,128)(2,1)S(1)}, u32[]{:S(2)}, u32[]{:S(2)}) %collective-permute-start.1) | collective-permute-done | bytes 557088 | tf_op jit(solution)/shard_map/ppermute | solution.py:302
  100.4 8.3 %all-to-all-done.1 = bf16[16,4,16,256]{3,2,1,0:T(8,128)(2,1)S(1)} async-done(((bf16[16,4,16,256]{3,2,1,0:T(8,128)(2,1)}), bf16[16,4,16,256]{3,2,1,0:T(8,128)(2,1)S(1)}, u32[]{:S(2)}, u32[]{:S(2)}) %all-to-all-start.1) | async-done | bytes 524320 | tf_op jit(solution)/shard_map/all_to_all | solution.py:314
  108.7 19.5 %gradients.1 = (bf16[128,1024]{1,0:T(8,128)(2,1)S(1)}, bf16[128,1024]{1,0:T(8,128)(2,1)S(1)}, bf16[128,1024]{1,0:T(8,128)(2,1)S(1)}, bf16[128,1024]{1,0:T(8,128)(2,1)S(1)}, bf16[1024,256]{1,0:T(8,128)(2,1)}) custom-call(f32[1,1]{1,0:T(1,128)} %bitcast.11.gate, bf16[1024,256]{1,0:T(8,128)(2,1)S(1)} %bitcast.12, bf16[272,1024]{1,0:T(8,128)(2,1)S(1)} %copy-done.4, ...), custom_call_target="tpu_custom_call" | custom-call | flops 5368709120 | bytes 4194304 | tf_op jit(solution)/shard_map/gradients/pallas_call | solution.py:190
  128.3 0.7 copy-done
  129.0 5.1 %all-to-all-start.2 = ((bf16[16,4,16,256]{3,2,1,0:T(8,128)(2,1)}), bf16[16,4,16,256]{3,2,1,0:T(8,128)(2,1)S(1)}, u32[]{:S(2)}, u32[]{:S(2)}) async-start(bf16[16,4,16,256]{3,2,1,0:T(8,128)(2,1)} %bitcast.9), calls=%async_computation.2 | async-start | bytes 1048576 | tf_op jit(solution)/shard_map/all_to_all | solution.py:317
  134.1 2.6 %collective-permute-start.3 = (bf16[128,1024]{1,0:T(8,128)(2,1)S(1)}, bf16[128,1024]{1,0:T(8,128)(2,1)S(1)}, u32[]{:S(2)}, u32[]{:S(2)}) collective-permute-start(bf16[128,1024]{1,0:T(8,128)(2,1)S(1)} %get-tuple-element.16), channel_id=1, source_target_pairs={{0,3},{1,0},{2,1},{3,2},{4,7},{5,4},{6,5},{7,6},{8,11},{9,8},{10,9... | collective-permute-start | bytes 786440 | tf_op jit(solution)/shard_map/ppermute | solution.py:316
  136.7 0.6 collective-permute-start.4
  137.2 0.6 collective-permute-start.5
  137.8 7.1 %all-to-all-done.2.got = bf16[16,4,16,256]{3,2,1,0:T(8,128)(2,1)S(1)} async-done(((bf16[16,4,16,256]{3,2,1,0:T(8,128)(2,1)}), bf16[16,4,16,256]{3,2,1,0:T(8,128)(2,1)S(1)}, u32[]{:S(2)}, u32[]{:S(2)}) %all-to-all-start.2) | async-done | bytes 524320 | tf_op jit(solution)/shard_map/all_to_all | solution.py:317
  144.9 1.3 sum.1
  146.2 9.7 %all-to-all-start.3 = ((bf16[8,16,1024]{2,1,0:T(8,128)(2,1)}), bf16[8,16,1024]{2,1,0:T(8,128)(2,1)S(1)}, u32[]{:S(2)}, u32[]{:S(2)}) async-start(bf16[8,16,1024]{2,1,0:T(8,128)(2,1)} %sum.1), calls=%async_computation.3 | async-start | bytes 524288 | tf_op jit(solution)/shard_map/all_to_all | solution.py:319
  155.9 0.0 collective-permute-done.3.refs_1_
  155.9 0.0 collective-permute-done.4.refs_2_
  156.0 0.0 collective-permute-done.5.refs_3_
  156.0 0.7 copy-done.6
  156.7 0.1 copy-done.7
  156.7 0.1 copy-done.8
  156.8 33.7 %merge.1 = bf16[128,4096]{1,0:T(8,128)(2,1)} custom-call(s32[2]{0:T(128)} %pad_add_fusion.me, bf16[128,1024]{1,0:T(8,128)(2,1)} %copy-done, bf16[128,1024]{1,0:T(8,128)(2,1)} %copy-done.6, bf16[128,1024]{1,0:T(8,128)(2,1)} %copy-done.7, bf16[128,1024]{1,0:T(8,128)(2,1)} %copy-done.8), custom_call_target="tpu_custom_call" | custom-call | tf_op jit(solution)/shard_map/merge/pallas_call | solution.py:325
  190.6 1.4 place.1
  (14 shorter events, 0.0 us)
Async XLA Ops:
  11.8 76.3 %all-to-all-start = ((bf16[8,16,1024]{2,1,0:T(8,128)(2,1)}), bf16[8,16,1024]{2,1,0:T(8,128)(2,1)S(1)}, u32[]{:S(2)}, u32[]{:S(2)}) async-start(bf16[8,16,1024]{2,1,0:T(8,128)(2,1)} %pack.1), calls=%async_computation | async-start | bytes 524288 | tf_op jit(solution)/shard_map/all_to_all | solution.py:290
  83.1 13.8 %collective-permute-start = (bf16[272,1024]{1,0:T(8,128)(2,1)}, bf16[272,1024]{1,0:T(8,128)(2,1)S(1)}, u32[]{:S(2)}, u32[]{:S(2)}) collective-permute-start(bf16[272,1024]{1,0:T(8,128)(2,1)} %get-tuple-element.12), channel_id=1, source_target_pairs={{0,1},{1,2},{2,3},{3,0},{4,5},{5,6},{6,7},{7,4},{8,9},{9,10},{10,1... | collective-permute-start | bytes 1671176 | tf_op jit(solution)/shard_map/ppermute | solution.py:302
  84.4 16.0 %collective-permute-start.1 = (bf16[272,1024]{1,0:T(8,128)(2,1)}, bf16[272,1024]{1,0:T(8,128)(2,1)S(1)}, u32[]{:S(2)}, u32[]{:S(2)}) collective-permute-start(bf16[272,1024]{1,0:T(8,128)(2,1)} %get-tuple-element.13), channel_id=1, source_target_pairs={{0,2},{1,3},{2,0},{3,1},{4,6},{5,7},{6,4},{7,5},{8,10},{9,11},{10,... | collective-permute-start | bytes 1671176 | tf_op jit(solution)/shard_map/ppermute | solution.py:302
  87.0 13.4 %collective-permute-start.2 = (bf16[272,1024]{1,0:T(8,128)(2,1)}, bf16[272,1024]{1,0:T(8,128)(2,1)S(1)}, u32[]{:S(2)}, u32[]{:S(2)}) collective-permute-start(bf16[272,1024]{1,0:T(8,128)(2,1)} %get-tuple-element.14), channel_id=1, source_target_pairs={{0,3},{1,0},{2,1},{3,2},{4,7},{5,4},{6,5},{7,6},{8,11},{9,8},{10,9... | collective-permute-start | bytes 1671176 | tf_op jit(solution)/shard_map/ppermute | solution.py:302
  88.1 0.7 copy-start.5
  90.8 17.9 %copy-start.4 = (bf16[272,1024]{1,0:T(8,128)(2,1)S(1)}, bf16[272,1024]{1,0:T(8,128)(2,1)}, u32[]{:S(2)}) copy-start(bf16[272,1024]{1,0:T(8,128)(2,1)} %get-tuple-element.11.refs_0_) | copy-start | bytes 1671172
  90.8 17.9 %all-to-all-start.1 = ((bf16[16,4,16,256]{3,2,1,0:T(8,128)(2,1)}), bf16[16,4,16,256]{3,2,1,0:T(8,128)(2,1)S(1)}, u32[]{:S(2)}, u32[]{:S(2)}) async-start(bf16[16,4,16,256]{3,2,1,0:T(8,128)(2,1)} %pick.1), calls=%async_computation.1 | async-start | bytes 1048576 | tf_op jit(solution)/shard_map/all_to_all | solution.py:314
  128.3 0.7 copy-start
  129.0 15.9 %all-to-all-start.2 = ((bf16[16,4,16,256]{3,2,1,0:T(8,128)(2,1)}), bf16[16,4,16,256]{3,2,1,0:T(8,128)(2,1)S(1)}, u32[]{:S(2)}, u32[]{:S(2)}) async-start(bf16[16,4,16,256]{3,2,1,0:T(8,128)(2,1)} %bitcast.9), calls=%async_computation.2 | async-start | bytes 1048576 | tf_op jit(solution)/shard_map/all_to_all | solution.py:317
  134.1 21.9 %collective-permute-start.3 = (bf16[128,1024]{1,0:T(8,128)(2,1)S(1)}, bf16[128,1024]{1,0:T(8,128)(2,1)S(1)}, u32[]{:S(2)}, u32[]{:S(2)}) collective-permute-start(bf16[128,1024]{1,0:T(8,128)(2,1)S(1)} %get-tuple-element.16), channel_id=1, source_target_pairs={{0,3},{1,0},{2,1},{3,2},{4,7},{5,4},{6,5},{7,6},{8,11},{9,8},{10,9... | collective-permute-start | bytes 786440 | tf_op jit(solution)/shard_map/ppermute | solution.py:316
  136.7 8.2 %copy-start.1 = (s32[2]{0:T(128)S(1)}, s32[2]{0:T(128)}, u32[]{:S(2)}) copy-start(s32[2]{0:T(128)} %pad_add_fusion.me) | copy-start | bytes 28
  136.7 8.2 %copy-start.3 = (s32[32]{0:T(128)S(1)}, s32[32]{0:T(128)}, u32[]{:S(2)}) copy-start(s32[32]{0:T(128)} %slots.5) | copy-start | bytes 388
  136.7 19.3 %collective-permute-start.4 = (bf16[128,1024]{1,0:T(8,128)(2,1)S(1)}, bf16[128,1024]{1,0:T(8,128)(2,1)S(1)}, u32[]{:S(2)}, u32[]{:S(2)}) collective-permute-start(bf16[128,1024]{1,0:T(8,128)(2,1)S(1)} %get-tuple-element.17), channel_id=1, source_target_pairs={{0,2},{1,3},{2,0},{3,1},{4,6},{5,7},{6,4},{7,5},{8,10},{9,11},{10,... | collective-permute-start | bytes 786440 | tf_op jit(solution)/shard_map/ppermute | solution.py:316
  137.2 18.7 %collective-permute-start.5 = (bf16[128,1024]{1,0:T(8,128)(2,1)S(1)}, bf16[128,1024]{1,0:T(8,128)(2,1)S(1)}, u32[]{:S(2)}, u32[]{:S(2)}) collective-permute-start(bf16[128,1024]{1,0:T(8,128)(2,1)S(1)} %get-tuple-element.18), channel_id=1, source_target_pairs={{0,1},{1,2},{2,3},{3,0},{4,5},{5,6},{6,7},{7,4},{8,9},{9,10},{10,1... | collective-permute-start | bytes 786440 | tf_op jit(solution)/shard_map/ppermute | solution.py:316
  146.2 44.3 %all-to-all-start.3 = ((bf16[8,16,1024]{2,1,0:T(8,128)(2,1)}), bf16[8,16,1024]{2,1,0:T(8,128)(2,1)S(1)}, u32[]{:S(2)}, u32[]{:S(2)}) async-start(bf16[8,16,1024]{2,1,0:T(8,128)(2,1)} %sum.1), calls=%async_computation.3 | async-start | bytes 524288 | tf_op jit(solution)/shard_map/all_to_all | solution.py:319
  155.9 0.7 copy-start.6
  156.0 0.8 copy-start.7
  156.0 0.9 copy-start.8
  156.8 33.7 %copy-start.2 = (s32[2]{0:T(128)S(1)}, s32[2]{0:T(128)}, u32[]{:S(2)}) copy-start(s32[2]{0:T(128)} %pad_add_fusion.me) | copy-start | bytes 28

commit v5 on v3

v5 whole, which is shorter than its diff:
```python
import functools

import jax
import jax.numpy as jnp
from jax import lax
from jax.experimental import pallas as pl
from jax.experimental.pallas import tpu as pltpu
from jax.sharding import PartitionSpec as P

KV_HEADS = 4
WIDTH = 128
GROUP = 8
KEY_COLUMNS = 512
IMAGES = 4
LOW = -1e30
SCALE = WIDTH ** (-0.5)
LOG2E = 1.4426950408889634
LINE = 4
BLOCK_HEADS = 2
PAD = 16
VMEM_LIMIT = 48 * 1024 * 1024

SMEM = pltpu.MemorySpace.SMEM
VMEM = pltpu.MemorySpace.VMEM
HBM = pltpu.MemorySpace.HBM


def place_on_line():
    doc, text = lax.axis_index("doc"), lax.axis_index("ctx")
    return doc, jnp.where(doc % 2 == 0, text % LINE, text // LINE)


def pack_kernel(docs, slots_any, kv, out, slots, held, sems):
    fetch_slots = pltpu.make_async_copy(slots_any, slots, sems.at[docs])
    fetch = pltpu.make_async_copy(kv, held, sems.at[docs + 1])
    fetch_slots.start()
    fetch.start()
    fetch_slots.wait()
    doc, _ = place_on_line()
    copies = []
    for d in range(docs):
        local = 0
        for j in range(IMAGES):
            s = slots[d * IMAGES + j]
            local += jnp.where(s // IMAGES == doc, s % IMAGES, 0)
        copies.append(pltpu.make_async_copy(held.at[local], out.at[d], sems.at[d]))
    fetch.wait()
    for copy in copies:
        copy.start()
    for copy in copies:
        copy.wait()


def pick_kernel(slots, got, out):
    doc, _ = place_on_line()
    for j in range(IMAGES):
        rows = got[slots[doc * IMAGES + j] // IMAGES]
        heads = [
            jnp.concatenate(
                [
                    rows[:, c * WIDTH : (c + 1) * WIDTH],
                    rows[:, KEY_COLUMNS + c * WIDTH : KEY_COLUMNS + (c + 1) * WIDTH],
                ],
                axis=1,
            )
            for c in range(KV_HEADS)
        ]
        along_z = doc % 2 == 0
        for y in range(LINE):
            for z in range(LINE):
                out[y * LINE + z, j] = jnp.where(along_z, heads[z], heads[y])


def payload_kernel(q, d_out, spans, *refs):
    outs, held, sems = refs[:LINE], refs[LINE], refs[LINE + 1]
    tokens = q.shape[0]
    width = q.shape[1] // KV_HEADS
    _, place = place_on_line()
    order = [2, 1, 3, 0]
    fetches = []
    for k in order:
        columns = pl.ds(pl.multiple_of(lax.rem(place + k, LINE) * width, WIDTH), width)
        pair = [
            pltpu.make_async_copy(q.at[:, columns], held.at[k, :tokens], sems.at[3 * k]),
            pltpu.make_async_copy(
                d_out.at[:, columns], held.at[k, tokens : 2 * tokens], sems.at[3 * k + 1]
            ),
        ]
        for copy in pair:
            copy.start()
        fetches.append(pair)
    for k in order:
        held[k, 2 * tokens :] = jnp.zeros_like(held[k, 2 * tokens :])
        held[k, 2 * tokens : 2 * tokens + 2, :tokens] = spans[...].astype(jnp.bfloat16)
    copies = []
    for k, pair in zip(order, fetches):
        for copy in pair:
            copy.wait()
        copies.append(pltpu.make_async_copy(held.at[k], outs[k], sems.at[3 * k + 2]))
        copies[-1].start()
    for copy in copies:
        copy.wait()


def merge_kernel(*refs):
    _, place = place_on_line()
    *parts, out = refs
    width = out.shape[1] // KV_HEADS
    for k, part in enumerate(parts):
        columns = pl.ds(pl.multiple_of(lax.rem(place + k, LINE) * width, WIDTH), width)
        out[:, columns] = part[...]


def softmax_gradients(scores, d_probs, seen):
    keys, rows = scores.shape
    scores = scores.reshape(-1, IMAGES, 16, rows)
    d_probs = d_probs.reshape(-1, IMAGES, 16, rows)
    row_max = None
    for j in range(IMAGES):
        top = jnp.max(jnp.max(scores[:, j], axis=0), axis=0, keepdims=True)
        top = jnp.where(seen[j], top, LOW)
        row_max = top if row_max is None else jnp.maximum(row_max, top)
    row_max = row_max * (SCALE * LOG2E)
    terms = []
    total = 0.0
    dots = 0.0
    for j in range(IMAGES):
        term = jnp.exp2(scores[:, j] * (SCALE * LOG2E) - jnp.where(seen[j], row_max, -LOW))
        total += jnp.sum(jnp.sum(term, axis=0), axis=0, keepdims=True)
        dots += jnp.sum(jnp.sum(term * d_probs[:, j], axis=0), axis=0, keepdims=True)
        terms.append(term)
    inverse = 1.0 / total
    delta = dots * inverse
    low_probs = []
    d_scores = []
    for j in range(IMAGES):
        probs = terms[j] * inverse
        low_probs.append(probs.astype(jnp.bfloat16)[:, None])
        d_scores.append((probs * (d_probs[:, j] - delta)).astype(jnp.bfloat16)[:, None])
    low_probs = jnp.concatenate(low_probs, axis=1).reshape(keys, rows)
    d_scores = jnp.concatenate(d_scores, axis=1).reshape(keys, rows)
    return low_probs, d_scores


def grad_kernel(gate, kv_any, *refs):
    pieces, dqs, dkv_any = refs[:LINE], refs[LINE : 2 * LINE], refs[2 * LINE]
    kv, held, dq, dkv, keys_t, probs, d_scores, q_rows, d_rows, acc, sems = refs[2 * LINE + 1 :]
    tokens = dqs[0].shape[0]
    block = BLOCK_HEADS * tokens
    fetch_kv = pltpu.make_async_copy(kv_any, kv, sems.at[2 * LINE])
    fetch_kv.start()
    for k in range(LINE):
        pltpu.make_async_copy(pieces[k], held.at[k], sems.at[k]).start()
    fetch_kv.wait()
    keys_t[...] = kv[:, :WIDTH].T
    acc[...] = jnp.zeros_like(acc)
    factor = jnp.tanh(gate[...])
    transposed = (((1,), (1,)), ((), ()))

    def work(step, carry):
        pltpu.make_async_copy(pieces[0], held.at[step], sems.at[step]).wait()
        for h in range(GROUP):
            rows, columns = slice(h * tokens, (h + 1) * tokens), slice(h * WIDTH, (h + 1) * WIDTH)
            q_rows[rows] = held[step, :tokens, columns]
            wide = held[step, tokens : 2 * tokens, columns].astype(jnp.float32)
            d_rows[rows] = (wide * factor).astype(jnp.bfloat16)
        spans = held[step, 2 * tokens :, :tokens].astype(jnp.float32)
        low = jnp.concatenate([spans[0:1]] * BLOCK_HEADS, axis=1)
        high = jnp.concatenate([spans[1:2]] * BLOCK_HEADS, axis=1)
        seen = [(low <= j) & (j < high) for j in range(IMAGES)]
        for at in range(0, GROUP * tokens, block):
            rows = slice(at, at + block)
            scores = lax.dot_general(
                kv[:, :WIDTH], q_rows[rows], transposed, preferred_element_type=jnp.float32
            )
            d_probs = lax.dot_general(
                kv[:, WIDTH:], d_rows[rows], transposed, preferred_element_type=jnp.float32
            )
            probs[:, rows], d_scores[:, rows] = softmax_gradients(scores, d_probs, seen)
        acc[:, :WIDTH] += jnp.dot(d_scores[...], q_rows[...], preferred_element_type=jnp.float32)
        acc[:, WIDTH:] += jnp.dot(probs[...], d_rows[...], preferred_element_type=jnp.float32)
        dq_t = jnp.dot(keys_t[...], d_scores[...], preferred_element_type=jnp.float32) * SCALE
        dq_rows = dq_t.T.astype(jnp.bfloat16)
        for h in range(GROUP):
            dq[step, :, h * WIDTH : (h + 1) * WIDTH] = dq_rows[h * tokens : (h + 1) * tokens]
        for k in range(LINE):

            @pl.when(step == k)
            def _():
                pltpu.make_async_copy(dq.at[k], dqs[k], sems.at[LINE + k]).start()

        return carry

    lax.fori_loop(0, LINE, work, 0)
    dkv[:, :WIDTH] = (acc[:, :WIDTH] * SCALE).astype(jnp.bfloat16)
    dkv[:, WIDTH:] = acc[:, WIDTH:].astype(jnp.bfloat16)
    give = pltpu.make_async_copy(dkv, dkv_any, sems.at[2 * LINE])
    give.start()
    for k in range(LINE):
        pltpu.make_async_copy(dq.at[k], dqs[k], sems.at[LINE + k]).wait()
    give.wait()


def gradients(gate, kv, pieces):
    key_rows = kv.shape[0]
    tokens = (pieces[0].shape[0] - PAD) // 2
    width = pieces[0].shape[1]
    rows = GROUP * tokens
    in_hbm = pl.BlockSpec(memory_space=HBM)
    return pl.pallas_call(
        grad_kernel,
        in_specs=[pl.BlockSpec(memory_space=VMEM)] + [in_hbm] * (LINE + 1),
        out_specs=[in_hbm] * (LINE + 1),
        out_shape=[jax.ShapeDtypeStruct((tokens, width), jnp.bfloat16)] * LINE
        + [jax.ShapeDtypeStruct(kv.shape, jnp.bfloat16)],
        scratch_shapes=[
            pltpu.VMEM(kv.shape, jnp.bfloat16),
            pltpu.VMEM((LINE,) + pieces[0].shape, jnp.bfloat16),
            pltpu.VMEM((LINE, tokens, width), jnp.bfloat16),
            pltpu.VMEM(kv.shape, jnp.bfloat16),
            pltpu.VMEM((WIDTH, key_rows), jnp.bfloat16),
            pltpu.VMEM((key_rows, rows), jnp.bfloat16),
            pltpu.VMEM((key_rows, rows), jnp.bfloat16),
            pltpu.VMEM((rows, WIDTH), jnp.bfloat16),
            pltpu.VMEM((rows, WIDTH), jnp.bfloat16),
            pltpu.VMEM(kv.shape, jnp.float32),
            pltpu.SemaphoreType.DMA((2 * LINE + 1,)),
        ],
        compiler_params=pltpu.CompilerParams(vmem_limit_bytes=VMEM_LIMIT),
        cost_estimate=pl.CostEstimate(
            flops=10 * LINE * rows * key_rows * WIDTH,
            bytes_accessed=4 * 1024 * 1024,
            transcendentals=LINE * rows * key_rows,
        ),
        name="gradients",
    )(gate, kv, *pieces)


def sum_kernel(slots, got, out):
    doc, _ = place_on_line()
    out[...] = jnp.zeros_like(out)
    along_z = doc % 2 == 0
    for j in range(IMAGES):
        owner = slots[doc * IMAGES + j] // IMAGES
        for c in range(KV_HEADS):
            total = 0.0
            for line in range(LINE):
                at = jnp.where(along_z, line * LINE + c, c * LINE + line)
                total += got[at, j].astype(jnp.float32)
            out[owner, :, c * WIDTH : (c + 1) * WIDTH] = total[:, :WIDTH].astype(jnp.bfloat16)
            out[owner, :, KEY_COLUMNS + c * WIDTH : KEY_COLUMNS + (c + 1) * WIDTH] = total[
                :, WIDTH:
            ].astype(jnp.bfloat16)


def place_kernel(docs, slots, got, out):
    doc_here, _ = place_on_line()
    for s in range(IMAGES):
        doc = 0
        for d in range(docs):
            for j in range(IMAGES):
                doc += jnp.where(slots[d * IMAGES + j] == doc_here * IMAGES + s, d, 0)
        out[s] = got[doc].astype(jnp.float32)


def small(kernel, out_shape, name):
    return pl.pallas_call(
        kernel,
        in_specs=[
            pl.BlockSpec(memory_space=SMEM),
            pl.BlockSpec(memory_space=VMEM),
        ],
        out_specs=pl.BlockSpec(memory_space=VMEM),
        out_shape=out_shape,
        compiler_params=pltpu.CompilerParams(vmem_limit_bytes=VMEM_LIMIT),
        name=name,
    )


def shift(docs, k):
    pairs = []
    for d in range(docs):
        for a in range(LINE):
            for b in range(LINE):
                to = (b + k) % LINE
                ends = (a * LINE + b, a * LINE + to) if d % 2 == 0 else (b * LINE + a, to * LINE + a)
                pairs.append((d * LINE * LINE + ends[0], d * LINE * LINE + ends[1]))
    return pairs


def shards(queries, image_kv, d_out, attn_gate, image_slots, spans):
    docs = lax.axis_size("doc")
    texts = lax.axis_size("ctx")
    images, rows, columns = image_kv.shape
    tokens, width = queries.shape[1], queries.shape[2] // KV_HEADS
    both = ("doc", "ctx")
    in_hbm = pl.BlockSpec(memory_space=HBM)
    in_vmem = pl.BlockSpec(memory_space=VMEM)
    params = pltpu.CompilerParams(vmem_limit_bytes=VMEM_LIMIT)
    block = jax.ShapeDtypeStruct((docs, rows, columns), jnp.bfloat16)
    send = pl.pallas_call(
        functools.partial(pack_kernel, docs),
        in_specs=[in_hbm, in_hbm],
        out_specs=in_hbm,
        out_shape=block,
        scratch_shapes=[
            pltpu.SMEM(image_slots.shape, jnp.int32),
            pltpu.VMEM(image_kv.shape, jnp.bfloat16),
            pltpu.SemaphoreType.DMA((docs + 2,)),
        ],
        compiler_params=params,
        name="pack",
    )(image_slots, image_kv)
    got = lax.all_to_all(send, "doc", 0, 0)
    pieces = pl.pallas_call(
        payload_kernel,
        in_specs=[in_hbm, in_hbm, in_vmem],
        out_specs=[in_hbm] * LINE,
        out_shape=[jax.ShapeDtypeStruct((2 * tokens + PAD, width), jnp.bfloat16)] * LINE,
        scratch_shapes=[
            pltpu.VMEM((LINE, 2 * tokens + PAD, width), jnp.bfloat16),
            pltpu.SemaphoreType.DMA((3 * LINE,)),
        ],
        compiler_params=params,
        name="payload",
    )(queries[0], d_out[0], spans[0].T)
    pieces = [pieces[0]] + [lax.ppermute(pieces[k], both, shift(docs, k)) for k in range(1, LINE)]
    one_head = jax.ShapeDtypeStruct((texts, images, rows, 2 * WIDTH), jnp.bfloat16)
    send = small(pick_kernel, one_head, "pick")(image_slots, got)
    kv = lax.all_to_all(send, "ctx", 0, 0).reshape(texts * images * rows, 2 * WIDTH)
    *dqs, dkv = gradients(attn_gate.reshape(1, 1), kv, pieces)
    dqs = [dqs[0]] + [lax.ppermute(dqs[k], both, shift(docs, -k)) for k in range(1, LINE)]
    parts = lax.all_to_all(dkv.reshape(texts, images, rows, 2 * WIDTH), "ctx", 0, 0)
    send = small(sum_kernel, block, "sum")(image_slots, parts)
    got = lax.all_to_all(send, "doc", 0, 0)
    d_image_kv = small(
        functools.partial(place_kernel, docs),
        jax.ShapeDtypeStruct(image_kv.shape, jnp.float32),
        "place",
    )(image_slots, got)
    d_queries = pl.pallas_call(
        merge_kernel,
        in_specs=[in_vmem] * LINE,
        out_specs=in_vmem,
        out_shape=jax.ShapeDtypeStruct(queries.shape[1:], jnp.bfloat16),
        compiler_params=params,
        name="merge",
    )(*dqs)
    return d_queries[None], d_image_kv


def solution(mesh):
    return jax.shard_map(
        shards,
        mesh=mesh,
        in_specs=(
            P("doc", "ctx", None),
            P("doc", "ctx", None),
            P("doc", "ctx", None),
            P(),
            P(),
            P("doc", "ctx", None),
        ),
        out_specs=(P("doc", "ctx", None), P("doc", "ctx", None)),
        check_vma=False,
    )
```

time: 96.7 us -> 95.5 us (0.988)
  Pallas kernels: 28.6 us -> 26.9 us
    pallas_call x6, Pallas kernels: 27.2 us -> 25.5 us  [the longest x1 18.7 us: gradients(): pl.pallas_call(grad_kernel, in_specs=[pl.BlockSpec(memory_space=VMEM)] +...]
    unnamed x18 -> x20, local copies, waits for them, and re-layouts: 6.02 us -> 6.09 us
where the time goes in v5:
time: 95.5 us; the launch traced here: 94.9 us
  starting transfers between devices  34.5 us (36%)
  Pallas kernels  26.9 us (28%)
  waiting for transfers between devices  26 us (27%)
  local copies, waits for them, and re-layouts  6.09 us (6%)
  between operations  1.38 us (1%)
    pallas_call x1, Pallas kernels, gradients(): pl.pallas_call(grad_kernel, in_specs=[pl.BlockSpec(memory_space=VMEM)] +...  18.7 us
    all_to_all x2, starting transfers between devices, shards(): got = lax.all_to_all(send, 'doc', 0, 0)  15.8 us
    all_to_all x1, waiting for transfers between devices, shards(): lax.all_to_all(send, 'ctx', 0, 0).reshape(texts * images * rows, 2 * WIDTH)  7.13 us
    ppermute x3, waiting for transfers between devices, shards(): lax.ppermute(pieces[k], both, shift(docs, k))  6.74 us
    all_to_all x1, waiting for transfers between devices, shards(): lax.all_to_all(dkv.reshape(texts, images, rows, 2 * WIDTH), 'ctx', 0, 0)  6.7 us
    unnamed x20, local copies, waits for them, and re-layouts  6.09 us
    all_to_all x2, waiting for transfers between devices, shards(): got = lax.all_to_all(send, 'doc', 0, 0)  5.42 us
    all_to_all x1, starting transfers between devices, shards(): lax.all_to_all(send, 'ctx', 0, 0).reshape(texts * images * rows, 2 * WIDTH)  5.25 us
  transfers between devices with their start and end apart: 10, of which 5 were waited for; matrix products, arithmetic and copies ran while one was open for 0% of the time, Pallas kernels for 6%

profile of v5, /device:TPU:1, one launch (start us, length us, event | category | flops | bytes accessed | tf_op | source)
XLA Modules:
  0.0 94.9 jit_solution(16651970313203470920)
XLA Ops:
  0.6 0.9 copy-done.2
  1.5 0.7 copy-done.3
  2.2 1.5 %pack.1 = bf16[8,16,1024]{2,1,0:T(8,128)(2,1)} custom-call(s32[32]{0:T(128)S(1)} %copy-done.3, bf16[4,16,1024]{2,1,0:T(8,128)(2,1)S(1)} %copy-done.2), custom_call_target="tpu_custom_call" | custom-call | tf_op jit(solution)/shard_map/pack/pallas_call | solution.py:301
  3.7 5.8 %all-to-all-start = ((bf16[8,16,1024]{2,1,0:T(8,128)(2,1)}), bf16[8,16,1024]{2,1,0:T(8,128)(2,1)S(1)}, u32[]{:S(2)}, u32[]{:S(2)}) async-start(bf16[8,16,1024]{2,1,0:T(8,128)(2,1)} %pack.1), calls=%async_computation | async-start | bytes 524288 | tf_op jit(solution)/shard_map/all_to_all | solution.py:314
  9.5 0.7 copy-done.5
  10.2 1.2 %copy-done = bf16[1,128,4096]{2,1,0:T(8,128)(2,1)S(1)} copy-done((bf16[1,128,4096]{2,1,0:T(8,128)(2,1)S(1)}, bf16[1,128,4096]{2,1,0:T(8,128)(2,1)}, u32[]{:S(2)}) %copy-start) | copy-done | bytes 1048600
  11.4 1.2 %copy-done.1 = bf16[1,128,4096]{2,1,0:T(8,128)(2,1)S(1)} copy-done((bf16[1,128,4096]{2,1,0:T(8,128)(2,1)S(1)}, bf16[1,128,4096]{2,1,0:T(8,128)(2,1)}, u32[]{:S(2)}) %copy-start.1) | copy-done | bytes 1048600
  12.7 1.5 %payload.1 = (bf16[272,1024]{1,0:T(8,128)(2,1)S(1)}, bf16[272,1024]{1,0:T(8,128)(2,1)}, bf16[272,1024]{1,0:T(8,128)(2,1)}, bf16[272,1024]{1,0:T(8,128)(2,1)}) custom-call(bf16[128,4096]{1,0:T(8,128)(2,1)S(1)} %bitcast.10, bf16[128,4096]{1,0:T(8,128)(2,1)S(1)} %bitcast.11, s32[2,128]{1,0:T(2,128)S(1)} %bitcast.13), custom_call_target="tpu_custom_call" | custom-call | tf_op jit(solution)/shard_map/payload/pallas_call | solution.py:315
  14.1 1.4 %collective-permute-start = (bf16[272,1024]{1,0:T(8,128)(2,1)}, bf16[272,1024]{1,0:T(8,128)(2,1)S(1)}, u32[]{:S(2)}, u32[]{:S(2)}) collective-permute-start(bf16[272,1024]{1,0:T(8,128)(2,1)} %get-tuple-element.12), channel_id=1, source_target_pairs={{0,1},{1,2},{2,3},{3,0},{4,5},{5,6},{6,7},{7,4},{8,9},{9,10},{10,1... | collective-permute-start | bytes 1671176 | tf_op jit(solution)/shard_map/ppermute | solution.py:327
  15.5 2.6 %collective-permute-start.1 = (bf16[272,1024]{1,0:T(8,128)(2,1)}, bf16[272,1024]{1,0:T(8,128)(2,1)S(1)}, u32[]{:S(2)}, u32[]{:S(2)}) collective-permute-start(bf16[272,1024]{1,0:T(8,128)(2,1)} %get-tuple-element.13), channel_id=1, source_target_pairs={{0,2},{1,3},{2,0},{3,1},{4,6},{5,7},{6,4},{7,5},{8,10},{9,11},{10,... | collective-permute-start | bytes 1671176 | tf_op jit(solution)/shard_map/ppermute | solution.py:327
  18.1 1.1 %collective-permute-start.2 = (bf16[272,1024]{1,0:T(8,128)(2,1)}, bf16[272,1024]{1,0:T(8,128)(2,1)S(1)}, u32[]{:S(2)}, u32[]{:S(2)}) collective-permute-start(bf16[272,1024]{1,0:T(8,128)(2,1)} %get-tuple-element.14), channel_id=1, source_target_pairs={{0,3},{1,0},{2,1},{3,2},{4,7},{5,4},{6,5},{7,6},{8,11},{9,8},{10,9... | collective-permute-start | bytes 1671176 | tf_op jit(solution)/shard_map/ppermute | solution.py:327
  19.2 0.0 all-to-all-done.got
  19.2 1.4 %pick.1 = bf16[16,4,16,256]{3,2,1,0:T(8,128)(2,1)} custom-call(s32[32]{0:T(128)S(1)} %copy-done.4, bf16[8,16,1024]{2,1,0:T(8,128)(2,1)S(1)} %all-to-all-done.got), custom_call_target="tpu_custom_call" | custom-call | tf_op jit(solution)/shard_map/pick/pallas_call | solution.py:329
  20.6 5.3 %all-to-all-start.1 = ((bf16[16,4,16,256]{3,2,1,0:T(8,128)(2,1)}), bf16[16,4,16,256]{3,2,1,0:T(8,128)(2,1)S(1)}, u32[]{:S(2)}, u32[]{:S(2)}) async-start(bf16[16,4,16,256]{3,2,1,0:T(8,128)(2,1)} %pick.1), calls=%async_computation.1 | async-start | bytes 1048576 | tf_op jit(solution)/shard_map/all_to_all | solution.py:330
  26.5 5.0 %collective-permute-done.1.refs_2_ = bf16[272,1024]{1,0:T(8,128)(2,1)S(1)} collective-permute-done((bf16[272,1024]{1,0:T(8,128)(2,1)}, bf16[272,1024]{1,0:T(8,128)(2,1)S(1)}, u32[]{:S(2)}, u32[]{:S(2)}) %collective-permute-start.1) | collective-permute-done | bytes 557088 | tf_op jit(solution)/shard_map/ppermute | solution.py:327
  31.5 1.7 %collective-permute-done.2.refs_3_ = bf16[272,1024]{1,0:T(8,128)(2,1)S(1)} collective-permute-done((bf16[272,1024]{1,0:T(8,128)(2,1)}, bf16[272,1024]{1,0:T(8,128)(2,1)S(1)}, u32[]{:S(2)}, u32[]{:S(2)}) %collective-permute-start.2) | collective-permute-done | bytes 557088 | tf_op jit(solution)/shard_map/ppermute | solution.py:327
  33.3 7.1 %all-to-all-done.1 = bf16[16,4,16,256]{3,2,1,0:T(8,128)(2,1)S(1)} async-done(((bf16[16,4,16,256]{3,2,1,0:T(8,128)(2,1)}), bf16[16,4,16,256]{3,2,1,0:T(8,128)(2,1)S(1)}, u32[]{:S(2)}, u32[]{:S(2)}) %all-to-all-start.1) | async-done | bytes 524320 | tf_op jit(solution)/shard_map/all_to_all | solution.py:330
  40.4 18.7 %gradients.1 = (bf16[128,1024]{1,0:T(8,128)(2,1)S(1)}, bf16[128,1024]{1,0:T(8,128)(2,1)S(1)}, bf16[128,1024]{1,0:T(8,128)(2,1)S(1)}, bf16[128,1024]{1,0:T(8,128)(2,1)S(1)}, bf16[1024,256]{1,0:T(8,128)(2,1)}) custom-call(f32[1,1]{1,0:T(1,128)} %bitcast.9.gate, bf16[1024,256]{1,0:T(8,128)(2,1)S(1)} %bitcast.12, ...), custom_call_target="tpu_custom_call" | custom-call | flops 5368709120 | bytes 4194304 | tf_op jit(solution)/shard_map/gradients/pallas_call | solution.py:210
  59.1 0.7 copy-done.6
  59.8 0.7 copy-done.8
  60.5 4.6 %all-to-all-start.2 = ((bf16[16,4,16,256]{3,2,1,0:T(8,128)(2,1)}), bf16[16,4,16,256]{3,2,1,0:T(8,128)(2,1)S(1)}, u32[]{:S(2)}, u32[]{:S(2)}) async-start(bf16[16,4,16,256]{3,2,1,0:T(8,128)(2,1)} %bitcast.7), calls=%async_computation.2 | async-start | bytes 1048576 | tf_op jit(solution)/shard_map/all_to_all | solution.py:333
  65.1 2.6 %collective-permute-start.3 = (bf16[128,1024]{1,0:T(8,128)(2,1)S(1)}, bf16[128,1024]{1,0:T(8,128)(2,1)S(1)}, u32[]{:S(2)}, u32[]{:S(2)}) collective-permute-start(bf16[128,1024]{1,0:T(8,128)(2,1)S(1)} %copy-done.9), channel_id=1, source_target_pairs={{0,3},{1,0},{2,1},{3,2},{4,7},{5,4},{6,5},{7,6},{8,11},{9,8},{10,9... | collective-permute-start | bytes 786440 | tf_op jit(solution)/shard_map/ppermute | solution.py:332
  67.8 0.6 collective-permute-start.4
  68.4 0.6 collective-permute-start.5
  68.9 6.7 %all-to-all-done.2.got = bf16[16,4,16,256]{3,2,1,0:T(8,128)(2,1)S(1)} async-done(((bf16[16,4,16,256]{3,2,1,0:T(8,128)(2,1)}), bf16[16,4,16,256]{3,2,1,0:T(8,128)(2,1)S(1)}, u32[]{:S(2)}, u32[]{:S(2)}) %all-to-all-start.2) | async-done | bytes 524320 | tf_op jit(solution)/shard_map/all_to_all | solution.py:333
  75.6 1.3 %sum.1 = bf16[8,16,1024]{2,1,0:T(8,128)(2,1)} custom-call(s32[32]{0:T(128)S(1)} %copy-done.4, bf16[16,4,16,256]{3,2,1,0:T(8,128)(2,1)S(1)} %all-to-all-done.2.got), custom_call_target="tpu_custom_call" | custom-call | tf_op jit(solution)/shard_map/sum/pallas_call | solution.py:334
  77.0 10.0 %all-to-all-start.3 = ((bf16[8,16,1024]{2,1,0:T(8,128)(2,1)}), bf16[8,16,1024]{2,1,0:T(8,128)(2,1)S(1)}, u32[]{:S(2)}, u32[]{:S(2)}) async-start(bf16[8,16,1024]{2,1,0:T(8,128)(2,1)} %sum.1), calls=%async_computation.3 | async-start | bytes 524288 | tf_op jit(solution)/shard_map/all_to_all | solution.py:335
  87.0 0.0 collective-permute-done.3.refs_1_
  87.0 0.0 collective-permute-done.4.refs_2_
  87.0 1.1 %merge.1 = bf16[128,4096]{1,0:T(8,128)(2,1)} custom-call(bf16[128,1024]{1,0:T(8,128)(2,1)S(1)} %get-tuple-element.15.refs_0_, bf16[128,1024]{1,0:T(8,128)(2,1)S(1)} %collective-permute-done.3.refs_1_, bf16[128,1024]{1,0:T(8,128)(2,1)S(1)} %collective-permute-done.4.refs_2_, bf16[128,1024]{1,0:T(8,128)(2,1)S(1)} %collective-permute-done.5.refs_3_), custom_call_target="tpu_custom_call" | custom-call | tf_op jit(solution)/shard_map/merge/pallas_call | solution.py:341
  88.1 5.4 %all-to-all-done.3.got = bf16[8,16,1024]{2,1,0:T(8,128)(2,1)S(1)} async-done(((bf16[8,16,1024]{2,1,0:T(8,128)(2,1)}), bf16[8,16,1024]{2,1,0:T(8,128)(2,1)S(1)}, u32[]{:S(2)}, u32[]{:S(2)}) %all-to-all-start.3) | async-done | bytes 262176 | tf_op jit(solution)/shard_map/all_to_all | solution.py:335
  93.5 1.4 %place.1 = f32[4,16,1024]{2,1,0:T(8,128)} custom-call(s32[32]{0:T(128)S(1)} %copy-done.4, bf16[8,16,1024]{2,1,0:T(8,128)(2,1)S(1)} %all-to-all-done.3.got), custom_call_target="tpu_custom_call" | custom-call | tf_op jit(solution)/shard_map/place/pallas_call | solution.py:336
  (15 shorter events, 0.0 us)
Async XLA Ops:
  0.6 0.9 copy-start.2
  1.5 0.7 copy-start.3
  3.7 15.5 %all-to-all-start = ((bf16[8,16,1024]{2,1,0:T(8,128)(2,1)}), bf16[8,16,1024]{2,1,0:T(8,128)(2,1)S(1)}, u32[]{:S(2)}, u32[]{:S(2)}) async-start(bf16[8,16,1024]{2,1,0:T(8,128)(2,1)} %pack.1), calls=%async_computation | async-start | bytes 524288 | tf_op jit(solution)/shard_map/all_to_all | solution.py:314
  9.5 0.7 copy-start.5
  10.2 1.2 %copy-start = (bf16[1,128,4096]{2,1,0:T(8,128)(2,1)S(1)}, bf16[1,128,4096]{2,1,0:T(8,128)(2,1)}, u32[]{:S(2)}) copy-start(bf16[1,128,4096]{2,1,0:T(8,128)(2,1)} %param.6) | copy-start | bytes 3145732
  11.4 1.2 %copy-start.1 = (bf16[1,128,4096]{2,1,0:T(8,128)(2,1)S(1)}, bf16[1,128,4096]{2,1,0:T(8,128)(2,1)}, u32[]{:S(2)}) copy-start(bf16[1,128,4096]{2,1,0:T(8,128)(2,1)} %param.8) | copy-start | bytes 3145732
  14.1 12.4 %collective-permute-start = (bf16[272,1024]{1,0:T(8,128)(2,1)}, bf16[272,1024]{1,0:T(8,128)(2,1)S(1)}, u32[]{:S(2)}, u32[]{:S(2)}) collective-permute-start(bf16[272,1024]{1,0:T(8,128)(2,1)} %get-tuple-element.12), channel_id=1, source_target_pairs={{0,1},{1,2},{2,3},{3,0},{4,5},{5,6},{6,7},{7,4},{8,9},{9,10},{10,1... | collective-permute-start | bytes 1671176 | tf_op jit(solution)/shard_map/ppermute | solution.py:327
  15.5 3.7 %copy-start.4 = (s32[32]{0:T(128)S(1)}, s32[32]{0:T(128)}, u32[]{:S(2)}) copy-start(s32[32]{0:T(128)} %slots.5) | copy-start | bytes 388
  15.5 16.0 %collective-permute-start.1 = (bf16[272,1024]{1,0:T(8,128)(2,1)}, bf16[272,1024]{1,0:T(8,128)(2,1)S(1)}, u32[]{:S(2)}, u32[]{:S(2)}) collective-permute-start(bf16[272,1024]{1,0:T(8,128)(2,1)} %get-tuple-element.13), channel_id=1, source_target_pairs={{0,2},{1,3},{2,0},{3,1},{4,6},{5,7},{6,4},{7,5},{8,10},{9,11},{10,... | collective-permute-start | bytes 1671176 | tf_op jit(solution)/shard_map/ppermute | solution.py:327
  18.1 15.1 %collective-permute-start.2 = (bf16[272,1024]{1,0:T(8,128)(2,1)}, bf16[272,1024]{1,0:T(8,128)(2,1)S(1)}, u32[]{:S(2)}, u32[]{:S(2)}) collective-permute-start(bf16[272,1024]{1,0:T(8,128)(2,1)} %get-tuple-element.14), channel_id=1, source_target_pairs={{0,3},{1,0},{2,1},{3,2},{4,7},{5,4},{6,5},{7,6},{8,11},{9,8},{10,9... | collective-permute-start | bytes 1671176 | tf_op jit(solution)/shard_map/ppermute | solution.py:327
  20.6 19.8 %all-to-all-start.1 = ((bf16[16,4,16,256]{3,2,1,0:T(8,128)(2,1)}), bf16[16,4,16,256]{3,2,1,0:T(8,128)(2,1)S(1)}, u32[]{:S(2)}, u32[]{:S(2)}) async-start(bf16[16,4,16,256]{3,2,1,0:T(8,128)(2,1)} %pick.1), calls=%async_computation.1 | async-start | bytes 1048576 | tf_op jit(solution)/shard_map/all_to_all | solution.py:330
  59.1 0.7 copy-start.6
  59.8 0.7 copy-start.8
  60.5 4.6 %copy-start.9 = (bf16[128,1024]{1,0:T(8,128)(2,1)S(1)}, bf16[128,1024]{1,0:T(8,128)(2,1)}, u32[]{:S(2)}) copy-start(bf16[128,1024]{1,0:T(8,128)(2,1)} %copy-done.8) | copy-start | bytes 786436
  60.5 7.3 %copy-start.7 = (bf16[128,1024]{1,0:T(8,128)(2,1)S(1)}, bf16[128,1024]{1,0:T(8,128)(2,1)}, u32[]{:S(2)}) copy-start(bf16[128,1024]{1,0:T(8,128)(2,1)} %copy-done.6) | copy-start | bytes 786436
  60.5 15.1 %all-to-all-start.2 = ((bf16[16,4,16,256]{3,2,1,0:T(8,128)(2,1)}), bf16[16,4,16,256]{3,2,1,0:T(8,128)(2,1)S(1)}, u32[]{:S(2)}, u32[]{:S(2)}) async-start(bf16[16,4,16,256]{3,2,1,0:T(8,128)(2,1)} %bitcast.7), calls=%async_computation.2 | async-start | bytes 1048576 | tf_op jit(solution)/shard_map/all_to_all | solution.py:333
  65.1 21.8 %collective-permute-start.3 = (bf16[128,1024]{1,0:T(8,128)(2,1)S(1)}, bf16[128,1024]{1,0:T(8,128)(2,1)S(1)}, u32[]{:S(2)}, u32[]{:S(2)}) collective-permute-start(bf16[128,1024]{1,0:T(8,128)(2,1)S(1)} %copy-done.9), channel_id=1, source_target_pairs={{0,3},{1,0},{2,1},{3,2},{4,7},{5,4},{6,5},{7,6},{8,11},{9,8},{10,9... | collective-permute-start | bytes 786440 | tf_op jit(solution)/shard_map/ppermute | solution.py:332
  67.8 19.2 %collective-permute-start.4 = (bf16[128,1024]{1,0:T(8,128)(2,1)S(1)}, bf16[128,1024]{1,0:T(8,128)(2,1)S(1)}, u32[]{:S(2)}, u32[]{:S(2)}) collective-permute-start(bf16[128,1024]{1,0:T(8,128)(2,1)S(1)} %copy-done.7), channel_id=1, source_target_pairs={{0,2},{1,3},{2,0},{3,1},{4,6},{5,7},{6,4},{7,5},{8,10},{9,11},{10,... | collective-permute-start | bytes 786440 | tf_op jit(solution)/shard_map/ppermute | solution.py:332
  68.4 18.6 %collective-permute-start.5 = (bf16[128,1024]{1,0:T(8,128)(2,1)S(1)}, bf16[128,1024]{1,0:T(8,128)(2,1)S(1)}, u32[]{:S(2)}, u32[]{:S(2)}) collective-permute-start(bf16[128,1024]{1,0:T(8,128)(2,1)S(1)} %get-tuple-element.18), channel_id=1, source_target_pairs={{0,1},{1,2},{2,3},{3,0},{4,5},{5,6},{6,7},{7,4},{8,9},{9,10},{10,1... | collective-permute-start | bytes 786440 | tf_op jit(solution)/shard_map/ppermute | solution.py:332
  77.0 16.5 %all-to-all-start.3 = ((bf16[8,16,1024]{2,1,0:T(8,128)(2,1)}), bf16[8,16,1024]{2,1,0:T(8,128)(2,1)S(1)}, u32[]{:S(2)}, u32[]{:S(2)}) async-start(bf16[8,16,1024]{2,1,0:T(8,128)(2,1)} %sum.1), calls=%async_computation.3 | async-start | bytes 524288 | tf_op jit(solution)/shard_map/all_to_all | solution.py:335

commit v6 on v5

--- a/solution.py
+++ b/solution.py
@@ -19,6 +19,7 @@
 BLOCK_HEADS = 2
 PAD = 16
 VMEM_LIMIT = 48 * 1024 * 1024
+GRADIENT_VMEM = 60 * 1024 * 1024
 
 SMEM = pltpu.MemorySpace.SMEM
 VMEM = pltpu.MemorySpace.VMEM
@@ -71,12 +72,14 @@
                 out[y * LINE + z, j] = jnp.where(along_z, heads[z], heads[y])
 
 
-def payload_kernel(q, d_out, spans, *refs):
-    outs, held, sems = refs[:LINE], refs[LINE], refs[LINE + 1]
+def payload_kernel(q, d_out, spans_any, *refs):
+    outs, held, spans, sems = refs[:LINE], refs[LINE], refs[LINE + 1], refs[LINE + 2]
     tokens = q.shape[0]
     width = q.shape[1] // KV_HEADS
     _, place = place_on_line()
     order = [2, 1, 3, 0]
+    fetch_spans = pltpu.make_async_copy(spans_any, spans, sems.at[3 * LINE])
+    fetch_spans.start()
     fetches = []
     for k in order:
         columns = pl.ds(pl.multiple_of(lax.rem(place + k, LINE) * width, WIDTH), width)
@@ -89,6 +92,7 @@
         for copy in pair:
             copy.start()
         fetches.append(pair)
+    fetch_spans.wait()
     for k in order:
         held[k, 2 * tokens :] = jnp.zeros_like(held[k, 2 * tokens :])
         held[k, 2 * tokens : 2 * tokens + 2, :tokens] = spans[...].astype(jnp.bfloat16)
@@ -226,7 +230,7 @@
             pltpu.VMEM(kv.shape, jnp.float32),
             pltpu.SemaphoreType.DMA((2 * LINE + 1,)),
         ],
-        compiler_params=pltpu.CompilerParams(vmem_limit_bytes=VMEM_LIMIT),
+        compiler_params=pltpu.CompilerParams(vmem_limit_bytes=GRADIENT_VMEM),
         cost_estimate=pl.CostEstimate(
             flops=10 * LINE * rows * key_rows * WIDTH,
             bytes_accessed=4 * 1024 * 1024,
@@ -308,20 +312,19 @@
             pltpu.VMEM(image_kv.shape, jnp.bfloat16),
             pltpu.SemaphoreType.DMA((docs + 2,)),
         ],
-        compiler_params=params,
         name="pack",
     )(image_slots, image_kv)
     got = lax.all_to_all(send, "doc", 0, 0)
     pieces = pl.pallas_call(
         payload_kernel,
-        in_specs=[in_hbm, in_hbm, in_vmem],
+        in_specs=[in_hbm, in_hbm, in_hbm],
         out_specs=[in_hbm] * LINE,
         out_shape=[jax.ShapeDtypeStruct((2 * tokens + PAD, width), jnp.bfloat16)] * LINE,
         scratch_shapes=[
             pltpu.VMEM((LINE, 2 * tokens + PAD, width), jnp.bfloat16),
-            pltpu.SemaphoreType.DMA((3 * LINE,)),
+            pltpu.VMEM((2, tokens), jnp.int32),
+            pltpu.SemaphoreType.DMA((3 * LINE + 1,)),
         ],
-        compiler_params=params,
         name="payload",
     )(queries[0], d_out[0], spans[0].T)
     pieces = [pieces[0]] + [lax.ppermute(pieces[k], both, shift(docs, k)) for k in range(1, LINE)]

time: 95.5 us -> 92.2 us (0.965)
  local copies, waits for them, and re-layouts: 6.09 us -> 0.82 us
  starting transfers between devices: 34.5 us -> 36.4 us
  Pallas kernels: 26.9 us -> 28.7 us
  waiting for transfers between devices: 26 us -> 24.2 us
    unnamed x20 -> x18, local copies, waits for them, and re-layouts: 6.09 us -> 0.82 us
    ppermute x3, waiting for transfers between devices: 6.74 us -> 3.55 us  [shards(): lax.ppermute(pieces[k], both, shift(docs, k))]
    all_to_all x1, starting transfers between devices: 5.25 us -> 6.69 us  [shards(): lax.all_to_all(send, 'ctx', 0, 0).reshape(texts * images * rows, 2 * WIDTH)]
    all_to_all x1, waiting for transfers between devices: 7.13 us -> 8.27 us  [shards(): lax.all_to_all(send, 'ctx', 0, 0).reshape(texts * images * rows, 2 * WIDTH)]
    pallas_call x1, Pallas kernels: 1.47 us -> 2.51 us  [shards(): pl.pallas_call(payload_kernel, in_specs=[in_hbm, in_hbm, in_hbm], out_spe...]
  transfers between devices with their start and end apart: 10 -> 10, of which waited for: 5 -> 4; matrix products, arithmetic and copies ran while one was open for 0% -> 0% of each run, Pallas kernels for 6% -> 7%
where the time goes in v6:
time: 92.2 us; the launch traced here: 91.6 us
  starting transfers between devices  36.4 us (39%)
  Pallas kernels  28.7 us (31%)
  waiting for transfers between devices  24.2 us (26%)
  between operations  1.4 us (2%)
    pallas_call x1, Pallas kernels, gradients(): pl.pallas_call(grad_kernel, in_specs=[pl.BlockSpec(memory_space=VMEM)] +...  19.3 us
    all_to_all x2, starting transfers between devices, shards(): got = lax.all_to_all(send, 'doc', 0, 0)  15.6 us
    all_to_all x1, waiting for transfers between devices, shards(): lax.all_to_all(send, 'ctx', 0, 0).reshape(texts * images * rows, 2 * WIDTH)  8.27 us
    all_to_all x1, waiting for transfers between devices, shards(): lax.all_to_all(dkv.reshape(texts, images, rows, 2 * WIDTH), 'ctx', 0, 0)  6.98 us
    all_to_all x1, starting transfers between devices, shards(): lax.all_to_all(send, 'ctx', 0, 0).reshape(texts * images * rows, 2 * WIDTH)  6.69 us
    all_to_all x2, waiting for transfers between devices, shards(): got = lax.all_to_all(send, 'doc', 0, 0)  5.41 us
    all_to_all x1, starting transfers between devices, shards(): lax.all_to_all(dkv.reshape(texts, images, rows, 2 * WIDTH), 'ctx', 0, 0)  5.24 us
    ppermute x3, starting transfers between devices, shards(): lax.ppermute(pieces[k], both, shift(docs, k))  5.05 us
  transfers between devices with their start and end apart: 10, of which 4 were waited for; matrix products, arithmetic and copies ran while one was open for 0% of the time, Pallas kernels for 7%

profile of v6, /device:TPU:1, one launch (start us, length us, event | category | flops | bytes accessed | tf_op | source)
XLA Modules:
  0.0 91.6 jit_solution(124698584502014292)
XLA Ops:
  0.6 1.7 %pack.1 = bf16[8,16,1024]{2,1,0:T(8,128)(2,1)} custom-call(s32[32]{0:T(128)} %slots.5, bf16[4,16,1024]{2,1,0:T(8,128)(2,1)} %kv.1), custom_call_target="tpu_custom_call" | custom-call | tf_op jit(solution)/shard_map/pack/pallas_call | solution.py:305
  2.3 5.8 %all-to-all-start = ((bf16[8,16,1024]{2,1,0:T(8,128)(2,1)}), bf16[8,16,1024]{2,1,0:T(8,128)(2,1)S(1)}, u32[]{:S(2)}, u32[]{:S(2)}) async-start(bf16[8,16,1024]{2,1,0:T(8,128)(2,1)} %pack.1), calls=%async_computation | async-start | bytes 524288 | tf_op jit(solution)/shard_map/all_to_all | solution.py:317
  8.1 2.5 %payload.1 = (bf16[272,1024]{1,0:T(8,128)(2,1)}, bf16[272,1024]{1,0:T(8,128)(2,1)}, bf16[272,1024]{1,0:T(8,128)(2,1)}, bf16[272,1024]{1,0:T(8,128)(2,1)}) custom-call(bf16[128,4096]{1,0:T(8,128)(2,1)} %bitcast.11, bf16[128,4096]{1,0:T(8,128)(2,1)} %bitcast.12, s32[2,128]{1,0:T(2,128)} %bitcast.15), custom_call_target="tpu_custom_call" | custom-call | tf_op jit(solution)/shard_map/payload/pallas_call | solution.py:318
  10.7 1.4 %collective-permute-start = (bf16[272,1024]{1,0:T(8,128)(2,1)}, bf16[272,1024]{1,0:T(8,128)(2,1)S(1)}, u32[]{:S(2)}, u32[]{:S(2)}) collective-permute-start(bf16[272,1024]{1,0:T(8,128)(2,1)} %get-tuple-element.12), channel_id=1, source_target_pairs={{0,1},{1,2},{2,3},{3,0},{4,5},{5,6},{6,7},{7,4},{8,9},{9,10},{10,1... | collective-permute-start | bytes 1671176 | tf_op jit(solution)/shard_map/ppermute | solution.py:330
  12.0 2.6 %collective-permute-start.1 = (bf16[272,1024]{1,0:T(8,128)(2,1)}, bf16[272,1024]{1,0:T(8,128)(2,1)S(1)}, u32[]{:S(2)}, u32[]{:S(2)}) collective-permute-start(bf16[272,1024]{1,0:T(8,128)(2,1)} %get-tuple-element.13), channel_id=1, source_target_pairs={{0,2},{1,3},{2,0},{3,1},{4,6},{5,7},{6,4},{7,5},{8,10},{9,11},{10,... | collective-permute-start | bytes 1671176 | tf_op jit(solution)/shard_map/ppermute | solution.py:330
  14.6 1.1 %collective-permute-start.2 = (bf16[272,1024]{1,0:T(8,128)(2,1)}, bf16[272,1024]{1,0:T(8,128)(2,1)S(1)}, u32[]{:S(2)}, u32[]{:S(2)}) collective-permute-start(bf16[272,1024]{1,0:T(8,128)(2,1)} %get-tuple-element.14), channel_id=1, source_target_pairs={{0,3},{1,0},{2,1},{3,2},{4,7},{5,4},{6,5},{7,6},{8,11},{9,8},{10,9... | collective-permute-start | bytes 1671176 | tf_op jit(solution)/shard_map/ppermute | solution.py:330
  15.7 0.0 all-to-all-done.got
  15.7 0.0 copy-done.1
  15.7 1.4 %pick.1 = bf16[16,4,16,256]{3,2,1,0:T(8,128)(2,1)} custom-call(s32[32]{0:T(128)S(1)} %copy-done.1, bf16[8,16,1024]{2,1,0:T(8,128)(2,1)S(1)} %all-to-all-done.got), custom_call_target="tpu_custom_call" | custom-call | tf_op jit(solution)/shard_map/pick/pallas_call | solution.py:332
  17.1 6.7 %all-to-all-start.1 = ((bf16[16,4,16,256]{3,2,1,0:T(8,128)(2,1)}), bf16[16,4,16,256]{3,2,1,0:T(8,128)(2,1)S(1)}, u32[]{:S(2)}, u32[]{:S(2)}) async-start(bf16[16,4,16,256]{3,2,1,0:T(8,128)(2,1)} %pick.1), calls=%async_computation.1 | async-start | bytes 1048576 | tf_op jit(solution)/shard_map/all_to_all | solution.py:333
  24.5 0.0 collective-permute-done.refs_1_
  24.5 0.0 copy-start.3
  24.5 3.5 %collective-permute-done.1.refs_2_ = bf16[272,1024]{1,0:T(8,128)(2,1)S(1)} collective-permute-done((bf16[272,1024]{1,0:T(8,128)(2,1)}, bf16[272,1024]{1,0:T(8,128)(2,1)S(1)}, u32[]{:S(2)}, u32[]{:S(2)}) %collective-permute-start.1) | collective-permute-done | bytes 557088 | tf_op jit(solution)/shard_map/ppermute | solution.py:330
  28.0 0.0 collective-permute-done.2.refs_3_
  28.0 8.3 %all-to-all-done.1 = bf16[16,4,16,256]{3,2,1,0:T(8,128)(2,1)S(1)} async-done(((bf16[16,4,16,256]{3,2,1,0:T(8,128)(2,1)}), bf16[16,4,16,256]{3,2,1,0:T(8,128)(2,1)S(1)}, u32[]{:S(2)}, u32[]{:S(2)}) %all-to-all-start.1) | async-done | bytes 524320 | tf_op jit(solution)/shard_map/all_to_all | solution.py:333
  36.3 0.0 copy-done.3
  36.3 0.8 copy-done.2
  37.1 19.3 %gradients.1 = (bf16[128,1024]{1,0:T(8,128)(2,1)}, bf16[128,1024]{1,0:T(8,128)(2,1)}, bf16[128,1024]{1,0:T(8,128)(2,1)}, bf16[128,1024]{1,0:T(8,128)(2,1)}, bf16[1024,256]{1,0:T(8,128)(2,1)}) custom-call(f32[1,1]{1,0:T(1,128)} %bitcast.9.gate, bf16[1024,256]{1,0:T(8,128)(2,1)} %bitcast.13, bf16[272,1024]{1,0:T(8,128)(2,1)} %get-tuple-element.11.refs_0_, ...), custom_call_target="tpu_custom_call" | custom-call | flops 5368709120 | bytes 4194304 | tf_op jit(solution)/shard_map/gradients/pallas_call | solution.py:214
  56.5 5.2 %all-to-all-start.2 = ((bf16[16,4,16,256]{3,2,1,0:T(8,128)(2,1)}), bf16[16,4,16,256]{3,2,1,0:T(8,128)(2,1)S(1)}, u32[]{:S(2)}, u32[]{:S(2)}) async-start(bf16[16,4,16,256]{3,2,1,0:T(8,128)(2,1)} %bitcast.14), calls=%async_computation.2 | async-start | bytes 1048576 | tf_op jit(solution)/shard_map/all_to_all | solution.py:336
  61.7 2.6 %collective-permute-start.3 = (bf16[128,1024]{1,0:T(8,128)(2,1)S(1)}, bf16[128,1024]{1,0:T(8,128)(2,1)S(1)}, u32[]{:S(2)}, u32[]{:S(2)}) collective-permute-start(bf16[128,1024]{1,0:T(8,128)(2,1)S(1)} %copy-done.8), channel_id=1, source_target_pairs={{0,3},{1,0},{2,1},{3,2},{4,7},{5,4},{6,5},{7,6},{8,11},{9,8},{10,9... | collective-permute-start | bytes 786440 | tf_op jit(solution)/shard_map/ppermute | solution.py:335
  64.4 0.6 collective-permute-start.4
  65.0 0.6 collective-permute-start.5
  65.5 7.0 %all-to-all-done.2.got = bf16[16,4,16,256]{3,2,1,0:T(8,128)(2,1)S(1)} async-done(((bf16[16,4,16,256]{3,2,1,0:T(8,128)(2,1)}), bf16[16,4,16,256]{3,2,1,0:T(8,128)(2,1)S(1)}, u32[]{:S(2)}, u32[]{:S(2)}) %all-to-all-start.2) | async-done | bytes 524320 | tf_op jit(solution)/shard_map/all_to_all | solution.py:336
  72.5 1.3 %sum.1 = bf16[8,16,1024]{2,1,0:T(8,128)(2,1)} custom-call(s32[32]{0:T(128)S(1)} %copy-done.1, bf16[16,4,16,256]{3,2,1,0:T(8,128)(2,1)S(1)} %all-to-all-done.2.got), custom_call_target="tpu_custom_call" | custom-call | tf_op jit(solution)/shard_map/sum/pallas_call | solution.py:337
  73.9 9.8 %all-to-all-start.3 = ((bf16[8,16,1024]{2,1,0:T(8,128)(2,1)}), bf16[8,16,1024]{2,1,0:T(8,128)(2,1)S(1)}, u32[]{:S(2)}, u32[]{:S(2)}) async-start(bf16[8,16,1024]{2,1,0:T(8,128)(2,1)} %sum.1), calls=%async_computation.3 | async-start | bytes 524288 | tf_op jit(solution)/shard_map/all_to_all | solution.py:338
  83.7 0.0 collective-permute-done.3.refs_1_
  83.7 0.0 collective-permute-done.4.refs_2_
  83.7 0.0 collective-permute-done.5.refs_3_
  83.7 0.0 copy-done
  83.7 1.1 %merge.1 = bf16[128,4096]{1,0:T(8,128)(2,1)} custom-call(bf16[128,1024]{1,0:T(8,128)(2,1)S(1)} %copy-done, bf16[128,1024]{1,0:T(8,128)(2,1)S(1)} %collective-permute-done.3.refs_1_, bf16[128,1024]{1,0:T(8,128)(2,1)S(1)} %collective-permute-done.4.refs_2_, bf16[128,1024]{1,0:T(8,128)(2,1)S(1)} %collective-permute-done.5.refs_3_), custom_call_target="tpu_custom_call" | custom-call | tf_op jit(solution)/shard_map/merge/pallas_call | solution.py:344
  84.8 5.4 %all-to-all-done.3.got = bf16[8,16,1024]{2,1,0:T(8,128)(2,1)S(1)} async-done(((bf16[8,16,1024]{2,1,0:T(8,128)(2,1)}), bf16[8,16,1024]{2,1,0:T(8,128)(2,1)S(1)}, u32[]{:S(2)}, u32[]{:S(2)}) %all-to-all-start.3) | async-done | bytes 262176 | tf_op jit(solution)/shard_map/all_to_all | solution.py:338
  90.2 1.4 %place.1 = f32[4,16,1024]{2,1,0:T(8,128)} custom-call(s32[32]{0:T(128)S(1)} %copy-done.1, bf16[8,16,1024]{2,1,0:T(8,128)(2,1)S(1)} %all-to-all-done.3.got), custom_call_target="tpu_custom_call" | custom-call | tf_op jit(solution)/shard_map/place/pallas_call | solution.py:339
  (13 shorter events, 0.0 us)
Async XLA Ops:
  2.3 13.4 %all-to-all-start = ((bf16[8,16,1024]{2,1,0:T(8,128)(2,1)}), bf16[8,16,1024]{2,1,0:T(8,128)(2,1)S(1)}, u32[]{:S(2)}, u32[]{:S(2)}) async-start(bf16[8,16,1024]{2,1,0:T(8,128)(2,1)} %pack.1), calls=%async_computation | async-start | bytes 524288 | tf_op jit(solution)/shard_map/all_to_all | solution.py:317
  10.7 13.8 %collective-permute-start = (bf16[272,1024]{1,0:T(8,128)(2,1)}, bf16[272,1024]{1,0:T(8,128)(2,1)S(1)}, u32[]{:S(2)}, u32[]{:S(2)}) collective-permute-start(bf16[272,1024]{1,0:T(8,128)(2,1)} %get-tuple-element.12), channel_id=1, source_target_pairs={{0,1},{1,2},{2,3},{3,0},{4,5},{5,6},{6,7},{7,4},{8,9},{9,10},{10,1... | collective-permute-start | bytes 1671176 | tf_op jit(solution)/shard_map/ppermute | solution.py:330
  12.0 3.7 %copy-start.1 = (s32[32]{0:T(128)S(1)}, s32[32]{0:T(128)}, u32[]{:S(2)}) copy-start(s32[32]{0:T(128)} %slots.5) | copy-start | bytes 388
  12.0 16.0 %collective-permute-start.1 = (bf16[272,1024]{1,0:T(8,128)(2,1)}, bf16[272,1024]{1,0:T(8,128)(2,1)S(1)}, u32[]{:S(2)}, u32[]{:S(2)}) collective-permute-start(bf16[272,1024]{1,0:T(8,128)(2,1)} %get-tuple-element.13), channel_id=1, source_target_pairs={{0,2},{1,3},{2,0},{3,1},{4,6},{5,7},{6,4},{7,5},{8,10},{9,11},{10,... | collective-permute-start | bytes 1671176 | tf_op jit(solution)/shard_map/ppermute | solution.py:330
  14.6 13.4 %collective-permute-start.2 = (bf16[272,1024]{1,0:T(8,128)(2,1)}, bf16[272,1024]{1,0:T(8,128)(2,1)S(1)}, u32[]{:S(2)}, u32[]{:S(2)}) collective-permute-start(bf16[272,1024]{1,0:T(8,128)(2,1)} %get-tuple-element.14), channel_id=1, source_target_pairs={{0,3},{1,0},{2,1},{3,2},{4,7},{5,4},{6,5},{7,6},{8,11},{9,8},{10,9... | collective-permute-start | bytes 1671176 | tf_op jit(solution)/shard_map/ppermute | solution.py:330
  17.1 19.2 %all-to-all-start.1 = ((bf16[16,4,16,256]{3,2,1,0:T(8,128)(2,1)}), bf16[16,4,16,256]{3,2,1,0:T(8,128)(2,1)S(1)}, u32[]{:S(2)}, u32[]{:S(2)}) async-start(bf16[16,4,16,256]{3,2,1,0:T(8,128)(2,1)} %pick.1), calls=%async_computation.1 | async-start | bytes 1048576 | tf_op jit(solution)/shard_map/all_to_all | solution.py:333
  24.5 11.8 %copy-start.3 = (bf16[272,1024]{1,0:T(8,128)(2,1)}, bf16[272,1024]{1,0:T(8,128)(2,1)S(1)}, u32[]{:S(2)}) copy-start(bf16[272,1024]{1,0:T(8,128)(2,1)S(1)} %collective-permute-done.refs_1_) | copy-start | bytes 1671172
  28.0 8.3 %copy-start.4 = (bf16[272,1024]{1,0:T(8,128)(2,1)}, bf16[272,1024]{1,0:T(8,128)(2,1)S(1)}, u32[]{:S(2)}) copy-start(bf16[272,1024]{1,0:T(8,128)(2,1)S(1)} %collective-permute-done.1.refs_2_) | copy-start | bytes 1671172
  28.0 8.3 %copy-start.5 = (bf16[272,1024]{1,0:T(8,128)(2,1)}, bf16[272,1024]{1,0:T(8,128)(2,1)S(1)}, u32[]{:S(2)}) copy-start(bf16[272,1024]{1,0:T(8,128)(2,1)S(1)} %collective-permute-done.2.refs_3_) | copy-start | bytes 1671172
  36.3 0.8 copy-start.2
  56.5 5.3 %copy-start.8 = (bf16[128,1024]{1,0:T(8,128)(2,1)S(1)}, bf16[128,1024]{1,0:T(8,128)(2,1)}, u32[]{:S(2)}) copy-start(bf16[128,1024]{1,0:T(8,128)(2,1)} %get-tuple-element.16) | copy-start | bytes 786436
  56.5 7.9 %copy-start.7 = (bf16[128,1024]{1,0:T(8,128)(2,1)S(1)}, bf16[128,1024]{1,0:T(8,128)(2,1)}, u32[]{:S(2)}) copy-start(bf16[128,1024]{1,0:T(8,128)(2,1)} %get-tuple-element.17) | copy-start | bytes 786436
  56.5 8.5 %copy-start.6 = (bf16[128,1024]{1,0:T(8,128)(2,1)S(1)}, bf16[128,1024]{1,0:T(8,128)(2,1)}, u32[]{:S(2)}) copy-start(bf16[128,1024]{1,0:T(8,128)(2,1)} %get-tuple-element.18) | copy-start | bytes 786436
  56.5 16.0 %all-to-all-start.2 = ((bf16[16,4,16,256]{3,2,1,0:T(8,128)(2,1)}), bf16[16,4,16,256]{3,2,1,0:T(8,128)(2,1)S(1)}, u32[]{:S(2)}, u32[]{:S(2)}) async-start(bf16[16,4,16,256]{3,2,1,0:T(8,128)(2,1)} %bitcast.14), calls=%async_computation.2 | async-start | bytes 1048576 | tf_op jit(solution)/shard_map/all_to_all | solution.py:336
  61.7 22.0 %collective-permute-start.3 = (bf16[128,1024]{1,0:T(8,128)(2,1)S(1)}, bf16[128,1024]{1,0:T(8,128)(2,1)S(1)}, u32[]{:S(2)}, u32[]{:S(2)}) collective-permute-start(bf16[128,1024]{1,0:T(8,128)(2,1)S(1)} %copy-done.8), channel_id=1, source_target_pairs={{0,3},{1,0},{2,1},{3,2},{4,7},{5,4},{6,5},{7,6},{8,11},{9,8},{10,9... | collective-permute-start | bytes 786440 | tf_op jit(solution)/shard_map/ppermute | solution.py:335
  64.4 19.3 %collective-permute-start.4 = (bf16[128,1024]{1,0:T(8,128)(2,1)S(1)}, bf16[128,1024]{1,0:T(8,128)(2,1)S(1)}, u32[]{:S(2)}, u32[]{:S(2)}) collective-permute-start(bf16[128,1024]{1,0:T(8,128)(2,1)S(1)} %copy-done.7), channel_id=1, source_target_pairs={{0,2},{1,3},{2,0},{3,1},{4,6},{5,7},{6,4},{7,5},{8,10},{9,11},{10,... | collective-permute-start | bytes 786440 | tf_op jit(solution)/shard_map/ppermute | solution.py:335
  65.0 18.8 %collective-permute-start.5 = (bf16[128,1024]{1,0:T(8,128)(2,1)S(1)}, bf16[128,1024]{1,0:T(8,128)(2,1)S(1)}, u32[]{:S(2)}, u32[]{:S(2)}) collective-permute-start(bf16[128,1024]{1,0:T(8,128)(2,1)S(1)} %copy-done.6), channel_id=1, source_target_pairs={{0,1},{1,2},{2,3},{3,0},{4,5},{5,6},{6,7},{7,4},{8,9},{9,10},{10,1... | collective-permute-start | bytes 786440 | tf_op jit(solution)/shard_map/ppermute | solution.py:335
  73.9 9.9 %copy-start = (bf16[128,1024]{1,0:T(8,128)(2,1)S(1)}, bf16[128,1024]{1,0:T(8,128)(2,1)}, u32[]{:S(2)}) copy-start(bf16[128,1024]{1,0:T(8,128)(2,1)} %get-tuple-element.15.refs_0_) | copy-start | bytes 786436
  73.9 16.3 %all-to-all-start.3 = ((bf16[8,16,1024]{2,1,0:T(8,128)(2,1)}), bf16[8,16,1024]{2,1,0:T(8,128)(2,1)S(1)}, u32[]{:S(2)}, u32[]{:S(2)}) async-start(bf16[8,16,1024]{2,1,0:T(8,128)(2,1)} %sum.1), calls=%async_computation.3 | async-start | bytes 524288 | tf_op jit(solution)/shard_map/all_to_all | solution.py:338

commit v7 on v6

--- a/solution.py
+++ b/solution.py
@@ -124,40 +124,50 @@
         top = jnp.max(jnp.max(scores[:, j], axis=0), axis=0, keepdims=True)
         top = jnp.where(seen[j], top, LOW)
         row_max = top if row_max is None else jnp.maximum(row_max, top)
-    row_max = row_max * (SCALE * LOG2E)
+    row_max = row_max * SCALE
     terms = []
+    lows = []
     total = 0.0
     dots = 0.0
     for j in range(IMAGES):
-        term = jnp.exp2(scores[:, j] * (SCALE * LOG2E) - jnp.where(seen[j], row_max, -LOW))
+        term = jnp.exp(scores[:, j] * SCALE - jnp.where(seen[j], row_max, -LOW))
         total += jnp.sum(jnp.sum(term, axis=0), axis=0, keepdims=True)
         dots += jnp.sum(jnp.sum(term * d_probs[:, j], axis=0), axis=0, keepdims=True)
         terms.append(term)
+        lows.append(d_probs[:, j].astype(jnp.bfloat16))
     inverse = 1.0 / total
-    delta = dots * inverse
+    delta = (dots * inverse).astype(jnp.bfloat16)
     low_probs = []
     d_scores = []
     for j in range(IMAGES):
-        probs = terms[j] * inverse
-        low_probs.append(probs.astype(jnp.bfloat16)[:, None])
-        d_scores.append((probs * (d_probs[:, j] - delta)).astype(jnp.bfloat16)[:, None])
+        probs = (terms[j] * inverse).astype(jnp.bfloat16)
+        low_probs.append(probs[:, None])
+        d_scores.append((probs * (lows[j] - delta))[:, None])
     low_probs = jnp.concatenate(low_probs, axis=1).reshape(keys, rows)
     d_scores = jnp.concatenate(d_scores, axis=1).reshape(keys, rows)
     return low_probs, d_scores
 
 
-def grad_kernel(gate, kv_any, *refs):
-    pieces, dqs, dkv_any = refs[:LINE], refs[LINE : 2 * LINE], refs[2 * LINE]
-    kv, held, dq, dkv, keys_t, probs, d_scores, q_rows, d_rows, acc, sems = refs[2 * LINE + 1 :]
+def grad_kernel(count, first, last, gate, kv_any, *refs):
+    pieces, refs = refs[:count], refs[count:]
+    so_far, refs = (None, refs) if first else (refs[0], refs[1:])
+    dqs, dkv_any, refs = refs[:count], refs[count], refs[count + 1 :]
+    kv, held, dq, dkv, keys_t, probs, d_scores, q_rows, d_rows, acc, sems = refs
     tokens = dqs[0].shape[0]
     block = BLOCK_HEADS * tokens
-    fetch_kv = pltpu.make_async_copy(kv_any, kv, sems.at[2 * LINE])
+    fetch_kv = pltpu.make_async_copy(kv_any, kv, sems.at[2 * count])
     fetch_kv.start()
-    for k in range(LINE):
+    for k in range(count):
         pltpu.make_async_copy(pieces[k], held.at[k], sems.at[k]).start()
+    if not first:
+        fetch_sums = pltpu.make_async_copy(so_far, acc, sems.at[2 * count + 1])
+        fetch_sums.start()
     fetch_kv.wait()
     keys_t[...] = kv[:, :WIDTH].T
-    acc[...] = jnp.zeros_like(acc)
+    if first:
+        acc[...] = jnp.zeros_like(acc)
+    else:
+        fetch_sums.wait()
     factor = jnp.tanh(gate[...])
     transposed = (((1,), (1,)), ((), ()))
 
@@ -187,40 +197,44 @@
         dq_rows = dq_t.T.astype(jnp.bfloat16)
         for h in range(GROUP):
             dq[step, :, h * WIDTH : (h + 1) * WIDTH] = dq_rows[h * tokens : (h + 1) * tokens]
-        for k in range(LINE):
+        for k in range(count):
 
             @pl.when(step == k)
             def _():
-                pltpu.make_async_copy(dq.at[k], dqs[k], sems.at[LINE + k]).start()
+                pltpu.make_async_copy(dq.at[k], dqs[k], sems.at[count + k]).start()
 
         return carry
 
-    lax.fori_loop(0, LINE, work, 0)
-    dkv[:, :WIDTH] = (acc[:, :WIDTH] * SCALE).astype(jnp.bfloat16)
-    dkv[:, WIDTH:] = acc[:, WIDTH:].astype(jnp.bfloat16)
-    give = pltpu.make_async_copy(dkv, dkv_any, sems.at[2 * LINE])
+    lax.fori_loop(0, count, work, 0)
+    if last:
+        dkv[:, :WIDTH] = (acc[:, :WIDTH] * SCALE).astype(jnp.bfloat16)
+        dkv[:, WIDTH:] = acc[:, WIDTH:].astype(jnp.bfloat16)
+    give = pltpu.make_async_copy(dkv if last else acc, dkv_any, sems.at[2 * count])
     give.start()
-    for k in range(LINE):
-        pltpu.make_async_copy(dq.at[k], dqs[k], sems.at[LINE + k]).wait()
+    for k in range(count):
+        pltpu.make_async_copy(dq.at[k], dqs[k], sems.at[count + k]).wait()
     give.wait()
 
 
-def gradients(gate, kv, pieces):
+def gradients(gate, kv, pieces, so_far=None, last=True):
     key_rows = kv.shape[0]
+    count = len(pieces)
+    first = so_far is None
     tokens = (pieces[0].shape[0] - PAD) // 2
     width = pieces[0].shape[1]
     rows = GROUP * tokens
     in_hbm = pl.BlockSpec(memory_space=HBM)
+    operands = list(pieces) + ([] if first else [so_far])
     return pl.pallas_call(
-        grad_kernel,
-        in_specs=[pl.BlockSpec(memory_space=VMEM)] + [in_hbm] * (LINE + 1),
-        out_specs=[in_hbm] * (LINE + 1),
-        out_shape=[jax.ShapeDtypeStruct((tokens, width), jnp.bfloat16)] * LINE
-        + [jax.ShapeDtypeStruct(kv.shape, jnp.bfloat16)],
+        functools.partial(grad_kernel, count, first, last),
+        in_specs=[pl.BlockSpec(memory_space=VMEM)] + [in_hbm] * (len(operands) + 1),
+        out_specs=[in_hbm] * (count + 1),
+        out_shape=[jax.ShapeDtypeStruct((tokens, width), jnp.bfloat16)] * count
+        + [jax.ShapeDtypeStruct(kv.shape, jnp.bfloat16 if last else jnp.float32)],
         scratch_shapes=[
             pltpu.VMEM(kv.shape, jnp.bfloat16),
-            pltpu.VMEM((LINE,) + pieces[0].shape, jnp.bfloat16),
-            pltpu.VMEM((LINE, tokens, width), jnp.bfloat16),
+            pltpu.VMEM((count,) + pieces[0].shape, jnp.bfloat16),
+            pltpu.VMEM((count, tokens, width), jnp.bfloat16),
             pltpu.VMEM(kv.shape, jnp.bfloat16),
             pltpu.VMEM((WIDTH, key_rows), jnp.bfloat16),
             pltpu.VMEM((key_rows, rows), jnp.bfloat16),
@@ -228,16 +242,16 @@
             pltpu.VMEM((rows, WIDTH), jnp.bfloat16),
             pltpu.VMEM((rows, WIDTH), jnp.bfloat16),
             pltpu.VMEM(kv.shape, jnp.float32),
-            pltpu.SemaphoreType.DMA((2 * LINE + 1,)),
+            pltpu.SemaphoreType.DMA((2 * count + 2,)),
         ],
         compiler_params=pltpu.CompilerParams(vmem_limit_bytes=GRADIENT_VMEM),
         cost_estimate=pl.CostEstimate(
-            flops=10 * LINE * rows * key_rows * WIDTH,
+            flops=10 * count * rows * key_rows * WIDTH,
             bytes_accessed=4 * 1024 * 1024,
-            transcendentals=LINE * rows * key_rows,
+            transcendentals=count * rows * key_rows,
         ),
         name="gradients",
-    )(gate, kv, *pieces)
+    )(gate, kv, *operands)
 
 
 def sum_kernel(slots, got, out):
@@ -327,12 +341,21 @@
         ],
         name="payload",
     )(queries[0], d_out[0], spans[0].T)
-    pieces = [pieces[0]] + [lax.ppermute(pieces[k], both, shift(docs, k)) for k in range(1, LINE)]
     one_head = jax.ShapeDtypeStruct((texts, images, rows, 2 * WIDTH), jnp.bfloat16)
     send = small(pick_kernel, one_head, "pick")(image_slots, got)
+    own, after, far, before = pieces
+    after = lax.ppermute(after, both, shift(docs, 1))
+    before = lax.ppermute(before, both, shift(docs, -1))
+    far, send = lax.optimization_barrier((far, send))
+    far = lax.ppermute(far, both, shift(docs, 2))
     kv = lax.all_to_all(send, "ctx", 0, 0).reshape(texts * images * rows, 2 * WIDTH)
-    *dqs, dkv = gradients(attn_gate.reshape(1, 1), kv, pieces)
-    dqs = [dqs[0]] + [lax.ppermute(dqs[k], both, shift(docs, -k)) for k in range(1, LINE)]
+    gate = attn_gate.reshape(1, 1)
+    dq_own, dq_after, dq_before, sums = gradients(gate, kv, [own, after, before], last=False)
+    dq_far, dkv = gradients(gate, kv, [far], so_far=sums)
+    dq_after = lax.ppermute(dq_after, both, shift(docs, -1))
+    dq_before = lax.ppermute(dq_before, both, shift(docs, 1))
+    dq_far = lax.ppermute(dq_far, both, shift(docs, 2))
+    dqs = [dq_own, dq_after, dq_far, dq_before]
     parts = lax.all_to_all(dkv.reshape(texts, images, rows, 2 * WIDTH), "ctx", 0, 0)
     send = small(sum_kernel, block, "sum")(image_slots, parts)
     got = lax.all_to_all(send, "doc", 0, 0)

time: 92.2 us -> 92.1 us (level)
  waiting for transfers between devices: 24.2 us -> 16.5 us
  starting transfers between devices: 36.4 us -> 41.4 us
  Pallas kernels: 28.7 us -> 30.6 us
    ppermute x6, waiting for transfers between devices: 3.56 us -> 0.02 us  [the longest x1 0.01 us: shards(): after = lax.ppermute(after, both, shift(docs, 1))]
    all_to_all x2, starting transfers between devices: 15.6 us -> 18.7 us  [shards(): got = lax.all_to_all(send, 'doc', 0, 0)]
    all_to_all x1, waiting for transfers between devices: 8.27 us -> 5.41 us  [shards(): lax.all_to_all(send, 'ctx', 0, 0).reshape(texts * images * rows, 2 * WIDTH)]
    all_to_all x1, waiting for transfers between devices: 6.98 us -> 4.53 us  [shards(): lax.all_to_all(dkv.reshape(texts, images, rows, 2 * WIDTH), 'ctx', 0, 0)]
    pallas_call x1 -> x2, Pallas kernels: 19.3 us -> 21.1 us  [gradients(): pl.pallas_call(functools.partial(grad_kernel, count, first, last), in_spe...]
    ppermute x6, starting transfers between devices: 8.85 us -> 10.2 us  [the longest x1 2.95 us: shards(): far = lax.ppermute(far, both, shift(docs, 2))]
    all_to_all x1, starting transfers between devices: 6.69 us -> 7.9 us  [shards(): lax.all_to_all(send, 'ctx', 0, 0).reshape(texts * images * rows, 2 * WIDTH)]
    all_to_all x2, waiting for transfers between devices: 5.41 us -> 6.5 us  [shards(): got = lax.all_to_all(send, 'doc', 0, 0)]
  transfers between devices with their start and end apart: 10 -> 10, of which waited for: 4 -> 4; matrix products, arithmetic and copies ran while one was open for 0% -> 0% of each run, Pallas kernels for 7% -> 23%
where the time goes in v7:
time: 92.1 us; the launch traced here: 91.5 us
  starting transfers between devices  41.4 us (45%)
  Pallas kernels  30.6 us (33%)
  waiting for transfers between devices  16.5 us (18%)
  local copies, waits for them, and re-layouts  1.63 us (2%)
  between operations  1.46 us (2%)
    pallas_call x2, Pallas kernels, gradients(): pl.pallas_call(functools.partial(grad_kernel, count, first, last), in_spe...  21.1 us
    all_to_all x2, starting transfers between devices, shards(): got = lax.all_to_all(send, 'doc', 0, 0)  18.7 us
    all_to_all x1, starting transfers between devices, shards(): lax.all_to_all(send, 'ctx', 0, 0).reshape(texts * images * rows, 2 * WIDTH)  7.9 us
    all_to_all x2, waiting for transfers between devices, shards(): got = lax.all_to_all(send, 'doc', 0, 0)  6.5 us
    all_to_all x1, waiting for transfers between devices, shards(): lax.all_to_all(send, 'ctx', 0, 0).reshape(texts * images * rows, 2 * WIDTH)  5.41 us
    all_to_all x1, waiting for transfers between devices, shards(): lax.all_to_all(dkv.reshape(texts, images, rows, 2 * WIDTH), 'ctx', 0, 0)  4.53 us
    all_to_all x1, starting transfers between devices, shards(): lax.all_to_all(dkv.reshape(texts, images, rows, 2 * WIDTH), 'ctx', 0, 0)  4.5 us
    ppermute x1, starting transfers between devices, shards(): far = lax.ppermute(far, both, shift(docs, 2))  2.95 us
  transfers between devices with their start and end apart: 10, of which 4 were waited for; matrix products, arithmetic and copies ran while one was open for 0% of the time, Pallas kernels for 23%

profile of v7, /device:TPU:1, one launch (start us, length us, event | category | flops | bytes accessed | tf_op | source)
XLA Modules:
  0.0 91.5 jit_solution(14815578835031133876)
XLA Ops:
  0.6 1.7 %pack.1 = bf16[8,16,1024]{2,1,0:T(8,128)(2,1)} custom-call(s32[32]{0:T(128)} %slots.5, bf16[4,16,1024]{2,1,0:T(8,128)(2,1)} %kv.1), custom_call_target="tpu_custom_call" | custom-call | tf_op jit(solution)/shard_map/pack/pallas_call | solution.py:319
  2.3 5.8 %all-to-all-start = ((bf16[8,16,1024]{2,1,0:T(8,128)(2,1)}), bf16[8,16,1024]{2,1,0:T(8,128)(2,1)S(1)}, u32[]{:S(2)}, u32[]{:S(2)}) async-start(bf16[8,16,1024]{2,1,0:T(8,128)(2,1)} %pack.1), calls=%async_computation | async-start | bytes 524288 | tf_op jit(solution)/shard_map/all_to_all | solution.py:331
  8.1 2.5 %payload.1 = (bf16[272,1024]{1,0:T(8,128)(2,1)}, bf16[272,1024]{1,0:T(8,128)(2,1)}, bf16[272,1024]{1,0:T(8,128)(2,1)}, bf16[272,1024]{1,0:T(8,128)(2,1)}) custom-call(bf16[128,4096]{1,0:T(8,128)(2,1)} %bitcast.12, bf16[128,4096]{1,0:T(8,128)(2,1)} %bitcast.13, s32[2,128]{1,0:T(2,128)} %bitcast.17), custom_call_target="tpu_custom_call" | custom-call | tf_op jit(solution)/shard_map/payload/pallas_call | solution.py:332
  10.7 0.0 copy-start.1
  10.7 1.4 %collective-permute-start = (bf16[272,1024]{1,0:T(8,128)(2,1)}, bf16[272,1024]{1,0:T(8,128)(2,1)S(1)}, u32[]{:S(2)}, u32[]{:S(2)}) collective-permute-start(bf16[272,1024]{1,0:T(8,128)(2,1)} %get-tuple-element.17), channel_id=1, source_target_pairs={{0,1},{1,2},{2,3},{3,0},{4,5},{5,6},{6,7},{7,4},{8,9},{9,10},{10,1... | collective-permute-start | bytes 1671176 | tf_op jit(solution)/shard_map/ppermute | solution.py:347
  12.0 1.5 %collective-permute-start.1 = (bf16[272,1024]{1,0:T(8,128)(2,1)}, bf16[272,1024]{1,0:T(8,128)(2,1)S(1)}, u32[]{:S(2)}, u32[]{:S(2)}) collective-permute-start(bf16[272,1024]{1,0:T(8,128)(2,1)} %get-tuple-element.18), channel_id=1, source_target_pairs={{0,3},{1,0},{2,1},{3,2},{4,7},{5,4},{6,5},{7,6},{8,11},{9,8},{10,9... | collective-permute-start | bytes 1671176 | tf_op jit(solution)/shard_map/ppermute | solution.py:348
  13.6 1.1 %all-to-all-done.got = bf16[8,16,1024]{2,1,0:T(8,128)(2,1)S(1)} async-done(((bf16[8,16,1024]{2,1,0:T(8,128)(2,1)}), bf16[8,16,1024]{2,1,0:T(8,128)(2,1)S(1)}, u32[]{:S(2)}, u32[]{:S(2)}) %all-to-all-start) | async-done | bytes 262176 | tf_op jit(solution)/shard_map/all_to_all | solution.py:331
  14.6 0.0 copy-done.1
  14.6 1.4 %pick.1 = bf16[16,4,16,256]{3,2,1,0:T(8,128)(2,1)} custom-call(s32[32]{0:T(128)S(1)} %copy-done.1, bf16[8,16,1024]{2,1,0:T(8,128)(2,1)S(1)} %all-to-all-done.got), custom_call_target="tpu_custom_call" | custom-call | tf_op jit(solution)/shard_map/pick/pallas_call | solution.py:345
  16.0 7.9 %all-to-all-start.1 = ((bf16[16,4,16,256]{3,2,1,0:T(8,128)(2,1)}), bf16[16,4,16,256]{3,2,1,0:T(8,128)(2,1)S(1)}, u32[]{:S(2)}, u32[]{:S(2)}) async-start(bf16[16,4,16,256]{3,2,1,0:T(8,128)(2,1)} %pick.1), calls=%async_computation.1 | async-start | bytes 1048576 | tf_op jit(solution)/shard_map/all_to_all | solution.py:351
  24.0 2.9 %collective-permute-start.3 = (bf16[272,1024]{1,0:T(8,128)(2,1)S(1)}, bf16[272,1024]{1,0:T(8,128)(2,1)S(1)}, u32[]{:S(2)}, u32[]{:S(2)}) collective-permute-start(bf16[272,1024]{1,0:T(8,128)(2,1)S(1)} %copy-done.3), channel_id=1, source_target_pairs={{0,2},{1,3},{2,0},{3,1},{4,6},{5,7},{6,4},{7,5},{8,10},{9,11},{10,... | collective-permute-start | bytes 1671176 | tf_op jit(solution)/shard_map/ppermute | solution.py:350
  27.6 0.0 collective-permute-done.refs_1_
  27.6 0.0 collective-permute-done.1.refs_2_
  27.6 5.4 %all-to-all-done.1 = bf16[16,4,16,256]{3,2,1,0:T(8,128)(2,1)S(1)} async-done(((bf16[16,4,16,256]{3,2,1,0:T(8,128)(2,1)}), bf16[16,4,16,256]{3,2,1,0:T(8,128)(2,1)S(1)}, u32[]{:S(2)}, u32[]{:S(2)}) %all-to-all-start.1) | async-done | bytes 524320 | tf_op jit(solution)/shard_map/all_to_all | solution.py:351
  33.0 0.8 copy-done.2
  33.8 14.6 %gradients.2 = (bf16[128,1024]{1,0:T(8,128)(2,1)}, bf16[128,1024]{1,0:T(8,128)(2,1)}, bf16[128,1024]{1,0:T(8,128)(2,1)}, f32[1024,256]{1,0:T(8,128)}) custom-call(f32[1,1]{1,0:T(1,128)} %bitcast.9.gate, bf16[1024,256]{1,0:T(8,128)(2,1)} %bitcast.14, bf16[272,1024]{1,0:T(8,128)(2,1)} %get-tuple-element.16.refs_0_, bf16[272,1024]{1,0:T(8,128)(2,1)} %copy-done.4, ...), custom_call_target="tpu_custom_call" | custom-call | flops 4026531840 | bytes 4194304 | tf_op jit(solution)/shard_map/gradients/pallas_call | solution.py:228
  48.4 0.0 collective-permute-done.3.refs_0_
  48.4 0.8 copy-done.6
  49.2 6.6 %gradients.3 = (bf16[128,1024]{1,0:T(8,128)(2,1)}, bf16[1024,256]{1,0:T(8,128)(2,1)}) custom-call(f32[1,1]{1,0:T(1,128)} %bitcast.10.gate, bf16[1024,256]{1,0:T(8,128)(2,1)} %bitcast.15, bf16[272,1024]{1,0:T(8,128)(2,1)} %copy-done.6, f32[1024,256]{1,0:T(8,128)} %get-tuple-element.22.refs_1_), custom_call_target="tpu_custom_call" | custom-call | flops 1342177280 | bytes 4194304 | tf_op jit(solution)/shard_map/gradients/pallas_call | solution.py:228
  55.8 4.5 %all-to-all-start.2 = ((bf16[16,4,16,256]{3,2,1,0:T(8,128)(2,1)}), bf16[16,4,16,256]{3,2,1,0:T(8,128)(2,1)S(1)}, u32[]{:S(2)}, u32[]{:S(2)}) async-start(bf16[16,4,16,256]{3,2,1,0:T(8,128)(2,1)} %bitcast.16), calls=%async_computation.2 | async-start | bytes 1048576 | tf_op jit(solution)/shard_map/all_to_all | solution.py:359
  60.3 2.6 %collective-permute-start.2 = (bf16[128,1024]{1,0:T(8,128)(2,1)S(1)}, bf16[128,1024]{1,0:T(8,128)(2,1)S(1)}, u32[]{:S(2)}, u32[]{:S(2)}) collective-permute-start(bf16[128,1024]{1,0:T(8,128)(2,1)S(1)} %copy-done.8), channel_id=1, source_target_pairs={{0,3},{1,0},{2,1},{3,2},{4,7},{5,4},{6,5},{7,6},{8,11},{9,8},{10,9... | collective-permute-start | bytes 786440 | tf_op jit(solution)/shard_map/ppermute | solution.py:355
  63.0 0.0 collective-permute-start.5
  63.0 1.8 %collective-permute-start.4 = (bf16[128,1024]{1,0:T(8,128)(2,1)S(1)}, bf16[128,1024]{1,0:T(8,128)(2,1)S(1)}, u32[]{:S(2)}, u32[]{:S(2)}) collective-permute-start(bf16[128,1024]{1,0:T(8,128)(2,1)S(1)} %copy-done.9), channel_id=1, source_target_pairs={{0,2},{1,3},{2,0},{3,1},{4,6},{5,7},{6,4},{7,5},{8,10},{9,11},{10,... | collective-permute-start | bytes 786440 | tf_op jit(solution)/shard_map/ppermute | solution.py:357
  64.8 4.5 %all-to-all-done.2.got = bf16[16,4,16,256]{3,2,1,0:T(8,128)(2,1)S(1)} async-done(((bf16[16,4,16,256]{3,2,1,0:T(8,128)(2,1)}), bf16[16,4,16,256]{3,2,1,0:T(8,128)(2,1)S(1)}, u32[]{:S(2)}, u32[]{:S(2)}) %all-to-all-start.2) | async-done | bytes 524320 | tf_op jit(solution)/shard_map/all_to_all | solution.py:359
  69.3 1.3 %sum.1 = bf16[8,16,1024]{2,1,0:T(8,128)(2,1)} custom-call(s32[32]{0:T(128)S(1)} %copy-done.1, bf16[16,4,16,256]{3,2,1,0:T(8,128)(2,1)S(1)} %all-to-all-done.2.got), custom_call_target="tpu_custom_call" | custom-call | tf_op jit(solution)/shard_map/sum/pallas_call | solution.py:360
  70.6 12.9 %all-to-all-start.3 = ((bf16[8,16,1024]{2,1,0:T(8,128)(2,1)}), bf16[8,16,1024]{2,1,0:T(8,128)(2,1)S(1)}, u32[]{:S(2)}, u32[]{:S(2)}) async-start(bf16[8,16,1024]{2,1,0:T(8,128)(2,1)} %sum.1), calls=%async_computation.3 | async-start | bytes 524288 | tf_op jit(solution)/shard_map/all_to_all | solution.py:361
  83.5 0.0 collective-permute-done.2.refs_1_
  83.6 0.0 collective-permute-done.5.refs_3_
  83.6 0.0 collective-permute-done.4.refs_2_
  83.6 1.1 %merge.1 = bf16[128,4096]{1,0:T(8,128)(2,1)} custom-call(bf16[128,1024]{1,0:T(8,128)(2,1)S(1)} %copy-done, bf16[128,1024]{1,0:T(8,128)(2,1)S(1)} %collective-permute-done.2.refs_1_, bf16[128,1024]{1,0:T(8,128)(2,1)S(1)} %collective-permute-done.4.refs_2_, bf16[128,1024]{1,0:T(8,128)(2,1)S(1)} %collective-permute-done.5.refs_3_), custom_call_target="tpu_custom_call" | custom-call | tf_op jit(solution)/shard_map/merge/pallas_call | solution.py:367
  84.6 5.4 %all-to-all-done.3.got = bf16[8,16,1024]{2,1,0:T(8,128)(2,1)S(1)} async-done(((bf16[8,16,1024]{2,1,0:T(8,128)(2,1)}), bf16[8,16,1024]{2,1,0:T(8,128)(2,1)S(1)}, u32[]{:S(2)}, u32[]{:S(2)}) %all-to-all-start.3) | async-done | bytes 262176 | tf_op jit(solution)/shard_map/all_to_all | solution.py:361
  90.1 1.4 %place.1 = f32[4,16,1024]{2,1,0:T(8,128)} custom-call(s32[32]{0:T(128)S(1)} %copy-done.1, bf16[8,16,1024]{2,1,0:T(8,128)(2,1)S(1)} %all-to-all-done.3.got), custom_call_target="tpu_custom_call" | custom-call | tf_op jit(solution)/shard_map/place/pallas_call | solution.py:362
  (16 shorter events, 0.0 us)
Async XLA Ops:
  2.3 12.3 %all-to-all-start = ((bf16[8,16,1024]{2,1,0:T(8,128)(2,1)}), bf16[8,16,1024]{2,1,0:T(8,128)(2,1)S(1)}, u32[]{:S(2)}, u32[]{:S(2)}) async-start(bf16[8,16,1024]{2,1,0:T(8,128)(2,1)} %pack.1), calls=%async_computation | async-start | bytes 524288 | tf_op jit(solution)/shard_map/all_to_all | solution.py:331
  10.7 4.0 %copy-start.1 = (s32[32]{0:T(128)S(1)}, s32[32]{0:T(128)}, u32[]{:S(2)}) copy-start(s32[32]{0:T(128)} %slots.5) | copy-start | bytes 388
  10.7 16.9 %collective-permute-start = (bf16[272,1024]{1,0:T(8,128)(2,1)}, bf16[272,1024]{1,0:T(8,128)(2,1)S(1)}, u32[]{:S(2)}, u32[]{:S(2)}) collective-permute-start(bf16[272,1024]{1,0:T(8,128)(2,1)} %get-tuple-element.17), channel_id=1, source_target_pairs={{0,1},{1,2},{2,3},{3,0},{4,5},{5,6},{6,7},{7,4},{8,9},{9,10},{10,1... | collective-permute-start | bytes 1671176 | tf_op jit(solution)/shard_map/ppermute | solution.py:347
  12.0 15.5 %collective-permute-start.1 = (bf16[272,1024]{1,0:T(8,128)(2,1)}, bf16[272,1024]{1,0:T(8,128)(2,1)S(1)}, u32[]{:S(2)}, u32[]{:S(2)}) collective-permute-start(bf16[272,1024]{1,0:T(8,128)(2,1)} %get-tuple-element.18), channel_id=1, source_target_pairs={{0,3},{1,0},{2,1},{3,2},{4,7},{5,4},{6,5},{7,6},{8,11},{9,8},{10,9... | collective-permute-start | bytes 1671176 | tf_op jit(solution)/shard_map/ppermute | solution.py:348
  16.0 7.9 %copy-start.3 = (bf16[272,1024]{1,0:T(8,128)(2,1)S(1)}, bf16[272,1024]{1,0:T(8,128)(2,1)}, u32[]{:S(2)}) copy-start(bf16[272,1024]{1,0:T(8,128)(2,1)} %get-tuple-element.21) | copy-start | bytes 1671172
  16.0 17.0 %all-to-all-start.1 = ((bf16[16,4,16,256]{3,2,1,0:T(8,128)(2,1)}), bf16[16,4,16,256]{3,2,1,0:T(8,128)(2,1)S(1)}, u32[]{:S(2)}, u32[]{:S(2)}) async-start(bf16[16,4,16,256]{3,2,1,0:T(8,128)(2,1)} %pick.1), calls=%async_computation.1 | async-start | bytes 1048576 | tf_op jit(solution)/shard_map/all_to_all | solution.py:351
  24.0 24.4 %collective-permute-start.3 = (bf16[272,1024]{1,0:T(8,128)(2,1)S(1)}, bf16[272,1024]{1,0:T(8,128)(2,1)S(1)}, u32[]{:S(2)}, u32[]{:S(2)}) collective-permute-start(bf16[272,1024]{1,0:T(8,128)(2,1)S(1)} %copy-done.3), channel_id=1, source_target_pairs={{0,2},{1,3},{2,0},{3,1},{4,6},{5,7},{6,4},{7,5},{8,10},{9,11},{10,... | collective-permute-start | bytes 1671176 | tf_op jit(solution)/shard_map/ppermute | solution.py:350
  27.6 5.4 %copy-start.4 = (bf16[272,1024]{1,0:T(8,128)(2,1)}, bf16[272,1024]{1,0:T(8,128)(2,1)S(1)}, u32[]{:S(2)}) copy-start(bf16[272,1024]{1,0:T(8,128)(2,1)S(1)} %collective-permute-done.refs_1_) | copy-start | bytes 1671172
  27.6 5.4 %copy-start.5 = (bf16[272,1024]{1,0:T(8,128)(2,1)}, bf16[272,1024]{1,0:T(8,128)(2,1)S(1)}, u32[]{:S(2)}) copy-start(bf16[272,1024]{1,0:T(8,128)(2,1)S(1)} %collective-permute-done.1.refs_2_) | copy-start | bytes 1671172
  33.0 0.8 copy-start.2
  48.4 0.8 copy-start.6
  55.8 4.5 %copy-start.8 = (bf16[128,1024]{1,0:T(8,128)(2,1)S(1)}, bf16[128,1024]{1,0:T(8,128)(2,1)}, u32[]{:S(2)}) copy-start(bf16[128,1024]{1,0:T(8,128)(2,1)} %get-tuple-element.20) | copy-start | bytes 786436
  55.8 7.2 %copy-start.7 = (bf16[128,1024]{1,0:T(8,128)(2,1)S(1)}, bf16[128,1024]{1,0:T(8,128)(2,1)}, u32[]{:S(2)}) copy-start(bf16[128,1024]{1,0:T(8,128)(2,1)} %get-tuple-element.24) | copy-start | bytes 786436
  55.8 7.2 %copy-start.9 = (bf16[128,1024]{1,0:T(8,128)(2,1)S(1)}, bf16[128,1024]{1,0:T(8,128)(2,1)}, u32[]{:S(2)}) copy-start(bf16[128,1024]{1,0:T(8,128)(2,1)} %get-tuple-element.23) | copy-start | bytes 786436
  55.8 13.4 %all-to-all-start.2 = ((bf16[16,4,16,256]{3,2,1,0:T(8,128)(2,1)}), bf16[16,4,16,256]{3,2,1,0:T(8,128)(2,1)S(1)}, u32[]{:S(2)}, u32[]{:S(2)}) async-start(bf16[16,4,16,256]{3,2,1,0:T(8,128)(2,1)} %bitcast.16), calls=%async_computation.2 | async-start | bytes 1048576 | tf_op jit(solution)/shard_map/all_to_all | solution.py:359
  60.3 23.2 %collective-permute-start.2 = (bf16[128,1024]{1,0:T(8,128)(2,1)S(1)}, bf16[128,1024]{1,0:T(8,128)(2,1)S(1)}, u32[]{:S(2)}, u32[]{:S(2)}) collective-permute-start(bf16[128,1024]{1,0:T(8,128)(2,1)S(1)} %copy-done.8), channel_id=1, source_target_pairs={{0,3},{1,0},{2,1},{3,2},{4,7},{5,4},{6,5},{7,6},{8,11},{9,8},{10,9... | collective-permute-start | bytes 786440 | tf_op jit(solution)/shard_map/ppermute | solution.py:355
  63.0 20.6 %collective-permute-start.5 = (bf16[128,1024]{1,0:T(8,128)(2,1)S(1)}, bf16[128,1024]{1,0:T(8,128)(2,1)S(1)}, u32[]{:S(2)}, u32[]{:S(2)}) collective-permute-start(bf16[128,1024]{1,0:T(8,128)(2,1)S(1)} %copy-done.7), channel_id=1, source_target_pairs={{0,1},{1,2},{2,3},{3,0},{4,5},{5,6},{6,7},{7,4},{8,9},{9,10},{10,1... | collective-permute-start | bytes 786440 | tf_op jit(solution)/shard_map/ppermute | solution.py:356
  63.0 20.6 %collective-permute-start.4 = (bf16[128,1024]{1,0:T(8,128)(2,1)S(1)}, bf16[128,1024]{1,0:T(8,128)(2,1)S(1)}, u32[]{:S(2)}, u32[]{:S(2)}) collective-permute-start(bf16[128,1024]{1,0:T(8,128)(2,1)S(1)} %copy-done.9), channel_id=1, source_target_pairs={{0,2},{1,3},{2,0},{3,1},{4,6},{5,7},{6,4},{7,5},{8,10},{9,11},{10,... | collective-permute-start | bytes 786440 | tf_op jit(solution)/shard_map/ppermute | solution.py:357
  70.6 13.0 %copy-start = (bf16[128,1024]{1,0:T(8,128)(2,1)S(1)}, bf16[128,1024]{1,0:T(8,128)(2,1)}, u32[]{:S(2)}) copy-start(bf16[128,1024]{1,0:T(8,128)(2,1)} %get-tuple-element.19.refs_0_) | copy-start | bytes 786436
  70.6 19.5 %all-to-all-start.3 = ((bf16[8,16,1024]{2,1,0:T(8,128)(2,1)}), bf16[8,16,1024]{2,1,0:T(8,128)(2,1)S(1)}, u32[]{:S(2)}, u32[]{:S(2)}) async-start(bf16[8,16,1024]{2,1,0:T(8,128)(2,1)} %sum.1), calls=%async_computation.3 | async-start | bytes 524288 | tf_op jit(solution)/shard_map/all_to_all | solution.py:361

commit v8 on v7

--- a/solution.py
+++ b/solution.py
@@ -15,8 +15,9 @@
 LOW = -1e30
 SCALE = WIDTH ** (-0.5)
 LOG2E = 1.4426950408889634
-LINE = 4
-BLOCK_HEADS = 2
+GRID = 4
+BLOCK = 4
+BATCH_HEADS = 2
 PAD = 16
 VMEM_LIMIT = 48 * 1024 * 1024
 GRADIENT_VMEM = 60 * 1024 * 1024
@@ -26,9 +27,10 @@
 HBM = pltpu.MemorySpace.HBM
 
 
-def place_on_line():
+def place_in_block():
     doc, text = lax.axis_index("doc"), lax.axis_index("ctx")
-    return doc, jnp.where(doc % 2 == 0, text % LINE, text // LINE)
+    place = (text // GRID % 2) * 2 + text % GRID % 2
+    return doc, jnp.where(doc % 2 == 0, place, 3 - place)
 
 
 def pack_kernel(docs, slots_any, kv, out, slots, held, sems):
@@ -37,7 +39,7 @@
     fetch_slots.start()
     fetch.start()
     fetch_slots.wait()
-    doc, _ = place_on_line()
+    doc, _ = place_in_block()
     copies = []
     for d in range(docs):
         local = 0
@@ -53,7 +55,7 @@
 
 
 def pick_kernel(slots, got, out):
-    doc, _ = place_on_line()
+    doc, _ = place_in_block()
     for j in range(IMAGES):
         rows = got[slots[doc * IMAGES + j] // IMAGES]
         heads = [
@@ -66,23 +68,23 @@
             )
             for c in range(KV_HEADS)
         ]
-        along_z = doc % 2 == 0
-        for y in range(LINE):
-            for z in range(LINE):
-                out[y * LINE + z, j] = jnp.where(along_z, heads[z], heads[y])
+        for y in range(GRID):
+            for z in range(GRID):
+                place = y % 2 * 2 + z % 2
+                out[y * GRID + z, j] = jnp.where(doc % 2 == 0, heads[place], heads[3 - place])
 
 
 def payload_kernel(q, d_out, spans_any, *refs):
-    outs, held, spans, sems = refs[:LINE], refs[LINE], refs[LINE + 1], refs[LINE + 2]
+    outs, held, spans, sems = refs[:BLOCK], refs[BLOCK], refs[BLOCK + 1], refs[BLOCK + 2]
     tokens = q.shape[0]
     width = q.shape[1] // KV_HEADS
-    _, place = place_on_line()
-    order = [2, 1, 3, 0]
-    fetch_spans = pltpu.make_async_copy(spans_any, spans, sems.at[3 * LINE])
+    _, place = place_in_block()
+    order = [3, 1, 2, 0]
+    fetch_spans = pltpu.make_async_copy(spans_any, spans, sems.at[3 * BLOCK])
     fetch_spans.start()
     fetches = []
     for k in order:
-        columns = pl.ds(pl.multiple_of(lax.rem(place + k, LINE) * width, WIDTH), width)
+        columns = pl.ds(pl.multiple_of((place ^ k) * width, WIDTH), width)
         pair = [
             pltpu.make_async_copy(q.at[:, columns], held.at[k, :tokens], sems.at[3 * k]),
             pltpu.make_async_copy(
@@ -107,11 +109,11 @@
 
 
 def merge_kernel(*refs):
-    _, place = place_on_line()
+    _, place = place_in_block()
     *parts, out = refs
     width = out.shape[1] // KV_HEADS
     for k, part in enumerate(parts):
-        columns = pl.ds(pl.multiple_of(lax.rem(place + k, LINE) * width, WIDTH), width)
+        columns = pl.ds(pl.multiple_of((place ^ k) * width, WIDTH), width)
         out[:, columns] = part[...]
 
 
@@ -154,7 +156,7 @@
     dqs, dkv_any, refs = refs[:count], refs[count], refs[count + 1 :]
     kv, held, dq, dkv, keys_t, probs, d_scores, q_rows, d_rows, acc, sems = refs
     tokens = dqs[0].shape[0]
-    block = BLOCK_HEADS * tokens
+    block = BATCH_HEADS * tokens
     fetch_kv = pltpu.make_async_copy(kv_any, kv, sems.at[2 * count])
     fetch_kv.start()
     for k in range(count):
@@ -179,8 +181,8 @@
             wide = held[step, tokens : 2 * tokens, columns].astype(jnp.float32)
             d_rows[rows] = (wide * factor).astype(jnp.bfloat16)
         spans = held[step, 2 * tokens :, :tokens].astype(jnp.float32)
-        low = jnp.concatenate([spans[0:1]] * BLOCK_HEADS, axis=1)
-        high = jnp.concatenate([spans[1:2]] * BLOCK_HEADS, axis=1)
+        low = jnp.concatenate([spans[0:1]] * BATCH_HEADS, axis=1)
+        high = jnp.concatenate([spans[1:2]] * BATCH_HEADS, axis=1)
         seen = [(low <= j) & (j < high) for j in range(IMAGES)]
         for at in range(0, GROUP * tokens, block):
             rows = slice(at, at + block)
@@ -255,16 +257,17 @@
 
 
 def sum_kernel(slots, got, out):
-    doc, _ = place_on_line()
+    doc, _ = place_in_block()
     out[...] = jnp.zeros_like(out)
-    along_z = doc % 2 == 0
     for j in range(IMAGES):
         owner = slots[doc * IMAGES + j] // IMAGES
         for c in range(KV_HEADS):
             total = 0.0
-            for line in range(LINE):
-                at = jnp.where(along_z, line * LINE + c, c * LINE + line)
-                total += got[at, j].astype(jnp.float32)
+            place = jnp.where(doc % 2 == 0, c, 3 - c)
+            for y in range(0, GRID, 2):
+                for z in range(0, GRID, 2):
+                    at = (place // 2 + y) * GRID + place % 2 + z
+                    total += got[at, j].astype(jnp.float32)
             out[owner, :, c * WIDTH : (c + 1) * WIDTH] = total[:, :WIDTH].astype(jnp.bfloat16)
             out[owner, :, KEY_COLUMNS + c * WIDTH : KEY_COLUMNS + (c + 1) * WIDTH] = total[
                 :, WIDTH:
@@ -272,7 +275,7 @@
 
 
 def place_kernel(docs, slots, got, out):
-    doc_here, _ = place_on_line()
+    doc_here, _ = place_in_block()
     for s in range(IMAGES):
         doc = 0
         for d in range(docs):
@@ -295,14 +298,14 @@
     )
 
 
-def shift(docs, k):
+def swap(docs, k):
     pairs = []
     for d in range(docs):
-        for a in range(LINE):
-            for b in range(LINE):
-                to = (b + k) % LINE
-                ends = (a * LINE + b, a * LINE + to) if d % 2 == 0 else (b * LINE + a, to * LINE + a)
-                pairs.append((d * LINE * LINE + ends[0], d * LINE * LINE + ends[1]))
+        for y in range(GRID):
+            for z in range(GRID):
+                v, w = (y + d % 2) ^ (k // 2), (z + d % 2) ^ (k % 2)
+                to = (v - d % 2) % GRID * GRID + (w - d % 2) % GRID
+                pairs.append((d * GRID * GRID + y * GRID + z, d * GRID * GRID + to))
     return pairs
 
 
@@ -332,30 +335,21 @@
     pieces = pl.pallas_call(
         payload_kernel,
         in_specs=[in_hbm, in_hbm, in_hbm],
-        out_specs=[in_hbm] * LINE,
-        out_shape=[jax.ShapeDtypeStruct((2 * tokens + PAD, width), jnp.bfloat16)] * LINE,
+        out_specs=[in_hbm] * BLOCK,
+        out_shape=[jax.ShapeDtypeStruct((2 * tokens + PAD, width), jnp.bfloat16)] * BLOCK,
         scratch_shapes=[
-            pltpu.VMEM((LINE, 2 * tokens + PAD, width), jnp.bfloat16),
+            pltpu.VMEM((BLOCK, 2 * tokens + PAD, width), jnp.bfloat16),
             pltpu.VMEM((2, tokens), jnp.int32),
-            pltpu.SemaphoreType.DMA((3 * LINE + 1,)),
+            pltpu.SemaphoreType.DMA((3 * BLOCK + 1,)),
         ],
         name="payload",
     )(queries[0], d_out[0], spans[0].T)
     one_head = jax.ShapeDtypeStruct((texts, images, rows, 2 * WIDTH), jnp.bfloat16)
     send = small(pick_kernel, one_head, "pick")(image_slots, got)
-    own, after, far, before = pieces
-    after = lax.ppermute(after, both, shift(docs, 1))
-    before = lax.ppermute(before, both, shift(docs, -1))
-    far, send = lax.optimization_barrier((far, send))
-    far = lax.ppermute(far, both, shift(docs, 2))
+    pieces = [pieces[0]] + [lax.ppermute(pieces[k], both, swap(docs, k)) for k in range(1, BLOCK)]
     kv = lax.all_to_all(send, "ctx", 0, 0).reshape(texts * images * rows, 2 * WIDTH)
-    gate = attn_gate.reshape(1, 1)
-    dq_own, dq_after, dq_before, sums = gradients(gate, kv, [own, after, before], last=False)
-    dq_far, dkv = gradients(gate, kv, [far], so_far=sums)
-    dq_after = lax.ppermute(dq_after, both, shift(docs, -1))
-    dq_before = lax.ppermute(dq_before, both, shift(docs, 1))
-    dq_far = lax.ppermute(dq_far, both, shift(docs, 2))
-    dqs = [dq_own, dq_after, dq_far, dq_before]
+    *dqs, dkv = gradients(attn_gate.reshape(1, 1), kv, pieces)
+    dqs = [dqs[0]] + [lax.ppermute(dqs[k], both, swap(docs, k)) for k in range(1, BLOCK)]
     parts = lax.all_to_all(dkv.reshape(texts, images, rows, 2 * WIDTH), "ctx", 0, 0)
     send = small(sum_kernel, block, "sum")(image_slots, parts)
     got = lax.all_to_all(send, "doc", 0, 0)
@@ -366,7 +360,7 @@
     )(image_slots, got)
     d_queries = pl.pallas_call(
         merge_kernel,
-        in_specs=[in_vmem] * LINE,
+        in_specs=[in_vmem] * BLOCK,
         out_specs=in_vmem,
         out_shape=jax.ShapeDtypeStruct(queries.shape[1:], jnp.bfloat16),
         compiler_params=params,

time: 92.1 us -> 89.3 us (0.970)
  waiting for transfers between devices: 16.5 us -> 22.2 us
  starting transfers between devices: 41.4 us -> 36.2 us
  Pallas kernels: 30.6 us -> 28 us
    ppermute x6, waiting for transfers between devices: 0.02 us -> 9.16 us  [the longest x3 9.15 us: shards(): lax.ppermute(pieces[k], both, swap(docs, k))]
    all_to_all x2, starting transfers between devices: 18.7 us -> 11.7 us  [shards(): got = lax.all_to_all(send, 'doc', 0, 0)]
    all_to_all x1, waiting for transfers between devices: 5.41 us -> 1.42 us  [shards(): lax.all_to_all(send, 'ctx', 0, 0).reshape(texts * images * rows, 2 * WIDTH)]
    pallas_call x2 -> x1, Pallas kernels: 21.1 us -> 18.6 us  [gradients(): pl.pallas_call(functools.partial(grad_kernel, count, first, last), in_spe...]
    all_to_all x1, starting transfers between devices: 4.5 us -> 6.69 us  [shards(): lax.all_to_all(dkv.reshape(texts, images, rows, 2 * WIDTH), 'ctx', 0, 0)]
    all_to_all x1, starting transfers between devices: 7.9 us -> 6.16 us  [shards(): lax.all_to_all(send, 'ctx', 0, 0).reshape(texts * images * rows, 2 * WIDTH)]
    all_to_all x1, waiting for transfers between devices: 4.53 us -> 6.2 us  [shards(): lax.all_to_all(dkv.reshape(texts, images, rows, 2 * WIDTH), 'ctx', 0, 0)]
    ppermute x6, starting transfers between devices: 10.2 us -> 11.7 us  [the longest x3 6.57 us: shards(): lax.ppermute(pieces[k], both, swap(docs, k))]
  transfers between devices with their start and end apart: 10 -> 10, of which waited for: 4 -> 4; matrix products, arithmetic and copies ran while one was open for 0% -> 0% of each run, Pallas kernels for 23% -> 7%
where the time goes in v8:
time: 89.3 us; the launch traced here: 88.7 us
  starting transfers between devices  36.2 us (41%)
  Pallas kernels  28 us (31%)
  waiting for transfers between devices  22.2 us (25%)
  between operations  1.42 us (2%)
    pallas_call x1, Pallas kernels, gradients(): pl.pallas_call(functools.partial(grad_kernel, count, first, last), in_spe...  18.6 us
    all_to_all x2, starting transfers between devices, shards(): got = lax.all_to_all(send, 'doc', 0, 0)  11.7 us
    ppermute x3, waiting for transfers between devices, shards(): lax.ppermute(pieces[k], both, swap(docs, k))  9.15 us
    all_to_all x1, starting transfers between devices, shards(): lax.all_to_all(dkv.reshape(texts, images, rows, 2 * WIDTH), 'ctx', 0, 0)  6.69 us
    ppermute x3, starting transfers between devices, shards(): lax.ppermute(pieces[k], both, swap(docs, k))  6.57 us
    all_to_all x1, waiting for transfers between devices, shards(): lax.all_to_all(dkv.reshape(texts, images, rows, 2 * WIDTH), 'ctx', 0, 0)  6.2 us
    all_to_all x1, starting transfers between devices, shards(): lax.all_to_all(send, 'ctx', 0, 0).reshape(texts * images * rows, 2 * WIDTH)  6.16 us
    all_to_all x2, waiting for transfers between devices, shards(): got = lax.all_to_all(send, 'doc', 0, 0)  5.41 us
  transfers between devices with their start and end apart: 10, of which 4 were waited for; matrix products, arithmetic and copies ran while one was open for 0% of the time, Pallas kernels for 7%

profile of v8, /device:TPU:1, one launch (start us, length us, event | category | flops | bytes accessed | tf_op | source)
XLA Modules:
  0.0 88.7 jit_solution(11464866987183376048)
XLA Ops:
  0.6 1.7 %pack.1 = bf16[8,16,1024]{2,1,0:T(8,128)(2,1)} custom-call(s32[32]{0:T(128)} %slots.5, bf16[4,16,1024]{2,1,0:T(8,128)(2,1)} %kv.1), custom_call_target="tpu_custom_call" | custom-call | tf_op jit(solution)/shard_map/pack/pallas_call | solution.py:322
  2.3 5.8 %all-to-all-start = ((bf16[8,16,1024]{2,1,0:T(8,128)(2,1)}), bf16[8,16,1024]{2,1,0:T(8,128)(2,1)S(1)}, u32[]{:S(2)}, u32[]{:S(2)}) async-start(bf16[8,16,1024]{2,1,0:T(8,128)(2,1)} %pack.1), calls=%async_computation | async-start | bytes 524288 | tf_op jit(solution)/shard_map/all_to_all | solution.py:334
  8.1 2.5 %payload.1 = (bf16[272,1024]{1,0:T(8,128)(2,1)}, bf16[272,1024]{1,0:T(8,128)(2,1)}, bf16[272,1024]{1,0:T(8,128)(2,1)}, bf16[272,1024]{1,0:T(8,128)(2,1)}) custom-call(bf16[128,4096]{1,0:T(8,128)(2,1)} %bitcast.11, bf16[128,4096]{1,0:T(8,128)(2,1)} %bitcast.12, s32[2,128]{1,0:T(2,128)} %bitcast.15), custom_call_target="tpu_custom_call" | custom-call | tf_op jit(solution)/shard_map/payload/pallas_call | solution.py:335
  10.7 3.8 %collective-permute-start = (bf16[272,1024]{1,0:T(8,128)(2,1)}, bf16[272,1024]{1,0:T(8,128)(2,1)S(1)}, u32[]{:S(2)}, u32[]{:S(2)}) collective-permute-start(bf16[272,1024]{1,0:T(8,128)(2,1)} %get-tuple-element.12), channel_id=1, source_target_pairs={{0,1},{1,0},{2,3},{3,2},{4,5},{5,4},{6,7},{7,6},{8,9},{9,8},{10,11... | collective-permute-start | bytes 1671176 | tf_op jit(solution)/shard_map/ppermute | solution.py:349
  14.5 2.7 %collective-permute-start.1 = (bf16[272,1024]{1,0:T(8,128)(2,1)}, bf16[272,1024]{1,0:T(8,128)(2,1)S(1)}, u32[]{:S(2)}, u32[]{:S(2)}) collective-permute-start(bf16[272,1024]{1,0:T(8,128)(2,1)} %get-tuple-element.13), channel_id=1, source_target_pairs={{0,4},{1,5},{2,6},{3,7},{4,0},{5,1},{6,2},{7,3},{8,12},{9,13},{10,... | collective-permute-start | bytes 1671176 | tf_op jit(solution)/shard_map/ppermute | solution.py:349
  17.2 0.0 collective-permute-start.2
  17.2 0.0 all-to-all-done.got
  17.2 1.4 %pick.1 = bf16[16,4,16,256]{3,2,1,0:T(8,128)(2,1)} custom-call(s32[32]{0:T(128)S(1)} %copy-done.1, bf16[8,16,1024]{2,1,0:T(8,128)(2,1)S(1)} %all-to-all-done.got), custom_call_target="tpu_custom_call" | custom-call | tf_op jit(solution)/shard_map/pick/pallas_call | solution.py:348
  18.6 6.2 %all-to-all-start.1 = ((bf16[16,4,16,256]{3,2,1,0:T(8,128)(2,1)}), bf16[16,4,16,256]{3,2,1,0:T(8,128)(2,1)S(1)}, u32[]{:S(2)}, u32[]{:S(2)}) async-start(bf16[16,4,16,256]{3,2,1,0:T(8,128)(2,1)} %pick.1), calls=%async_computation.1 | async-start | bytes 1048576 | tf_op jit(solution)/shard_map/all_to_all | solution.py:350
  25.5 0.0 collective-permute-done.refs_1_
  25.5 0.0 collective-permute-done.1.refs_2_
  25.5 9.1 %collective-permute-done.2.refs_3_ = bf16[272,1024]{1,0:T(8,128)(2,1)S(1)} collective-permute-done((bf16[272,1024]{1,0:T(8,128)(2,1)}, bf16[272,1024]{1,0:T(8,128)(2,1)S(1)}, u32[]{:S(2)}, u32[]{:S(2)}) %collective-permute-start.2) | collective-permute-done | bytes 557088 | tf_op jit(solution)/shard_map/ppermute | solution.py:349
  34.6 1.4 %all-to-all-done.1 = bf16[16,4,16,256]{3,2,1,0:T(8,128)(2,1)S(1)} async-done(((bf16[16,4,16,256]{3,2,1,0:T(8,128)(2,1)}), bf16[16,4,16,256]{3,2,1,0:T(8,128)(2,1)S(1)}, u32[]{:S(2)}, u32[]{:S(2)}) %all-to-all-start.1) | async-done | bytes 524320 | tf_op jit(solution)/shard_map/all_to_all | solution.py:350
  36.1 0.8 copy-done.2
  36.9 18.6 %gradients.1 = (bf16[128,1024]{1,0:T(8,128)(2,1)}, bf16[128,1024]{1,0:T(8,128)(2,1)}, bf16[128,1024]{1,0:T(8,128)(2,1)}, bf16[128,1024]{1,0:T(8,128)(2,1)}, bf16[1024,256]{1,0:T(8,128)(2,1)}) custom-call(f32[1,1]{1,0:T(1,128)} %bitcast.9.gate, bf16[1024,256]{1,0:T(8,128)(2,1)} %bitcast.13, bf16[272,1024]{1,0:T(8,128)(2,1)} %get-tuple-element.11.refs_0_, ...), custom_call_target="tpu_custom_call" | custom-call | flops 5368709120 | bytes 4194304 | tf_op jit(solution)/shard_map/gradients/pallas_call | solution.py:230
  55.4 0.0 copy-start.8
  55.5 0.0 copy-start.7
  55.5 0.0 copy-start.6
  55.5 6.7 %all-to-all-start.2 = ((bf16[16,4,16,256]{3,2,1,0:T(8,128)(2,1)}), bf16[16,4,16,256]{3,2,1,0:T(8,128)(2,1)S(1)}, u32[]{:S(2)}, u32[]{:S(2)}) async-start(bf16[16,4,16,256]{3,2,1,0:T(8,128)(2,1)} %bitcast.14), calls=%async_computation.2 | async-start | bytes 1048576 | tf_op jit(solution)/shard_map/all_to_all | solution.py:353
  62.2 0.0 copy-done.8
  62.2 2.7 %collective-permute-start.3 = (bf16[128,1024]{1,0:T(8,128)(2,1)S(1)}, bf16[128,1024]{1,0:T(8,128)(2,1)S(1)}, u32[]{:S(2)}, u32[]{:S(2)}) collective-permute-start(bf16[128,1024]{1,0:T(8,128)(2,1)S(1)} %copy-done.8), channel_id=1, source_target_pairs={{0,1},{1,0},{2,3},{3,2},{4,5},{5,4},{6,7},{7,6},{8,9},{9,8},{10,11... | collective-permute-start | bytes 786440 | tf_op jit(solution)/shard_map/ppermute | solution.py:352
  64.8 2.4 %collective-permute-start.4 = (bf16[128,1024]{1,0:T(8,128)(2,1)S(1)}, bf16[128,1024]{1,0:T(8,128)(2,1)S(1)}, u32[]{:S(2)}, u32[]{:S(2)}) collective-permute-start(bf16[128,1024]{1,0:T(8,128)(2,1)S(1)} %copy-done.7), channel_id=1, source_target_pairs={{0,4},{1,5},{2,6},{3,7},{4,0},{5,1},{6,2},{7,3},{8,12},{9,13},{10,... | collective-permute-start | bytes 786440 | tf_op jit(solution)/shard_map/ppermute | solution.py:352
  67.2 0.1 collective-permute-start.5
  67.3 6.2 %all-to-all-done.2.got = bf16[16,4,16,256]{3,2,1,0:T(8,128)(2,1)S(1)} async-done(((bf16[16,4,16,256]{3,2,1,0:T(8,128)(2,1)}), bf16[16,4,16,256]{3,2,1,0:T(8,128)(2,1)S(1)}, u32[]{:S(2)}, u32[]{:S(2)}) %all-to-all-start.2) | async-done | bytes 524320 | tf_op jit(solution)/shard_map/all_to_all | solution.py:353
  73.5 1.3 %sum.1 = bf16[8,16,1024]{2,1,0:T(8,128)(2,1)} custom-call(s32[32]{0:T(128)S(1)} %copy-done.1, bf16[16,4,16,256]{3,2,1,0:T(8,128)(2,1)S(1)} %all-to-all-done.2.got), custom_call_target="tpu_custom_call" | custom-call | tf_op jit(solution)/shard_map/sum/pallas_call | solution.py:354
  74.9 5.9 %all-to-all-start.3 = ((bf16[8,16,1024]{2,1,0:T(8,128)(2,1)}), bf16[8,16,1024]{2,1,0:T(8,128)(2,1)S(1)}, u32[]{:S(2)}, u32[]{:S(2)}) async-start(bf16[8,16,1024]{2,1,0:T(8,128)(2,1)} %sum.1), calls=%async_computation.3 | async-start | bytes 524288 | tf_op jit(solution)/shard_map/all_to_all | solution.py:355
  80.7 0.0 collective-permute-done.3.refs_1_
  80.7 0.0 collective-permute-done.4.refs_2_
  80.8 0.0 collective-permute-done.5.refs_3_
  80.8 1.1 %merge.1 = bf16[128,4096]{1,0:T(8,128)(2,1)} custom-call(bf16[128,1024]{1,0:T(8,128)(2,1)S(1)} %copy-done, bf16[128,1024]{1,0:T(8,128)(2,1)S(1)} %collective-permute-done.3.refs_1_, bf16[128,1024]{1,0:T(8,128)(2,1)S(1)} %collective-permute-done.4.refs_2_, bf16[128,1024]{1,0:T(8,128)(2,1)S(1)} %collective-permute-done.5.refs_3_), custom_call_target="tpu_custom_call" | custom-call | tf_op jit(solution)/shard_map/merge/pallas_call | solution.py:361
  81.8 5.4 %all-to-all-done.3.got = bf16[8,16,1024]{2,1,0:T(8,128)(2,1)S(1)} async-done(((bf16[8,16,1024]{2,1,0:T(8,128)(2,1)}), bf16[8,16,1024]{2,1,0:T(8,128)(2,1)S(1)}, u32[]{:S(2)}, u32[]{:S(2)}) %all-to-all-start.3) | async-done | bytes 262176 | tf_op jit(solution)/shard_map/all_to_all | solution.py:355
  87.3 1.4 %place.1 = f32[4,16,1024]{2,1,0:T(8,128)} custom-call(s32[32]{0:T(128)S(1)} %copy-done.1, bf16[8,16,1024]{2,1,0:T(8,128)(2,1)S(1)} %all-to-all-done.3.got), custom_call_target="tpu_custom_call" | custom-call | tf_op jit(solution)/shard_map/place/pallas_call | solution.py:356
  (13 shorter events, 0.0 us)
Async XLA Ops:
  2.3 14.9 %all-to-all-start = ((bf16[8,16,1024]{2,1,0:T(8,128)(2,1)}), bf16[8,16,1024]{2,1,0:T(8,128)(2,1)S(1)}, u32[]{:S(2)}, u32[]{:S(2)}) async-start(bf16[8,16,1024]{2,1,0:T(8,128)(2,1)} %pack.1), calls=%async_computation | async-start | bytes 524288 | tf_op jit(solution)/shard_map/all_to_all | solution.py:334
  10.7 14.8 %collective-permute-start = (bf16[272,1024]{1,0:T(8,128)(2,1)}, bf16[272,1024]{1,0:T(8,128)(2,1)S(1)}, u32[]{:S(2)}, u32[]{:S(2)}) collective-permute-start(bf16[272,1024]{1,0:T(8,128)(2,1)} %get-tuple-element.12), channel_id=1, source_target_pairs={{0,1},{1,0},{2,3},{3,2},{4,5},{5,4},{6,7},{7,6},{8,9},{9,8},{10,11... | collective-permute-start | bytes 1671176 | tf_op jit(solution)/shard_map/ppermute | solution.py:349
  14.5 2.7 %copy-start.1 = (s32[32]{0:T(128)S(1)}, s32[32]{0:T(128)}, u32[]{:S(2)}) copy-start(s32[32]{0:T(128)} %slots.5) | copy-start | bytes 388
  14.5 11.0 %collective-permute-start.1 = (bf16[272,1024]{1,0:T(8,128)(2,1)}, bf16[272,1024]{1,0:T(8,128)(2,1)S(1)}, u32[]{:S(2)}, u32[]{:S(2)}) collective-permute-start(bf16[272,1024]{1,0:T(8,128)(2,1)} %get-tuple-element.13), channel_id=1, source_target_pairs={{0,4},{1,5},{2,6},{3,7},{4,0},{5,1},{6,2},{7,3},{8,12},{9,13},{10,... | collective-permute-start | bytes 1671176 | tf_op jit(solution)/shard_map/ppermute | solution.py:349
  17.2 17.4 %collective-permute-start.2 = (bf16[272,1024]{1,0:T(8,128)(2,1)}, bf16[272,1024]{1,0:T(8,128)(2,1)S(1)}, u32[]{:S(2)}, u32[]{:S(2)}) collective-permute-start(bf16[272,1024]{1,0:T(8,128)(2,1)} %get-tuple-element.14), channel_id=1, source_target_pairs={{0,5},{1,4},{2,7},{3,6},{4,1},{5,0},{6,3},{7,2},{8,13},{9,12},{10,... | collective-permute-start | bytes 1671176 | tf_op jit(solution)/shard_map/ppermute | solution.py:349
  18.6 17.4 %all-to-all-start.1 = ((bf16[16,4,16,256]{3,2,1,0:T(8,128)(2,1)}), bf16[16,4,16,256]{3,2,1,0:T(8,128)(2,1)S(1)}, u32[]{:S(2)}, u32[]{:S(2)}) async-start(bf16[16,4,16,256]{3,2,1,0:T(8,128)(2,1)} %pick.1), calls=%async_computation.1 | async-start | bytes 1048576 | tf_op jit(solution)/shard_map/all_to_all | solution.py:350
  25.5 10.6 %copy-start.3 = (bf16[272,1024]{1,0:T(8,128)(2,1)}, bf16[272,1024]{1,0:T(8,128)(2,1)S(1)}, u32[]{:S(2)}) copy-start(bf16[272,1024]{1,0:T(8,128)(2,1)S(1)} %collective-permute-done.refs_1_) | copy-start | bytes 1671172
  25.5 10.6 %copy-start.4 = (bf16[272,1024]{1,0:T(8,128)(2,1)}, bf16[272,1024]{1,0:T(8,128)(2,1)S(1)}, u32[]{:S(2)}) copy-start(bf16[272,1024]{1,0:T(8,128)(2,1)S(1)} %collective-permute-done.1.refs_2_) | copy-start | bytes 1671172
  34.6 1.4 %copy-start.5 = (bf16[272,1024]{1,0:T(8,128)(2,1)}, bf16[272,1024]{1,0:T(8,128)(2,1)S(1)}, u32[]{:S(2)}) copy-start(bf16[272,1024]{1,0:T(8,128)(2,1)S(1)} %collective-permute-done.2.refs_3_) | copy-start | bytes 1671172
  36.1 0.8 copy-start.2
  55.4 6.7 %copy-start.8 = (bf16[128,1024]{1,0:T(8,128)(2,1)S(1)}, bf16[128,1024]{1,0:T(8,128)(2,1)}, u32[]{:S(2)}) copy-start(bf16[128,1024]{1,0:T(8,128)(2,1)} %get-tuple-element.16) | copy-start | bytes 786436
  55.5 9.4 %copy-start.7 = (bf16[128,1024]{1,0:T(8,128)(2,1)S(1)}, bf16[128,1024]{1,0:T(8,128)(2,1)}, u32[]{:S(2)}) copy-start(bf16[128,1024]{1,0:T(8,128)(2,1)} %get-tuple-element.17) | copy-start | bytes 786436
  55.5 11.8 %copy-start.6 = (bf16[128,1024]{1,0:T(8,128)(2,1)S(1)}, bf16[128,1024]{1,0:T(8,128)(2,1)}, u32[]{:S(2)}) copy-start(bf16[128,1024]{1,0:T(8,128)(2,1)} %get-tuple-element.18) | copy-start | bytes 786436
  55.5 18.1 %all-to-all-start.2 = ((bf16[16,4,16,256]{3,2,1,0:T(8,128)(2,1)}), bf16[16,4,16,256]{3,2,1,0:T(8,128)(2,1)S(1)}, u32[]{:S(2)}, u32[]{:S(2)}) async-start(bf16[16,4,16,256]{3,2,1,0:T(8,128)(2,1)} %bitcast.14), calls=%async_computation.2 | async-start | bytes 1048576 | tf_op jit(solution)/shard_map/all_to_all | solution.py:353
  62.2 18.6 %collective-permute-start.3 = (bf16[128,1024]{1,0:T(8,128)(2,1)S(1)}, bf16[128,1024]{1,0:T(8,128)(2,1)S(1)}, u32[]{:S(2)}, u32[]{:S(2)}) collective-permute-start(bf16[128,1024]{1,0:T(8,128)(2,1)S(1)} %copy-done.8), channel_id=1, source_target_pairs={{0,1},{1,0},{2,3},{3,2},{4,5},{5,4},{6,7},{7,6},{8,9},{9,8},{10,11... | collective-permute-start | bytes 786440 | tf_op jit(solution)/shard_map/ppermute | solution.py:352
  64.8 15.9 %collective-permute-start.4 = (bf16[128,1024]{1,0:T(8,128)(2,1)S(1)}, bf16[128,1024]{1,0:T(8,128)(2,1)S(1)}, u32[]{:S(2)}, u32[]{:S(2)}) collective-permute-start(bf16[128,1024]{1,0:T(8,128)(2,1)S(1)} %copy-done.7), channel_id=1, source_target_pairs={{0,4},{1,5},{2,6},{3,7},{4,0},{5,1},{6,2},{7,3},{8,12},{9,13},{10,... | collective-permute-start | bytes 786440 | tf_op jit(solution)/shard_map/ppermute | solution.py:352
  67.2 13.5 %collective-permute-start.5 = (bf16[128,1024]{1,0:T(8,128)(2,1)S(1)}, bf16[128,1024]{1,0:T(8,128)(2,1)S(1)}, u32[]{:S(2)}, u32[]{:S(2)}) collective-permute-start(bf16[128,1024]{1,0:T(8,128)(2,1)S(1)} %copy-done.6), channel_id=1, source_target_pairs={{0,5},{1,4},{2,7},{3,6},{4,1},{5,0},{6,3},{7,2},{8,13},{9,12},{10,... | collective-permute-start | bytes 786440 | tf_op jit(solution)/shard_map/ppermute | solution.py:352
  74.9 5.9 %copy-start = (bf16[128,1024]{1,0:T(8,128)(2,1)S(1)}, bf16[128,1024]{1,0:T(8,128)(2,1)}, u32[]{:S(2)}) copy-start(bf16[128,1024]{1,0:T(8,128)(2,1)} %get-tuple-element.15.refs_0_) | copy-start | bytes 786436
  74.9 12.4 %all-to-all-start.3 = ((bf16[8,16,1024]{2,1,0:T(8,128)(2,1)}), bf16[8,16,1024]{2,1,0:T(8,128)(2,1)S(1)}, u32[]{:S(2)}, u32[]{:S(2)}) async-start(bf16[8,16,1024]{2,1,0:T(8,128)(2,1)} %sum.1), calls=%async_computation.3 | async-start | bytes 524288 | tf_op jit(solution)/shard_map/all_to_all | solution.py:355

commit v9 on v8

--- a/solution.py
+++ b/solution.py
@@ -346,13 +346,21 @@
     )(queries[0], d_out[0], spans[0].T)
     one_head = jax.ShapeDtypeStruct((texts, images, rows, 2 * WIDTH), jnp.bfloat16)
     send = small(pick_kernel, one_head, "pick")(image_slots, got)
-    pieces = [pieces[0]] + [lax.ppermute(pieces[k], both, swap(docs, k)) for k in range(1, BLOCK)]
+    own, *others = pieces
+    beside, above = [lax.ppermute(others[k - 1], both, swap(docs, k)) for k in (1, 2)]
+    across, send = lax.optimization_barrier((others[2], send))
+    across = lax.ppermute(across, both, swap(docs, 3))
     kv = lax.all_to_all(send, "ctx", 0, 0).reshape(texts * images * rows, 2 * WIDTH)
-    *dqs, dkv = gradients(attn_gate.reshape(1, 1), kv, pieces)
-    dqs = [dqs[0]] + [lax.ppermute(dqs[k], both, swap(docs, k)) for k in range(1, BLOCK)]
+    gate = attn_gate.reshape(1, 1)
+    dq_own, dq_beside, dq_above, sums = gradients(gate, kv, [own, beside, above], last=False)
+    dq_across, dkv = gradients(gate, kv, [across], so_far=sums)
+    dq_beside = lax.ppermute(dq_beside, both, swap(docs, 1))
+    dq_above = lax.ppermute(dq_above, both, swap(docs, 2))
+    dq_across = lax.ppermute(dq_across, both, swap(docs, 3))
     parts = lax.all_to_all(dkv.reshape(texts, images, rows, 2 * WIDTH), "ctx", 0, 0)
     send = small(sum_kernel, block, "sum")(image_slots, parts)
     got = lax.all_to_all(send, "doc", 0, 0)
+    dqs = [dq_own, dq_beside, dq_above, dq_across]
     d_image_kv = small(
         functools.partial(place_kernel, docs),
         jax.ShapeDtypeStruct(image_kv.shape, jnp.float32),

time: 89.3 us -> 91.8 us (1.028)
  waiting for transfers between devices: 22.2 us -> 12.7 us
  starting transfers between devices: 36.2 us -> 44.8 us
  Pallas kernels: 28 us -> 30.6 us
    ppermute x6, waiting for transfers between devices: 9.16 us -> 0.02 us  [the longest x2 0.01 us: shards(): lax.ppermute(others[k - 1], both, swap(docs, k))]
    all_to_all x2, starting transfers between devices: 11.7 us -> 18.6 us  [shards(): got = lax.all_to_all(send, 'doc', 0, 0)]
    ppermute x6, starting transfers between devices: 11.7 us -> 16.5 us  [the longest x2 6.57 us: shards(): lax.ppermute(others[k - 1], both, swap(docs, k))]
    pallas_call x1 -> x2, Pallas kernels: 18.6 us -> 21.2 us  [gradients(): pl.pallas_call(functools.partial(grad_kernel, count, first, last), in_spe...]
    all_to_all x1, waiting for transfers between devices: 6.2 us -> 3.79 us  [shards(): lax.all_to_all(dkv.reshape(texts, images, rows, 2 * WIDTH), 'ctx', 0, 0)]
    all_to_all x1, starting transfers between devices: 6.69 us -> 4.37 us  [shards(): lax.all_to_all(dkv.reshape(texts, images, rows, 2 * WIDTH), 'ctx', 0, 0)]
    all_to_all x1, waiting for transfers between devices: 1.42 us -> 3.53 us  [shards(): lax.all_to_all(send, 'ctx', 0, 0).reshape(texts * images * rows, 2 * WIDTH)]
  transfers between devices with their start and end apart: 10 -> 10, of which waited for: 4 -> 3; matrix products, arithmetic and copies ran while one was open for 0% -> 0% of each run, Pallas kernels for 7% -> 23%
where the time goes in v9:
time: 91.8 us; the launch traced here: 91.2 us
  starting transfers between devices  44.8 us (49%)
  Pallas kernels  30.6 us (33%)
  waiting for transfers between devices  12.7 us (14%)
  local copies, waits for them, and re-layouts  1.63 us (2%)
  between operations  1.46 us (2%)
    pallas_call x2, Pallas kernels, gradients(): pl.pallas_call(functools.partial(grad_kernel, count, first, last), in_spe...  21.2 us
    all_to_all x2, starting transfers between devices, shards(): got = lax.all_to_all(send, 'doc', 0, 0)  18.6 us
    ppermute x2, starting transfers between devices, shards(): lax.ppermute(others[k - 1], both, swap(docs, k))  6.57 us
    all_to_all x2, waiting for transfers between devices, shards(): got = lax.all_to_all(send, 'doc', 0, 0)  5.41 us
    all_to_all x1, starting transfers between devices, shards(): lax.all_to_all(send, 'ctx', 0, 0).reshape(texts * images * rows, 2 * WIDTH)  5.28 us
    ppermute x1, starting transfers between devices, shards(): across = lax.ppermute(across, both, swap(docs, 3))  4.77 us
    all_to_all x1, starting transfers between devices, shards(): lax.all_to_all(dkv.reshape(texts, images, rows, 2 * WIDTH), 'ctx', 0, 0)  4.37 us
    all_to_all x1, waiting for transfers between devices, shards(): lax.all_to_all(dkv.reshape(texts, images, rows, 2 * WIDTH), 'ctx', 0, 0)  3.79 us
  transfers between devices with their start and end apart: 10, of which 3 were waited for; matrix products, arithmetic and copies ran while one was open for 0% of the time, Pallas kernels for 23%

profile of v9, /device:TPU:1, one launch (start us, length us, event | category | flops | bytes accessed | tf_op | source)
XLA Modules:
  0.0 91.2 jit_solution(13674735673512050391)
XLA Ops:
  0.6 1.7 %pack.1 = bf16[8,16,1024]{2,1,0:T(8,128)(2,1)} custom-call(s32[32]{0:T(128)} %slots.5, bf16[4,16,1024]{2,1,0:T(8,128)(2,1)} %kv.1), custom_call_target="tpu_custom_call" | custom-call | tf_op jit(solution)/shard_map/pack/pallas_call | solution.py:322
  2.3 5.8 %all-to-all-start = ((bf16[8,16,1024]{2,1,0:T(8,128)(2,1)}), bf16[8,16,1024]{2,1,0:T(8,128)(2,1)S(1)}, u32[]{:S(2)}, u32[]{:S(2)}) async-start(bf16[8,16,1024]{2,1,0:T(8,128)(2,1)} %pack.1), calls=%async_computation | async-start | bytes 524288 | tf_op jit(solution)/shard_map/all_to_all | solution.py:334
  8.1 2.5 %payload.1 = (bf16[272,1024]{1,0:T(8,128)(2,1)}, bf16[272,1024]{1,0:T(8,128)(2,1)}, bf16[272,1024]{1,0:T(8,128)(2,1)}, bf16[272,1024]{1,0:T(8,128)(2,1)}) custom-call(bf16[128,4096]{1,0:T(8,128)(2,1)} %bitcast.12, bf16[128,4096]{1,0:T(8,128)(2,1)} %bitcast.13, s32[2,128]{1,0:T(2,128)} %bitcast.17), custom_call_target="tpu_custom_call" | custom-call | tf_op jit(solution)/shard_map/payload/pallas_call | solution.py:335
  10.7 0.0 copy-start.1
  10.7 3.8 %collective-permute-start = (bf16[272,1024]{1,0:T(8,128)(2,1)}, bf16[272,1024]{1,0:T(8,128)(2,1)S(1)}, u32[]{:S(2)}, u32[]{:S(2)}) collective-permute-start(bf16[272,1024]{1,0:T(8,128)(2,1)} %get-tuple-element.17), channel_id=1, source_target_pairs={{0,1},{1,0},{2,3},{3,2},{4,5},{5,4},{6,7},{7,6},{8,9},{9,8},{10,11... | collective-permute-start | bytes 1671176 | tf_op jit(solution)/shard_map/ppermute | solution.py:350
  14.5 2.7 %collective-permute-start.1 = (bf16[272,1024]{1,0:T(8,128)(2,1)}, bf16[272,1024]{1,0:T(8,128)(2,1)S(1)}, u32[]{:S(2)}, u32[]{:S(2)}) collective-permute-start(bf16[272,1024]{1,0:T(8,128)(2,1)} %get-tuple-element.18), channel_id=1, source_target_pairs={{0,4},{1,5},{2,6},{3,7},{4,0},{5,1},{6,2},{7,3},{8,12},{9,13},{10,... | collective-permute-start | bytes 1671176 | tf_op jit(solution)/shard_map/ppermute | solution.py:350
  17.2 0.0 all-to-all-done.got
  17.3 1.4 %pick.1 = bf16[16,4,16,256]{3,2,1,0:T(8,128)(2,1)} custom-call(s32[32]{0:T(128)S(1)} %copy-done.1, bf16[8,16,1024]{2,1,0:T(8,128)(2,1)S(1)} %all-to-all-done.got), custom_call_target="tpu_custom_call" | custom-call | tf_op jit(solution)/shard_map/pick/pallas_call | solution.py:348
  18.7 5.3 %all-to-all-start.1 = ((bf16[16,4,16,256]{3,2,1,0:T(8,128)(2,1)}), bf16[16,4,16,256]{3,2,1,0:T(8,128)(2,1)S(1)}, u32[]{:S(2)}, u32[]{:S(2)}) async-start(bf16[16,4,16,256]{3,2,1,0:T(8,128)(2,1)} %pick.1), calls=%async_computation.1 | async-start | bytes 1048576 | tf_op jit(solution)/shard_map/all_to_all | solution.py:353
  24.0 4.8 %collective-permute-start.4 = (bf16[272,1024]{1,0:T(8,128)(2,1)S(1)}, bf16[272,1024]{1,0:T(8,128)(2,1)S(1)}, u32[]{:S(2)}, u32[]{:S(2)}) collective-permute-start(bf16[272,1024]{1,0:T(8,128)(2,1)S(1)} %copy-done.3), channel_id=1, source_target_pairs={{0,5},{1,4},{2,7},{3,6},{4,1},{5,0},{6,3},{7,2},{8,13},{9,12},{10,... | collective-permute-start | bytes 1671176 | tf_op jit(solution)/shard_map/ppermute | solution.py:352
  29.4 0.0 collective-permute-done.refs_1_
  29.4 0.0 copy-start.4
  29.4 0.0 collective-permute-done.1.refs_2_
  29.4 3.5 %all-to-all-done.1 = bf16[16,4,16,256]{3,2,1,0:T(8,128)(2,1)S(1)} async-done(((bf16[16,4,16,256]{3,2,1,0:T(8,128)(2,1)}), bf16[16,4,16,256]{3,2,1,0:T(8,128)(2,1)S(1)}, u32[]{:S(2)}, u32[]{:S(2)}) %all-to-all-start.1) | async-done | bytes 524320 | tf_op jit(solution)/shard_map/all_to_all | solution.py:353
  33.0 0.8 copy-done.2
  33.7 14.6 %gradients.2 = (bf16[128,1024]{1,0:T(8,128)(2,1)}, bf16[128,1024]{1,0:T(8,128)(2,1)}, bf16[128,1024]{1,0:T(8,128)(2,1)}, f32[1024,256]{1,0:T(8,128)}) custom-call(f32[1,1]{1,0:T(1,128)} %bitcast.9.gate, bf16[1024,256]{1,0:T(8,128)(2,1)} %bitcast.14, bf16[272,1024]{1,0:T(8,128)(2,1)} %get-tuple-element.16.refs_0_, bf16[272,1024]{1,0:T(8,128)(2,1)} %copy-done.4, ...), custom_call_target="tpu_custom_call" | custom-call | flops 4026531840 | bytes 4194304 | tf_op jit(solution)/shard_map/gradients/pallas_call | solution.py:230
  48.3 0.0 collective-permute-done.4.refs_0_
  48.4 0.8 copy-done.6
  49.2 6.6 %gradients.3 = (bf16[128,1024]{1,0:T(8,128)(2,1)}, bf16[1024,256]{1,0:T(8,128)(2,1)}) custom-call(f32[1,1]{1,0:T(1,128)} %bitcast.10.gate, bf16[1024,256]{1,0:T(8,128)(2,1)} %bitcast.15, bf16[272,1024]{1,0:T(8,128)(2,1)} %copy-done.6, f32[1024,256]{1,0:T(8,128)} %get-tuple-element.23.refs_1_), custom_call_target="tpu_custom_call" | custom-call | flops 1342177280 | bytes 4194304 | tf_op jit(solution)/shard_map/gradients/pallas_call | solution.py:230
  55.8 4.4 %all-to-all-start.2 = ((bf16[16,4,16,256]{3,2,1,0:T(8,128)(2,1)}), bf16[16,4,16,256]{3,2,1,0:T(8,128)(2,1)S(1)}, u32[]{:S(2)}, u32[]{:S(2)}) async-start(bf16[16,4,16,256]{3,2,1,0:T(8,128)(2,1)} %bitcast.16), calls=%async_computation.2 | async-start | bytes 1048576 | tf_op jit(solution)/shard_map/all_to_all | solution.py:360
  60.2 2.7 %collective-permute-start.2 = (bf16[128,1024]{1,0:T(8,128)(2,1)S(1)}, bf16[128,1024]{1,0:T(8,128)(2,1)S(1)}, u32[]{:S(2)}, u32[]{:S(2)}) collective-permute-start(bf16[128,1024]{1,0:T(8,128)(2,1)S(1)} %copy-done.8), channel_id=1, source_target_pairs={{0,1},{1,0},{2,3},{3,2},{4,5},{5,4},{6,7},{7,6},{8,9},{9,8},{10,11... | collective-permute-start | bytes 786440 | tf_op jit(solution)/shard_map/ppermute | solution.py:357
  62.8 2.4 %collective-permute-start.3 = (bf16[128,1024]{1,0:T(8,128)(2,1)S(1)}, bf16[128,1024]{1,0:T(8,128)(2,1)S(1)}, u32[]{:S(2)}, u32[]{:S(2)}) collective-permute-start(bf16[128,1024]{1,0:T(8,128)(2,1)S(1)} %copy-done.7), channel_id=1, source_target_pairs={{0,4},{1,5},{2,6},{3,7},{4,0},{5,1},{6,2},{7,3},{8,12},{9,13},{10,... | collective-permute-start | bytes 786440 | tf_op jit(solution)/shard_map/ppermute | solution.py:358
  65.2 0.1 collective-permute-start.5
  65.3 3.8 %all-to-all-done.2.got = bf16[16,4,16,256]{3,2,1,0:T(8,128)(2,1)S(1)} async-done(((bf16[16,4,16,256]{3,2,1,0:T(8,128)(2,1)}), bf16[16,4,16,256]{3,2,1,0:T(8,128)(2,1)S(1)}, u32[]{:S(2)}, u32[]{:S(2)}) %all-to-all-start.2) | async-done | bytes 524320 | tf_op jit(solution)/shard_map/all_to_all | solution.py:360
  69.1 1.3 %sum.1 = bf16[8,16,1024]{2,1,0:T(8,128)(2,1)} custom-call(s32[32]{0:T(128)S(1)} %copy-done.1, bf16[16,4,16,256]{3,2,1,0:T(8,128)(2,1)S(1)} %all-to-all-done.2.got), custom_call_target="tpu_custom_call" | custom-call | tf_op jit(solution)/shard_map/sum/pallas_call | solution.py:361
  70.5 12.8 %all-to-all-start.3 = ((bf16[8,16,1024]{2,1,0:T(8,128)(2,1)}), bf16[8,16,1024]{2,1,0:T(8,128)(2,1)S(1)}, u32[]{:S(2)}, u32[]{:S(2)}) async-start(bf16[8,16,1024]{2,1,0:T(8,128)(2,1)} %sum.1), calls=%async_computation.3 | async-start | bytes 524288 | tf_op jit(solution)/shard_map/all_to_all | solution.py:362
  83.3 0.0 collective-permute-done.2.refs_1_
  83.3 0.0 collective-permute-done.3.refs_2_
  83.3 0.0 collective-permute-done.5.refs_3_
  83.3 1.1 %merge.1 = bf16[128,4096]{1,0:T(8,128)(2,1)} custom-call(bf16[128,1024]{1,0:T(8,128)(2,1)S(1)} %copy-done, bf16[128,1024]{1,0:T(8,128)(2,1)S(1)} %collective-permute-done.2.refs_1_, bf16[128,1024]{1,0:T(8,128)(2,1)S(1)} %collective-permute-done.3.refs_2_, bf16[128,1024]{1,0:T(8,128)(2,1)S(1)} %collective-permute-done.5.refs_3_), custom_call_target="tpu_custom_call" | custom-call | tf_op jit(solution)/shard_map/merge/pallas_call | solution.py:369
  84.4 5.4 %all-to-all-done.3.got = bf16[8,16,1024]{2,1,0:T(8,128)(2,1)S(1)} async-done(((bf16[8,16,1024]{2,1,0:T(8,128)(2,1)}), bf16[8,16,1024]{2,1,0:T(8,128)(2,1)S(1)}, u32[]{:S(2)}, u32[]{:S(2)}) %all-to-all-start.3) | async-done | bytes 262176 | tf_op jit(solution)/shard_map/all_to_all | solution.py:362
  89.8 1.4 %place.1 = f32[4,16,1024]{2,1,0:T(8,128)} custom-call(s32[32]{0:T(128)S(1)} %copy-done.1, bf16[8,16,1024]{2,1,0:T(8,128)(2,1)S(1)} %all-to-all-done.3.got), custom_call_target="tpu_custom_call" | custom-call | tf_op jit(solution)/shard_map/place/pallas_call | solution.py:364
  (16 shorter events, 0.0 us)
Async XLA Ops:
  2.3 14.9 %all-to-all-start = ((bf16[8,16,1024]{2,1,0:T(8,128)(2,1)}), bf16[8,16,1024]{2,1,0:T(8,128)(2,1)S(1)}, u32[]{:S(2)}, u32[]{:S(2)}) async-start(bf16[8,16,1024]{2,1,0:T(8,128)(2,1)} %pack.1), calls=%async_computation | async-start | bytes 524288 | tf_op jit(solution)/shard_map/all_to_all | solution.py:334
  10.7 6.6 %copy-start.1 = (s32[32]{0:T(128)S(1)}, s32[32]{0:T(128)}, u32[]{:S(2)}) copy-start(s32[32]{0:T(128)} %slots.5) | copy-start | bytes 388
  10.7 18.7 %collective-permute-start = (bf16[272,1024]{1,0:T(8,128)(2,1)}, bf16[272,1024]{1,0:T(8,128)(2,1)S(1)}, u32[]{:S(2)}, u32[]{:S(2)}) collective-permute-start(bf16[272,1024]{1,0:T(8,128)(2,1)} %get-tuple-element.17), channel_id=1, source_target_pairs={{0,1},{1,0},{2,3},{3,2},{4,5},{5,4},{6,7},{7,6},{8,9},{9,8},{10,11... | collective-permute-start | bytes 1671176 | tf_op jit(solution)/shard_map/ppermute | solution.py:350
  14.5 14.9 %collective-permute-start.1 = (bf16[272,1024]{1,0:T(8,128)(2,1)}, bf16[272,1024]{1,0:T(8,128)(2,1)S(1)}, u32[]{:S(2)}, u32[]{:S(2)}) collective-permute-start(bf16[272,1024]{1,0:T(8,128)(2,1)} %get-tuple-element.18), channel_id=1, source_target_pairs={{0,4},{1,5},{2,6},{3,7},{4,0},{5,1},{6,2},{7,3},{8,12},{9,13},{10,... | collective-permute-start | bytes 1671176 | tf_op jit(solution)/shard_map/ppermute | solution.py:350
  18.7 5.3 %copy-start.3 = (bf16[272,1024]{1,0:T(8,128)(2,1)S(1)}, bf16[272,1024]{1,0:T(8,128)(2,1)}, u32[]{:S(2)}) copy-start(bf16[272,1024]{1,0:T(8,128)(2,1)} %get-tuple-element.22) | copy-start | bytes 1671172
  18.7 14.3 %all-to-all-start.1 = ((bf16[16,4,16,256]{3,2,1,0:T(8,128)(2,1)}), bf16[16,4,16,256]{3,2,1,0:T(8,128)(2,1)S(1)}, u32[]{:S(2)}, u32[]{:S(2)}) async-start(bf16[16,4,16,256]{3,2,1,0:T(8,128)(2,1)} %pick.1), calls=%async_computation.1 | async-start | bytes 1048576 | tf_op jit(solution)/shard_map/all_to_all | solution.py:353
  24.0 24.4 %collective-permute-start.4 = (bf16[272,1024]{1,0:T(8,128)(2,1)S(1)}, bf16[272,1024]{1,0:T(8,128)(2,1)S(1)}, u32[]{:S(2)}, u32[]{:S(2)}) collective-permute-start(bf16[272,1024]{1,0:T(8,128)(2,1)S(1)} %copy-done.3), channel_id=1, source_target_pairs={{0,5},{1,4},{2,7},{3,6},{4,1},{5,0},{6,3},{7,2},{8,13},{9,12},{10,... | collective-permute-start | bytes 1671176 | tf_op jit(solution)/shard_map/ppermute | solution.py:352
  29.4 3.6 %copy-start.4 = (bf16[272,1024]{1,0:T(8,128)(2,1)}, bf16[272,1024]{1,0:T(8,128)(2,1)S(1)}, u32[]{:S(2)}) copy-start(bf16[272,1024]{1,0:T(8,128)(2,1)S(1)} %collective-permute-done.refs_1_) | copy-start | bytes 1671172
  29.4 3.5 %copy-start.5 = (bf16[272,1024]{1,0:T(8,128)(2,1)}, bf16[272,1024]{1,0:T(8,128)(2,1)S(1)}, u32[]{:S(2)}) copy-start(bf16[272,1024]{1,0:T(8,128)(2,1)S(1)} %collective-permute-done.1.refs_2_) | copy-start | bytes 1671172
  33.0 0.8 copy-start.2
  48.4 0.8 copy-start.6
  55.8 4.4 %copy-start.8 = (bf16[128,1024]{1,0:T(8,128)(2,1)S(1)}, bf16[128,1024]{1,0:T(8,128)(2,1)}, u32[]{:S(2)}) copy-start(bf16[128,1024]{1,0:T(8,128)(2,1)} %get-tuple-element.20) | copy-start | bytes 786436
  55.8 7.1 %copy-start.7 = (bf16[128,1024]{1,0:T(8,128)(2,1)S(1)}, bf16[128,1024]{1,0:T(8,128)(2,1)}, u32[]{:S(2)}) copy-start(bf16[128,1024]{1,0:T(8,128)(2,1)} %get-tuple-element.21) | copy-start | bytes 786436
  55.8 9.5 %copy-start.9 = (bf16[128,1024]{1,0:T(8,128)(2,1)S(1)}, bf16[128,1024]{1,0:T(8,128)(2,1)}, u32[]{:S(2)}) copy-start(bf16[128,1024]{1,0:T(8,128)(2,1)} %get-tuple-element.24) | copy-start | bytes 786436
  55.8 13.3 %all-to-all-start.2 = ((bf16[16,4,16,256]{3,2,1,0:T(8,128)(2,1)}), bf16[16,4,16,256]{3,2,1,0:T(8,128)(2,1)S(1)}, u32[]{:S(2)}, u32[]{:S(2)}) async-start(bf16[16,4,16,256]{3,2,1,0:T(8,128)(2,1)} %bitcast.16), calls=%async_computation.2 | async-start | bytes 1048576 | tf_op jit(solution)/shard_map/all_to_all | solution.py:360
  60.2 23.1 %collective-permute-start.2 = (bf16[128,1024]{1,0:T(8,128)(2,1)S(1)}, bf16[128,1024]{1,0:T(8,128)(2,1)S(1)}, u32[]{:S(2)}, u32[]{:S(2)}) collective-permute-start(bf16[128,1024]{1,0:T(8,128)(2,1)S(1)} %copy-done.8), channel_id=1, source_target_pairs={{0,1},{1,0},{2,3},{3,2},{4,5},{5,4},{6,7},{7,6},{8,9},{9,8},{10,11... | collective-permute-start | bytes 786440 | tf_op jit(solution)/shard_map/ppermute | solution.py:357
  62.8 20.4 %collective-permute-start.3 = (bf16[128,1024]{1,0:T(8,128)(2,1)S(1)}, bf16[128,1024]{1,0:T(8,128)(2,1)S(1)}, u32[]{:S(2)}, u32[]{:S(2)}) collective-permute-start(bf16[128,1024]{1,0:T(8,128)(2,1)S(1)} %copy-done.7), channel_id=1, source_target_pairs={{0,4},{1,5},{2,6},{3,7},{4,0},{5,1},{6,2},{7,3},{8,12},{9,13},{10,... | collective-permute-start | bytes 786440 | tf_op jit(solution)/shard_map/ppermute | solution.py:358
  65.2 18.0 %collective-permute-start.5 = (bf16[128,1024]{1,0:T(8,128)(2,1)S(1)}, bf16[128,1024]{1,0:T(8,128)(2,1)S(1)}, u32[]{:S(2)}, u32[]{:S(2)}) collective-permute-start(bf16[128,1024]{1,0:T(8,128)(2,1)S(1)} %copy-done.9), channel_id=1, source_target_pairs={{0,5},{1,4},{2,7},{3,6},{4,1},{5,0},{6,3},{7,2},{8,13},{9,12},{10,... | collective-permute-start | bytes 786440 | tf_op jit(solution)/shard_map/ppermute | solution.py:359
  70.5 12.8 %copy-start = (bf16[128,1024]{1,0:T(8,128)(2,1)S(1)}, bf16[128,1024]{1,0:T(8,128)(2,1)}, u32[]{:S(2)}) copy-start(bf16[128,1024]{1,0:T(8,128)(2,1)} %get-tuple-element.19.refs_0_) | copy-start | bytes 786436
  70.5 19.3 %all-to-all-start.3 = ((bf16[8,16,1024]{2,1,0:T(8,128)(2,1)}), bf16[8,16,1024]{2,1,0:T(8,128)(2,1)S(1)}, u32[]{:S(2)}, u32[]{:S(2)}) async-start(bf16[8,16,1024]{2,1,0:T(8,128)(2,1)} %sum.1), calls=%async_computation.3 | async-start | bytes 524288 | tf_op jit(solution)/shard_map/all_to_all | solution.py:362

commit v10 on v8

--- a/solution.py
+++ b/solution.py
@@ -33,79 +33,69 @@
     return doc, jnp.where(doc % 2 == 0, place, 3 - place)
 
 
-def pack_kernel(docs, slots_any, kv, out, slots, held, sems):
+def prepare_kernel(docs, slots_any, kv, q, d_out, spans_any, *refs):
+    send, pieces, (slots, rows, held, spans, sems) = refs[0], refs[1:BLOCK], refs[BLOCK:]
+    tokens = q.shape[0]
+    width = q.shape[1] // KV_HEADS
+    doc, place = place_in_block()
     fetch_slots = pltpu.make_async_copy(slots_any, slots, sems.at[docs])
-    fetch = pltpu.make_async_copy(kv, held, sems.at[docs + 1])
+    fetch_rows = pltpu.make_async_copy(kv, rows, sems.at[docs + 1])
+    fetch_spans = pltpu.make_async_copy(spans_any, spans, sems.at[docs + 2])
     fetch_slots.start()
-    fetch.start()
+    fetch_rows.start()
+    fetch_spans.start()
+    at = docs + 3
+    fetches = []
+    for k in range(1, BLOCK):
+        columns = pl.ds(pl.multiple_of((place ^ k) * width, WIDTH), width)
+        pair = [
+            pltpu.make_async_copy(q.at[:, columns], held.at[k - 1, :tokens], sems.at[at]),
+            pltpu.make_async_copy(
+                d_out.at[:, columns], held.at[k - 1, tokens : 2 * tokens], sems.at[at + 1]
+            ),
+        ]
+        for copy in pair:
+            copy.start()
+        fetches.append(pair)
+        at += 2
     fetch_slots.wait()
-    doc, _ = place_in_block()
     copies = []
     for d in range(docs):
         local = 0
         for j in range(IMAGES):
             s = slots[d * IMAGES + j]
             local += jnp.where(s // IMAGES == doc, s % IMAGES, 0)
-        copies.append(pltpu.make_async_copy(held.at[local], out.at[d], sems.at[d]))
-    fetch.wait()
+        copies.append(pltpu.make_async_copy(rows.at[local], send.at[d], sems.at[d]))
+    fetch_rows.wait()
     for copy in copies:
         copy.start()
+    fetch_spans.wait()
+    for k in range(1, BLOCK):
+        held[k - 1, 2 * tokens :] = jnp.zeros_like(held[k - 1, 2 * tokens :])
+        held[k - 1, 2 * tokens : 2 * tokens + 2, :tokens] = spans[...].astype(jnp.bfloat16)
+    for k, pair in zip(range(1, BLOCK), fetches):
+        for copy in pair:
+            copy.wait()
+        copies.append(pltpu.make_async_copy(held.at[k - 1], pieces[k - 1], sems.at[at]))
+        copies[-1].start()
+        at += 1
     for copy in copies:
         copy.wait()
 
 
-def pick_kernel(slots, got, out):
+def pick_kernel(slots, got, out, heads):
     doc, _ = place_in_block()
     for j in range(IMAGES):
-        rows = got[slots[doc * IMAGES + j] // IMAGES]
-        heads = [
-            jnp.concatenate(
-                [
-                    rows[:, c * WIDTH : (c + 1) * WIDTH],
-                    rows[:, KEY_COLUMNS + c * WIDTH : KEY_COLUMNS + (c + 1) * WIDTH],
-                ],
-                axis=1,
-            )
-            for c in range(KV_HEADS)
-        ]
-        for y in range(GRID):
-            for z in range(GRID):
-                place = y % 2 * 2 + z % 2
-                out[y * GRID + z, j] = jnp.where(doc % 2 == 0, heads[place], heads[3 - place])
-
-
-def payload_kernel(q, d_out, spans_any, *refs):
-    outs, held, spans, sems = refs[:BLOCK], refs[BLOCK], refs[BLOCK + 1], refs[BLOCK + 2]
-    tokens = q.shape[0]
-    width = q.shape[1] // KV_HEADS
-    _, place = place_in_block()
-    order = [3, 1, 2, 0]
-    fetch_spans = pltpu.make_async_copy(spans_any, spans, sems.at[3 * BLOCK])
-    fetch_spans.start()
-    fetches = []
-    for k in order:
-        columns = pl.ds(pl.multiple_of((place ^ k) * width, WIDTH), width)
-        pair = [
-            pltpu.make_async_copy(q.at[:, columns], held.at[k, :tokens], sems.at[3 * k]),
-            pltpu.make_async_copy(
-                d_out.at[:, columns], held.at[k, tokens : 2 * tokens], sems.at[3 * k + 1]
-            ),
-        ]
-        for copy in pair:
-            copy.start()
-        fetches.append(pair)
-    fetch_spans.wait()
-    for k in order:
-        held[k, 2 * tokens :] = jnp.zeros_like(held[k, 2 * tokens :])
-        held[k, 2 * tokens : 2 * tokens + 2, :tokens] = spans[...].astype(jnp.bfloat16)
-    copies = []
-    for k, pair in zip(order, fetches):
-        for copy in pair:
-            copy.wait()
-        copies.append(pltpu.make_async_copy(held.at[k], outs[k], sems.at[3 * k + 2]))
-        copies[-1].start()
-    for copy in copies:
-        copy.wait()
+        owner = slots[doc * IMAGES + j] // IMAGES
+        for c in range(KV_HEADS):
+            columns = slice(c * WIDTH, (c + 1) * WIDTH)
+            heads[c, j, :, :WIDTH] = got[owner, :, columns]
+            columns = slice(KEY_COLUMNS + c * WIDTH, KEY_COLUMNS + (c + 1) * WIDTH)
+            heads[c, j, :, WIDTH:] = got[owner, :, columns]
+    for y in range(GRID):
+        for z in range(GRID):
+            place = y % 2 * 2 + z % 2
+            out[y * GRID + z] = heads[jnp.where(doc % 2 == 0, place, 3 - place)]
 
 
 def merge_kernel(*refs):
@@ -150,31 +140,42 @@
     return low_probs, d_scores
 
 
-def grad_kernel(count, first, last, gate, kv_any, *refs):
-    pieces, refs = refs[:count], refs[count:]
-    so_far, refs = (None, refs) if first else (refs[0], refs[1:])
-    dqs, dkv_any, refs = refs[:count], refs[count], refs[count + 1 :]
-    kv, held, dq, dkv, keys_t, probs, d_scores, q_rows, d_rows, acc, sems = refs
+def grad_kernel(gate, kv_any, q, d_out, spans_any, *refs):
+    pieces, dqs, dkv_any, refs = refs[: BLOCK - 1], refs[BLOCK - 1 : 2 * BLOCK - 1], refs[2 * BLOCK - 1], refs[2 * BLOCK :]
+    kv, held, own_spans, dq, dkv, keys_t, probs, d_scores, q_rows, d_rows, acc, sems = refs
     tokens = dqs[0].shape[0]
+    width = dqs[0].shape[1]
     block = BATCH_HEADS * tokens
-    fetch_kv = pltpu.make_async_copy(kv_any, kv, sems.at[2 * count])
+    _, place = place_in_block()
+    fetch_kv = pltpu.make_async_copy(kv_any, kv, sems.at[2 * BLOCK])
     fetch_kv.start()
-    for k in range(count):
-        pltpu.make_async_copy(pieces[k], held.at[k], sems.at[k]).start()
-    if not first:
-        fetch_sums = pltpu.make_async_copy(so_far, acc, sems.at[2 * count + 1])
-        fetch_sums.start()
+    columns = pl.ds(pl.multiple_of(place * width, WIDTH), width)
+    fetch_own = [
+        pltpu.make_async_copy(q.at[:, columns], held.at[0, :tokens], sems.at[0]),
+        pltpu.make_async_copy(
+            d_out.at[:, columns], held.at[0, tokens : 2 * tokens], sems.at[2 * BLOCK + 1]
+        ),
+        pltpu.make_async_copy(spans_any, own_spans, sems.at[2 * BLOCK + 2]),
+    ]
+    for copy in fetch_own:
+        copy.start()
+    for k in range(1, BLOCK):
+        pltpu.make_async_copy(pieces[k - 1], held.at[k], sems.at[k]).start()
+    acc[...] = jnp.zeros_like(acc)
     fetch_kv.wait()
     keys_t[...] = kv[:, :WIDTH].T
-    if first:
-        acc[...] = jnp.zeros_like(acc)
-    else:
-        fetch_sums.wait()
+    for copy in fetch_own:
+        copy.wait()
+    held[0, 2 * tokens :] = jnp.zeros_like(held[0, 2 * tokens :])
+    held[0, 2 * tokens : 2 * tokens + 2, :tokens] = own_spans[...].astype(jnp.bfloat16)
     factor = jnp.tanh(gate[...])
     transposed = (((1,), (1,)), ((), ()))
 
     def work(step, carry):
-        pltpu.make_async_copy(pieces[0], held.at[step], sems.at[step]).wait()
+        @pl.when(step > 0)
+        def _():
+            pltpu.make_async_copy(pieces[0], held.at[step], sems.at[step]).wait()
+
         for h in range(GROUP):
             rows, columns = slice(h * tokens, (h + 1) * tokens), slice(h * WIDTH, (h + 1) * WIDTH)
             q_rows[rows] = held[step, :tokens, columns]
@@ -199,44 +200,41 @@
         dq_rows = dq_t.T.astype(jnp.bfloat16)
         for h in range(GROUP):
             dq[step, :, h * WIDTH : (h + 1) * WIDTH] = dq_rows[h * tokens : (h + 1) * tokens]
-        for k in range(count):
+        for k in range(BLOCK):
 
             @pl.when(step == k)
             def _():
-                pltpu.make_async_copy(dq.at[k], dqs[k], sems.at[count + k]).start()
+                pltpu.make_async_copy(dq.at[k], dqs[k], sems.at[BLOCK + k]).start()
 
         return carry
 
-    lax.fori_loop(0, count, work, 0)
-    if last:
-        dkv[:, :WIDTH] = (acc[:, :WIDTH] * SCALE).astype(jnp.bfloat16)
-        dkv[:, WIDTH:] = acc[:, WIDTH:].astype(jnp.bfloat16)
-    give = pltpu.make_async_copy(dkv if last else acc, dkv_any, sems.at[2 * count])
+    lax.fori_loop(0, BLOCK, work, 0)
+    dkv[:, :WIDTH] = (acc[:, :WIDTH] * SCALE).astype(jnp.bfloat16)
+    dkv[:, WIDTH:] = acc[:, WIDTH:].astype(jnp.bfloat16)
+    give = pltpu.make_async_copy(dkv, dkv_any, sems.at[2 * BLOCK])
     give.start()
-    for k in range(count):
-        pltpu.make_async_copy(dq.at[k], dqs[k], sems.at[count + k]).wait()
+    for k in range(BLOCK):
+        pltpu.make_async_copy(dq.at[k], dqs[k], sems.at[BLOCK + k]).wait()
     give.wait()
 
 
-def gradients(gate, kv, pieces, so_far=None, last=True):
+def gradients(gate, kv, q, d_out, spans, pieces):
     key_rows = kv.shape[0]
-    count = len(pieces)
-    first = so_far is None
-    tokens = (pieces[0].shape[0] - PAD) // 2
+    tokens = q.shape[0]
     width = pieces[0].shape[1]
     rows = GROUP * tokens
     in_hbm = pl.BlockSpec(memory_space=HBM)
-    operands = list(pieces) + ([] if first else [so_far])
     return pl.pallas_call(
-        functools.partial(grad_kernel, count, first, last),
-        in_specs=[pl.BlockSpec(memory_space=VMEM)] + [in_hbm] * (len(operands) + 1),
-        out_specs=[in_hbm] * (count + 1),
-        out_shape=[jax.ShapeDtypeStruct((tokens, width), jnp.bfloat16)] * count
-        + [jax.ShapeDtypeStruct(kv.shape, jnp.bfloat16 if last else jnp.float32)],
+        grad_kernel,
+        in_specs=[pl.BlockSpec(memory_space=VMEM)] + [in_hbm] * (BLOCK + 3),
+        out_specs=[in_hbm] * (BLOCK + 1),
+        out_shape=[jax.ShapeDtypeStruct((tokens, width), jnp.bfloat16)] * BLOCK
+        + [jax.ShapeDtypeStruct(kv.shape, jnp.bfloat16)],
         scratch_shapes=[
             pltpu.VMEM(kv.shape, jnp.bfloat16),
-            pltpu.VMEM((count,) + pieces[0].shape, jnp.bfloat16),
-            pltpu.VMEM((count, tokens, width), jnp.bfloat16),
+            pltpu.VMEM((BLOCK,) + pieces[0].shape, jnp.bfloat16),
+            pltpu.VMEM(spans.shape, jnp.int32),
+            pltpu.VMEM((BLOCK, tokens, width), jnp.bfloat16),
             pltpu.VMEM(kv.shape, jnp.bfloat16),
             pltpu.VMEM((WIDTH, key_rows), jnp.bfloat16),
             pltpu.VMEM((key_rows, rows), jnp.bfloat16),
@@ -244,16 +242,16 @@
             pltpu.VMEM((rows, WIDTH), jnp.bfloat16),
             pltpu.VMEM((rows, WIDTH), jnp.bfloat16),
             pltpu.VMEM(kv.shape, jnp.float32),
-            pltpu.SemaphoreType.DMA((2 * count + 2,)),
+            pltpu.SemaphoreType.DMA((2 * BLOCK + 3,)),
         ],
         compiler_params=pltpu.CompilerParams(vmem_limit_bytes=GRADIENT_VMEM),
         cost_estimate=pl.CostEstimate(
-            flops=10 * count * rows * key_rows * WIDTH,
+            flops=10 * BLOCK * rows * key_rows * WIDTH,
             bytes_accessed=4 * 1024 * 1024,
-            transcendentals=count * rows * key_rows,
+            transcendentals=BLOCK * rows * key_rows,
         ),
         name="gradients",
-    )(gate, kv, *operands)
+    )(gate, kv, q, d_out, spans, *pieces)
 
 
 def sum_kernel(slots, got, out):
@@ -284,7 +282,7 @@
         out[s] = got[doc].astype(jnp.float32)
 
 
-def small(kernel, out_shape, name):
+def small(kernel, out_shape, name, scratch=()):
     return pl.pallas_call(
         kernel,
         in_specs=[
@@ -293,6 +291,7 @@
         ],
         out_specs=pl.BlockSpec(memory_space=VMEM),
         out_shape=out_shape,
+        scratch_shapes=scratch,
         compiler_params=pltpu.CompilerParams(vmem_limit_bytes=VMEM_LIMIT),
         name=name,
     )
@@ -319,36 +318,35 @@
     in_vmem = pl.BlockSpec(memory_space=VMEM)
     params = pltpu.CompilerParams(vmem_limit_bytes=VMEM_LIMIT)
     block = jax.ShapeDtypeStruct((docs, rows, columns), jnp.bfloat16)
-    send = pl.pallas_call(
-        functools.partial(pack_kernel, docs),
-        in_specs=[in_hbm, in_hbm],
-        out_specs=in_hbm,
-        out_shape=block,
+    span_rows = spans[0].T
+    piece = jax.ShapeDtypeStruct((2 * tokens + PAD, width), jnp.bfloat16)
+    send, *pieces = pl.pallas_call(
+        functools.partial(prepare_kernel, docs),
+        in_specs=[in_hbm] * 5,
+        out_specs=[in_hbm] * BLOCK,
+        out_shape=[block] + [piece] * (BLOCK - 1),
         scratch_shapes=[
             pltpu.SMEM(image_slots.shape, jnp.int32),
             pltpu.VMEM(image_kv.shape, jnp.bfloat16),
-            pltpu.SemaphoreType.DMA((docs + 2,)),
+            pltpu.VMEM((BLOCK - 1,) + piece.shape, jnp.bfloat16),
+            pltpu.VMEM(span_rows.shape, jnp.int32),
+            pltpu.SemaphoreType.DMA((docs + 3 * BLOCK,)),
         ],
-        name="pack",
-    )(image_slots, image_kv)
+        name="prepare",
+    )(image_slots, image_kv, queries[0], d_out[0], span_rows)
     got = lax.all_to_all(send, "doc", 0, 0)
-    pieces = pl.pallas_call(
-        payload_kernel,
-        in_specs=[in_hbm, in_hbm, in_hbm],
-        out_specs=[in_hbm] * BLOCK,
-        out_shape=[jax.ShapeDtypeStruct((2 * tokens + PAD, width), jnp.bfloat16)] * BLOCK,
-        scratch_shapes=[
-            pltpu.VMEM((BLOCK, 2 * tokens + PAD, width), jnp.bfloat16),
-            pltpu.VMEM((2, tokens), jnp.int32),
-            pltpu.SemaphoreType.DMA((3 * BLOCK + 1,)),
-        ],
-        name="payload",
-    )(queries[0], d_out[0], spans[0].T)
     one_head = jax.ShapeDtypeStruct((texts, images, rows, 2 * WIDTH), jnp.bfloat16)
-    send = small(pick_kernel, one_head, "pick")(image_slots, got)
-    pieces = [pieces[0]] + [lax.ppermute(pieces[k], both, swap(docs, k)) for k in range(1, BLOCK)]
+    send = small(
+        pick_kernel,
+        one_head,
+        "pick",
+        [pltpu.VMEM((KV_HEADS, images, rows, 2 * WIDTH), jnp.bfloat16)],
+    )(image_slots, got)
+    pieces = [lax.ppermute(pieces[k - 1], both, swap(docs, k)) for k in range(1, BLOCK)]
     kv = lax.all_to_all(send, "ctx", 0, 0).reshape(texts * images * rows, 2 * WIDTH)
-    *dqs, dkv = gradients(attn_gate.reshape(1, 1), kv, pieces)
+    *dqs, dkv = gradients(
+        attn_gate.reshape(1, 1), kv, queries[0], d_out[0], span_rows, pieces
+    )
     dqs = [dqs[0]] + [lax.ppermute(dqs[k], both, swap(docs, k)) for k in range(1, BLOCK)]
     parts = lax.all_to_all(dkv.reshape(texts, images, rows, 2 * WIDTH), "ctx", 0, 0)
     send = small(sum_kernel, block, "sum")(image_slots, parts)

time: 89.3 us -> 86.8 us (0.972)
  waiting for transfers between devices: 22.2 us -> 19.1 us
  starting transfers between devices: 36.2 us -> 38.5 us
  Pallas kernels: 28 us -> 26.4 us
    ppermute x3, waiting for transfers between devices: 9.15 us -> 7.01 us  [shards(): lax.ppermute(pieces[k - 1], both, swap(docs, k))]
    pallas_call x4 -> x3, Pallas kernels: 24.2 us -> 22.5 us  [the longest x1 18.6 us: gradients(): pl.pallas_call(grad_kernel, in_specs=[pl.BlockSpec(memory_space=VMEM)] +...]
    all_to_all x1, starting transfers between devices: 6.16 us -> 7.77 us  [shards(): lax.all_to_all(send, 'ctx', 0, 0).reshape(texts * images * rows, 2 * WIDTH)]
    all_to_all x1, waiting for transfers between devices: 6.2 us -> 5.21 us  [shards(): lax.all_to_all(dkv.reshape(texts, images, rows, 2 * WIDTH), 'ctx', 0, 0)]
  transfers between devices with their start and end apart: 10 -> 10, of which waited for: 4 -> 4; matrix products, arithmetic and copies ran while one was open for 0% -> 0% of each run, Pallas kernels for 7% -> 4%
where the time goes in v10:
time: 86.8 us; the launch traced here: 86.2 us
  starting transfers between devices  38.5 us (44%)
  Pallas kernels  26.4 us (30%)
  waiting for transfers between devices  19.1 us (22%)
  between operations  1.41 us (2%)
    pallas_call x1, Pallas kernels, gradients(): pl.pallas_call(grad_kernel, in_specs=[pl.BlockSpec(memory_space=VMEM)] +...  18.6 us
    all_to_all x2, starting transfers between devices, shards(): got = lax.all_to_all(send, 'doc', 0, 0)  12.4 us
    all_to_all x1, starting transfers between devices, shards(): lax.all_to_all(send, 'ctx', 0, 0).reshape(texts * images * rows, 2 * WIDTH)  7.77 us
    ppermute x3, waiting for transfers between devices, shards(): lax.ppermute(pieces[k - 1], both, swap(docs, k))  7.01 us
    all_to_all x1, starting transfers between devices, shards(): lax.all_to_all(dkv.reshape(texts, images, rows, 2 * WIDTH), 'ctx', 0, 0)  6.65 us
    ppermute x3, starting transfers between devices, shards(): lax.ppermute(pieces[k - 1], both, swap(docs, k))  6.49 us
    all_to_all x2, waiting for transfers between devices, shards(): got = lax.all_to_all(send, 'doc', 0, 0)  5.41 us
    all_to_all x1, waiting for transfers between devices, shards(): lax.all_to_all(dkv.reshape(texts, images, rows, 2 * WIDTH), 'ctx', 0, 0)  5.21 us
  transfers between devices with their start and end apart: 10, of which 4 were waited for; matrix products, arithmetic and copies ran while one was open for 0% of the time, Pallas kernels for 4%

profile of v10, /device:TPU:1, one launch (start us, length us, event | category | flops | bytes accessed | tf_op | source)
XLA Modules:
  0.0 86.2 jit_solution(8706962083398082093)
XLA Ops:
  0.6 2.5 %prepare.1 = (bf16[8,16,1024]{2,1,0:T(8,128)(2,1)}, bf16[272,1024]{1,0:T(8,128)(2,1)}, bf16[272,1024]{1,0:T(8,128)(2,1)}, bf16[272,1024]{1,0:T(8,128)(2,1)}) custom-call(s32[32]{0:T(128)} %slots.5, bf16[4,16,1024]{2,1,0:T(8,128)(2,1)} %kv.1, bf16[128,4096]{1,0:T(8,128)(2,1)} %bitcast.10, bf16[128,4096]{1,0:T(8,128)(2,1)} %bitcast.12, s32[2,128]{1,0:T(2,128)} %bitcast.17), custom_call_target="tpu_custom_call" | custom-call | tf_op jit(solution)/shard_map/prepare/pallas_call | solution.py:323
  3.1 5.8 %all-to-all-start = ((bf16[8,16,1024]{2,1,0:T(8,128)(2,1)}), bf16[8,16,1024]{2,1,0:T(8,128)(2,1)S(1)}, u32[]{:S(2)}, u32[]{:S(2)}) async-start(bf16[8,16,1024]{2,1,0:T(8,128)(2,1)} %get-tuple-element.11), calls=%async_computation | async-start | bytes 524288 | tf_op jit(solution)/shard_map/all_to_all | solution.py:337
  9.0 3.8 %collective-permute-start = (bf16[272,1024]{1,0:T(8,128)(2,1)}, bf16[272,1024]{1,0:T(8,128)(2,1)S(1)}, u32[]{:S(2)}, u32[]{:S(2)}) collective-permute-start(bf16[272,1024]{1,0:T(8,128)(2,1)} %get-tuple-element.12), channel_id=1, source_target_pairs={{0,1},{1,0},{2,3},{3,2},{4,5},{5,4},{6,7},{7,6},{8,9},{9,8},{10,11... | collective-permute-start | bytes 1671176 | tf_op jit(solution)/shard_map/ppermute | solution.py:345
  12.7 2.7 %collective-permute-start.1 = (bf16[272,1024]{1,0:T(8,128)(2,1)}, bf16[272,1024]{1,0:T(8,128)(2,1)S(1)}, u32[]{:S(2)}, u32[]{:S(2)}) collective-permute-start(bf16[272,1024]{1,0:T(8,128)(2,1)} %get-tuple-element.13), channel_id=1, source_target_pairs={{0,4},{1,5},{2,6},{3,7},{4,0},{5,1},{6,2},{7,3},{8,12},{9,13},{10,... | collective-permute-start | bytes 1671176 | tf_op jit(solution)/shard_map/ppermute | solution.py:345
  15.4 0.0 collective-permute-start.2
  15.5 0.0 all-to-all-done.got
  15.5 1.4 %pick.1 = bf16[16,4,16,256]{3,2,1,0:T(8,128)(2,1)} custom-call(s32[32]{0:T(128)S(1)} %copy-done.1, bf16[8,16,1024]{2,1,0:T(8,128)(2,1)S(1)} %all-to-all-done.got), custom_call_target="tpu_custom_call" | custom-call | tf_op jit(solution)/shard_map/pick/pallas_call | solution.py:339
  16.9 7.8 %all-to-all-start.1 = ((bf16[16,4,16,256]{3,2,1,0:T(8,128)(2,1)}), bf16[16,4,16,256]{3,2,1,0:T(8,128)(2,1)S(1)}, u32[]{:S(2)}, u32[]{:S(2)}) async-start(bf16[16,4,16,256]{3,2,1,0:T(8,128)(2,1)} %pick.1), calls=%async_computation.1 | async-start | bytes 1048576 | tf_op jit(solution)/shard_map/all_to_all | solution.py:346
  25.3 0.0 collective-permute-done.refs_0_
  25.3 0.0 copy-start.3
  25.3 0.0 collective-permute-done.1.refs_1_
  25.4 7.0 %collective-permute-done.2.refs_2_ = bf16[272,1024]{1,0:T(8,128)(2,1)S(1)} collective-permute-done((bf16[272,1024]{1,0:T(8,128)(2,1)}, bf16[272,1024]{1,0:T(8,128)(2,1)S(1)}, u32[]{:S(2)}, u32[]{:S(2)}) %collective-permute-start.2) | collective-permute-done | bytes 557088 | tf_op jit(solution)/shard_map/ppermute | solution.py:345
  32.4 1.5 %all-to-all-done.1 = bf16[16,4,16,256]{3,2,1,0:T(8,128)(2,1)S(1)} async-done(((bf16[16,4,16,256]{3,2,1,0:T(8,128)(2,1)}), bf16[16,4,16,256]{3,2,1,0:T(8,128)(2,1)S(1)}, u32[]{:S(2)}, u32[]{:S(2)}) %all-to-all-start.1) | async-done | bytes 524320 | tf_op jit(solution)/shard_map/all_to_all | solution.py:346
  33.8 0.0 copy-done.5
  33.8 0.8 copy-done.2
  34.6 18.6 %gradients.1 = (bf16[128,1024]{1,0:T(8,128)(2,1)}, bf16[128,1024]{1,0:T(8,128)(2,1)}, bf16[128,1024]{1,0:T(8,128)(2,1)}, bf16[128,1024]{1,0:T(8,128)(2,1)}, bf16[1024,256]{1,0:T(8,128)(2,1)}) custom-call(f32[1,1]{1,0:T(1,128)} %bitcast.9.gate, bf16[1024,256]{1,0:T(8,128)(2,1)} %bitcast.15, bf16[128,4096]{1,0:T(8,128)(2,1)} %bitcast.11, ...), custom_call_target="tpu_custom_call" | custom-call | flops 5368709120 | bytes 4194304 | tf_op jit(solution)/shard_map/gradients/pallas_call | solution.py:227
  53.2 0.0 copy-start.8
  53.2 0.0 copy-start.7
  53.2 0.0 copy-start.6
  53.3 6.6 %all-to-all-start.2 = ((bf16[16,4,16,256]{3,2,1,0:T(8,128)(2,1)}), bf16[16,4,16,256]{3,2,1,0:T(8,128)(2,1)S(1)}, u32[]{:S(2)}, u32[]{:S(2)}) async-start(bf16[16,4,16,256]{3,2,1,0:T(8,128)(2,1)} %bitcast.16), calls=%async_computation.2 | async-start | bytes 1048576 | tf_op jit(solution)/shard_map/all_to_all | solution.py:351
  59.9 2.7 %collective-permute-start.3 = (bf16[128,1024]{1,0:T(8,128)(2,1)S(1)}, bf16[128,1024]{1,0:T(8,128)(2,1)S(1)}, u32[]{:S(2)}, u32[]{:S(2)}) collective-permute-start(bf16[128,1024]{1,0:T(8,128)(2,1)S(1)} %copy-done.8), channel_id=1, source_target_pairs={{0,1},{1,0},{2,3},{3,2},{4,5},{5,4},{6,7},{7,6},{8,9},{9,8},{10,11... | collective-permute-start | bytes 786440 | tf_op jit(solution)/shard_map/ppermute | solution.py:350
  62.6 2.4 %collective-permute-start.4 = (bf16[128,1024]{1,0:T(8,128)(2,1)S(1)}, bf16[128,1024]{1,0:T(8,128)(2,1)S(1)}, u32[]{:S(2)}, u32[]{:S(2)}) collective-permute-start(bf16[128,1024]{1,0:T(8,128)(2,1)S(1)} %copy-done.7), channel_id=1, source_target_pairs={{0,4},{1,5},{2,6},{3,7},{4,0},{5,1},{6,2},{7,3},{8,12},{9,13},{10,... | collective-permute-start | bytes 786440 | tf_op jit(solution)/shard_map/ppermute | solution.py:350
  65.0 0.1 collective-permute-start.5
  65.1 5.2 %all-to-all-done.2.got = bf16[16,4,16,256]{3,2,1,0:T(8,128)(2,1)S(1)} async-done(((bf16[16,4,16,256]{3,2,1,0:T(8,128)(2,1)}), bf16[16,4,16,256]{3,2,1,0:T(8,128)(2,1)S(1)}, u32[]{:S(2)}, u32[]{:S(2)}) %all-to-all-start.2) | async-done | bytes 524320 | tf_op jit(solution)/shard_map/all_to_all | solution.py:351
  70.3 1.3 %sum.1 = bf16[8,16,1024]{2,1,0:T(8,128)(2,1)} custom-call(s32[32]{0:T(128)S(1)} %copy-done.1, bf16[16,4,16,256]{3,2,1,0:T(8,128)(2,1)S(1)} %all-to-all-done.2.got), custom_call_target="tpu_custom_call" | custom-call | tf_op jit(solution)/shard_map/sum/pallas_call | solution.py:352
  71.6 6.6 %all-to-all-start.3 = ((bf16[8,16,1024]{2,1,0:T(8,128)(2,1)}), bf16[8,16,1024]{2,1,0:T(8,128)(2,1)S(1)}, u32[]{:S(2)}, u32[]{:S(2)}) async-start(bf16[8,16,1024]{2,1,0:T(8,128)(2,1)} %sum.1), calls=%async_computation.3 | async-start | bytes 524288 | tf_op jit(solution)/shard_map/all_to_all | solution.py:353
  78.3 0.0 collective-permute-done.3.refs_1_
  78.3 0.0 collective-permute-done.4.refs_2_
  78.3 0.0 collective-permute-done.5.refs_3_
  78.3 1.1 %merge.1 = bf16[128,4096]{1,0:T(8,128)(2,1)} custom-call(bf16[128,1024]{1,0:T(8,128)(2,1)S(1)} %copy-done, bf16[128,1024]{1,0:T(8,128)(2,1)S(1)} %collective-permute-done.3.refs_1_, bf16[128,1024]{1,0:T(8,128)(2,1)S(1)} %collective-permute-done.4.refs_2_, bf16[128,1024]{1,0:T(8,128)(2,1)S(1)} %collective-permute-done.5.refs_3_), custom_call_target="tpu_custom_call" | custom-call | tf_op jit(solution)/shard_map/merge/pallas_call | solution.py:359
  79.4 5.4 %all-to-all-done.3.got = bf16[8,16,1024]{2,1,0:T(8,128)(2,1)S(1)} async-done(((bf16[8,16,1024]{2,1,0:T(8,128)(2,1)}), bf16[8,16,1024]{2,1,0:T(8,128)(2,1)S(1)}, u32[]{:S(2)}, u32[]{:S(2)}) %all-to-all-start.3) | async-done | bytes 262176 | tf_op jit(solution)/shard_map/all_to_all | solution.py:353
  84.8 1.4 %place.1 = f32[4,16,1024]{2,1,0:T(8,128)} custom-call(s32[32]{0:T(128)S(1)} %copy-done.1, bf16[8,16,1024]{2,1,0:T(8,128)(2,1)S(1)} %all-to-all-done.3.got), custom_call_target="tpu_custom_call" | custom-call | tf_op jit(solution)/shard_map/place/pallas_call | solution.py:354
  (12 shorter events, 0.0 us)
Async XLA Ops:
  3.1 12.3 %all-to-all-start = ((bf16[8,16,1024]{2,1,0:T(8,128)(2,1)}), bf16[8,16,1024]{2,1,0:T(8,128)(2,1)S(1)}, u32[]{:S(2)}, u32[]{:S(2)}) async-start(bf16[8,16,1024]{2,1,0:T(8,128)(2,1)} %get-tuple-element.11), calls=%async_computation | async-start | bytes 524288 | tf_op jit(solution)/shard_map/all_to_all | solution.py:337
  9.0 16.4 %collective-permute-start = (bf16[272,1024]{1,0:T(8,128)(2,1)}, bf16[272,1024]{1,0:T(8,128)(2,1)S(1)}, u32[]{:S(2)}, u32[]{:S(2)}) collective-permute-start(bf16[272,1024]{1,0:T(8,128)(2,1)} %get-tuple-element.12), channel_id=1, source_target_pairs={{0,1},{1,0},{2,3},{3,2},{4,5},{5,4},{6,7},{7,6},{8,9},{9,8},{10,11... | collective-permute-start | bytes 1671176 | tf_op jit(solution)/shard_map/ppermute | solution.py:345
  12.7 2.7 %copy-start.1 = (s32[32]{0:T(128)S(1)}, s32[32]{0:T(128)}, u32[]{:S(2)}) copy-start(s32[32]{0:T(128)} %slots.5) | copy-start | bytes 388
  12.7 12.6 %collective-permute-start.1 = (bf16[272,1024]{1,0:T(8,128)(2,1)}, bf16[272,1024]{1,0:T(8,128)(2,1)S(1)}, u32[]{:S(2)}, u32[]{:S(2)}) collective-permute-start(bf16[272,1024]{1,0:T(8,128)(2,1)} %get-tuple-element.13), channel_id=1, source_target_pairs={{0,4},{1,5},{2,6},{3,7},{4,0},{5,1},{6,2},{7,3},{8,12},{9,13},{10,... | collective-permute-start | bytes 1671176 | tf_op jit(solution)/shard_map/ppermute | solution.py:345
  15.4 16.9 %collective-permute-start.2 = (bf16[272,1024]{1,0:T(8,128)(2,1)}, bf16[272,1024]{1,0:T(8,128)(2,1)S(1)}, u32[]{:S(2)}, u32[]{:S(2)}) collective-permute-start(bf16[272,1024]{1,0:T(8,128)(2,1)} %get-tuple-element.14), channel_id=1, source_target_pairs={{0,5},{1,4},{2,7},{3,6},{4,1},{5,0},{6,3},{7,2},{8,13},{9,12},{10,... | collective-permute-start | bytes 1671176 | tf_op jit(solution)/shard_map/ppermute | solution.py:345
  16.9 16.9 %all-to-all-start.1 = ((bf16[16,4,16,256]{3,2,1,0:T(8,128)(2,1)}), bf16[16,4,16,256]{3,2,1,0:T(8,128)(2,1)S(1)}, u32[]{:S(2)}, u32[]{:S(2)}) async-start(bf16[16,4,16,256]{3,2,1,0:T(8,128)(2,1)} %pick.1), calls=%async_computation.1 | async-start | bytes 1048576 | tf_op jit(solution)/shard_map/all_to_all | solution.py:346
  25.3 8.5 %copy-start.3 = (bf16[272,1024]{1,0:T(8,128)(2,1)}, bf16[272,1024]{1,0:T(8,128)(2,1)S(1)}, u32[]{:S(2)}) copy-start(bf16[272,1024]{1,0:T(8,128)(2,1)S(1)} %collective-permute-done.refs_0_) | copy-start | bytes 1671172
  25.3 8.5 %copy-start.4 = (bf16[272,1024]{1,0:T(8,128)(2,1)}, bf16[272,1024]{1,0:T(8,128)(2,1)S(1)}, u32[]{:S(2)}) copy-start(bf16[272,1024]{1,0:T(8,128)(2,1)S(1)} %collective-permute-done.1.refs_1_) | copy-start | bytes 1671172
  32.4 1.5 %copy-start.5 = (bf16[272,1024]{1,0:T(8,128)(2,1)}, bf16[272,1024]{1,0:T(8,128)(2,1)S(1)}, u32[]{:S(2)}) copy-start(bf16[272,1024]{1,0:T(8,128)(2,1)S(1)} %collective-permute-done.2.refs_2_) | copy-start | bytes 1671172
  33.8 0.8 copy-start.2
  53.2 6.7 %copy-start.8 = (bf16[128,1024]{1,0:T(8,128)(2,1)S(1)}, bf16[128,1024]{1,0:T(8,128)(2,1)}, u32[]{:S(2)}) copy-start(bf16[128,1024]{1,0:T(8,128)(2,1)} %get-tuple-element.16) | copy-start | bytes 786436
  53.2 9.3 %copy-start.7 = (bf16[128,1024]{1,0:T(8,128)(2,1)S(1)}, bf16[128,1024]{1,0:T(8,128)(2,1)}, u32[]{:S(2)}) copy-start(bf16[128,1024]{1,0:T(8,128)(2,1)} %get-tuple-element.17) | copy-start | bytes 786436
  53.2 11.7 %copy-start.6 = (bf16[128,1024]{1,0:T(8,128)(2,1)S(1)}, bf16[128,1024]{1,0:T(8,128)(2,1)}, u32[]{:S(2)}) copy-start(bf16[128,1024]{1,0:T(8,128)(2,1)} %get-tuple-element.18) | copy-start | bytes 786436
  53.3 17.0 %all-to-all-start.2 = ((bf16[16,4,16,256]{3,2,1,0:T(8,128)(2,1)}), bf16[16,4,16,256]{3,2,1,0:T(8,128)(2,1)S(1)}, u32[]{:S(2)}, u32[]{:S(2)}) async-start(bf16[16,4,16,256]{3,2,1,0:T(8,128)(2,1)} %bitcast.16), calls=%async_computation.2 | async-start | bytes 1048576 | tf_op jit(solution)/shard_map/all_to_all | solution.py:351
  59.9 18.3 %collective-permute-start.3 = (bf16[128,1024]{1,0:T(8,128)(2,1)S(1)}, bf16[128,1024]{1,0:T(8,128)(2,1)S(1)}, u32[]{:S(2)}, u32[]{:S(2)}) collective-permute-start(bf16[128,1024]{1,0:T(8,128)(2,1)S(1)} %copy-done.8), channel_id=1, source_target_pairs={{0,1},{1,0},{2,3},{3,2},{4,5},{5,4},{6,7},{7,6},{8,9},{9,8},{10,11... | collective-permute-start | bytes 786440 | tf_op jit(solution)/shard_map/ppermute | solution.py:350
  62.6 15.7 %collective-permute-start.4 = (bf16[128,1024]{1,0:T(8,128)(2,1)S(1)}, bf16[128,1024]{1,0:T(8,128)(2,1)S(1)}, u32[]{:S(2)}, u32[]{:S(2)}) collective-permute-start(bf16[128,1024]{1,0:T(8,128)(2,1)S(1)} %copy-done.7), channel_id=1, source_target_pairs={{0,4},{1,5},{2,6},{3,7},{4,0},{5,1},{6,2},{7,3},{8,12},{9,13},{10,... | collective-permute-start | bytes 786440 | tf_op jit(solution)/shard_map/ppermute | solution.py:350
  65.0 13.3 %collective-permute-start.5 = (bf16[128,1024]{1,0:T(8,128)(2,1)S(1)}, bf16[128,1024]{1,0:T(8,128)(2,1)S(1)}, u32[]{:S(2)}, u32[]{:S(2)}) collective-permute-start(bf16[128,1024]{1,0:T(8,128)(2,1)S(1)} %copy-done.6), channel_id=1, source_target_pairs={{0,5},{1,4},{2,7},{3,6},{4,1},{5,0},{6,3},{7,2},{8,13},{9,12},{10,... | collective-permute-start | bytes 786440 | tf_op jit(solution)/shard_map/ppermute | solution.py:350
  71.6 6.6 %copy-start = (bf16[128,1024]{1,0:T(8,128)(2,1)S(1)}, bf16[128,1024]{1,0:T(8,128)(2,1)}, u32[]{:S(2)}) copy-start(bf16[128,1024]{1,0:T(8,128)(2,1)} %get-tuple-element.15.refs_0_) | copy-start | bytes 786436
  71.6 13.1 %all-to-all-start.3 = ((bf16[8,16,1024]{2,1,0:T(8,128)(2,1)}), bf16[8,16,1024]{2,1,0:T(8,128)(2,1)S(1)}, u32[]{:S(2)}, u32[]{:S(2)}) async-start(bf16[8,16,1024]{2,1,0:T(8,128)(2,1)} %sum.1), calls=%async_computation.3 | async-start | bytes 524288 | tf_op jit(solution)/shard_map/all_to_all | solution.py:353

commit v11 on v10

--- a/solution.py
+++ b/solution.py
@@ -13,6 +13,7 @@
 KEY_COLUMNS = 512
 IMAGES = 4
 LOW = -1e30
+SAFE_SCORE = 68.0
 SCALE = WIDTH ** (-0.5)
 LOG2E = 1.4426950408889634
 GRID = 4
@@ -107,22 +108,25 @@
         out[:, columns] = part[...]
 
 
-def softmax_gradients(scores, d_probs, seen):
+def softmax_gradients(scores, d_probs, seen, shifted):
     keys, rows = scores.shape
     scores = scores.reshape(-1, IMAGES, 16, rows)
     d_probs = d_probs.reshape(-1, IMAGES, 16, rows)
-    row_max = None
-    for j in range(IMAGES):
-        top = jnp.max(jnp.max(scores[:, j], axis=0), axis=0, keepdims=True)
-        top = jnp.where(seen[j], top, LOW)
-        row_max = top if row_max is None else jnp.maximum(row_max, top)
-    row_max = row_max * SCALE
+    shifts = [jnp.where(seen[j], 0.0, -LOW) for j in range(IMAGES)]
+    if shifted:
+        row_max = None
+        for j in range(IMAGES):
+            top = jnp.max(jnp.max(scores[:, j], axis=0), axis=0, keepdims=True)
+            top = jnp.where(seen[j], top, LOW)
+            row_max = top if row_max is None else jnp.maximum(row_max, top)
+        row_max = row_max * SCALE
+        shifts = [jnp.where(seen[j], row_max, -LOW) for j in range(IMAGES)]
     terms = []
     lows = []
     total = 0.0
     dots = 0.0
     for j in range(IMAGES):
-        term = jnp.exp(scores[:, j] * SCALE - jnp.where(seen[j], row_max, -LOW))
+        term = jnp.exp(scores[:, j] * SCALE - shifts[j])
         total += jnp.sum(jnp.sum(term, axis=0), axis=0, keepdims=True)
         dots += jnp.sum(jnp.sum(term * d_probs[:, j], axis=0), axis=0, keepdims=True)
         terms.append(term)
@@ -171,11 +175,22 @@
     factor = jnp.tanh(gate[...])
     transposed = (((1,), (1,)), ((), ()))
 
-    def work(step, carry):
-        @pl.when(step > 0)
-        def _():
-            pltpu.make_async_copy(pieces[0], held.at[step], sems.at[step]).wait()
-
+    for k in range(1, BLOCK):
+        pltpu.make_async_copy(pieces[k - 1], held.at[k], sems.at[k]).wait()
+    key_squares = jnp.square(keys_t[...].astype(jnp.float32))
+    key_bound = jnp.max(jnp.sum(key_squares, axis=0, keepdims=True))
+    largest = 0.0
+    for k in range(BLOCK):
+        largest = jnp.maximum(
+            largest, jnp.max(jnp.abs(held[k, :tokens].astype(jnp.float32)), axis=0, keepdims=True)
+        )
+    column = largest[:, :WIDTH]
+    for h in range(1, GROUP):
+        column = jnp.maximum(column, largest[:, h * WIDTH : (h + 1) * WIDTH])
+    query_bound = jnp.sum(jnp.square(column))
+    safe = query_bound * key_bound * SCALE * SCALE < SAFE_SCORE * SAFE_SCORE
+
+    def work(shifted, step, carry):
         for h in range(GROUP):
             rows, columns = slice(h * tokens, (h + 1) * tokens), slice(h * WIDTH, (h + 1) * WIDTH)
             q_rows[rows] = held[step, :tokens, columns]
@@ -193,7 +208,9 @@
             d_probs = lax.dot_general(
                 kv[:, WIDTH:], d_rows[rows], transposed, preferred_element_type=jnp.float32
             )
-            probs[:, rows], d_scores[:, rows] = softmax_gradients(scores, d_probs, seen)
+            probs[:, rows], d_scores[:, rows] = softmax_gradients(
+                scores, d_probs, seen, shifted
+            )
         acc[:, :WIDTH] += jnp.dot(d_scores[...], q_rows[...], preferred_element_type=jnp.float32)
         acc[:, WIDTH:] += jnp.dot(probs[...], d_rows[...], preferred_element_type=jnp.float32)
         dq_t = jnp.dot(keys_t[...], d_scores[...], preferred_element_type=jnp.float32) * SCALE
@@ -208,7 +225,14 @@
 
         return carry
 
-    lax.fori_loop(0, BLOCK, work, 0)
+    @pl.when(safe)
+    def _():
+        lax.fori_loop(0, BLOCK, functools.partial(work, False), 0)
+
+    @pl.when(jnp.logical_not(safe))
+    def _():
+        lax.fori_loop(0, BLOCK, functools.partial(work, True), 0)
+
     dkv[:, :WIDTH] = (acc[:, :WIDTH] * SCALE).astype(jnp.bfloat16)
     dkv[:, WIDTH:] = acc[:, WIDTH:].astype(jnp.bfloat16)
     give = pltpu.make_async_copy(dkv, dkv_any, sems.at[2 * BLOCK])

time: 86.8 us -> 91.7 us (1.056)
  Pallas kernels: 26.4 us -> 31.3 us
    pallas_call x1, Pallas kernels: 18.6 us -> 23.5 us  [gradients(): pl.pallas_call(grad_kernel, in_specs=[pl.BlockSpec(memory_space=VMEM)] +...]
where the time goes in v11:
time: 91.7 us; the launch traced here: 91.1 us
  starting transfers between devices  38.5 us (42%)
  Pallas kernels  31.3 us (34%)
  waiting for transfers between devices  19.1 us (21%)
  between operations  1.41 us (2%)
    pallas_call x1, Pallas kernels, gradients(): pl.pallas_call(grad_kernel, in_specs=[pl.BlockSpec(memory_space=VMEM)] +...  23.5 us
    all_to_all x2, starting transfers between devices, shards(): got = lax.all_to_all(send, 'doc', 0, 0)  12.4 us
    all_to_all x1, starting transfers between devices, shards(): lax.all_to_all(send, 'ctx', 0, 0).reshape(texts * images * rows, 2 * WIDTH)  7.77 us
    ppermute x3, waiting for transfers between devices, shards(): lax.ppermute(pieces[k - 1], both, swap(docs, k))  7.01 us
    all_to_all x1, starting transfers between devices, shards(): lax.all_to_all(dkv.reshape(texts, images, rows, 2 * WIDTH), 'ctx', 0, 0)  6.65 us
    ppermute x3, starting transfers between devices, shards(): lax.ppermute(pieces[k - 1], both, swap(docs, k))  6.49 us
    all_to_all x2, waiting for transfers between devices, shards(): got = lax.all_to_all(send, 'doc', 0, 0)  5.41 us
    all_to_all x1, waiting for transfers between devices, shards(): lax.all_to_all(dkv.reshape(texts, images, rows, 2 * WIDTH), 'ctx', 0, 0)  5.21 us
  transfers between devices with their start and end apart: 10, of which 4 were waited for; matrix products, arithmetic and copies ran while one was open for 0% of the time, Pallas kernels for 4%

profile of v11, /device:TPU:1, one launch (start us, length us, event | category | flops | bytes accessed | tf_op | source)
XLA Modules:
  0.0 91.1 jit_solution(6623107086699171575)
XLA Ops:
  0.6 2.5 %prepare.1 = (bf16[8,16,1024]{2,1,0:T(8,128)(2,1)}, bf16[272,1024]{1,0:T(8,128)(2,1)}, bf16[272,1024]{1,0:T(8,128)(2,1)}, bf16[272,1024]{1,0:T(8,128)(2,1)}) custom-call(s32[32]{0:T(128)} %slots.5, bf16[4,16,1024]{2,1,0:T(8,128)(2,1)} %kv.1, bf16[128,4096]{1,0:T(8,128)(2,1)} %bitcast.10, bf16[128,4096]{1,0:T(8,128)(2,1)} %bitcast.12, s32[2,128]{1,0:T(2,128)} %bitcast.17), custom_call_target="tpu_custom_call" | custom-call | tf_op jit(solution)/shard_map/prepare/pallas_call | solution.py:347
  3.1 5.8 %all-to-all-start = ((bf16[8,16,1024]{2,1,0:T(8,128)(2,1)}), bf16[8,16,1024]{2,1,0:T(8,128)(2,1)S(1)}, u32[]{:S(2)}, u32[]{:S(2)}) async-start(bf16[8,16,1024]{2,1,0:T(8,128)(2,1)} %get-tuple-element.11), calls=%async_computation | async-start | bytes 524288 | tf_op jit(solution)/shard_map/all_to_all | solution.py:361
  9.0 3.8 %collective-permute-start = (bf16[272,1024]{1,0:T(8,128)(2,1)}, bf16[272,1024]{1,0:T(8,128)(2,1)S(1)}, u32[]{:S(2)}, u32[]{:S(2)}) collective-permute-start(bf16[272,1024]{1,0:T(8,128)(2,1)} %get-tuple-element.12), channel_id=1, source_target_pairs={{0,1},{1,0},{2,3},{3,2},{4,5},{5,4},{6,7},{7,6},{8,9},{9,8},{10,11... | collective-permute-start | bytes 1671176 | tf_op jit(solution)/shard_map/ppermute | solution.py:369
  12.7 2.7 %collective-permute-start.1 = (bf16[272,1024]{1,0:T(8,128)(2,1)}, bf16[272,1024]{1,0:T(8,128)(2,1)S(1)}, u32[]{:S(2)}, u32[]{:S(2)}) collective-permute-start(bf16[272,1024]{1,0:T(8,128)(2,1)} %get-tuple-element.13), channel_id=1, source_target_pairs={{0,4},{1,5},{2,6},{3,7},{4,0},{5,1},{6,2},{7,3},{8,12},{9,13},{10,... | collective-permute-start | bytes 1671176 | tf_op jit(solution)/shard_map/ppermute | solution.py:369
  15.4 0.0 collective-permute-start.2
  15.5 0.0 all-to-all-done.got
  15.5 0.0 copy-done.1
  15.5 1.4 %pick.1 = bf16[16,4,16,256]{3,2,1,0:T(8,128)(2,1)} custom-call(s32[32]{0:T(128)S(1)} %copy-done.1, bf16[8,16,1024]{2,1,0:T(8,128)(2,1)S(1)} %all-to-all-done.got), custom_call_target="tpu_custom_call" | custom-call | tf_op jit(solution)/shard_map/pick/pallas_call | solution.py:363
  16.9 7.8 %all-to-all-start.1 = ((bf16[16,4,16,256]{3,2,1,0:T(8,128)(2,1)}), bf16[16,4,16,256]{3,2,1,0:T(8,128)(2,1)S(1)}, u32[]{:S(2)}, u32[]{:S(2)}) async-start(bf16[16,4,16,256]{3,2,1,0:T(8,128)(2,1)} %pick.1), calls=%async_computation.1 | async-start | bytes 1048576 | tf_op jit(solution)/shard_map/all_to_all | solution.py:370
  25.3 0.0 collective-permute-done.refs_0_
  25.3 0.0 copy-start.3
  25.3 0.0 collective-permute-done.1.refs_1_
  25.3 0.0 copy-start.4
  25.4 7.0 %collective-permute-done.2.refs_2_ = bf16[272,1024]{1,0:T(8,128)(2,1)S(1)} collective-permute-done((bf16[272,1024]{1,0:T(8,128)(2,1)}, bf16[272,1024]{1,0:T(8,128)(2,1)S(1)}, u32[]{:S(2)}, u32[]{:S(2)}) %collective-permute-start.2) | collective-permute-done | bytes 557088 | tf_op jit(solution)/shard_map/ppermute | solution.py:369
  32.4 1.5 %all-to-all-done.1 = bf16[16,4,16,256]{3,2,1,0:T(8,128)(2,1)S(1)} async-done(((bf16[16,4,16,256]{3,2,1,0:T(8,128)(2,1)}), bf16[16,4,16,256]{3,2,1,0:T(8,128)(2,1)S(1)}, u32[]{:S(2)}, u32[]{:S(2)}) %all-to-all-start.1) | async-done | bytes 524320 | tf_op jit(solution)/shard_map/all_to_all | solution.py:370
  33.8 0.0 copy-done.5
  33.8 0.8 copy-done.2
  34.6 23.5 %gradients.1 = (bf16[128,1024]{1,0:T(8,128)(2,1)}, bf16[128,1024]{1,0:T(8,128)(2,1)}, bf16[128,1024]{1,0:T(8,128)(2,1)}, bf16[128,1024]{1,0:T(8,128)(2,1)}, bf16[1024,256]{1,0:T(8,128)(2,1)}) custom-call(f32[1,1]{1,0:T(1,128)} %bitcast.9.gate, bf16[1024,256]{1,0:T(8,128)(2,1)} %bitcast.15, bf16[128,4096]{1,0:T(8,128)(2,1)} %bitcast.11, ...), custom_call_target="tpu_custom_call" | custom-call | flops 5368709120 | bytes 4194304 | tf_op jit(solution)/shard_map/gradients/pallas_call | solution.py:251
  58.2 6.6 %all-to-all-start.2 = ((bf16[16,4,16,256]{3,2,1,0:T(8,128)(2,1)}), bf16[16,4,16,256]{3,2,1,0:T(8,128)(2,1)S(1)}, u32[]{:S(2)}, u32[]{:S(2)}) async-start(bf16[16,4,16,256]{3,2,1,0:T(8,128)(2,1)} %bitcast.16), calls=%async_computation.2 | async-start | bytes 1048576 | tf_op jit(solution)/shard_map/all_to_all | solution.py:375
  64.9 2.7 %collective-permute-start.3 = (bf16[128,1024]{1,0:T(8,128)(2,1)S(1)}, bf16[128,1024]{1,0:T(8,128)(2,1)S(1)}, u32[]{:S(2)}, u32[]{:S(2)}) collective-permute-start(bf16[128,1024]{1,0:T(8,128)(2,1)S(1)} %copy-done.8), channel_id=1, source_target_pairs={{0,1},{1,0},{2,3},{3,2},{4,5},{5,4},{6,7},{7,6},{8,9},{9,8},{10,11... | collective-permute-start | bytes 786440 | tf_op jit(solution)/shard_map/ppermute | solution.py:374
  67.5 0.0 copy-done.7
  67.5 2.4 %collective-permute-start.4 = (bf16[128,1024]{1,0:T(8,128)(2,1)S(1)}, bf16[128,1024]{1,0:T(8,128)(2,1)S(1)}, u32[]{:S(2)}, u32[]{:S(2)}) collective-permute-start(bf16[128,1024]{1,0:T(8,128)(2,1)S(1)} %copy-done.7), channel_id=1, source_target_pairs={{0,4},{1,5},{2,6},{3,7},{4,0},{5,1},{6,2},{7,3},{8,12},{9,13},{10,... | collective-permute-start | bytes 786440 | tf_op jit(solution)/shard_map/ppermute | solution.py:374
  69.9 0.1 collective-permute-start.5
  70.0 5.2 %all-to-all-done.2.got = bf16[16,4,16,256]{3,2,1,0:T(8,128)(2,1)S(1)} async-done(((bf16[16,4,16,256]{3,2,1,0:T(8,128)(2,1)}), bf16[16,4,16,256]{3,2,1,0:T(8,128)(2,1)S(1)}, u32[]{:S(2)}, u32[]{:S(2)}) %all-to-all-start.2) | async-done | bytes 524320 | tf_op jit(solution)/shard_map/all_to_all | solution.py:375
  75.2 1.3 %sum.1 = bf16[8,16,1024]{2,1,0:T(8,128)(2,1)} custom-call(s32[32]{0:T(128)S(1)} %copy-done.1, bf16[16,4,16,256]{3,2,1,0:T(8,128)(2,1)S(1)} %all-to-all-done.2.got), custom_call_target="tpu_custom_call" | custom-call | tf_op jit(solution)/shard_map/sum/pallas_call | solution.py:376
  76.6 6.6 %all-to-all-start.3 = ((bf16[8,16,1024]{2,1,0:T(8,128)(2,1)}), bf16[8,16,1024]{2,1,0:T(8,128)(2,1)S(1)}, u32[]{:S(2)}, u32[]{:S(2)}) async-start(bf16[8,16,1024]{2,1,0:T(8,128)(2,1)} %sum.1), calls=%async_computation.3 | async-start | bytes 524288 | tf_op jit(solution)/shard_map/all_to_all | solution.py:377
  83.2 0.0 collective-permute-done.3.refs_1_
  83.2 0.0 collective-permute-done.4.refs_2_
  83.2 0.0 collective-permute-done.5.refs_3_
  83.2 1.1 %merge.1 = bf16[128,4096]{1,0:T(8,128)(2,1)} custom-call(bf16[128,1024]{1,0:T(8,128)(2,1)S(1)} %copy-done, bf16[128,1024]{1,0:T(8,128)(2,1)S(1)} %collective-permute-done.3.refs_1_, bf16[128,1024]{1,0:T(8,128)(2,1)S(1)} %collective-permute-done.4.refs_2_, bf16[128,1024]{1,0:T(8,128)(2,1)S(1)} %collective-permute-done.5.refs_3_), custom_call_target="tpu_custom_call" | custom-call | tf_op jit(solution)/shard_map/merge/pallas_call | solution.py:383
  84.3 5.4 %all-to-all-done.3.got = bf16[8,16,1024]{2,1,0:T(8,128)(2,1)S(1)} async-done(((bf16[8,16,1024]{2,1,0:T(8,128)(2,1)}), bf16[8,16,1024]{2,1,0:T(8,128)(2,1)S(1)}, u32[]{:S(2)}, u32[]{:S(2)}) %all-to-all-start.3) | async-done | bytes 262176 | tf_op jit(solution)/shard_map/all_to_all | solution.py:377
  89.7 1.4 %place.1 = f32[4,16,1024]{2,1,0:T(8,128)} custom-call(s32[32]{0:T(128)S(1)} %copy-done.1, bf16[8,16,1024]{2,1,0:T(8,128)(2,1)S(1)} %all-to-all-done.3.got), custom_call_target="tpu_custom_call" | custom-call | tf_op jit(solution)/shard_map/place/pallas_call | solution.py:378
  (12 shorter events, 0.0 us)
Async XLA Ops:
  3.1 12.3 %all-to-all-start = ((bf16[8,16,1024]{2,1,0:T(8,128)(2,1)}), bf16[8,16,1024]{2,1,0:T(8,128)(2,1)S(1)}, u32[]{:S(2)}, u32[]{:S(2)}) async-start(bf16[8,16,1024]{2,1,0:T(8,128)(2,1)} %get-tuple-element.11), calls=%async_computation | async-start | bytes 524288 | tf_op jit(solution)/shard_map/all_to_all | solution.py:361
  9.0 16.4 %collective-permute-start = (bf16[272,1024]{1,0:T(8,128)(2,1)}, bf16[272,1024]{1,0:T(8,128)(2,1)S(1)}, u32[]{:S(2)}, u32[]{:S(2)}) collective-permute-start(bf16[272,1024]{1,0:T(8,128)(2,1)} %get-tuple-element.12), channel_id=1, source_target_pairs={{0,1},{1,0},{2,3},{3,2},{4,5},{5,4},{6,7},{7,6},{8,9},{9,8},{10,11... | collective-permute-start | bytes 1671176 | tf_op jit(solution)/shard_map/ppermute | solution.py:369
  12.7 2.7 %copy-start.1 = (s32[32]{0:T(128)S(1)}, s32[32]{0:T(128)}, u32[]{:S(2)}) copy-start(s32[32]{0:T(128)} %slots.5) | copy-start | bytes 388
  12.7 12.6 %collective-permute-start.1 = (bf16[272,1024]{1,0:T(8,128)(2,1)}, bf16[272,1024]{1,0:T(8,128)(2,1)S(1)}, u32[]{:S(2)}, u32[]{:S(2)}) collective-permute-start(bf16[272,1024]{1,0:T(8,128)(2,1)} %get-tuple-element.13), channel_id=1, source_target_pairs={{0,4},{1,5},{2,6},{3,7},{4,0},{5,1},{6,2},{7,3},{8,12},{9,13},{10,... | collective-permute-start | bytes 1671176 | tf_op jit(solution)/shard_map/ppermute | solution.py:369
  15.4 16.9 %collective-permute-start.2 = (bf16[272,1024]{1,0:T(8,128)(2,1)}, bf16[272,1024]{1,0:T(8,128)(2,1)S(1)}, u32[]{:S(2)}, u32[]{:S(2)}) collective-permute-start(bf16[272,1024]{1,0:T(8,128)(2,1)} %get-tuple-element.14), channel_id=1, source_target_pairs={{0,5},{1,4},{2,7},{3,6},{4,1},{5,0},{6,3},{7,2},{8,13},{9,12},{10,... | collective-permute-start | bytes 1671176 | tf_op jit(solution)/shard_map/ppermute | solution.py:369
  16.9 16.9 %all-to-all-start.1 = ((bf16[16,4,16,256]{3,2,1,0:T(8,128)(2,1)}), bf16[16,4,16,256]{3,2,1,0:T(8,128)(2,1)S(1)}, u32[]{:S(2)}, u32[]{:S(2)}) async-start(bf16[16,4,16,256]{3,2,1,0:T(8,128)(2,1)} %pick.1), calls=%async_computation.1 | async-start | bytes 1048576 | tf_op jit(solution)/shard_map/all_to_all | solution.py:370
  25.3 8.5 %copy-start.3 = (bf16[272,1024]{1,0:T(8,128)(2,1)}, bf16[272,1024]{1,0:T(8,128)(2,1)S(1)}, u32[]{:S(2)}) copy-start(bf16[272,1024]{1,0:T(8,128)(2,1)S(1)} %collective-permute-done.refs_0_) | copy-start | bytes 1671172
  25.3 8.5 %copy-start.4 = (bf16[272,1024]{1,0:T(8,128)(2,1)}, bf16[272,1024]{1,0:T(8,128)(2,1)S(1)}, u32[]{:S(2)}) copy-start(bf16[272,1024]{1,0:T(8,128)(2,1)S(1)} %collective-permute-done.1.refs_1_) | copy-start | bytes 1671172
  32.4 1.5 %copy-start.5 = (bf16[272,1024]{1,0:T(8,128)(2,1)}, bf16[272,1024]{1,0:T(8,128)(2,1)S(1)}, u32[]{:S(2)}) copy-start(bf16[272,1024]{1,0:T(8,128)(2,1)S(1)} %collective-permute-done.2.refs_2_) | copy-start | bytes 1671172
  33.8 0.8 copy-start.2
  58.2 6.7 %copy-start.8 = (bf16[128,1024]{1,0:T(8,128)(2,1)S(1)}, bf16[128,1024]{1,0:T(8,128)(2,1)}, u32[]{:S(2)}) copy-start(bf16[128,1024]{1,0:T(8,128)(2,1)} %get-tuple-element.16) | copy-start | bytes 786436
  58.2 9.3 %copy-start.7 = (bf16[128,1024]{1,0:T(8,128)(2,1)S(1)}, bf16[128,1024]{1,0:T(8,128)(2,1)}, u32[]{:S(2)}) copy-start(bf16[128,1024]{1,0:T(8,128)(2,1)} %get-tuple-element.17) | copy-start | bytes 786436
  58.2 11.7 %copy-start.6 = (bf16[128,1024]{1,0:T(8,128)(2,1)S(1)}, bf16[128,1024]{1,0:T(8,128)(2,1)}, u32[]{:S(2)}) copy-start(bf16[128,1024]{1,0:T(8,128)(2,1)} %get-tuple-element.18) | copy-start | bytes 786436
  58.2 17.0 %all-to-all-start.2 = ((bf16[16,4,16,256]{3,2,1,0:T(8,128)(2,1)}), bf16[16,4,16,256]{3,2,1,0:T(8,128)(2,1)S(1)}, u32[]{:S(2)}, u32[]{:S(2)}) async-start(bf16[16,4,16,256]{3,2,1,0:T(8,128)(2,1)} %bitcast.16), calls=%async_computation.2 | async-start | bytes 1048576 | tf_op jit(solution)/shard_map/all_to_all | solution.py:375
  64.9 18.3 %collective-permute-start.3 = (bf16[128,1024]{1,0:T(8,128)(2,1)S(1)}, bf16[128,1024]{1,0:T(8,128)(2,1)S(1)}, u32[]{:S(2)}, u32[]{:S(2)}) collective-permute-start(bf16[128,1024]{1,0:T(8,128)(2,1)S(1)} %copy-done.8), channel_id=1, source_target_pairs={{0,1},{1,0},{2,3},{3,2},{4,5},{5,4},{6,7},{7,6},{8,9},{9,8},{10,11... | collective-permute-start | bytes 786440 | tf_op jit(solution)/shard_map/ppermute | solution.py:374
  67.5 15.7 %collective-permute-start.4 = (bf16[128,1024]{1,0:T(8,128)(2,1)S(1)}, bf16[128,1024]{1,0:T(8,128)(2,1)S(1)}, u32[]{:S(2)}, u32[]{:S(2)}) collective-permute-start(bf16[128,1024]{1,0:T(8,128)(2,1)S(1)} %copy-done.7), channel_id=1, source_target_pairs={{0,4},{1,5},{2,6},{3,7},{4,0},{5,1},{6,2},{7,3},{8,12},{9,13},{10,... | collective-permute-start | bytes 786440 | tf_op jit(solution)/shard_map/ppermute | solution.py:374
  69.9 13.3 %collective-permute-start.5 = (bf16[128,1024]{1,0:T(8,128)(2,1)S(1)}, bf16[128,1024]{1,0:T(8,128)(2,1)S(1)}, u32[]{:S(2)}, u32[]{:S(2)}) collective-permute-start(bf16[128,1024]{1,0:T(8,128)(2,1)S(1)} %copy-done.6), channel_id=1, source_target_pairs={{0,5},{1,4},{2,7},{3,6},{4,1},{5,0},{6,3},{7,2},{8,13},{9,12},{10,... | collective-permute-start | bytes 786440 | tf_op jit(solution)/shard_map/ppermute | solution.py:374
  76.6 6.6 %copy-start = (bf16[128,1024]{1,0:T(8,128)(2,1)S(1)}, bf16[128,1024]{1,0:T(8,128)(2,1)}, u32[]{:S(2)}) copy-start(bf16[128,1024]{1,0:T(8,128)(2,1)} %get-tuple-element.15.refs_0_) | copy-start | bytes 786436
  76.6 13.1 %all-to-all-start.3 = ((bf16[8,16,1024]{2,1,0:T(8,128)(2,1)}), bf16[8,16,1024]{2,1,0:T(8,128)(2,1)S(1)}, u32[]{:S(2)}, u32[]{:S(2)}) async-start(bf16[8,16,1024]{2,1,0:T(8,128)(2,1)} %sum.1), calls=%async_computation.3 | async-start | bytes 524288 | tf_op jit(solution)/shard_map/all_to_all | solution.py:377

commit v12 on v11

--- a/solution.py
+++ b/solution.py
@@ -15,7 +15,6 @@
 LOW = -1e30
 SAFE_SCORE = 68.0
 SCALE = WIDTH ** (-0.5)
-LOG2E = 1.4426950408889634
 GRID = 4
 BLOCK = 4
 BATCH_HEADS = 2
@@ -190,7 +189,7 @@
     query_bound = jnp.sum(jnp.square(column))
     safe = query_bound * key_bound * SCALE * SCALE < SAFE_SCORE * SAFE_SCORE
 
-    def work(shifted, step, carry):
+    def work(step, carry):
         for h in range(GROUP):
             rows, columns = slice(h * tokens, (h + 1) * tokens), slice(h * WIDTH, (h + 1) * WIDTH)
             q_rows[rows] = held[step, :tokens, columns]
@@ -209,7 +208,7 @@
                 kv[:, WIDTH:], d_rows[rows], transposed, preferred_element_type=jnp.float32
             )
             probs[:, rows], d_scores[:, rows] = softmax_gradients(
-                scores, d_probs, seen, shifted
+                scores, d_probs, seen, False
             )
         acc[:, :WIDTH] += jnp.dot(d_scores[...], q_rows[...], preferred_element_type=jnp.float32)
         acc[:, WIDTH:] += jnp.dot(probs[...], d_rows[...], preferred_element_type=jnp.float32)
@@ -225,13 +224,36 @@
 
         return carry
 
+    def careful_work(index, carry):
+        step, h = index // GROUP, index % GROUP
+        columns = pl.ds(pl.multiple_of(h * WIDTH, WIDTH), WIDTH)
+        q_one = held[step, :tokens, columns]
+        wide = held[step, tokens : 2 * tokens, columns].astype(jnp.float32)
+        d_one = (wide * factor).astype(jnp.bfloat16)
+        spans = held[step, 2 * tokens :, :tokens].astype(jnp.float32)
+        seen = [(spans[0:1] <= j) & (j < spans[1:2]) for j in range(IMAGES)]
+        scores = lax.dot_general(
+            kv[:, :WIDTH], q_one, transposed, preferred_element_type=jnp.float32
+        )
+        d_probs = lax.dot_general(
+            kv[:, WIDTH:], d_one, transposed, preferred_element_type=jnp.float32
+        )
+        probs_one, d_scores_one = softmax_gradients(scores, d_probs, seen, True)
+        acc[:, :WIDTH] += jnp.dot(d_scores_one, q_one, preferred_element_type=jnp.float32)
+        acc[:, WIDTH:] += jnp.dot(probs_one, d_one, preferred_element_type=jnp.float32)
+        dq_t = jnp.dot(keys_t[...], d_scores_one, preferred_element_type=jnp.float32) * SCALE
+        dq[step, :, columns] = dq_t.T.astype(jnp.bfloat16)
+        return carry
+
     @pl.when(safe)
     def _():
-        lax.fori_loop(0, BLOCK, functools.partial(work, False), 0)
+        lax.fori_loop(0, BLOCK, work, 0)
 
     @pl.when(jnp.logical_not(safe))
     def _():
-        lax.fori_loop(0, BLOCK, functools.partial(work, True), 0)
+        lax.fori_loop(0, BLOCK * GROUP, careful_work, 0)
+        for k in range(BLOCK):
+            pltpu.make_async_copy(dq.at[k], dqs[k], sems.at[BLOCK + k]).start()
 
     dkv[:, :WIDTH] = (acc[:, :WIDTH] * SCALE).astype(jnp.bfloat16)
     dkv[:, WIDTH:] = acc[:, WIDTH:].astype(jnp.bfloat16)

time: 91.7 us -> 99.7 us (1.087)
  Pallas kernels: 31.3 us -> 39.3 us
    pallas_call x1, Pallas kernels: 23.5 us -> 31.6 us  [gradients(): pl.pallas_call(grad_kernel, in_specs=[pl.BlockSpec(memory_space=VMEM)] +...]
where the time goes in v12:
time: 99.7 us; the launch traced here: 99.1 us
  Pallas kernels  39.3 us (39%)
  starting transfers between devices  38.4 us (39%)
  waiting for transfers between devices  19.1 us (19%)
  between operations  1.41 us (1%)
    pallas_call x1, Pallas kernels, gradients(): pl.pallas_call(grad_kernel, in_specs=[pl.BlockSpec(memory_space=VMEM)] +...  31.6 us
    all_to_all x2, starting transfers between devices, shards(): got = lax.all_to_all(send, 'doc', 0, 0)  12.3 us
    all_to_all x1, starting transfers between devices, shards(): lax.all_to_all(send, 'ctx', 0, 0).reshape(texts * images * rows, 2 * WIDTH)  7.77 us
    ppermute x3, waiting for transfers between devices, shards(): lax.ppermute(pieces[k - 1], both, swap(docs, k))  7.01 us
    all_to_all x1, starting transfers between devices, shards(): lax.all_to_all(dkv.reshape(texts, images, rows, 2 * WIDTH), 'ctx', 0, 0)  6.66 us
    ppermute x3, starting transfers between devices, shards(): lax.ppermute(pieces[k - 1], both, swap(docs, k))  6.49 us
    all_to_all x2, waiting for transfers between devices, shards(): got = lax.all_to_all(send, 'doc', 0, 0)  5.41 us
    all_to_all x1, waiting for transfers between devices, shards(): lax.all_to_all(dkv.reshape(texts, images, rows, 2 * WIDTH), 'ctx', 0, 0)  5.22 us
  transfers between devices with their start and end apart: 10, of which 4 were waited for; matrix products, arithmetic and copies ran while one was open for 0% of the time, Pallas kernels for 4%

profile of v12, /device:TPU:1, one launch (start us, length us, event | category | flops | bytes accessed | tf_op | source)
XLA Modules:
  0.0 99.1 jit_solution(4069674338864284160)
XLA Ops:
  0.6 2.5 %prepare.1 = (bf16[8,16,1024]{2,1,0:T(8,128)(2,1)}, bf16[272,1024]{1,0:T(8,128)(2,1)}, bf16[272,1024]{1,0:T(8,128)(2,1)}, bf16[272,1024]{1,0:T(8,128)(2,1)}) custom-call(s32[32]{0:T(128)} %slots.5, bf16[4,16,1024]{2,1,0:T(8,128)(2,1)} %kv.1, bf16[128,4096]{1,0:T(8,128)(2,1)} %bitcast.10, bf16[128,4096]{1,0:T(8,128)(2,1)} %bitcast.12, s32[2,128]{1,0:T(2,128)} %bitcast.17), custom_call_target="tpu_custom_call" | custom-call | tf_op jit(solution)/shard_map/prepare/pallas_call | solution.py:369
  3.1 5.8 %all-to-all-start = ((bf16[8,16,1024]{2,1,0:T(8,128)(2,1)}), bf16[8,16,1024]{2,1,0:T(8,128)(2,1)S(1)}, u32[]{:S(2)}, u32[]{:S(2)}) async-start(bf16[8,16,1024]{2,1,0:T(8,128)(2,1)} %get-tuple-element.11), calls=%async_computation | async-start | bytes 524288 | tf_op jit(solution)/shard_map/all_to_all | solution.py:383
  9.0 3.8 %collective-permute-start = (bf16[272,1024]{1,0:T(8,128)(2,1)}, bf16[272,1024]{1,0:T(8,128)(2,1)S(1)}, u32[]{:S(2)}, u32[]{:S(2)}) collective-permute-start(bf16[272,1024]{1,0:T(8,128)(2,1)} %get-tuple-element.12), channel_id=1, source_target_pairs={{0,1},{1,0},{2,3},{3,2},{4,5},{5,4},{6,7},{7,6},{8,9},{9,8},{10,11... | collective-permute-start | bytes 1671176 | tf_op jit(solution)/shard_map/ppermute | solution.py:391
  12.7 2.7 %collective-permute-start.1 = (bf16[272,1024]{1,0:T(8,128)(2,1)}, bf16[272,1024]{1,0:T(8,128)(2,1)S(1)}, u32[]{:S(2)}, u32[]{:S(2)}) collective-permute-start(bf16[272,1024]{1,0:T(8,128)(2,1)} %get-tuple-element.13), channel_id=1, source_target_pairs={{0,4},{1,5},{2,6},{3,7},{4,0},{5,1},{6,2},{7,3},{8,12},{9,13},{10,... | collective-permute-start | bytes 1671176 | tf_op jit(solution)/shard_map/ppermute | solution.py:391
  15.4 0.0 collective-permute-start.2
  15.5 0.0 all-to-all-done.got
  15.5 0.0 copy-done.1
  15.5 1.4 %pick.1 = bf16[16,4,16,256]{3,2,1,0:T(8,128)(2,1)} custom-call(s32[32]{0:T(128)S(1)} %copy-done.1, bf16[8,16,1024]{2,1,0:T(8,128)(2,1)S(1)} %all-to-all-done.got), custom_call_target="tpu_custom_call" | custom-call | tf_op jit(solution)/shard_map/pick/pallas_call | solution.py:385
  16.9 7.8 %all-to-all-start.1 = ((bf16[16,4,16,256]{3,2,1,0:T(8,128)(2,1)}), bf16[16,4,16,256]{3,2,1,0:T(8,128)(2,1)S(1)}, u32[]{:S(2)}, u32[]{:S(2)}) async-start(bf16[16,4,16,256]{3,2,1,0:T(8,128)(2,1)} %pick.1), calls=%async_computation.1 | async-start | bytes 1048576 | tf_op jit(solution)/shard_map/all_to_all | solution.py:392
  25.3 0.0 collective-permute-done.refs_0_
  25.3 0.0 copy-start.3
  25.3 0.0 collective-permute-done.1.refs_1_
  25.3 0.0 copy-start.4
  25.4 7.0 %collective-permute-done.2.refs_2_ = bf16[272,1024]{1,0:T(8,128)(2,1)S(1)} collective-permute-done((bf16[272,1024]{1,0:T(8,128)(2,1)}, bf16[272,1024]{1,0:T(8,128)(2,1)S(1)}, u32[]{:S(2)}, u32[]{:S(2)}) %collective-permute-start.2) | collective-permute-done | bytes 557088 | tf_op jit(solution)/shard_map/ppermute | solution.py:391
  32.4 1.5 %all-to-all-done.1 = bf16[16,4,16,256]{3,2,1,0:T(8,128)(2,1)S(1)} async-done(((bf16[16,4,16,256]{3,2,1,0:T(8,128)(2,1)}), bf16[16,4,16,256]{3,2,1,0:T(8,128)(2,1)S(1)}, u32[]{:S(2)}, u32[]{:S(2)}) %all-to-all-start.1) | async-done | bytes 524320 | tf_op jit(solution)/shard_map/all_to_all | solution.py:392
  33.8 0.0 copy-done.5
  33.8 0.8 copy-done.2
  34.6 31.6 %gradients.1 = (bf16[128,1024]{1,0:T(8,128)(2,1)}, bf16[128,1024]{1,0:T(8,128)(2,1)}, bf16[128,1024]{1,0:T(8,128)(2,1)}, bf16[128,1024]{1,0:T(8,128)(2,1)}, bf16[1024,256]{1,0:T(8,128)(2,1)}) custom-call(f32[1,1]{1,0:T(1,128)} %bitcast.9.gate, bf16[1024,256]{1,0:T(8,128)(2,1)} %bitcast.15, bf16[128,4096]{1,0:T(8,128)(2,1)} %bitcast.11, ...), custom_call_target="tpu_custom_call" | custom-call | flops 5368709120 | bytes 4194304 | tf_op jit(solution)/shard_map/gradients/pallas_call | solution.py:273
  66.2 6.7 %all-to-all-start.2 = ((bf16[16,4,16,256]{3,2,1,0:T(8,128)(2,1)}), bf16[16,4,16,256]{3,2,1,0:T(8,128)(2,1)S(1)}, u32[]{:S(2)}, u32[]{:S(2)}) async-start(bf16[16,4,16,256]{3,2,1,0:T(8,128)(2,1)} %bitcast.16), calls=%async_computation.2 | async-start | bytes 1048576 | tf_op jit(solution)/shard_map/all_to_all | solution.py:397
  72.9 2.7 %collective-permute-start.3 = (bf16[128,1024]{1,0:T(8,128)(2,1)S(1)}, bf16[128,1024]{1,0:T(8,128)(2,1)S(1)}, u32[]{:S(2)}, u32[]{:S(2)}) collective-permute-start(bf16[128,1024]{1,0:T(8,128)(2,1)S(1)} %copy-done.8), channel_id=1, source_target_pairs={{0,1},{1,0},{2,3},{3,2},{4,5},{5,4},{6,7},{7,6},{8,9},{9,8},{10,11... | collective-permute-start | bytes 786440 | tf_op jit(solution)/shard_map/ppermute | solution.py:396
  75.5 2.4 %collective-permute-start.4 = (bf16[128,1024]{1,0:T(8,128)(2,1)S(1)}, bf16[128,1024]{1,0:T(8,128)(2,1)S(1)}, u32[]{:S(2)}, u32[]{:S(2)}) collective-permute-start(bf16[128,1024]{1,0:T(8,128)(2,1)S(1)} %copy-done.7), channel_id=1, source_target_pairs={{0,4},{1,5},{2,6},{3,7},{4,0},{5,1},{6,2},{7,3},{8,12},{9,13},{10,... | collective-permute-start | bytes 786440 | tf_op jit(solution)/shard_map/ppermute | solution.py:396
  78.0 0.0 copy-done.6
  78.0 0.1 collective-permute-start.5
  78.1 5.2 %all-to-all-done.2.got = bf16[16,4,16,256]{3,2,1,0:T(8,128)(2,1)S(1)} async-done(((bf16[16,4,16,256]{3,2,1,0:T(8,128)(2,1)}), bf16[16,4,16,256]{3,2,1,0:T(8,128)(2,1)S(1)}, u32[]{:S(2)}, u32[]{:S(2)}) %all-to-all-start.2) | async-done | bytes 524320 | tf_op jit(solution)/shard_map/all_to_all | solution.py:397
  83.3 1.3 %sum.1 = bf16[8,16,1024]{2,1,0:T(8,128)(2,1)} custom-call(s32[32]{0:T(128)S(1)} %copy-done.1, bf16[16,4,16,256]{3,2,1,0:T(8,128)(2,1)S(1)} %all-to-all-done.2.got), custom_call_target="tpu_custom_call" | custom-call | tf_op jit(solution)/shard_map/sum/pallas_call | solution.py:398
  84.6 6.5 %all-to-all-start.3 = ((bf16[8,16,1024]{2,1,0:T(8,128)(2,1)}), bf16[8,16,1024]{2,1,0:T(8,128)(2,1)S(1)}, u32[]{:S(2)}, u32[]{:S(2)}) async-start(bf16[8,16,1024]{2,1,0:T(8,128)(2,1)} %sum.1), calls=%async_computation.3 | async-start | bytes 524288 | tf_op jit(solution)/shard_map/all_to_all | solution.py:399
  91.2 0.0 collective-permute-done.3.refs_1_
  91.2 0.0 collective-permute-done.4.refs_2_
  91.2 0.0 collective-permute-done.5.refs_3_
  91.2 1.1 %merge.1 = bf16[128,4096]{1,0:T(8,128)(2,1)} custom-call(bf16[128,1024]{1,0:T(8,128)(2,1)S(1)} %copy-done, bf16[128,1024]{1,0:T(8,128)(2,1)S(1)} %collective-permute-done.3.refs_1_, bf16[128,1024]{1,0:T(8,128)(2,1)S(1)} %collective-permute-done.4.refs_2_, bf16[128,1024]{1,0:T(8,128)(2,1)S(1)} %collective-permute-done.5.refs_3_), custom_call_target="tpu_custom_call" | custom-call | tf_op jit(solution)/shard_map/merge/pallas_call | solution.py:405
  92.2 5.4 %all-to-all-done.3.got = bf16[8,16,1024]{2,1,0:T(8,128)(2,1)S(1)} async-done(((bf16[8,16,1024]{2,1,0:T(8,128)(2,1)}), bf16[8,16,1024]{2,1,0:T(8,128)(2,1)S(1)}, u32[]{:S(2)}, u32[]{:S(2)}) %all-to-all-start.3) | async-done | bytes 262176 | tf_op jit(solution)/shard_map/all_to_all | solution.py:399
  97.7 1.4 %place.1 = f32[4,16,1024]{2,1,0:T(8,128)} custom-call(s32[32]{0:T(128)S(1)} %copy-done.1, bf16[8,16,1024]{2,1,0:T(8,128)(2,1)S(1)} %all-to-all-done.3.got), custom_call_target="tpu_custom_call" | custom-call | tf_op jit(solution)/shard_map/place/pallas_call | solution.py:400
  (12 shorter events, 0.0 us)
Async XLA Ops:
  3.1 12.3 %all-to-all-start = ((bf16[8,16,1024]{2,1,0:T(8,128)(2,1)}), bf16[8,16,1024]{2,1,0:T(8,128)(2,1)S(1)}, u32[]{:S(2)}, u32[]{:S(2)}) async-start(bf16[8,16,1024]{2,1,0:T(8,128)(2,1)} %get-tuple-element.11), calls=%async_computation | async-start | bytes 524288 | tf_op jit(solution)/shard_map/all_to_all | solution.py:383
  9.0 16.4 %collective-permute-start = (bf16[272,1024]{1,0:T(8,128)(2,1)}, bf16[272,1024]{1,0:T(8,128)(2,1)S(1)}, u32[]{:S(2)}, u32[]{:S(2)}) collective-permute-start(bf16[272,1024]{1,0:T(8,128)(2,1)} %get-tuple-element.12), channel_id=1, source_target_pairs={{0,1},{1,0},{2,3},{3,2},{4,5},{5,4},{6,7},{7,6},{8,9},{9,8},{10,11... | collective-permute-start | bytes 1671176 | tf_op jit(solution)/shard_map/ppermute | solution.py:391
  12.7 2.7 %copy-start.1 = (s32[32]{0:T(128)S(1)}, s32[32]{0:T(128)}, u32[]{:S(2)}) copy-start(s32[32]{0:T(128)} %slots.5) | copy-start | bytes 388
  12.7 12.6 %collective-permute-start.1 = (bf16[272,1024]{1,0:T(8,128)(2,1)}, bf16[272,1024]{1,0:T(8,128)(2,1)S(1)}, u32[]{:S(2)}, u32[]{:S(2)}) collective-permute-start(bf16[272,1024]{1,0:T(8,128)(2,1)} %get-tuple-element.13), channel_id=1, source_target_pairs={{0,4},{1,5},{2,6},{3,7},{4,0},{5,1},{6,2},{7,3},{8,12},{9,13},{10,... | collective-permute-start | bytes 1671176 | tf_op jit(solution)/shard_map/ppermute | solution.py:391
  15.4 16.9 %collective-permute-start.2 = (bf16[272,1024]{1,0:T(8,128)(2,1)}, bf16[272,1024]{1,0:T(8,128)(2,1)S(1)}, u32[]{:S(2)}, u32[]{:S(2)}) collective-permute-start(bf16[272,1024]{1,0:T(8,128)(2,1)} %get-tuple-element.14), channel_id=1, source_target_pairs={{0,5},{1,4},{2,7},{3,6},{4,1},{5,0},{6,3},{7,2},{8,13},{9,12},{10,... | collective-permute-start | bytes 1671176 | tf_op jit(solution)/shard_map/ppermute | solution.py:391
  16.9 16.9 %all-to-all-start.1 = ((bf16[16,4,16,256]{3,2,1,0:T(8,128)(2,1)}), bf16[16,4,16,256]{3,2,1,0:T(8,128)(2,1)S(1)}, u32[]{:S(2)}, u32[]{:S(2)}) async-start(bf16[16,4,16,256]{3,2,1,0:T(8,128)(2,1)} %pick.1), calls=%async_computation.1 | async-start | bytes 1048576 | tf_op jit(solution)/shard_map/all_to_all | solution.py:392
  25.3 8.5 %copy-start.3 = (bf16[272,1024]{1,0:T(8,128)(2,1)}, bf16[272,1024]{1,0:T(8,128)(2,1)S(1)}, u32[]{:S(2)}) copy-start(bf16[272,1024]{1,0:T(8,128)(2,1)S(1)} %collective-permute-done.refs_0_) | copy-start | bytes 1671172
  25.3 8.5 %copy-start.4 = (bf16[272,1024]{1,0:T(8,128)(2,1)}, bf16[272,1024]{1,0:T(8,128)(2,1)S(1)}, u32[]{:S(2)}) copy-start(bf16[272,1024]{1,0:T(8,128)(2,1)S(1)} %collective-permute-done.1.refs_1_) | copy-start | bytes 1671172
  32.4 1.5 %copy-start.5 = (bf16[272,1024]{1,0:T(8,128)(2,1)}, bf16[272,1024]{1,0:T(8,128)(2,1)S(1)}, u32[]{:S(2)}) copy-start(bf16[272,1024]{1,0:T(8,128)(2,1)S(1)} %collective-permute-done.2.refs_2_) | copy-start | bytes 1671172
  33.8 0.8 copy-start.2
  66.2 6.7 %copy-start.8 = (bf16[128,1024]{1,0:T(8,128)(2,1)S(1)}, bf16[128,1024]{1,0:T(8,128)(2,1)}, u32[]{:S(2)}) copy-start(bf16[128,1024]{1,0:T(8,128)(2,1)} %get-tuple-element.16) | copy-start | bytes 786436
  66.2 9.4 %copy-start.7 = (bf16[128,1024]{1,0:T(8,128)(2,1)S(1)}, bf16[128,1024]{1,0:T(8,128)(2,1)}, u32[]{:S(2)}) copy-start(bf16[128,1024]{1,0:T(8,128)(2,1)} %get-tuple-element.17) | copy-start | bytes 786436
  66.2 11.7 %copy-start.6 = (bf16[128,1024]{1,0:T(8,128)(2,1)S(1)}, bf16[128,1024]{1,0:T(8,128)(2,1)}, u32[]{:S(2)}) copy-start(bf16[128,1024]{1,0:T(8,128)(2,1)} %get-tuple-element.18) | copy-start | bytes 786436
  66.2 17.1 %all-to-all-start.2 = ((bf16[16,4,16,256]{3,2,1,0:T(8,128)(2,1)}), bf16[16,4,16,256]{3,2,1,0:T(8,128)(2,1)S(1)}, u32[]{:S(2)}, u32[]{:S(2)}) async-start(bf16[16,4,16,256]{3,2,1,0:T(8,128)(2,1)} %bitcast.16), calls=%async_computation.2 | async-start | bytes 1048576 | tf_op jit(solution)/shard_map/all_to_all | solution.py:397
  72.9 18.3 %collective-permute-start.3 = (bf16[128,1024]{1,0:T(8,128)(2,1)S(1)}, bf16[128,1024]{1,0:T(8,128)(2,1)S(1)}, u32[]{:S(2)}, u32[]{:S(2)}) collective-permute-start(bf16[128,1024]{1,0:T(8,128)(2,1)S(1)} %copy-done.8), channel_id=1, source_target_pairs={{0,1},{1,0},{2,3},{3,2},{4,5},{5,4},{6,7},{7,6},{8,9},{9,8},{10,11... | collective-permute-start | bytes 786440 | tf_op jit(solution)/shard_map/ppermute | solution.py:396
  75.5 15.6 %collective-permute-start.4 = (bf16[128,1024]{1,0:T(8,128)(2,1)S(1)}, bf16[128,1024]{1,0:T(8,128)(2,1)S(1)}, u32[]{:S(2)}, u32[]{:S(2)}) collective-permute-start(bf16[128,1024]{1,0:T(8,128)(2,1)S(1)} %copy-done.7), channel_id=1, source_target_pairs={{0,4},{1,5},{2,6},{3,7},{4,0},{5,1},{6,2},{7,3},{8,12},{9,13},{10,... | collective-permute-start | bytes 786440 | tf_op jit(solution)/shard_map/ppermute | solution.py:396
  78.0 13.2 %collective-permute-start.5 = (bf16[128,1024]{1,0:T(8,128)(2,1)S(1)}, bf16[128,1024]{1,0:T(8,128)(2,1)S(1)}, u32[]{:S(2)}, u32[]{:S(2)}) collective-permute-start(bf16[128,1024]{1,0:T(8,128)(2,1)S(1)} %copy-done.6), channel_id=1, source_target_pairs={{0,5},{1,4},{2,7},{3,6},{4,1},{5,0},{6,3},{7,2},{8,13},{9,12},{10,... | collective-permute-start | bytes 786440 | tf_op jit(solution)/shard_map/ppermute | solution.py:396
  84.6 6.6 %copy-start = (bf16[128,1024]{1,0:T(8,128)(2,1)S(1)}, bf16[128,1024]{1,0:T(8,128)(2,1)}, u32[]{:S(2)}) copy-start(bf16[128,1024]{1,0:T(8,128)(2,1)} %get-tuple-element.15.refs_0_) | copy-start | bytes 786436
  84.6 13.0 %all-to-all-start.3 = ((bf16[8,16,1024]{2,1,0:T(8,128)(2,1)}), bf16[8,16,1024]{2,1,0:T(8,128)(2,1)S(1)}, u32[]{:S(2)}, u32[]{:S(2)}) async-start(bf16[8,16,1024]{2,1,0:T(8,128)(2,1)} %sum.1), calls=%async_computation.3 | async-start | bytes 524288 | tf_op jit(solution)/shard_map/all_to_all | solution.py:399

commit v13 on v12

--- a/solution.py
+++ b/solution.py
@@ -34,7 +34,7 @@
 
 
 def prepare_kernel(docs, slots_any, kv, q, d_out, spans_any, *refs):
-    send, pieces, (slots, rows, held, spans, sems) = refs[0], refs[1:BLOCK], refs[BLOCK:]
+    send, pieces, (slots, rows, held, spans, padded, sems) = refs[0], refs[1:BLOCK], refs[BLOCK:]
     tokens = q.shape[0]
     width = q.shape[1] // KV_HEADS
     doc, place = place_in_block()
@@ -70,9 +70,11 @@
     for copy in copies:
         copy.start()
     fetch_spans.wait()
+    padded[...] = jnp.zeros_like(padded)
+    padded[:2] = spans[...].astype(jnp.float32)
     for k in range(1, BLOCK):
         held[k - 1, 2 * tokens :] = jnp.zeros_like(held[k - 1, 2 * tokens :])
-        held[k - 1, 2 * tokens : 2 * tokens + 2, :tokens] = spans[...].astype(jnp.bfloat16)
+        held[k - 1, 2 * tokens :, :tokens] = padded[...].astype(jnp.bfloat16)
     for k, pair in zip(range(1, BLOCK), fetches):
         for copy in pair:
             copy.wait()
@@ -145,7 +147,7 @@
 
 def grad_kernel(gate, kv_any, q, d_out, spans_any, *refs):
     pieces, dqs, dkv_any, refs = refs[: BLOCK - 1], refs[BLOCK - 1 : 2 * BLOCK - 1], refs[2 * BLOCK - 1], refs[2 * BLOCK :]
-    kv, held, own_spans, dq, dkv, keys_t, probs, d_scores, q_rows, d_rows, acc, sems = refs
+    kv, held, own_spans, padded, dq, dkv, keys_t, probs, d_scores, q_rows, d_rows, acc, sems = refs
     tokens = dqs[0].shape[0]
     width = dqs[0].shape[1]
     block = BATCH_HEADS * tokens
@@ -169,8 +171,9 @@
     keys_t[...] = kv[:, :WIDTH].T
     for copy in fetch_own:
         copy.wait()
-    held[0, 2 * tokens :] = jnp.zeros_like(held[0, 2 * tokens :])
-    held[0, 2 * tokens : 2 * tokens + 2, :tokens] = own_spans[...].astype(jnp.bfloat16)
+    padded[...] = jnp.zeros_like(padded)
+    padded[:2] = own_spans[...].astype(jnp.float32)
+    held[0, 2 * tokens :, :tokens] = padded[...].astype(jnp.bfloat16)
     factor = jnp.tanh(gate[...])
     transposed = (((1,), (1,)), ((), ()))
 
@@ -280,6 +283,7 @@
             pltpu.VMEM(kv.shape, jnp.bfloat16),
             pltpu.VMEM((BLOCK,) + pieces[0].shape, jnp.bfloat16),
             pltpu.VMEM(spans.shape, jnp.int32),
+            pltpu.VMEM((PAD, tokens), jnp.float32),
             pltpu.VMEM((BLOCK, tokens, width), jnp.bfloat16),
             pltpu.VMEM(kv.shape, jnp.bfloat16),
             pltpu.VMEM((WIDTH, key_rows), jnp.bfloat16),
@@ -376,6 +380,7 @@
             pltpu.VMEM(image_kv.shape, jnp.bfloat16),
             pltpu.VMEM((BLOCK - 1,) + piece.shape, jnp.bfloat16),
             pltpu.VMEM(span_rows.shape, jnp.int32),
+            pltpu.VMEM((PAD, tokens), jnp.float32),
             pltpu.SemaphoreType.DMA((docs + 3 * BLOCK,)),
         ],
         name="prepare",

time: 99.7 us -> 99.7 us (level)
  no operation moved by 1% of the time
where the time goes in v13:
time: 99.7 us; the launch traced here: 99.1 us
  Pallas kernels  39.3 us (39%)
  starting transfers between devices  38.4 us (39%)
  waiting for transfers between devices  19.1 us (19%)
  between operations  1.41 us (1%)
    pallas_call x1, Pallas kernels, gradients(): pl.pallas_call(grad_kernel, in_specs=[pl.BlockSpec(memory_space=VMEM)] +...  31.6 us
    all_to_all x2, starting transfers between devices, shards(): got = lax.all_to_all(send, 'doc', 0, 0)  12.3 us
    all_to_all x1, starting transfers between devices, shards(): lax.all_to_all(send, 'ctx', 0, 0).reshape(texts * images * rows, 2 * WIDTH)  7.77 us
    ppermute x3, waiting for transfers between devices, shards(): lax.ppermute(pieces[k - 1], both, swap(docs, k))  7.01 us
    all_to_all x1, starting transfers between devices, shards(): lax.all_to_all(dkv.reshape(texts, images, rows, 2 * WIDTH), 'ctx', 0, 0)  6.66 us
    ppermute x3, starting transfers between devices, shards(): lax.ppermute(pieces[k - 1], both, swap(docs, k))  6.49 us
    all_to_all x2, waiting for transfers between devices, shards(): got = lax.all_to_all(send, 'doc', 0, 0)  5.41 us
    all_to_all x1, waiting for transfers between devices, shards(): lax.all_to_all(dkv.reshape(texts, images, rows, 2 * WIDTH), 'ctx', 0, 0)  5.22 us
  transfers between devices with their start and end apart: 10, of which 4 were waited for; matrix products, arithmetic and copies ran while one was open for 0% of the time, Pallas kernels for 4%

profile of v13, /device:TPU:1, one launch (start us, length us, event | category | flops | bytes accessed | tf_op | source)
XLA Modules:
  0.0 99.1 jit_solution(4752011565254180411)
XLA Ops:
  0.6 2.5 %prepare.1 = (bf16[8,16,1024]{2,1,0:T(8,128)(2,1)}, bf16[272,1024]{1,0:T(8,128)(2,1)}, bf16[272,1024]{1,0:T(8,128)(2,1)}, bf16[272,1024]{1,0:T(8,128)(2,1)}) custom-call(s32[32]{0:T(128)} %slots.5, bf16[4,16,1024]{2,1,0:T(8,128)(2,1)} %kv.1, bf16[128,4096]{1,0:T(8,128)(2,1)} %bitcast.10, bf16[128,4096]{1,0:T(8,128)(2,1)} %bitcast.12, s32[2,128]{1,0:T(2,128)} %bitcast.17), custom_call_target="tpu_custom_call" | custom-call | tf_op jit(solution)/shard_map/prepare/pallas_call | solution.py:373
  3.1 5.8 %all-to-all-start = ((bf16[8,16,1024]{2,1,0:T(8,128)(2,1)}), bf16[8,16,1024]{2,1,0:T(8,128)(2,1)S(1)}, u32[]{:S(2)}, u32[]{:S(2)}) async-start(bf16[8,16,1024]{2,1,0:T(8,128)(2,1)} %get-tuple-element.11), calls=%async_computation | async-start | bytes 524288 | tf_op jit(solution)/shard_map/all_to_all | solution.py:388
  9.0 3.8 %collective-permute-start = (bf16[272,1024]{1,0:T(8,128)(2,1)}, bf16[272,1024]{1,0:T(8,128)(2,1)S(1)}, u32[]{:S(2)}, u32[]{:S(2)}) collective-permute-start(bf16[272,1024]{1,0:T(8,128)(2,1)} %get-tuple-element.12), channel_id=1, source_target_pairs={{0,1},{1,0},{2,3},{3,2},{4,5},{5,4},{6,7},{7,6},{8,9},{9,8},{10,11... | collective-permute-start | bytes 1671176 | tf_op jit(solution)/shard_map/ppermute | solution.py:396
  12.7 2.7 %collective-permute-start.1 = (bf16[272,1024]{1,0:T(8,128)(2,1)}, bf16[272,1024]{1,0:T(8,128)(2,1)S(1)}, u32[]{:S(2)}, u32[]{:S(2)}) collective-permute-start(bf16[272,1024]{1,0:T(8,128)(2,1)} %get-tuple-element.13), channel_id=1, source_target_pairs={{0,4},{1,5},{2,6},{3,7},{4,0},{5,1},{6,2},{7,3},{8,12},{9,13},{10,... | collective-permute-start | bytes 1671176 | tf_op jit(solution)/shard_map/ppermute | solution.py:396
  15.4 0.0 collective-permute-start.2
  15.5 0.0 all-to-all-done.got
  15.5 0.0 copy-done.1
  15.5 1.4 %pick.1 = bf16[16,4,16,256]{3,2,1,0:T(8,128)(2,1)} custom-call(s32[32]{0:T(128)S(1)} %copy-done.1, bf16[8,16,1024]{2,1,0:T(8,128)(2,1)S(1)} %all-to-all-done.got), custom_call_target="tpu_custom_call" | custom-call | tf_op jit(solution)/shard_map/pick/pallas_call | solution.py:390
  16.9 7.8 %all-to-all-start.1 = ((bf16[16,4,16,256]{3,2,1,0:T(8,128)(2,1)}), bf16[16,4,16,256]{3,2,1,0:T(8,128)(2,1)S(1)}, u32[]{:S(2)}, u32[]{:S(2)}) async-start(bf16[16,4,16,256]{3,2,1,0:T(8,128)(2,1)} %pick.1), calls=%async_computation.1 | async-start | bytes 1048576 | tf_op jit(solution)/shard_map/all_to_all | solution.py:397
  25.3 0.0 collective-permute-done.refs_0_
  25.3 0.0 copy-start.3
  25.3 0.0 collective-permute-done.1.refs_1_
  25.3 0.0 copy-start.4
  25.4 7.0 %collective-permute-done.2.refs_2_ = bf16[272,1024]{1,0:T(8,128)(2,1)S(1)} collective-permute-done((bf16[272,1024]{1,0:T(8,128)(2,1)}, bf16[272,1024]{1,0:T(8,128)(2,1)S(1)}, u32[]{:S(2)}, u32[]{:S(2)}) %collective-permute-start.2) | collective-permute-done | bytes 557088 | tf_op jit(solution)/shard_map/ppermute | solution.py:396
  32.4 1.5 %all-to-all-done.1 = bf16[16,4,16,256]{3,2,1,0:T(8,128)(2,1)S(1)} async-done(((bf16[16,4,16,256]{3,2,1,0:T(8,128)(2,1)}), bf16[16,4,16,256]{3,2,1,0:T(8,128)(2,1)S(1)}, u32[]{:S(2)}, u32[]{:S(2)}) %all-to-all-start.1) | async-done | bytes 524320 | tf_op jit(solution)/shard_map/all_to_all | solution.py:397
  33.8 0.0 copy-done.5
  33.8 0.8 copy-done.2
  34.6 31.6 %gradients.1 = (bf16[128,1024]{1,0:T(8,128)(2,1)}, bf16[128,1024]{1,0:T(8,128)(2,1)}, bf16[128,1024]{1,0:T(8,128)(2,1)}, bf16[128,1024]{1,0:T(8,128)(2,1)}, bf16[1024,256]{1,0:T(8,128)(2,1)}) custom-call(f32[1,1]{1,0:T(1,128)} %bitcast.9.gate, bf16[1024,256]{1,0:T(8,128)(2,1)} %bitcast.15, bf16[128,4096]{1,0:T(8,128)(2,1)} %bitcast.11, ...), custom_call_target="tpu_custom_call" | custom-call | flops 5368709120 | bytes 4194304 | tf_op jit(solution)/shard_map/gradients/pallas_call | solution.py:276
  66.2 6.7 %all-to-all-start.2 = ((bf16[16,4,16,256]{3,2,1,0:T(8,128)(2,1)}), bf16[16,4,16,256]{3,2,1,0:T(8,128)(2,1)S(1)}, u32[]{:S(2)}, u32[]{:S(2)}) async-start(bf16[16,4,16,256]{3,2,1,0:T(8,128)(2,1)} %bitcast.16), calls=%async_computation.2 | async-start | bytes 1048576 | tf_op jit(solution)/shard_map/all_to_all | solution.py:402
  72.9 2.7 %collective-permute-start.3 = (bf16[128,1024]{1,0:T(8,128)(2,1)S(1)}, bf16[128,1024]{1,0:T(8,128)(2,1)S(1)}, u32[]{:S(2)}, u32[]{:S(2)}) collective-permute-start(bf16[128,1024]{1,0:T(8,128)(2,1)S(1)} %copy-done.8), channel_id=1, source_target_pairs={{0,1},{1,0},{2,3},{3,2},{4,5},{5,4},{6,7},{7,6},{8,9},{9,8},{10,11... | collective-permute-start | bytes 786440 | tf_op jit(solution)/shard_map/ppermute | solution.py:401
  75.5 2.4 %collective-permute-start.4 = (bf16[128,1024]{1,0:T(8,128)(2,1)S(1)}, bf16[128,1024]{1,0:T(8,128)(2,1)S(1)}, u32[]{:S(2)}, u32[]{:S(2)}) collective-permute-start(bf16[128,1024]{1,0:T(8,128)(2,1)S(1)} %copy-done.7), channel_id=1, source_target_pairs={{0,4},{1,5},{2,6},{3,7},{4,0},{5,1},{6,2},{7,3},{8,12},{9,13},{10,... | collective-permute-start | bytes 786440 | tf_op jit(solution)/shard_map/ppermute | solution.py:401
  78.0 0.0 copy-done.6
  78.0 0.1 collective-permute-start.5
  78.1 5.2 %all-to-all-done.2.got = bf16[16,4,16,256]{3,2,1,0:T(8,128)(2,1)S(1)} async-done(((bf16[16,4,16,256]{3,2,1,0:T(8,128)(2,1)}), bf16[16,4,16,256]{3,2,1,0:T(8,128)(2,1)S(1)}, u32[]{:S(2)}, u32[]{:S(2)}) %all-to-all-start.2) | async-done | bytes 524320 | tf_op jit(solution)/shard_map/all_to_all | solution.py:402
  83.3 1.3 %sum.1 = bf16[8,16,1024]{2,1,0:T(8,128)(2,1)} custom-call(s32[32]{0:T(128)S(1)} %copy-done.1, bf16[16,4,16,256]{3,2,1,0:T(8,128)(2,1)S(1)} %all-to-all-done.2.got), custom_call_target="tpu_custom_call" | custom-call | tf_op jit(solution)/shard_map/sum/pallas_call | solution.py:403
  84.6 6.5 %all-to-all-start.3 = ((bf16[8,16,1024]{2,1,0:T(8,128)(2,1)}), bf16[8,16,1024]{2,1,0:T(8,128)(2,1)S(1)}, u32[]{:S(2)}, u32[]{:S(2)}) async-start(bf16[8,16,1024]{2,1,0:T(8,128)(2,1)} %sum.1), calls=%async_computation.3 | async-start | bytes 524288 | tf_op jit(solution)/shard_map/all_to_all | solution.py:404
  91.2 0.0 collective-permute-done.3.refs_1_
  91.2 0.0 collective-permute-done.4.refs_2_
  91.2 0.0 collective-permute-done.5.refs_3_
  91.2 1.1 %merge.1 = bf16[128,4096]{1,0:T(8,128)(2,1)} custom-call(bf16[128,1024]{1,0:T(8,128)(2,1)S(1)} %copy-done, bf16[128,1024]{1,0:T(8,128)(2,1)S(1)} %collective-permute-done.3.refs_1_, bf16[128,1024]{1,0:T(8,128)(2,1)S(1)} %collective-permute-done.4.refs_2_, bf16[128,1024]{1,0:T(8,128)(2,1)S(1)} %collective-permute-done.5.refs_3_), custom_call_target="tpu_custom_call" | custom-call | tf_op jit(solution)/shard_map/merge/pallas_call | solution.py:410
  92.2 5.4 %all-to-all-done.3.got = bf16[8,16,1024]{2,1,0:T(8,128)(2,1)S(1)} async-done(((bf16[8,16,1024]{2,1,0:T(8,128)(2,1)}), bf16[8,16,1024]{2,1,0:T(8,128)(2,1)S(1)}, u32[]{:S(2)}, u32[]{:S(2)}) %all-to-all-start.3) | async-done | bytes 262176 | tf_op jit(solution)/shard_map/all_to_all | solution.py:404
  97.7 1.4 %place.1 = f32[4,16,1024]{2,1,0:T(8,128)} custom-call(s32[32]{0:T(128)S(1)} %copy-done.1, bf16[8,16,1024]{2,1,0:T(8,128)(2,1)S(1)} %all-to-all-done.3.got), custom_call_target="tpu_custom_call" | custom-call | tf_op jit(solution)/shard_map/place/pallas_call | solution.py:405
  (12 shorter events, 0.0 us)
Async XLA Ops:
  3.1 12.3 %all-to-all-start = ((bf16[8,16,1024]{2,1,0:T(8,128)(2,1)}), bf16[8,16,1024]{2,1,0:T(8,128)(2,1)S(1)}, u32[]{:S(2)}, u32[]{:S(2)}) async-start(bf16[8,16,1024]{2,1,0:T(8,128)(2,1)} %get-tuple-element.11), calls=%async_computation | async-start | bytes 524288 | tf_op jit(solution)/shard_map/all_to_all | solution.py:388
  9.0 16.4 %collective-permute-start = (bf16[272,1024]{1,0:T(8,128)(2,1)}, bf16[272,1024]{1,0:T(8,128)(2,1)S(1)}, u32[]{:S(2)}, u32[]{:S(2)}) collective-permute-start(bf16[272,1024]{1,0:T(8,128)(2,1)} %get-tuple-element.12), channel_id=1, source_target_pairs={{0,1},{1,0},{2,3},{3,2},{4,5},{5,4},{6,7},{7,6},{8,9},{9,8},{10,11... | collective-permute-start | bytes 1671176 | tf_op jit(solution)/shard_map/ppermute | solution.py:396
  12.7 2.7 %copy-start.1 = (s32[32]{0:T(128)S(1)}, s32[32]{0:T(128)}, u32[]{:S(2)}) copy-start(s32[32]{0:T(128)} %slots.5) | copy-start | bytes 388
  12.7 12.6 %collective-permute-start.1 = (bf16[272,1024]{1,0:T(8,128)(2,1)}, bf16[272,1024]{1,0:T(8,128)(2,1)S(1)}, u32[]{:S(2)}, u32[]{:S(2)}) collective-permute-start(bf16[272,1024]{1,0:T(8,128)(2,1)} %get-tuple-element.13), channel_id=1, source_target_pairs={{0,4},{1,5},{2,6},{3,7},{4,0},{5,1},{6,2},{7,3},{8,12},{9,13},{10,... | collective-permute-start | bytes 1671176 | tf_op jit(solution)/shard_map/ppermute | solution.py:396
  15.4 16.9 %collective-permute-start.2 = (bf16[272,1024]{1,0:T(8,128)(2,1)}, bf16[272,1024]{1,0:T(8,128)(2,1)S(1)}, u32[]{:S(2)}, u32[]{:S(2)}) collective-permute-start(bf16[272,1024]{1,0:T(8,128)(2,1)} %get-tuple-element.14), channel_id=1, source_target_pairs={{0,5},{1,4},{2,7},{3,6},{4,1},{5,0},{6,3},{7,2},{8,13},{9,12},{10,... | collective-permute-start | bytes 1671176 | tf_op jit(solution)/shard_map/ppermute | solution.py:396
  16.9 16.9 %all-to-all-start.1 = ((bf16[16,4,16,256]{3,2,1,0:T(8,128)(2,1)}), bf16[16,4,16,256]{3,2,1,0:T(8,128)(2,1)S(1)}, u32[]{:S(2)}, u32[]{:S(2)}) async-start(bf16[16,4,16,256]{3,2,1,0:T(8,128)(2,1)} %pick.1), calls=%async_computation.1 | async-start | bytes 1048576 | tf_op jit(solution)/shard_map/all_to_all | solution.py:397
  25.3 8.5 %copy-start.3 = (bf16[272,1024]{1,0:T(8,128)(2,1)}, bf16[272,1024]{1,0:T(8,128)(2,1)S(1)}, u32[]{:S(2)}) copy-start(bf16[272,1024]{1,0:T(8,128)(2,1)S(1)} %collective-permute-done.refs_0_) | copy-start | bytes 1671172
  25.3 8.5 %copy-start.4 = (bf16[272,1024]{1,0:T(8,128)(2,1)}, bf16[272,1024]{1,0:T(8,128)(2,1)S(1)}, u32[]{:S(2)}) copy-start(bf16[272,1024]{1,0:T(8,128)(2,1)S(1)} %collective-permute-done.1.refs_1_) | copy-start | bytes 1671172
  32.4 1.5 %copy-start.5 = (bf16[272,1024]{1,0:T(8,128)(2,1)}, bf16[272,1024]{1,0:T(8,128)(2,1)S(1)}, u32[]{:S(2)}) copy-start(bf16[272,1024]{1,0:T(8,128)(2,1)S(1)} %collective-permute-done.2.refs_2_) | copy-start | bytes 1671172
  33.8 0.8 copy-start.2
  66.2 6.7 %copy-start.8 = (bf16[128,1024]{1,0:T(8,128)(2,1)S(1)}, bf16[128,1024]{1,0:T(8,128)(2,1)}, u32[]{:S(2)}) copy-start(bf16[128,1024]{1,0:T(8,128)(2,1)} %get-tuple-element.16) | copy-start | bytes 786436
  66.2 9.4 %copy-start.7 = (bf16[128,1024]{1,0:T(8,128)(2,1)S(1)}, bf16[128,1024]{1,0:T(8,128)(2,1)}, u32[]{:S(2)}) copy-start(bf16[128,1024]{1,0:T(8,128)(2,1)} %get-tuple-element.17) | copy-start | bytes 786436
  66.2 11.7 %copy-start.6 = (bf16[128,1024]{1,0:T(8,128)(2,1)S(1)}, bf16[128,1024]{1,0:T(8,128)(2,1)}, u32[]{:S(2)}) copy-start(bf16[128,1024]{1,0:T(8,128)(2,1)} %get-tuple-element.18) | copy-start | bytes 786436
  66.2 17.1 %all-to-all-start.2 = ((bf16[16,4,16,256]{3,2,1,0:T(8,128)(2,1)}), bf16[16,4,16,256]{3,2,1,0:T(8,128)(2,1)S(1)}, u32[]{:S(2)}, u32[]{:S(2)}) async-start(bf16[16,4,16,256]{3,2,1,0:T(8,128)(2,1)} %bitcast.16), calls=%async_computation.2 | async-start | bytes 1048576 | tf_op jit(solution)/shard_map/all_to_all | solution.py:402
  72.9 18.3 %collective-permute-start.3 = (bf16[128,1024]{1,0:T(8,128)(2,1)S(1)}, bf16[128,1024]{1,0:T(8,128)(2,1)S(1)}, u32[]{:S(2)}, u32[]{:S(2)}) collective-permute-start(bf16[128,1024]{1,0:T(8,128)(2,1)S(1)} %copy-done.8), channel_id=1, source_target_pairs={{0,1},{1,0},{2,3},{3,2},{4,5},{5,4},{6,7},{7,6},{8,9},{9,8},{10,11... | collective-permute-start | bytes 786440 | tf_op jit(solution)/shard_map/ppermute | solution.py:401
  75.5 15.6 %collective-permute-start.4 = (bf16[128,1024]{1,0:T(8,128)(2,1)S(1)}, bf16[128,1024]{1,0:T(8,128)(2,1)S(1)}, u32[]{:S(2)}, u32[]{:S(2)}) collective-permute-start(bf16[128,1024]{1,0:T(8,128)(2,1)S(1)} %copy-done.7), channel_id=1, source_target_pairs={{0,4},{1,5},{2,6},{3,7},{4,0},{5,1},{6,2},{7,3},{8,12},{9,13},{10,... | collective-permute-start | bytes 786440 | tf_op jit(solution)/shard_map/ppermute | solution.py:401
  78.0 13.2 %collective-permute-start.5 = (bf16[128,1024]{1,0:T(8,128)(2,1)S(1)}, bf16[128,1024]{1,0:T(8,128)(2,1)S(1)}, u32[]{:S(2)}, u32[]{:S(2)}) collective-permute-start(bf16[128,1024]{1,0:T(8,128)(2,1)S(1)} %copy-done.6), channel_id=1, source_target_pairs={{0,5},{1,4},{2,7},{3,6},{4,1},{5,0},{6,3},{7,2},{8,13},{9,12},{10,... | collective-permute-start | bytes 786440 | tf_op jit(solution)/shard_map/ppermute | solution.py:401
  84.6 6.6 %copy-start = (bf16[128,1024]{1,0:T(8,128)(2,1)S(1)}, bf16[128,1024]{1,0:T(8,128)(2,1)}, u32[]{:S(2)}) copy-start(bf16[128,1024]{1,0:T(8,128)(2,1)} %get-tuple-element.15.refs_0_) | copy-start | bytes 786436
  84.6 13.0 %all-to-all-start.3 = ((bf16[8,16,1024]{2,1,0:T(8,128)(2,1)}), bf16[8,16,1024]{2,1,0:T(8,128)(2,1)S(1)}, u32[]{:S(2)}, u32[]{:S(2)}) async-start(bf16[8,16,1024]{2,1,0:T(8,128)(2,1)} %sum.1), calls=%async_computation.3 | async-start | bytes 524288 | tf_op jit(solution)/shard_map/all_to_all | solution.py:404

commit v14 on v13

--- a/solution.py
+++ b/solution.py
@@ -17,7 +17,7 @@
 SCALE = WIDTH ** (-0.5)
 GRID = 4
 BLOCK = 4
-BATCH_HEADS = 2
+BATCH_HEADS = 4
 PAD = 16
 VMEM_LIMIT = 48 * 1024 * 1024
 GRADIENT_VMEM = 60 * 1024 * 1024

time: 99.7 us -> 99.7 us (level)
  no operation moved by 1% of the time
where the time goes in v14:
time: 99.7 us; the launch traced here: 99.1 us
  Pallas kernels  39.3 us (39%)
  starting transfers between devices  38.4 us (39%)
  waiting for transfers between devices  19.1 us (19%)
  between operations  1.41 us (1%)
    pallas_call x1, Pallas kernels, gradients(): pl.pallas_call(grad_kernel, in_specs=[pl.BlockSpec(memory_space=VMEM)] +...  31.6 us
    all_to_all x2, starting transfers between devices, shards(): got = lax.all_to_all(send, 'doc', 0, 0)  12.3 us
    all_to_all x1, starting transfers between devices, shards(): lax.all_to_all(send, 'ctx', 0, 0).reshape(texts * images * rows, 2 * WIDTH)  7.77 us
    ppermute x3, waiting for transfers between devices, shards(): lax.ppermute(pieces[k - 1], both, swap(docs, k))  7.01 us
    all_to_all x1, starting transfers between devices, shards(): lax.all_to_all(dkv.reshape(texts, images, rows, 2 * WIDTH), 'ctx', 0, 0)  6.66 us
    ppermute x3, starting transfers between devices, shards(): lax.ppermute(pieces[k - 1], both, swap(docs, k))  6.49 us
    all_to_all x2, waiting for transfers between devices, shards(): got = lax.all_to_all(send, 'doc', 0, 0)  5.41 us
    all_to_all x1, waiting for transfers between devices, shards(): lax.all_to_all(dkv.reshape(texts, images, rows, 2 * WIDTH), 'ctx', 0, 0)  5.22 us
  transfers between devices with their start and end apart: 10, of which 4 were waited for; matrix products, arithmetic and copies ran while one was open for 0% of the time, Pallas kernels for 4%

profile of v14, /device:TPU:1, one launch (start us, length us, event | category | flops | bytes accessed | tf_op | source)
XLA Modules:
  0.0 99.1 jit_solution(7412890064162366140)
XLA Ops:
  0.6 2.5 %prepare.1 = (bf16[8,16,1024]{2,1,0:T(8,128)(2,1)}, bf16[272,1024]{1,0:T(8,128)(2,1)}, bf16[272,1024]{1,0:T(8,128)(2,1)}, bf16[272,1024]{1,0:T(8,128)(2,1)}) custom-call(s32[32]{0:T(128)} %slots.5, bf16[4,16,1024]{2,1,0:T(8,128)(2,1)} %kv.1, bf16[128,4096]{1,0:T(8,128)(2,1)} %bitcast.10, bf16[128,4096]{1,0:T(8,128)(2,1)} %bitcast.12, s32[2,128]{1,0:T(2,128)} %bitcast.17), custom_call_target="tpu_custom_call" | custom-call | tf_op jit(solution)/shard_map/prepare/pallas_call | solution.py:373
  3.1 5.8 %all-to-all-start = ((bf16[8,16,1024]{2,1,0:T(8,128)(2,1)}), bf16[8,16,1024]{2,1,0:T(8,128)(2,1)S(1)}, u32[]{:S(2)}, u32[]{:S(2)}) async-start(bf16[8,16,1024]{2,1,0:T(8,128)(2,1)} %get-tuple-element.11), calls=%async_computation | async-start | bytes 524288 | tf_op jit(solution)/shard_map/all_to_all | solution.py:388
  9.0 3.8 %collective-permute-start = (bf16[272,1024]{1,0:T(8,128)(2,1)}, bf16[272,1024]{1,0:T(8,128)(2,1)S(1)}, u32[]{:S(2)}, u32[]{:S(2)}) collective-permute-start(bf16[272,1024]{1,0:T(8,128)(2,1)} %get-tuple-element.12), channel_id=1, source_target_pairs={{0,1},{1,0},{2,3},{3,2},{4,5},{5,4},{6,7},{7,6},{8,9},{9,8},{10,11... | collective-permute-start | bytes 1671176 | tf_op jit(solution)/shard_map/ppermute | solution.py:396
  12.7 2.7 %collective-permute-start.1 = (bf16[272,1024]{1,0:T(8,128)(2,1)}, bf16[272,1024]{1,0:T(8,128)(2,1)S(1)}, u32[]{:S(2)}, u32[]{:S(2)}) collective-permute-start(bf16[272,1024]{1,0:T(8,128)(2,1)} %get-tuple-element.13), channel_id=1, source_target_pairs={{0,4},{1,5},{2,6},{3,7},{4,0},{5,1},{6,2},{7,3},{8,12},{9,13},{10,... | collective-permute-start | bytes 1671176 | tf_op jit(solution)/shard_map/ppermute | solution.py:396
  15.4 0.0 collective-permute-start.2
  15.5 0.0 all-to-all-done.got
  15.5 0.0 copy-done.1
  15.5 1.4 %pick.1 = bf16[16,4,16,256]{3,2,1,0:T(8,128)(2,1)} custom-call(s32[32]{0:T(128)S(1)} %copy-done.1, bf16[8,16,1024]{2,1,0:T(8,128)(2,1)S(1)} %all-to-all-done.got), custom_call_target="tpu_custom_call" | custom-call | tf_op jit(solution)/shard_map/pick/pallas_call | solution.py:390
  16.9 7.8 %all-to-all-start.1 = ((bf16[16,4,16,256]{3,2,1,0:T(8,128)(2,1)}), bf16[16,4,16,256]{3,2,1,0:T(8,128)(2,1)S(1)}, u32[]{:S(2)}, u32[]{:S(2)}) async-start(bf16[16,4,16,256]{3,2,1,0:T(8,128)(2,1)} %pick.1), calls=%async_computation.1 | async-start | bytes 1048576 | tf_op jit(solution)/shard_map/all_to_all | solution.py:397
  25.3 0.0 collective-permute-done.refs_0_
  25.3 0.0 copy-start.3
  25.3 0.0 collective-permute-done.1.refs_1_
  25.3 0.0 copy-start.4
  25.4 7.0 %collective-permute-done.2.refs_2_ = bf16[272,1024]{1,0:T(8,128)(2,1)S(1)} collective-permute-done((bf16[272,1024]{1,0:T(8,128)(2,1)}, bf16[272,1024]{1,0:T(8,128)(2,1)S(1)}, u32[]{:S(2)}, u32[]{:S(2)}) %collective-permute-start.2) | collective-permute-done | bytes 557088 | tf_op jit(solution)/shard_map/ppermute | solution.py:396
  32.4 1.5 %all-to-all-done.1 = bf16[16,4,16,256]{3,2,1,0:T(8,128)(2,1)S(1)} async-done(((bf16[16,4,16,256]{3,2,1,0:T(8,128)(2,1)}), bf16[16,4,16,256]{3,2,1,0:T(8,128)(2,1)S(1)}, u32[]{:S(2)}, u32[]{:S(2)}) %all-to-all-start.1) | async-done | bytes 524320 | tf_op jit(solution)/shard_map/all_to_all | solution.py:397
  33.8 0.0 copy-done.5
  33.8 0.8 copy-done.2
  34.6 31.6 %gradients.1 = (bf16[128,1024]{1,0:T(8,128)(2,1)}, bf16[128,1024]{1,0:T(8,128)(2,1)}, bf16[128,1024]{1,0:T(8,128)(2,1)}, bf16[128,1024]{1,0:T(8,128)(2,1)}, bf16[1024,256]{1,0:T(8,128)(2,1)}) custom-call(f32[1,1]{1,0:T(1,128)} %bitcast.9.gate, bf16[1024,256]{1,0:T(8,128)(2,1)} %bitcast.15, bf16[128,4096]{1,0:T(8,128)(2,1)} %bitcast.11, ...), custom_call_target="tpu_custom_call" | custom-call | flops 5368709120 | bytes 4194304 | tf_op jit(solution)/shard_map/gradients/pallas_call | solution.py:276
  66.2 6.7 %all-to-all-start.2 = ((bf16[16,4,16,256]{3,2,1,0:T(8,128)(2,1)}), bf16[16,4,16,256]{3,2,1,0:T(8,128)(2,1)S(1)}, u32[]{:S(2)}, u32[]{:S(2)}) async-start(bf16[16,4,16,256]{3,2,1,0:T(8,128)(2,1)} %bitcast.16), calls=%async_computation.2 | async-start | bytes 1048576 | tf_op jit(solution)/shard_map/all_to_all | solution.py:402
  72.9 2.7 %collective-permute-start.3 = (bf16[128,1024]{1,0:T(8,128)(2,1)S(1)}, bf16[128,1024]{1,0:T(8,128)(2,1)S(1)}, u32[]{:S(2)}, u32[]{:S(2)}) collective-permute-start(bf16[128,1024]{1,0:T(8,128)(2,1)S(1)} %copy-done.8), channel_id=1, source_target_pairs={{0,1},{1,0},{2,3},{3,2},{4,5},{5,4},{6,7},{7,6},{8,9},{9,8},{10,11... | collective-permute-start | bytes 786440 | tf_op jit(solution)/shard_map/ppermute | solution.py:401
  75.5 2.4 %collective-permute-start.4 = (bf16[128,1024]{1,0:T(8,128)(2,1)S(1)}, bf16[128,1024]{1,0:T(8,128)(2,1)S(1)}, u32[]{:S(2)}, u32[]{:S(2)}) collective-permute-start(bf16[128,1024]{1,0:T(8,128)(2,1)S(1)} %copy-done.7), channel_id=1, source_target_pairs={{0,4},{1,5},{2,6},{3,7},{4,0},{5,1},{6,2},{7,3},{8,12},{9,13},{10,... | collective-permute-start | bytes 786440 | tf_op jit(solution)/shard_map/ppermute | solution.py:401
  78.0 0.0 copy-done.6
  78.0 0.1 collective-permute-start.5
  78.1 5.2 %all-to-all-done.2.got = bf16[16,4,16,256]{3,2,1,0:T(8,128)(2,1)S(1)} async-done(((bf16[16,4,16,256]{3,2,1,0:T(8,128)(2,1)}), bf16[16,4,16,256]{3,2,1,0:T(8,128)(2,1)S(1)}, u32[]{:S(2)}, u32[]{:S(2)}) %all-to-all-start.2) | async-done | bytes 524320 | tf_op jit(solution)/shard_map/all_to_all | solution.py:402
  83.3 1.3 %sum.1 = bf16[8,16,1024]{2,1,0:T(8,128)(2,1)} custom-call(s32[32]{0:T(128)S(1)} %copy-done.1, bf16[16,4,16,256]{3,2,1,0:T(8,128)(2,1)S(1)} %all-to-all-done.2.got), custom_call_target="tpu_custom_call" | custom-call | tf_op jit(solution)/shard_map/sum/pallas_call | solution.py:403
  84.6 6.5 %all-to-all-start.3 = ((bf16[8,16,1024]{2,1,0:T(8,128)(2,1)}), bf16[8,16,1024]{2,1,0:T(8,128)(2,1)S(1)}, u32[]{:S(2)}, u32[]{:S(2)}) async-start(bf16[8,16,1024]{2,1,0:T(8,128)(2,1)} %sum.1), calls=%async_computation.3 | async-start | bytes 524288 | tf_op jit(solution)/shard_map/all_to_all | solution.py:404
  91.2 0.0 collective-permute-done.3.refs_1_
  91.2 0.0 collective-permute-done.4.refs_2_
  91.2 0.0 collective-permute-done.5.refs_3_
  91.2 1.1 %merge.1 = bf16[128,4096]{1,0:T(8,128)(2,1)} custom-call(bf16[128,1024]{1,0:T(8,128)(2,1)S(1)} %copy-done, bf16[128,1024]{1,0:T(8,128)(2,1)S(1)} %collective-permute-done.3.refs_1_, bf16[128,1024]{1,0:T(8,128)(2,1)S(1)} %collective-permute-done.4.refs_2_, bf16[128,1024]{1,0:T(8,128)(2,1)S(1)} %collective-permute-done.5.refs_3_), custom_call_target="tpu_custom_call" | custom-call | tf_op jit(solution)/shard_map/merge/pallas_call | solution.py:410
  92.2 5.4 %all-to-all-done.3.got = bf16[8,16,1024]{2,1,0:T(8,128)(2,1)S(1)} async-done(((bf16[8,16,1024]{2,1,0:T(8,128)(2,1)}), bf16[8,16,1024]{2,1,0:T(8,128)(2,1)S(1)}, u32[]{:S(2)}, u32[]{:S(2)}) %all-to-all-start.3) | async-done | bytes 262176 | tf_op jit(solution)/shard_map/all_to_all | solution.py:404
  97.7 1.4 %place.1 = f32[4,16,1024]{2,1,0:T(8,128)} custom-call(s32[32]{0:T(128)S(1)} %copy-done.1, bf16[8,16,1024]{2,1,0:T(8,128)(2,1)S(1)} %all-to-all-done.3.got), custom_call_target="tpu_custom_call" | custom-call | tf_op jit(solution)/shard_map/place/pallas_call | solution.py:405
  (12 shorter events, 0.0 us)
Async XLA Ops:
  3.1 12.3 %all-to-all-start = ((bf16[8,16,1024]{2,1,0:T(8,128)(2,1)}), bf16[8,16,1024]{2,1,0:T(8,128)(2,1)S(1)}, u32[]{:S(2)}, u32[]{:S(2)}) async-start(bf16[8,16,1024]{2,1,0:T(8,128)(2,1)} %get-tuple-element.11), calls=%async_computation | async-start | bytes 524288 | tf_op jit(solution)/shard_map/all_to_all | solution.py:388
  9.0 16.4 %collective-permute-start = (bf16[272,1024]{1,0:T(8,128)(2,1)}, bf16[272,1024]{1,0:T(8,128)(2,1)S(1)}, u32[]{:S(2)}, u32[]{:S(2)}) collective-permute-start(bf16[272,1024]{1,0:T(8,128)(2,1)} %get-tuple-element.12), channel_id=1, source_target_pairs={{0,1},{1,0},{2,3},{3,2},{4,5},{5,4},{6,7},{7,6},{8,9},{9,8},{10,11... | collective-permute-start | bytes 1671176 | tf_op jit(solution)/shard_map/ppermute | solution.py:396
  12.7 2.7 %copy-start.1 = (s32[32]{0:T(128)S(1)}, s32[32]{0:T(128)}, u32[]{:S(2)}) copy-start(s32[32]{0:T(128)} %slots.5) | copy-start | bytes 388
  12.7 12.6 %collective-permute-start.1 = (bf16[272,1024]{1,0:T(8,128)(2,1)}, bf16[272,1024]{1,0:T(8,128)(2,1)S(1)}, u32[]{:S(2)}, u32[]{:S(2)}) collective-permute-start(bf16[272,1024]{1,0:T(8,128)(2,1)} %get-tuple-element.13), channel_id=1, source_target_pairs={{0,4},{1,5},{2,6},{3,7},{4,0},{5,1},{6,2},{7,3},{8,12},{9,13},{10,... | collective-permute-start | bytes 1671176 | tf_op jit(solution)/shard_map/ppermute | solution.py:396
  15.4 16.9 %collective-permute-start.2 = (bf16[272,1024]{1,0:T(8,128)(2,1)}, bf16[272,1024]{1,0:T(8,128)(2,1)S(1)}, u32[]{:S(2)}, u32[]{:S(2)}) collective-permute-start(bf16[272,1024]{1,0:T(8,128)(2,1)} %get-tuple-element.14), channel_id=1, source_target_pairs={{0,5},{1,4},{2,7},{3,6},{4,1},{5,0},{6,3},{7,2},{8,13},{9,12},{10,... | collective-permute-start | bytes 1671176 | tf_op jit(solution)/shard_map/ppermute | solution.py:396
  16.9 16.9 %all-to-all-start.1 = ((bf16[16,4,16,256]{3,2,1,0:T(8,128)(2,1)}), bf16[16,4,16,256]{3,2,1,0:T(8,128)(2,1)S(1)}, u32[]{:S(2)}, u32[]{:S(2)}) async-start(bf16[16,4,16,256]{3,2,1,0:T(8,128)(2,1)} %pick.1), calls=%async_computation.1 | async-start | bytes 1048576 | tf_op jit(solution)/shard_map/all_to_all | solution.py:397
  25.3 8.5 %copy-start.3 = (bf16[272,1024]{1,0:T(8,128)(2,1)}, bf16[272,1024]{1,0:T(8,128)(2,1)S(1)}, u32[]{:S(2)}) copy-start(bf16[272,1024]{1,0:T(8,128)(2,1)S(1)} %collective-permute-done.refs_0_) | copy-start | bytes 1671172
  25.3 8.5 %copy-start.4 = (bf16[272,1024]{1,0:T(8,128)(2,1)}, bf16[272,1024]{1,0:T(8,128)(2,1)S(1)}, u32[]{:S(2)}) copy-start(bf16[272,1024]{1,0:T(8,128)(2,1)S(1)} %collective-permute-done.1.refs_1_) | copy-start | bytes 1671172
  32.4 1.5 %copy-start.5 = (bf16[272,1024]{1,0:T(8,128)(2,1)}, bf16[272,1024]{1,0:T(8,128)(2,1)S(1)}, u32[]{:S(2)}) copy-start(bf16[272,1024]{1,0:T(8,128)(2,1)S(1)} %collective-permute-done.2.refs_2_) | copy-start | bytes 1671172
  33.8 0.8 copy-start.2
  66.2 6.7 %copy-start.8 = (bf16[128,1024]{1,0:T(8,128)(2,1)S(1)}, bf16[128,1024]{1,0:T(8,128)(2,1)}, u32[]{:S(2)}) copy-start(bf16[128,1024]{1,0:T(8,128)(2,1)} %get-tuple-element.16) | copy-start | bytes 786436
  66.2 9.4 %copy-start.7 = (bf16[128,1024]{1,0:T(8,128)(2,1)S(1)}, bf16[128,1024]{1,0:T(8,128)(2,1)}, u32[]{:S(2)}) copy-start(bf16[128,1024]{1,0:T(8,128)(2,1)} %get-tuple-element.17) | copy-start | bytes 786436
  66.2 11.7 %copy-start.6 = (bf16[128,1024]{1,0:T(8,128)(2,1)S(1)}, bf16[128,1024]{1,0:T(8,128)(2,1)}, u32[]{:S(2)}) copy-start(bf16[128,1024]{1,0:T(8,128)(2,1)} %get-tuple-element.18) | copy-start | bytes 786436
  66.2 17.1 %all-to-all-start.2 = ((bf16[16,4,16,256]{3,2,1,0:T(8,128)(2,1)}), bf16[16,4,16,256]{3,2,1,0:T(8,128)(2,1)S(1)}, u32[]{:S(2)}, u32[]{:S(2)}) async-start(bf16[16,4,16,256]{3,2,1,0:T(8,128)(2,1)} %bitcast.16), calls=%async_computation.2 | async-start | bytes 1048576 | tf_op jit(solution)/shard_map/all_to_all | solution.py:402
  72.9 18.3 %collective-permute-start.3 = (bf16[128,1024]{1,0:T(8,128)(2,1)S(1)}, bf16[128,1024]{1,0:T(8,128)(2,1)S(1)}, u32[]{:S(2)}, u32[]{:S(2)}) collective-permute-start(bf16[128,1024]{1,0:T(8,128)(2,1)S(1)} %copy-done.8), channel_id=1, source_target_pairs={{0,1},{1,0},{2,3},{3,2},{4,5},{5,4},{6,7},{7,6},{8,9},{9,8},{10,11... | collective-permute-start | bytes 786440 | tf_op jit(solution)/shard_map/ppermute | solution.py:401
  75.5 15.6 %collective-permute-start.4 = (bf16[128,1024]{1,0:T(8,128)(2,1)S(1)}, bf16[128,1024]{1,0:T(8,128)(2,1)S(1)}, u32[]{:S(2)}, u32[]{:S(2)}) collective-permute-start(bf16[128,1024]{1,0:T(8,128)(2,1)S(1)} %copy-done.7), channel_id=1, source_target_pairs={{0,4},{1,5},{2,6},{3,7},{4,0},{5,1},{6,2},{7,3},{8,12},{9,13},{10,... | collective-permute-start | bytes 786440 | tf_op jit(solution)/shard_map/ppermute | solution.py:401
  78.0 13.2 %collective-permute-start.5 = (bf16[128,1024]{1,0:T(8,128)(2,1)S(1)}, bf16[128,1024]{1,0:T(8,128)(2,1)S(1)}, u32[]{:S(2)}, u32[]{:S(2)}) collective-permute-start(bf16[128,1024]{1,0:T(8,128)(2,1)S(1)} %copy-done.6), channel_id=1, source_target_pairs={{0,5},{1,4},{2,7},{3,6},{4,1},{5,0},{6,3},{7,2},{8,13},{9,12},{10,... | collective-permute-start | bytes 786440 | tf_op jit(solution)/shard_map/ppermute | solution.py:401
  84.6 6.6 %copy-start = (bf16[128,1024]{1,0:T(8,128)(2,1)S(1)}, bf16[128,1024]{1,0:T(8,128)(2,1)}, u32[]{:S(2)}) copy-start(bf16[128,1024]{1,0:T(8,128)(2,1)} %get-tuple-element.15.refs_0_) | copy-start | bytes 786436
  84.6 13.0 %all-to-all-start.3 = ((bf16[8,16,1024]{2,1,0:T(8,128)(2,1)}), bf16[8,16,1024]{2,1,0:T(8,128)(2,1)S(1)}, u32[]{:S(2)}, u32[]{:S(2)}) async-start(bf16[8,16,1024]{2,1,0:T(8,128)(2,1)} %sum.1), calls=%async_computation.3 | async-start | bytes 524288 | tf_op jit(solution)/shard_map/all_to_all | solution.py:404
